TPU v7x, 512 devices: a whole 4x4x16 slice. The times are simulated.
512 devices in a mesh: tile: 128 (over z, x, core), grp: 4 (over y).
Axes of the slice: x: 4, y: 4, z: 16, core: 2. Of those that a mesh axis runs over, the one named last changes fastest.
Arguments:
- features: bfloat16 [4, 512, 64, 512], P('grp', 'tile'), may hold values from -6 to 6
- brick_count: int32 [4, 128], P('grp', 'tile'), may hold values from 1 to 4, as said below
- send_list: int32 [4, 128, 4, 4], P('grp', 'tile'), may hold values from 0 to 24, as said below
- halo_src: int32 [4, 512, 26], P('grp', 'tile'), may hold values from 0 to 40, as said below
- kernel: bfloat16 [64, 1728], replicated, may hold values from -0.15625 to 0.15625
- down_kernel: bfloat16 [128, 512], replicated, may hold values from -0.25 to 0.25
- out_grad: bfloat16 [4, 512, 64, 128], P('grp', 'tile'), may hold values from -6 to 6
Outputs:
- coarse: bfloat16 [4, 512, 64, 128], P('grp', 'tile')
- grad_features: bfloat16 [4, 512, 64, 512], P('grp', 'tile')
- grad_kernel: float32 [64, 1728], replicated
- grad_down: float32 [128, 512], replicated
Inputs may be any that keep to these rules, and one draw needn't show every extreme that they name: `brick_count`: some device of every region holds all 4 slots occupied. `send_list`: used places hold 6 s + f for an occupied slot s and face f and come first; 24 marks an unused place; places towards offsets that leave the tile axis are unused; some device of every region fills all 4 places towards every offset. `halo_src`: entries below 24 name local faces, 24 a zero block, larger ones used received places.
All inputs are finite; a program needn't handle non-finite values.
Results may differ from a plain program's by a relative error of at most 0.005.
Values may be sent and summed in bfloat16 or wider, within the bound.
No kernel may reach another device: no remote copies, remote signals or barrier semaphores. Data moves between devices by JAX's collectives and lax.ppermute only.
A program may use at most 64 MiB of HBM per device.

v0:
```python
import jax
import jax.numpy as jnp
from jax import lax
from jax.sharding import PartitionSpec as P

DIRECTIONS = [
    (a, b, c) for a in (-1, 0, 1) for b in (-1, 0, 1) for c in (-1, 0, 1) if (a, b, c) != (0, 0, 0)
]
STENCIL = [(a, b, c) for a in (-1, 0, 1) for b in (-1, 0, 1) for c in (-1, 0, 1)]


def from_behind(block, axis, distance):
    devices = range(lax.axis_size(axis))
    route = [(i - distance, i) for i in devices if i - distance in devices]
    return lax.ppermute(block, axis, route)


def target_slices(direction):
    return tuple(
        (slice(0, 1) if s == -1 else slice(9, 10) if s == 1 else slice(1, 9) for s in direction)
    )


def face_select(direction):
    leading = [i for i in range(3) if direction[i] != 0][0]
    others = [i for i in range(3) if i != leading]
    chosen = tuple(
        (
            slice(0, 1) if direction[i] == 1 else slice(7, 8) if direction[i] == -1 else slice(0, 8)
            for i in others
        )
    )
    return (leading, chosen)


def pad_brick(brick_cube, entries):
    channels = brick_cube.shape[0]
    padded = jnp.pad(brick_cube.reshape(channels, 8, 8, 8), ((0, 0), (1, 1), (1, 1), (1, 1)))
    for position, direction in enumerate(DIRECTIONS):
        leading, chosen = face_select(direction)
        face_piece = entries[position].reshape(channels, 8, 8)[(slice(None),) + chosen]
        face_piece = jnp.expand_dims(face_piece, 1 + leading)
        padded = padded.at[(slice(None),) + target_slices(direction)].set(face_piece)
    return padded


def unfold_brick(padded):
    channels = padded.shape[0]
    return jnp.concatenate(
        [
            padded[:, 1 + a : 9 + a, 1 + b : 9 + b, 1 + c : 9 + c].reshape(channels, 512)
            for a, b, c in STENCIL
        ],
        axis=0,
    )


def fold_columns(columns, channels):
    result = jnp.zeros((channels, 10, 10, 10), jnp.float32)
    for position, (a, b, c) in enumerate(STENCIL):
        part_cols = columns[position * channels : (position + 1) * channels].reshape(
            channels, 8, 8, 8
        )
        result = result.at[:, 1 + a : 9 + a, 1 + b : 9 + b, 1 + c : 9 + c].add(part_cols)
    return result


def rim_grad(grad_pad, direction):
    channels = grad_pad.shape[0]
    leading, chosen = face_select(direction)
    region = jnp.squeeze(grad_pad[(slice(None),) + target_slices(direction)], axis=1 + leading)
    grad_block = jnp.zeros((channels, 8, 8), jnp.float32).at[(slice(None),) + chosen].set(region)
    return grad_block.reshape(channels, 64)


def down_columns(active):
    channels = active.shape[0]
    return (
        active.reshape(channels, 4, 2, 4, 2, 4, 2)
        .transpose(2, 4, 6, 0, 1, 3, 5)
        .reshape(8 * channels, 64)
    )


def up_columns(columns, channels):
    return (
        columns.reshape(2, 2, 2, channels, 4, 4, 4)
        .transpose(3, 4, 0, 5, 1, 6, 2)
        .reshape(channels, 512)
    )


def face_table(brick_cubes):
    brick_total, channels = (brick_cubes.shape[0], brick_cubes.shape[1])
    shaped = brick_cubes.reshape(brick_total, channels, 8, 8, 8)
    layers = [jnp.take(shaped, 7 * e, axis=2 + a) for a in range(3) for e in range(2)]
    stacked = jnp.stack(layers, axis=1).reshape(brick_total * 6, channels, 64)
    return jnp.concatenate([stacked, jnp.zeros((1, channels, 64), brick_cubes.dtype)], axis=0)


def add_faces(interior, grad_faces):
    brick_total, channels = (interior.shape[0], interior.shape[1])
    shaped = interior.reshape(brick_total, channels, 8, 8, 8)
    layered = grad_faces.reshape(brick_total, 6, channels, 8, 8)
    for a in range(3):
        for e in range(2):
            spot = [slice(None)] * 5
            spot[2 + a] = 7 * e
            shaped = shaped.at[tuple(spot)].add(layered[:, 2 * a + e])
    return shaped.reshape(brick_total, channels, 512)


def scatter_rows(values, targets, row_total):
    return jax.ops.segment_sum(values, targets, num_segments=row_total)


def on_device(features, brick_count, send_list, halo_src, kernel, down_kernel, out_grad):
    slot_total = features.shape[1]
    channels = features.shape[2]
    reach = send_list.shape[2] // 2
    capacity = send_list.shape[3]
    offsets = [o for step in range(1, reach + 1) for o in (step, -step)]
    occupied = (jnp.arange(slot_total) < brick_count[0, 0]).astype(jnp.float32)
    masked = features[0] * occupied[:, None, None].astype(jnp.bfloat16)
    faces = face_table(masked)
    remote_start = 6 * slot_total + 1
    received = []
    for j, offset in enumerate(offsets):
        outgoing = faces[send_list[0, 0, j]]
        received.append(from_behind(outgoing, "tile", offset))
    halo_table = jnp.concatenate([faces] + received, axis=0)
    dims_first = (((0,), (1,)), ((), ()))

    def per_brick(totals, brick_items):
        brick_cube, source_row, filled, grad_out = brick_items
        padded = pad_brick(brick_cube, halo_table[source_row])
        columns = unfold_brick(padded)
        preact = jnp.dot(kernel, columns, preferred_element_type=jnp.float32)
        sigmoid_part = jax.nn.sigmoid(preact)
        active = (preact * sigmoid_part * filled).astype(jnp.bfloat16)
        lowered = down_columns(active)
        coarse = lax.dot_general(
            lowered, down_kernel, dims_first, preferred_element_type=jnp.float32
        ).astype(jnp.bfloat16)
        grad_down = lax.dot_general(
            grad_out, lowered, (((0,), (1,)), ((), ())), preferred_element_type=jnp.float32
        )
        grad_low = lax.dot_general(
            down_kernel, grad_out, (((0,), (1,)), ((), ())), preferred_element_type=jnp.float32
        )
        grad_active = up_columns(grad_low, channels)
        grad_preact = (
            grad_active * sigmoid_part * (1.0 + preact * (1.0 - sigmoid_part)) * filled
        ).astype(jnp.bfloat16)
        grad_kernel = lax.dot_general(
            grad_preact, columns, (((1,), (1,)), ((), ())), preferred_element_type=jnp.float32
        )
        grad_cols = lax.dot_general(
            kernel, grad_preact, (((0,), (0,)), ((), ())), preferred_element_type=jnp.float32
        )
        grad_pad = fold_columns(grad_cols, channels)
        interior = grad_pad[:, 1:9, 1:9, 1:9].reshape(channels, 512)
        rims = jnp.stack([rim_grad(grad_pad, direction) for direction in DIRECTIONS])
        return ((totals[0] + grad_kernel, totals[1] + grad_down), (coarse, interior, rims))

    start = (jnp.zeros(kernel.shape, jnp.float32), jnp.zeros(down_kernel.shape, jnp.float32))
    sources = halo_src[0]
    (grad_kernel, grad_down), (coarse, interior, rims) = lax.scan(
        per_brick, start, (masked, sources, occupied, out_grad[0])
    )
    grad_table = scatter_rows(
        rims.reshape(-1, channels, 64), sources.reshape(-1), halo_table.shape[0]
    )
    grad_faces = grad_table[:remote_start]
    for j, offset in enumerate(offsets):
        grad_block = grad_table[remote_start + j * capacity : remote_start + (j + 1) * capacity]
        returned = from_behind(grad_block.astype(jnp.bfloat16), "tile", -offset).astype(
            grad_block.dtype
        )
        grad_faces = grad_faces + scatter_rows(returned, send_list[0, 0, j], remote_start)
    grad_cubes = add_faces(interior, grad_faces[: 6 * slot_total]) * occupied[:, None, None]
    grad_kernel, grad_down = lax.psum((grad_kernel, grad_down), ("tile", "grp"))
    return (coarse[None], grad_cubes.astype(jnp.bfloat16)[None], grad_kernel, grad_down)


def solution(mesh):
    in_specs = (
        P("grp", "tile", None, None),
        P("grp", "tile"),
        P("grp", "tile", None, None),
        P("grp", "tile", None),
        P(),
        P(),
        P("grp", "tile", None, None),
    )
    out_specs = (P("grp", "tile", None, None), P("grp", "tile", None, None), P(), P())
    return jax.shard_map(
        on_device, mesh=mesh, in_specs=in_specs, out_specs=out_specs, check_vma=False
    )
```

profile of v0, /device:TPU:1, one launch (start us, length us, event | category | flops | bytes accessed | tf_op | source)
XLA Modules:
  0.0 770.8 jit_solution(523943618229443696)
XLA Ops:
  7.2 1.2 copy.318
  10.3 4.5 collective-permute-start
  15.4 5.6 collective-permute-start.1
  21.6 1.3 collective-permute-start.2
  23.5 1.3 collective-permute-start.3
  26.0 3.2 collective-permute-done.3
  30.3 223.2 %while.119 = (s32[]{:T(128)}, f32[64,1728]{1,0:T(8,128)S(1)}, f32[128,512]{1,0:T(8,128)}, bf16[4,64,128]{2,1,0:T(8,128)(2,1)}, f32[4,64,512]{1,2,0:T(8,128)}, /*...) while((s32[]{:T(128)}, f32[64,1728]{1,0:T(8,128)S(1)}, ...), condition=%wide.region_2.9_spmd.clone, body=%wide.region_0.8_spmd.clone.sunk | while | flops 366544064 | bytes 72965904 | solution.py:168
  34.2 1.7 gather_fusion
  41.0 1.5 fusion.107
  42.5 5.0 concatenate.404
  47.5 2.5 multiply_convert_fusion.4
  51.8 1.8 fusion.108
  54.3 1.7 copy-done
  58.9 2.0 dynamic-slice_add_fusion.2
  61.0 2.3 scatter-add.273
  64.0 2.7 fusion.113
  82.1 1.3 scatter.401
  83.8 1.3 scatter.402
  90.0 1.7 gather_fusion
  96.8 1.5 fusion.107
  98.2 5.0 concatenate.404
  103.3 2.5 multiply_convert_fusion.4
  107.6 1.8 fusion.108
  110.1 1.7 copy-done
  114.7 2.0 dynamic-slice_add_fusion.2
  116.7 2.3 scatter-add.273
  119.8 2.7 fusion.113
  137.9 1.3 scatter.401
  139.5 1.3 scatter.402
  145.7 1.7 gather_fusion
  152.5 1.5 fusion.107
  154.0 5.0 concatenate.404
  159.1 2.5 multiply_convert_fusion.4
  163.4 1.8 fusion.108
  165.9 1.7 copy-done
  170.5 2.0 dynamic-slice_add_fusion.2
  172.5 2.3 scatter-add.273
  175.6 2.7 fusion.113
  193.7 1.3 scatter.401
  195.3 1.3 scatter.402
  201.5 1.7 gather_fusion
  208.3 1.5 fusion.107
  209.8 5.0 concatenate.404
  214.8 2.5 multiply_convert_fusion.4
  219.2 1.8 fusion.108
  221.6 1.7 copy-done
  226.3 2.0 dynamic-slice_add_fusion.2
  228.3 2.3 scatter-add.273
  231.4 2.7 fusion.113
  249.5 1.3 scatter.401
  251.2 1.3 scatter.402
  253.5 5.2 copy.322
  258.9 11.8 %scatter_fusion = f32[41,64,64]{2,1,0:T(8,128)S(1)} fusion(f32[41,64,64]{2,1,0:T(8,128)S(1)} %broadcast_in_dim.101, s32[104]{0:T(128)S(1)} %reshape.4735, f32[104,64,64]{2,1,0:T(8,128)} %copy.322), kind=kCustom, calls=%fused_computation.5 | custom fusion | flops 425984 | bytes 5112224 | tf_op jit(solution)/shard_map/scatter-add | solution.py:114
  270.9 1.4 collective-permute-start.7
  272.3 1.3 collective-permute-start.6
  273.6 6.8 collective-permute-start.5
  280.4 1.9 collective-permute-start.4
  282.6 3.4 collective-permute-done.4
  286.1 1.3 scatter_fusion.1
  288.2 2.7 scatter-add.125
  291.0 2.7 scatter-add.126
  294.8 465.7 %all-reduce.24.cloned.1.call-done = (f32[64,1728]{1,0:T(8,128)}, f32[128,512]{1,0:T(8,128)}) async-done(((f32[64,1728]{1,0:T(8,128)}, f32[128,512]{1,0:T(8,128)}), (f32[64,1728]{1,0:T(8,128)}, f32[128,512]{1,0:T(8,128)})) %all-reduce.24.cloned.1.call-update) | async-done | bytes 704528 | tf_op jit(solution)/shard_map/psum | solution.py:182
  760.5 1.8 copy.584
  762.3 1.7 copy.585
  (919 shorter events, 129.6 us)
Async XLA Ops:
  7.2 2.5 copy-start.7
  7.2 753.3 %all-reduce.24.cloned.1.call-start = ((), (), s32[]{:S(2)}) async-start(), calls=%async_computation | async-start | bytes 1441792 | tf_op jit(solution)/shard_map/psum | solution.py:182
  8.4 17.4 %copy-start.8 = (s32[1,4,26]{2,1,0:T(4,128)S(1)}, s32[1,4,26]{2,1,0:T(4,128)}, u32[]{:S(2)}) copy-start(s32[1,4,26]{2,1,0:T(4,128)} %param.206) | copy-start | bytes 1252
  9.4 20.9 %copy-start.6 = (s32[3]{0:T(128)S(1)}, s32[3]{0:T(128)}, u32[]{:S(2)}) copy-start(s32[3]{0:T(128)} %constant.2907.clone.2) | copy-start | bytes 40
  10.3 15.6 %collective-permute-start = (bf16[4,64,64]{1,2,0:T(8,128)(2,1)S(1)}, bf16[4,64,64]{1,2,0:T(8,128)(2,1)S(1)}, u32[]{:S(2)}, u32[]{:S(2)}) collective-permute-start(bf16[4,64,64]{1,2,0:T(8,128)(2,1)S(1)} %gather_fusion.1), channel_id=1, source_target_pairs={{0,4},{4,8},{8,12},{12,16},{16,20},{20,24},{24,28},{28,32},{32,36}... | collective-permute-start | bytes 98312 | tf_op jit(solution)/shard_map/ppermute | solution.py:15
  15.4 10.5 %collective-permute-start.1 = (bf16[4,64,64]{1,2,0:T(8,128)(2,1)S(1)}, bf16[4,64,64]{1,2,0:T(8,128)(2,1)S(1)}, u32[]{:S(2)}, u32[]{:S(2)}) collective-permute-start(bf16[4,64,64]{1,2,0:T(8,128)(2,1)S(1)} %gather_fusion.2), channel_id=1, source_target_pairs={{4,0},{8,4},{12,8},{16,12},{20,16},{24,20},{28,24},{32,28},{36,32}... | collective-permute-start | bytes 98312 | tf_op jit(solution)/shard_map/ppermute | solution.py:15
  21.6 4.4 collective-permute-start.2
  23.5 5.7 collective-permute-start.3
  47.5 3.4 copy-start.2
  47.5 6.1 copy-start.4
  51.8 1.8 copy-start.3
  54.3 1.8 copy-start
  103.2 3.4 copy-start.2
  103.3 6.1 copy-start.4
  107.6 1.8 copy-start.3
  110.1 1.8 copy-start
  159.0 3.4 copy-start.2
  159.0 6.1 copy-start.4
  163.4 1.8 copy-start.3
  165.8 1.8 copy-start
  214.8 3.4 copy-start.2
  214.8 6.1 copy-start.4
  219.2 1.8 copy-start.3
  221.6 1.8 copy-start
  253.5 5.2 copy-start.1
  270.9 11.7 %collective-permute-start.7 = (bf16[4,64,64]{2,1,0:T(8,128)(2,1)S(1)}, bf16[4,64,64]{2,1,0:T(8,128)(2,1)S(1)}, u32[]{:S(2)}, u32[]{:S(2)}) collective-permute-start(bf16[4,64,64]{2,1,0:T(8,128)(2,1)S(1)} %get-tuple-element.1838), channel_id=1, source_target_pairs={{0,8},{4,12},{8,16},{12,20},{16,24},{20,28},{24,32},{28,36},{32,40... | collective-permute-start | bytes 98312 | tf_op jit(solution)/shard_map/ppermute | solution.py:15
  272.3 10.3 %collective-permute-start.6 = (bf16[4,64,64]{2,1,0:T(8,128)(2,1)S(1)}, bf16[4,64,64]{2,1,0:T(8,128)(2,1)S(1)}, u32[]{:S(2)}, u32[]{:S(2)}) collective-permute-start(bf16[4,64,64]{2,1,0:T(8,128)(2,1)S(1)} %get-tuple-element.1839), channel_id=1, source_target_pairs={{8,0},{12,4},{16,8},{20,12},{24,16},{28,20},{32,24},{36,28},{40,32... | collective-permute-start | bytes 98312 | tf_op jit(solution)/shard_map/ppermute | solution.py:15
  273.6 9.0 %collective-permute-start.5 = (bf16[4,64,64]{2,1,0:T(8,128)(2,1)S(1)}, bf16[4,64,64]{2,1,0:T(8,128)(2,1)S(1)}, u32[]{:S(2)}, u32[]{:S(2)}) collective-permute-start(bf16[4,64,64]{2,1,0:T(8,128)(2,1)S(1)} %get-tuple-element.1840), channel_id=1, source_target_pairs={{0,4},{4,8},{8,12},{12,16},{16,20},{20,24},{24,28},{28,32},{32,36}... | collective-permute-start | bytes 98312 | tf_op jit(solution)/shard_map/ppermute | solution.py:15
  280.4 5.6 collective-permute-start.4
  282.5 5.3 copy-start.5
Sparse Core Ops, SparseCore 0:
  282.7 477.7 all-reduce.23
where the time goes:
time: 775 us; the launch traced here: 771 us
  waiting for transfers between devices  472 us (61%)
  local copies, waits for them, and re-layouts  191 us (25%)
  other arithmetic  33.8 us (4%)
  matrix products  29.7 us (4%)
  starting transfers between devices  24.1 us (3%)
  between operations  15.2 us (2%)
    psum x1, waiting for transfers between devices, on_device(): grad_kernel, grad_down = lax.psum((grad_kernel, grad_down), ('tile', 'grp'))  466 us
    slice x116, local copies, waits for them, and re-layouts, fold_columns(): columns[position * channels:(position + 1) * channels]  42.6 us
    scatter-add x76, local copies, waits for them, and re-layouts, fold_columns(): result = result.at[:, 1 + a:9 + a, 1 + b:9 + b, 1 + c:9 + c].add(part_cols)  32.1 us
    ppermute x8, starting transfers between devices, from_behind(): return lax.ppermute(block, axis, route)  24.1 us
    concatenate x4, local copies, waits for them, and re-layouts, unfold_brick(): jnp.concatenate([padded[:, 1 + a:9 + a, 1 + b:9 + b, 1 + c:9 + c].reshape...  19.9 us
  transfers between devices with their start and end apart: 9, of which 3 were waited for; matrix products, arithmetic and copies ran while one was open for 2% of the time, Pallas kernels for 0%

commit v1 on v0

v1 whole, which is shorter than its diff:
```python
import jax
import jax.numpy as jnp
import ml_dtypes
import numpy as np
from jax import lax
from jax.experimental import pallas as pl
from jax.experimental.pallas import tpu as pltpu
from jax.sharding import Mesh
from jax.sharding import PartitionSpec as P

BF = jnp.bfloat16
F32 = jnp.float32
DIRECTIONS = [
    (a, b, c) for a in (-1, 0, 1) for b in (-1, 0, 1) for c in (-1, 0, 1) if (a, b, c) != (0, 0, 0)
]
SHIFTS = [10 * b + c for b in (-1, 0, 1) for c in (-1, 0, 1)]
SLOTS, C, C2, NOFF, CAP = 4, 64, 128, 4, 4
LOCAL = 6 * SLOTS + 1
TABLE = LOCAL + NOFF * CAP
OFFSETS = (1, -1, 2, -2)
VMEM_LIMIT = 56 * 2**20


def rim_cells(d, full):
    if d == -1:
        return [(7, 0)]
    if d == 1:
        return [(0, 9)]
    return [(i, i + 1) for i in range(full)]


def one_hot_tables():
    faces = np.zeros((512, 6, 128), np.float32)
    for x in range(8):
        for y in range(8):
            for z in range(8):
                v = (x, y, z)
                for a in range(3):
                    p, q = [v[i] for i in range(3) if i != a]
                    for e in range(2):
                        if v[a] == 7 * e:
                            faces[x * 64 + y * 8 + z, 2 * a + e, p * 8 + q] = 1
    inner = np.zeros((2, 64, 2, 128), np.float32)
    for s in range(2):
        for y in range(8):
            for z in range(8):
                inner[s, y * 8 + z, s, (y + 1) * 10 + z + 1] = 1
    cap = np.zeros((9, 128, 128), np.float32)
    side = np.zeros((8, 128, 8, 128), np.float32)
    for m, d in enumerate([d for d in DIRECTIONS if d[0] == 0]):
        if d[1] != 0:
            yy = 0 if d[1] == -1 else 9
            for x in range(8):
                for i, zz in rim_cells(d[2], 8):
                    side[m, x * 8 + i, x, yy * 10 + zz] = 1
        else:
            zz = 0 if d[2] == -1 else 9
            for x in range(8):
                for y in range(8):
                    side[m, x * 8 + y, x, (y + 1) * 10 + zz] = 1
    for m, (dy, dz) in enumerate([(b, c) for b in (-1, 0, 1) for c in (-1, 0, 1)]):
        for i, yy in rim_cells(dy, 8):
            for k, zz in rim_cells(dz, 8):
                cap[m, i * 8 + k, yy * 10 + zz] = 1
    down = np.zeros((2, 2, 4, 4, 4, 4, 128), np.float32)
    for ty in range(2):
        for tz in range(2):
            for X in range(4):
                for Y in range(4):
                    for Z in range(4):
                        lane = (2 * Y + ty + 1) * 10 + 2 * Z + tz + 1
                        down[ty, tz, X, Y, Z, X, lane] = 1
    b = ml_dtypes.bfloat16
    return (
        faces.reshape(512, 768).astype(b),
        inner.reshape(128, 256).astype(b),
        cap.reshape(1152, 128).astype(b),
        side.reshape(1024, 1024).astype(b),
        down.reshape(256, 512).astype(b),
    )


def nn(a, b):
    return jnp.dot(a, b, preferred_element_type=F32)


def nt(a, b):
    return lax.dot_general(a, b, (((1,), (1,)), ((), ())), preferred_element_type=F32)


def masked_rows(features, count):
    return jnp.concatenate(
        [features[0, s] * jnp.where(s < count, 1.0, 0.0).astype(BF) for s in range(SLOTS)], axis=0
    )


def faces_kernel(count, sends, features, face_hot, table, outgoing):
    masked = masked_rows(features, count[0, 0])
    for f in range(6):
        layer = nn(masked, face_hot[:, f * 128 : (f + 1) * 128]).astype(BF)
        for s in range(SLOTS):
            table[6 * s + f] = layer[s * C : (s + 1) * C]
    table[6 * SLOTS] = jnp.zeros((C, 128), BF)
    for j in range(NOFF):
        for c in range(CAP):
            outgoing[j, c] = table[sends[0, 0, j, c]]


def upper_kernel(out_grad, down_hot, down_rows, grad_active):
    for s in range(SLOTS):
        turned = jnp.transpose(out_grad[0, s].astype(F32)).astype(BF)
        spread = jnp.concatenate(
            [nn(turned, down_hot[t * 64 : (t + 1) * 64]).astype(BF) for t in range(4)], axis=0
        )
        grad_active[s] = nn(down_rows[...], spread)


def main_kernel(
    count,
    sources,
    features,
    table,
    received,
    conv,
    down_cols,
    out_grad,
    grad_active,
    inner_hot,
    cap_hot,
    side_hot,
    down_hot,
    coarse,
    grad_preact,
    sums,
    halo,
    entries,
    padded,
    stack,
    shifted,
    lowered,
    total,
):
    halo[0:LOCAL] = table[...]
    for j in range(NOFF):
        halo[LOCAL + j * CAP : LOCAL + (j + 1) * CAP] = received[j]
    for s in range(SLOTS):
        for k in range(26):
            entries[s * C : (s + 1) * C, k * 128 : (k + 1) * 128] = halo[sources[0, s, k]]
    masked = masked_rows(features, count[0, 0])
    padded[:, 0:128] = nn(entries[:, 0:1152], cap_hot[...]).astype(BF)
    padded[:, 1152:1280] = nn(entries[:, 2176:3328], cap_hot[...]).astype(BF)
    for i in range(4):
        block = nn(entries[:, 1152:2176], side_hot[:, i * 256 : (i + 1) * 256])
        block = block + nn(masked[:, i * 128 : (i + 1) * 128], inner_hot[...])
        padded[:, 128 + i * 256 : 384 + i * 256] = block.astype(BF)

    lane = lax.broadcasted_iota(jnp.int32, (C, 1024), 1) & 127
    row, column = lane // 10, lane % 10
    valid = (row >= 1) & (row <= 8) & (column >= 1) & (column <= 8)
    shifted[...] = jnp.zeros_like(shifted)
    total[...] = jnp.zeros_like(total)

    def brick(s, carry):
        filled = jnp.where(s < count[0, 0], 1.0, 0.0).astype(F32)
        here = pl.ds(pl.multiple_of(s * C, C), C)
        for x in range(10):
            plane = padded[here, x * 128 : (x + 1) * 128]
            for k, shift in enumerate(SHIFTS):
                moved = plane if shift == 0 else pltpu.roll(plane, (-shift) % 128, 1)
                stack[k * C : (k + 1) * C, x * 128 : (x + 1) * 128] = moved
        triple = nn(conv[...], stack[...])
        preact = triple[0:C, 0:1024] + triple[C : 2 * C, 128:1152] + triple[2 * C :, 256:1280]
        sigmoid = jax.nn.sigmoid(preact)
        active = jnp.where(valid, preact * sigmoid * filled, 0.0).astype(BF)
        halves = jnp.concatenate(
            [
                jnp.concatenate(
                    [active[:, (2 * X + tx) * 128 : (2 * X + tx + 1) * 128] for X in range(4)],
                    axis=1,
                )
                for tx in range(2)
            ],
            axis=0,
        )
        picked = nt(down_hot[...], halves).astype(BF)
        for t in range(4):
            lowered[here, t * 128 : (t + 1) * 128] = picked[t * 64 : (t + 1) * 64]
        upper = jnp.concatenate(
            [
                grad_active[s, (x % 2) * C : (x % 2 + 1) * C, (x // 2) * 128 : (x // 2 + 1) * 128]
                for x in range(8)
            ],
            axis=1,
        )
        grads = upper * sigmoid * (1.0 + preact * (1.0 - sigmoid)) * filled
        grads = jnp.where(valid, grads, 0.0).astype(BF)
        grad_preact[s] = grads
        for o in range(3):
            shifted[o * C : (o + 1) * C, o * 128 : o * 128 + 1024] = grads
        total[...] += nt(shifted[...], stack[...])
        return carry

    lax.fori_loop(0, SLOTS, brick, 0)
    rows = lowered[...]
    coarse[...] = nt(rows, down_cols[...]).astype(BF).reshape(coarse.shape)
    turned = jnp.transpose(out_grad[...].reshape(SLOTS * 64, C2).astype(F32)).astype(BF)
    grad_down = nn(turned, rows)
    for j in range(5):
        width = min(128, 576 - j * 128)
        sums[j * 192 : (j + 1) * 192, 0:width] = total[:, j * 128 : j * 128 + width].astype(BF)
    sums[4 * 192 : 5 * 192, 64:128] = jnp.zeros((192, 64), BF)
    for j in range(4):
        sums[960 + j * C2 : 960 + (j + 1) * C2] = grad_down[:, j * 128 : (j + 1) * 128].astype(BF)
    sums[1472:1536] = jnp.zeros((64, 128), BF)


def fold_kernel(
    sources,
    grad_preact,
    conv_back,
    inner_hot,
    cap_hot,
    side_hot,
    interior,
    grad_local,
    grad_remote,
    stack,
    high,
    low,
    rims,
    grad_table,
):
    high[...] = jnp.zeros_like(high)

    def brick(s, carry):
        here = pl.ds(pl.multiple_of(s * C, C), C)
        for x in range(8):
            plane = grad_preact[s, :, x * 128 : (x + 1) * 128]
            for k, shift in enumerate(SHIFTS):
                moved = plane if shift == 0 else pltpu.roll(plane, shift % 128, 1)
                stack[k * C : (k + 1) * C, x * 128 : (x + 1) * 128] = moved
        triple = nn(conv_back[...], stack[...])
        for x in range(10):
            value = None
            for o in range(3):
                if 0 <= x - o < 8:
                    part = triple[o * C : (o + 1) * C, (x - o) * 128 : (x - o + 1) * 128]
                    value = part if value is None else value + part
            top = value.astype(BF)
            high[here, x * 128 : (x + 1) * 128] = top
            low[here, x * 128 : (x + 1) * 128] = (value - top.astype(F32)).astype(BF)
        return carry

    lax.fori_loop(0, SLOTS, brick, 0)
    rims[:, 0:1152] = nt(high[:, 0:128], cap_hot[...])
    rims[:, 1152:2176] = nt(high[:, 128:1152], side_hot[...])
    rims[:, 2176:3328] = nt(high[:, 1152:1280], cap_hot[...])
    grad_table[...] = jnp.zeros_like(grad_table)
    for s in range(SLOTS):
        for k in range(26):
            place = sources[0, s, k]
            grad_table[place] += rims[s * C : (s + 1) * C, k * 128 : (k + 1) * 128]
    for i in range(4):
        lanes = slice(128 + i * 256, 384 + i * 256)
        interior[:, i * 128 : (i + 1) * 128] = nt(high[:, lanes], inner_hot[...]) + nt(
            low[:, lanes], inner_hot[...]
        )
    grad_local[...] = grad_table[0:LOCAL]
    for j in range(NOFF):
        grad_remote[j] = grad_table[LOCAL + j * CAP : LOCAL + (j + 1) * CAP].astype(BF)


def finish_kernel(
    count, sends, interior, grad_local, returned, face_hot, grad_features, table, layers
):
    table[...] = grad_local[...]
    for j in range(NOFF):
        for c in range(CAP):
            table[sends[0, 0, j, c]] += returned[j, c].astype(F32)
    for s in range(SLOTS):
        for f in range(6):
            layers[s * C : (s + 1) * C, f * 128 : (f + 1) * 128] = table[6 * s + f].astype(BF)
    whole = interior[...] + nt(layers[...], face_hot[...])
    for s in range(SLOTS):
        filled = jnp.where(s < count[0, 0], 1.0, 0.0).astype(F32)
        grad_features[0, s] = (whole[s * C : (s + 1) * C] * filled).astype(BF)


def call(kernel, memories, outs, scratch, flops, *args):
    where = {"s": pltpu.SMEM, "v": pltpu.VMEM}
    return pl.pallas_call(
        kernel,
        in_specs=[pl.BlockSpec(memory_space=where[m]) for m in memories],
        out_specs=[pl.BlockSpec(memory_space=pltpu.VMEM) for _ in outs],
        out_shape=[jax.ShapeDtypeStruct(s, d) for s, d in outs],
        scratch_shapes=[pltpu.VMEM(s, d) for s, d in scratch],
        compiler_params=pltpu.CompilerParams(vmem_limit_bytes=VMEM_LIMIT),
        cost_estimate=pl.CostEstimate(flops=flops, bytes_accessed=2**20, transcendentals=0),
        name=kernel.__name__,
    )(*args)


def gather_sum(block, axes, parts):
    copies = jnp.broadcast_to(block[None], (parts,) + block.shape)
    got = lax.all_to_all(copies, axes, 0, 0)
    return got.astype(F32).sum(0)


def sum_over_all(block, sizes):
    near = ("x", "c", "grp")
    parts = sizes["x"] * sizes["c"] * sizes["grp"]
    rows = block.shape[0] // parts
    got = lax.all_to_all(block.reshape(parts, rows, 128), near, 0, 0)
    part = got.astype(F32).sum(0)
    for axis in ("zl", "zh"):
        if sizes[axis] > 1:
            part = gather_sum(part.astype(BF), (axis,), sizes[axis])
    copies = jnp.broadcast_to(part.astype(BF)[None], (parts, rows, 128))
    return lax.all_to_all(copies, near, 0, 0).reshape(block.shape)


def from_behind(block, axes, devices, distance):
    route = [(i - distance, i) for i in range(devices) if 0 <= i - distance < devices]
    return lax.ppermute(block, axes, route)


def on_device(sizes, features, brick_count, send_list, halo_src, kernel, down_kernel, out_grad):
    face_hot, inner_hot, cap_hot, side_hot, down_hot = one_hot_tables()
    tile = ("zh", "zl", "x", "c")
    devices = sizes["zh"] * sizes["zl"] * sizes["x"] * sizes["c"]
    conv5 = kernel.reshape(C, 3, 9, C)
    conv = conv5.transpose(1, 0, 2, 3).reshape(192, 576)
    conv_back = conv5.transpose(1, 3, 2, 0).reshape(192, 576)
    down5 = down_kernel.reshape(C2, 2, 4, C)
    down_cols = down5.transpose(0, 2, 1, 3).reshape(C2, 512)
    down_rows = down5.transpose(1, 3, 2, 0).reshape(2 * C, 4 * C2)

    table, outgoing = call(
        faces_kernel,
        "ssvv",
        [((LOCAL, C, 128), BF), ((NOFF, CAP, C, 128), BF)],
        [],
        2 * 256 * 512 * 768,
        brick_count,
        send_list,
        features,
        face_hot,
    )
    received = jnp.stack(
        [from_behind(outgoing[j], tile, devices, o) for j, o in enumerate(OFFSETS)]
    )
    (grad_active,) = call(
        upper_kernel,
        "vvv",
        [((SLOTS, 2 * C, 512), F32)],
        [],
        10**9,
        out_grad,
        down_hot,
        down_rows,
    )
    coarse, grad_preact, sums = call(
        main_kernel,
        "ssvvvvvvvvvvv",
        [((1, SLOTS, 64, C2), BF), ((SLOTS, C, 1024), BF), ((1536, 128), BF)],
        [
            ((TABLE, C, 128), BF),
            ((256, 26 * 128), BF),
            ((256, 1280), BF),
            ((576, 1280), BF),
            ((192, 1280), BF),
            ((256, 512), BF),
            ((192, 576), F32),
        ],
        5 * 10**9,
        brick_count,
        halo_src,
        features,
        table,
        received,
        conv,
        down_cols,
        out_grad,
        grad_active,
        inner_hot,
        cap_hot,
        side_hot,
        down_hot,
    )
    sums = sum_over_all(sums, sizes)
    grad_kernel = sums[:960].reshape(5, 3, C, 128).transpose(2, 1, 0, 3).reshape(C, 3, 640)
    grad_kernel = grad_kernel[:, :, :576].reshape(C, 1728).astype(F32)
    grad_down = sums[960:1472].reshape(4, C2, 2, C).transpose(1, 2, 0, 3)
    grad_down = grad_down.reshape(C2, 512).astype(F32)

    interior, grad_local, grad_remote = call(
        fold_kernel,
        "svvvvv",
        [((256, 512), F32), ((LOCAL, C, 128), F32), ((NOFF, CAP, C, 128), BF)],
        [
            ((576, 1024), BF),
            ((256, 1280), BF),
            ((256, 1280), BF),
            ((256, 26 * 128), F32),
            ((TABLE, C, 128), F32),
        ],
        3 * 10**9,
        halo_src,
        grad_preact,
        conv_back,
        inner_hot,
        cap_hot,
        side_hot,
    )
    returned = jnp.stack(
        [from_behind(grad_remote[j], tile, devices, -o) for j, o in enumerate(OFFSETS)]
    )
    (grad_features,) = call(
        finish_kernel,
        "ssvvvv",
        [((1, SLOTS, C, 512), BF)],
        [((LOCAL, C, 128), F32), ((256, 768), BF)],
        2 * 256 * 512 * 768,
        brick_count,
        send_list,
        interior,
        grad_local,
        returned,
        face_hot,
    )
    return coarse, grad_features, grad_kernel, grad_down


def solution(mesh):
    tile, grp = mesh.shape["tile"], mesh.shape["grp"]
    near = tile // 8
    low = 4 if near % 4 == 0 else near
    sizes = {"zh": near // low, "zl": low, "x": 4, "c": 2, "grp": grp}
    fine = Mesh(mesh.devices.reshape(tuple(sizes.values())), tuple(sizes))
    line = ("zh", "zl", "x", "c")
    in_specs = (
        P("grp", line, None, None),
        P("grp", line),
        P("grp", line, None, None),
        P("grp", line, None),
        P(),
        P(),
        P("grp", line, None, None),
    )
    out_specs = (P("grp", line, None, None), P("grp", line, None, None), P(), P())

    def step(*args):
        return on_device(sizes, *args)

    return jax.shard_map(step, mesh=fine, in_specs=in_specs, out_specs=out_specs, check_vma=False)
```

time: 775 us -> 128 us (0.17)
  the two profiles are of different devices: /device:TPU:1 before, /device:TPU:32 now
where the time goes in v1:
time: 128 us
  starting transfers between devices  54.5 us (43%)
  Pallas kernels  27 us (21%)
  blocking collectives  15.4 us (12%)
  waiting for transfers between devices  14.9 us (12%)
  local copies, waits for them, and re-layouts  12.6 us (10%)
  other arithmetic  1.61 us (1%)
  between operations  1.54 us (1%)
    ppermute x8, starting transfers between devices, from_behind(): return lax.ppermute(block, axes, route)  29.8 us
    pallas_call x5, Pallas kernels, call(): pl.pallas_call(kernel, in_specs=[pl.BlockSpec(memory_space=where[m]) for...  27 us
    all_to_all x2, starting transfers between devices, gather_sum(): got = lax.all_to_all(copies, axes, 0, 0)  20.9 us
    all_to_all x1, blocking collectives, sum_over_all(): got = lax.all_to_all(block.reshape(parts, rows, 128), near, 0, 0)  15.4 us
    all_to_all x2, waiting for transfers between devices, gather_sum(): got = lax.all_to_all(copies, axes, 0, 0)  9.11 us
    ppermute x8, waiting for transfers between devices, from_behind(): return lax.ppermute(block, axes, route)  5.75 us
    all_to_all x1, starting transfers between devices, sum_over_all(): return lax.all_to_all(copies, near, 0, 0).reshape(block.shape)  3.88 us
    unnamed x7, local copies, waits for them, and re-layouts  2.92 us
  transfers between devices with their start and end apart: 11, of which 3 were waited for; matrix products, arithmetic and copies ran while one was open for 6% of the time, Pallas kernels for 11%

profile of v1, /device:TPU:32, one launch (start us, length us, event | category | flops | bytes accessed | tf_op | source)
XLA Modules:
  0.0 127.5 jit_solution(5251882225734907496)
XLA Ops:
  0.6 0.0 copy-start
  1.3 2.6 %faces_kernel.1 = (bf16[25,64,128]{2,1,0:T(8,128)(2,1)}, bf16[4,4,64,128]{3,2,1,0:T(8,128)(2,1)}) custom-call(s32[1,1]{1,0:T(1,128)S(6)} %copy.59.count, s32[1,1,4,4]{3,2,1,0:T(4,128)} %sends.3, bf16[1,4,64,512]{3,2,1,0:T(8,128)(2,1)} %features.3, bf16[512,768]{1,0:T(8,128)(2,1)} %constant.15.clone.face_hot), custom_call_target="tpu_custom_call" | custom-call | flops 201326592 | bytes 1048576 | tf_op jit(solution)/shard_map/faces_kernel/pallas_call | solution.py:291
  4.0 1.0 slice_bitcast_fusion.7
  4.9 1.9 %collective-permute-start = (bf16[4,64,128]{2,1,0:T(8,128)(2,1)S(1)}, bf16[4,64,128]{2,1,0:T(8,128)(2,1)S(1)}, u32[]{:S(2)}, u32[]{:S(2)}) collective-permute-start(bf16[4,64,128]{2,1,0:T(8,128)(2,1)S(1)} %get-tuple-element.32), channel_id=1, source_target_pairs={{0,4},{4,8},{8,12},{12,16},{16,20},{20,24},{24,28},{28,32},{32,36}... | collective-permute-start | bytes 196616 | tf_op jit(solution)/shard_map/ppermute | solution.py:324
  6.8 4.2 %collective-permute-start.3 = (bf16[4,64,128]{2,1,0:T(8,128)(2,1)S(1)}, bf16[4,64,128]{2,1,0:T(8,128)(2,1)S(1)}, u32[]{:S(2)}, u32[]{:S(2)}) collective-permute-start(bf16[4,64,128]{2,1,0:T(8,128)(2,1)S(1)} %get-tuple-element.33), channel_id=1, source_target_pairs={{8,0},{12,4},{16,8},{20,12},{24,16},{28,20},{32,24},{36,28},{40,32... | collective-permute-start | bytes 196616 | tf_op jit(solution)/shard_map/ppermute | solution.py:324
  11.1 1.9 %collective-permute-start.2 = (bf16[4,64,128]{2,1,0:T(8,128)(2,1)S(1)}, bf16[4,64,128]{2,1,0:T(8,128)(2,1)S(1)}, u32[]{:S(2)}, u32[]{:S(2)}) collective-permute-start(bf16[4,64,128]{2,1,0:T(8,128)(2,1)S(1)} %get-tuple-element.34), channel_id=1, source_target_pairs={{0,8},{4,12},{8,16},{12,20},{16,24},{20,28},{24,32},{28,36},{32,40... | collective-permute-start | bytes 196616 | tf_op jit(solution)/shard_map/ppermute | solution.py:324
  13.0 7.0 %collective-permute-start.1 = (bf16[4,64,128]{2,1,0:T(8,128)(2,1)S(1)}, bf16[4,64,128]{2,1,0:T(8,128)(2,1)S(1)}, u32[]{:S(2)}, u32[]{:S(2)}) collective-permute-start(bf16[4,64,128]{2,1,0:T(8,128)(2,1)S(1)} %get-tuple-element.35), channel_id=1, source_target_pairs={{4,0},{8,4},{12,8},{16,12},{20,16},{24,20},{28,24},{32,28},{36,32}... | collective-permute-start | bytes 196616 | tf_op jit(solution)/shard_map/ppermute | solution.py:324
  20.0 1.0 copy.36
  21.0 0.1 copy.38
  21.2 0.7 copy.58
  21.8 0.8 copy.40.down_cols
  22.6 0.0 copy-done
  22.6 0.3 copy.34
  22.9 0.6 copy.48
  23.5 1.1 reshape.65.conv
  24.6 3.5 %upper_kernel.1.grad_active = f32[4,128,512]{2,1,0:T(8,128)} custom-call(bf16[1,4,64,128]{3,2,1,0:T(8,128)(2,1)} %out_grad.3, bf16[256,512]{1,0:T(8,128)(2,1)} %constant.16.clone.down_hot, bf16[128,512]{1,0:T(8,128)(2,1)} %bitcast.65), custom_call_target="tpu_custom_call" | custom-call | flops 1000000000 | bytes 1048576 | tf_op jit(solution)/shard_map/upper_kernel/pallas_call | solution.py:291
  28.1 0.0 collective-permute-done
  28.1 0.0 collective-permute-done.3
  28.1 0.0 collective-permute-done.2
  28.1 0.0 collective-permute-done.1
  28.1 0.7 pad_maximum_fusion.received
  28.8 10.8 %main_kernel.1 = (bf16[1,4,64,128]{3,2,1,0:T(8,128)(2,1)}, bf16[4,64,1024]{2,1,0:T(8,128)(2,1)}, bf16[1536,128]{1,0:T(8,128)(2,1)}) custom-call(s32[1,1]{1,0:T(1,128)S(6)} %copy.59.count, s32[1,4,26]{2,1,0:T(4,128)} %sources.3, bf16[1,4,64,512]{3,2,1,0:T(8,128)(2,1)} %features.3, bf16[25,64,128]{2,1,0:T(8,128)(2,1)} %get-tuple-element.12.table, ...), custom_call_target="tpu_custom_call" | custom-call | flops 5000000000 | bytes 1048576 | tf_op jit(solution)/shard_map/main_kernel/pallas_call | solution.py:291
  39.6 15.4 %all_to_all.20 = bf16[32,48,128]{2,1,0:T(8,128)(2,1)S(1)} all-to-all(bf16[32,48,128]{2,1,0:T(8,128)(2,1)} %bitcast.64), channel_id=1, replica_groups=mesh['zh'=4,'zl'=4,'x'=4,'c'=2,'grp'=4] {'x','c','grp'}, dimensions={0} | all-to-all | bytes 786432 | tf_op jit(solution)/shard_map/all_to_all | solution.py:313
  55.0 0.1 reduce_sum.36
  55.0 0.6 broadcast_in_dim.6
  55.7 8.3 %all-to-all-start.1 = ((bf16[4,48,128]{2,1,0:T(8,128)(2,1)}), bf16[4,48,128]{2,1,0:T(8,128)(2,1)S(1)}, u32[]{:S(2)}, u32[]{:S(2)}) async-start(bf16[4,48,128]{2,1,0:T(8,128)(2,1)} %broadcast_in_dim.6), calls=%async_computation.1 | async-start | bytes 98304 | tf_op jit(solution)/shard_map/all_to_all | solution.py:305
  64.0 0.3 copy.49
  64.3 1.1 reshape.66.conv_back
  65.4 3.1 %all-to-all-done.1 = bf16[4,48,128]{2,1,0:T(8,128)(2,1)S(1)} async-done(((bf16[4,48,128]{2,1,0:T(8,128)(2,1)}), bf16[4,48,128]{2,1,0:T(8,128)(2,1)S(1)}, u32[]{:S(2)}, u32[]{:S(2)}) %all-to-all-start.1) | async-done | bytes 49184 | tf_op jit(solution)/shard_map/all_to_all | solution.py:305
  68.5 0.6 broadcast_in_dim.7
  69.1 12.5 %all-to-all-start.2 = ((bf16[4,48,128]{2,1,0:T(8,128)(2,1)}), bf16[4,48,128]{2,1,0:T(8,128)(2,1)S(1)}, u32[]{:S(2)}, u32[]{:S(2)}) async-start(bf16[4,48,128]{2,1,0:T(8,128)(2,1)} %broadcast_in_dim.7), calls=%async_computation.2 | async-start | bytes 98304 | tf_op jit(solution)/shard_map/all_to_all | solution.py:305
  81.7 7.3 %fold_kernel.1 = (f32[256,512]{1,0:T(8,128)}, f32[25,64,128]{2,1,0:T(8,128)}, bf16[4,4,64,128]{3,2,1,0:T(8,128)(2,1)}) custom-call(s32[1,4,26]{2,1,0:T(4,128)} %sources.3, bf16[4,64,1024]{2,1,0:T(8,128)(2,1)} %get-tuple-element.15.grad_preact, bf16[192,576]{1,0:T(8,128)(2,1)} %reshape.66.conv_back, bf16[128,256]{1,0:T(8,128)(2,1)} %constant.17.clone.inner_hot, ...), custom_call_target="tpu_custom_call" | custom-call | flops 3000000000 | bytes 1048576 | tf_op jit(solution)/shard_map/fold_kernel/pallas_call | solution.py:291
  89.0 6.0 %all-to-all-done.2 = bf16[4,48,128]{2,1,0:T(8,128)(2,1)S(1)} async-done(((bf16[4,48,128]{2,1,0:T(8,128)(2,1)}), bf16[4,48,128]{2,1,0:T(8,128)(2,1)S(1)}, u32[]{:S(2)}, u32[]{:S(2)}) %all-to-all-start.2) | async-done | bytes 49184 | tf_op jit(solution)/shard_map/all_to_all | solution.py:305
  95.1 0.8 broadcast_in_dim.8
  95.9 3.9 %all-to-all-start.3 = ((bf16[32,48,128]{2,1,0:T(8,128)(2,1)}), bf16[32,48,128]{2,1,0:T(8,128)(2,1)S(1)}, u32[]{:S(2)}, u32[]{:S(2)}) async-start(bf16[32,48,128]{2,1,0:T(8,128)(2,1)} %broadcast_in_dim.8), calls=%async_computation.3 | async-start | bytes 786432 | tf_op jit(solution)/shard_map/all_to_all | solution.py:319
  99.8 1.0 slice_bitcast_fusion.3
  100.7 4.8 %collective-permute-start.4 = (bf16[4,64,128]{2,1,0:T(8,128)(2,1)S(1)}, bf16[4,64,128]{2,1,0:T(8,128)(2,1)S(1)}, u32[]{:S(2)}, u32[]{:S(2)}) collective-permute-start(bf16[4,64,128]{2,1,0:T(8,128)(2,1)S(1)} %get-tuple-element.28), channel_id=1, source_target_pairs={{4,0},{8,4},{12,8},{16,12},{20,16},{24,20},{28,24},{32,28},{36,32}... | collective-permute-start | bytes 196616 | tf_op jit(solution)/shard_map/ppermute | solution.py:324
  105.6 1.9 %collective-permute-start.7 = (bf16[4,64,128]{2,1,0:T(8,128)(2,1)S(1)}, bf16[4,64,128]{2,1,0:T(8,128)(2,1)S(1)}, u32[]{:S(2)}, u32[]{:S(2)}) collective-permute-start(bf16[4,64,128]{2,1,0:T(8,128)(2,1)S(1)} %get-tuple-element.29), channel_id=1, source_target_pairs={{0,8},{4,12},{8,16},{12,20},{16,24},{20,28},{24,32},{28,36},{32,40... | collective-permute-start | bytes 196616 | tf_op jit(solution)/shard_map/ppermute | solution.py:324
  107.5 6.0 %collective-permute-start.6 = (bf16[4,64,128]{2,1,0:T(8,128)(2,1)S(1)}, bf16[4,64,128]{2,1,0:T(8,128)(2,1)S(1)}, u32[]{:S(2)}, u32[]{:S(2)}) collective-permute-start(bf16[4,64,128]{2,1,0:T(8,128)(2,1)S(1)} %get-tuple-element.30), channel_id=1, source_target_pairs={{8,0},{12,4},{16,8},{20,12},{24,16},{28,20},{32,24},{36,28},{40,32... | collective-permute-start | bytes 196616 | tf_op jit(solution)/shard_map/ppermute | solution.py:324
  113.5 1.9 %collective-permute-start.5 = (bf16[4,64,128]{2,1,0:T(8,128)(2,1)S(1)}, bf16[4,64,128]{2,1,0:T(8,128)(2,1)S(1)}, u32[]{:S(2)}, u32[]{:S(2)}) collective-permute-start(bf16[4,64,128]{2,1,0:T(8,128)(2,1)S(1)} %get-tuple-element.31), channel_id=1, source_target_pairs={{0,4},{4,8},{8,12},{12,16},{16,20},{20,24},{24,28},{28,32},{32,36}... | collective-permute-start | bytes 196616 | tf_op jit(solution)/shard_map/ppermute | solution.py:324
  115.5 0.0 collective-permute-done.4
  115.5 0.0 collective-permute-done.7
  115.5 0.0 collective-permute-done.6
  115.5 5.7 %collective-permute-done.5 = bf16[4,64,128]{2,1,0:T(8,128)(2,1)S(1)} collective-permute-done((bf16[4,64,128]{2,1,0:T(8,128)(2,1)S(1)}, bf16[4,64,128]{2,1,0:T(8,128)(2,1)S(1)}, u32[]{:S(2)}, u32[]{:S(2)}) %collective-permute-start.5) | collective-permute-done | bytes 65568 | tf_op jit(solution)/shard_map/ppermute | solution.py:324
  121.2 0.7 pad_maximum_fusion.1.returned
  122.0 2.8 %finish_kernel.1 = bf16[1,4,64,512]{3,2,1,0:T(8,128)(2,1)} custom-call(s32[1,1]{1,0:T(1,128)S(6)} %copy.59.count, s32[1,1,4,4]{3,2,1,0:T(4,128)} %sends.3, f32[256,512]{1,0:T(8,128)} %get-tuple-element.16.interior, f32[25,64,128]{2,1,0:T(8,128)} %get-tuple-element.17.grad_local, bf16[4,4,64,128]{3,2,1,0:T(8,128)(2,1)} %pad_maximum_fusion.1.returned, ...), custom_call_target="tpu_custom_call" | custom-call | flops 201326592 | bytes 1048576 | tf_op jit(solution)/shard_map/finish_kernel/pallas_call | solution.py:291
  124.8 0.0 all-to-all-done.3
  124.8 0.1 copy.52
  124.9 0.1 reshape.64
  125.1 0.8 copy.47
  126.0 0.3 copy.44
  126.4 1.2 reshape.62
  (8 shorter events, 0.2 us)
Async XLA Ops:
  0.6 22.0 %copy-start = (bf16[64,1728]{1,0:T(8,128)(2,1)S(1)}, bf16[64,1728]{1,0:T(8,128)(2,1)}, u32[]{:S(2)}) copy-start(bf16[64,1728]{1,0:T(8,128)(2,1)} %param.16) | copy-start | bytes 663556
  4.9 23.1 %collective-permute-start = (bf16[4,64,128]{2,1,0:T(8,128)(2,1)S(1)}, bf16[4,64,128]{2,1,0:T(8,128)(2,1)S(1)}, u32[]{:S(2)}, u32[]{:S(2)}) collective-permute-start(bf16[4,64,128]{2,1,0:T(8,128)(2,1)S(1)} %get-tuple-element.32), channel_id=1, source_target_pairs={{0,4},{4,8},{8,12},{12,16},{16,20},{20,24},{24,28},{28,32},{32,36}... | collective-permute-start | bytes 196616 | tf_op jit(solution)/shard_map/ppermute | solution.py:324
  6.8 21.2 %collective-permute-start.3 = (bf16[4,64,128]{2,1,0:T(8,128)(2,1)S(1)}, bf16[4,64,128]{2,1,0:T(8,128)(2,1)S(1)}, u32[]{:S(2)}, u32[]{:S(2)}) collective-permute-start(bf16[4,64,128]{2,1,0:T(8,128)(2,1)S(1)} %get-tuple-element.33), channel_id=1, source_target_pairs={{8,0},{12,4},{16,8},{20,12},{24,16},{28,20},{32,24},{36,28},{40,32... | collective-permute-start | bytes 196616 | tf_op jit(solution)/shard_map/ppermute | solution.py:324
  11.1 17.0 %collective-permute-start.2 = (bf16[4,64,128]{2,1,0:T(8,128)(2,1)S(1)}, bf16[4,64,128]{2,1,0:T(8,128)(2,1)S(1)}, u32[]{:S(2)}, u32[]{:S(2)}) collective-permute-start(bf16[4,64,128]{2,1,0:T(8,128)(2,1)S(1)} %get-tuple-element.34), channel_id=1, source_target_pairs={{0,8},{4,12},{8,16},{12,20},{16,24},{20,28},{24,32},{28,36},{32,40... | collective-permute-start | bytes 196616 | tf_op jit(solution)/shard_map/ppermute | solution.py:324
  13.0 15.1 %collective-permute-start.1 = (bf16[4,64,128]{2,1,0:T(8,128)(2,1)S(1)}, bf16[4,64,128]{2,1,0:T(8,128)(2,1)S(1)}, u32[]{:S(2)}, u32[]{:S(2)}) collective-permute-start(bf16[4,64,128]{2,1,0:T(8,128)(2,1)S(1)} %get-tuple-element.35), channel_id=1, source_target_pairs={{4,0},{8,4},{12,8},{16,12},{20,16},{24,20},{28,24},{32,28},{36,32}... | collective-permute-start | bytes 196616 | tf_op jit(solution)/shard_map/ppermute | solution.py:324
  55.7 12.8 %all-to-all-start.1 = ((bf16[4,48,128]{2,1,0:T(8,128)(2,1)}), bf16[4,48,128]{2,1,0:T(8,128)(2,1)S(1)}, u32[]{:S(2)}, u32[]{:S(2)}) async-start(bf16[4,48,128]{2,1,0:T(8,128)(2,1)} %broadcast_in_dim.6), calls=%async_computation.1 | async-start | bytes 98304 | tf_op jit(solution)/shard_map/all_to_all | solution.py:305
  69.1 25.9 %all-to-all-start.2 = ((bf16[4,48,128]{2,1,0:T(8,128)(2,1)}), bf16[4,48,128]{2,1,0:T(8,128)(2,1)S(1)}, u32[]{:S(2)}, u32[]{:S(2)}) async-start(bf16[4,48,128]{2,1,0:T(8,128)(2,1)} %broadcast_in_dim.7), calls=%async_computation.2 | async-start | bytes 98304 | tf_op jit(solution)/shard_map/all_to_all | solution.py:305
  95.9 28.9 %all-to-all-start.3 = ((bf16[32,48,128]{2,1,0:T(8,128)(2,1)}), bf16[32,48,128]{2,1,0:T(8,128)(2,1)S(1)}, u32[]{:S(2)}, u32[]{:S(2)}) async-start(bf16[32,48,128]{2,1,0:T(8,128)(2,1)} %broadcast_in_dim.8), calls=%async_computation.3 | async-start | bytes 786432 | tf_op jit(solution)/shard_map/all_to_all | solution.py:319
  100.7 14.8 %collective-permute-start.4 = (bf16[4,64,128]{2,1,0:T(8,128)(2,1)S(1)}, bf16[4,64,128]{2,1,0:T(8,128)(2,1)S(1)}, u32[]{:S(2)}, u32[]{:S(2)}) collective-permute-start(bf16[4,64,128]{2,1,0:T(8,128)(2,1)S(1)} %get-tuple-element.28), channel_id=1, source_target_pairs={{4,0},{8,4},{12,8},{16,12},{20,16},{24,20},{28,24},{32,28},{36,32}... | collective-permute-start | bytes 196616 | tf_op jit(solution)/shard_map/ppermute | solution.py:324
  105.6 9.9 %collective-permute-start.7 = (bf16[4,64,128]{2,1,0:T(8,128)(2,1)S(1)}, bf16[4,64,128]{2,1,0:T(8,128)(2,1)S(1)}, u32[]{:S(2)}, u32[]{:S(2)}) collective-permute-start(bf16[4,64,128]{2,1,0:T(8,128)(2,1)S(1)} %get-tuple-element.29), channel_id=1, source_target_pairs={{0,8},{4,12},{8,16},{12,20},{16,24},{20,28},{24,32},{28,36},{32,40... | collective-permute-start | bytes 196616 | tf_op jit(solution)/shard_map/ppermute | solution.py:324
  107.5 8.0 %collective-permute-start.6 = (bf16[4,64,128]{2,1,0:T(8,128)(2,1)S(1)}, bf16[4,64,128]{2,1,0:T(8,128)(2,1)S(1)}, u32[]{:S(2)}, u32[]{:S(2)}) collective-permute-start(bf16[4,64,128]{2,1,0:T(8,128)(2,1)S(1)} %get-tuple-element.30), channel_id=1, source_target_pairs={{8,0},{12,4},{16,8},{20,12},{24,16},{28,20},{32,24},{36,28},{40,32... | collective-permute-start | bytes 196616 | tf_op jit(solution)/shard_map/ppermute | solution.py:324
  113.5 7.7 %collective-permute-start.5 = (bf16[4,64,128]{2,1,0:T(8,128)(2,1)S(1)}, bf16[4,64,128]{2,1,0:T(8,128)(2,1)S(1)}, u32[]{:S(2)}, u32[]{:S(2)}) collective-permute-start(bf16[4,64,128]{2,1,0:T(8,128)(2,1)S(1)} %get-tuple-element.31), channel_id=1, source_target_pairs={{0,4},{4,8},{8,12},{12,16},{16,20},{20,24},{24,28},{28,32},{32,36}... | collective-permute-start | bytes 196616 | tf_op jit(solution)/shard_map/ppermute | solution.py:324

commit v2 on v1

--- a/solution.py
+++ b/solution.py
@@ -18,7 +18,7 @@
 LOCAL = 6 * SLOTS + 1
 TABLE = LOCAL + NOFF * CAP
 OFFSETS = (1, -1, 2, -2)
-VMEM_LIMIT = 56 * 2**20
+NEAR = ("x", "c", "grp")
 
 
 def rim_cells(d, full):
@@ -94,7 +94,7 @@
     )
 
 
-def faces_kernel(count, sends, features, face_hot, table, outgoing):
+def faces_kernel(count, sends, features, face_hot, table, *outgoing):
     masked = masked_rows(features, count[0, 0])
     for f in range(6):
         layer = nn(masked, face_hot[:, f * 128 : (f + 1) * 128]).astype(BF)
@@ -103,16 +103,24 @@
     table[6 * SLOTS] = jnp.zeros((C, 128), BF)
     for j in range(NOFF):
         for c in range(CAP):
-            outgoing[j, c] = table[sends[0, 0, j, c]]
-
-
-def upper_kernel(out_grad, down_hot, down_rows, grad_active):
+            outgoing[j][c] = table[sends[0, 0, j, c]]
+
+
+def upper_kernel(out_grad, down_hot, down_kernel, grad_active):
+    tall = jnp.transpose(down_kernel[...].astype(F32)).astype(BF)
+    down_rows = jnp.concatenate(
+        [
+            jnp.concatenate([tall[(4 * tx + t) * C : (4 * tx + t + 1) * C] for t in range(4)], axis=1)
+            for tx in range(2)
+        ],
+        axis=0,
+    )
     for s in range(SLOTS):
         turned = jnp.transpose(out_grad[0, s].astype(F32)).astype(BF)
         spread = jnp.concatenate(
             [nn(turned, down_hot[t * 64 : (t + 1) * 64]).astype(BF) for t in range(4)], axis=0
         )
-        grad_active[s] = nn(down_rows[...], spread)
+        grad_active[s] = nn(down_rows, spread)
 
 
 def main_kernel(
@@ -120,9 +128,12 @@
     sources,
     features,
     table,
-    received,
-    conv,
-    down_cols,
+    ahead,
+    behind,
+    ahead2,
+    behind2,
+    kernel,
+    down_kernel,
     out_grad,
     grad_active,
     inner_hot,
@@ -133,6 +144,7 @@
     grad_preact,
     sums,
     halo,
+    conv,
     entries,
     padded,
     stack,
@@ -142,10 +154,12 @@
 ):
     halo[0:LOCAL] = table[...]
     for j in range(NOFF):
-        halo[LOCAL + j * CAP : LOCAL + (j + 1) * CAP] = received[j]
+        halo[LOCAL + j * CAP : LOCAL + (j + 1) * CAP] = (ahead, behind, ahead2, behind2)[j][...]
     for s in range(SLOTS):
         for k in range(26):
             entries[s * C : (s + 1) * C, k * 128 : (k + 1) * 128] = halo[sources[0, s, k]]
+    for o in range(3):
+        conv[o * C : (o + 1) * C] = kernel[:, o * 576 : (o + 1) * 576]
     masked = masked_rows(features, count[0, 0])
     padded[:, 0:128] = nn(entries[:, 0:1152], cap_hot[...]).astype(BF)
     padded[:, 1152:1280] = nn(entries[:, 2176:3328], cap_hot[...]).astype(BF)
@@ -202,7 +216,11 @@
 
     lax.fori_loop(0, SLOTS, brick, 0)
     rows = lowered[...]
-    coarse[...] = nt(rows, down_cols[...]).astype(BF).reshape(coarse.shape)
+    down_cols = jnp.concatenate(
+        [down_kernel[:, (4 * tx + t) * C : (4 * tx + t + 1) * C] for t in range(4) for tx in range(2)],
+        axis=1,
+    )
+    coarse[...] = nt(rows, down_cols).astype(BF).reshape(coarse.shape)
     turned = jnp.transpose(out_grad[...].reshape(SLOTS * 64, C2).astype(F32)).astype(BF)
     grad_down = nn(turned, rows)
     for j in range(5):
@@ -223,7 +241,10 @@
     side_hot,
     interior,
     grad_local,
-    grad_remote,
+    to_ahead,
+    to_behind,
+    to_ahead2,
+    to_behind2,
     stack,
     high,
     low,
@@ -267,16 +288,41 @@
         )
     grad_local[...] = grad_table[0:LOCAL]
     for j in range(NOFF):
-        grad_remote[j] = grad_table[LOCAL + j * CAP : LOCAL + (j + 1) * CAP].astype(BF)
+        block = grad_table[LOCAL + j * CAP : LOCAL + (j + 1) * CAP].astype(BF)
+        (to_ahead, to_behind, to_ahead2, to_behind2)[j][...] = block
+
+
+def unpack_kernel(sums, grad_kernel, grad_down):
+    parts = []
+    for o in range(3):
+        tiles = [sums[j * 192 + o * C : j * 192 + (o + 1) * C].astype(F32) for j in range(5)]
+        parts.append(jnp.concatenate(tiles, axis=1)[:, :576])
+    grad_kernel[...] = jnp.concatenate(parts, axis=1)
+    tiles = [sums[960 + t * C2 : 960 + (t + 1) * C2].astype(F32) for t in range(4)]
+    grad_down[...] = jnp.concatenate(
+        [tiles[t][:, tx * C : (tx + 1) * C] for tx in range(2) for t in range(4)], axis=1
+    )
 
 
 def finish_kernel(
-    count, sends, interior, grad_local, returned, face_hot, grad_features, table, layers
+    count,
+    sends,
+    interior,
+    grad_local,
+    ahead,
+    behind,
+    ahead2,
+    behind2,
+    face_hot,
+    grad_features,
+    table,
+    layers,
 ):
     table[...] = grad_local[...]
     for j in range(NOFF):
         for c in range(CAP):
-            table[sends[0, 0, j, c]] += returned[j, c].astype(F32)
+            block = (ahead, behind, ahead2, behind2)[j][c]
+            table[sends[0, 0, j, c]] += block.astype(F32)
     for s in range(SLOTS):
         for f in range(6):
             layers[s * C : (s + 1) * C, f * 128 : (f + 1) * 128] = table[6 * s + f].astype(BF)
@@ -286,7 +332,7 @@
         grad_features[0, s] = (whole[s * C : (s + 1) * C] * filled).astype(BF)
 
 
-def call(kernel, memories, outs, scratch, flops, *args):
+def call(kernel, limit, memories, outs, scratch, flops, *args):
     where = {"s": pltpu.SMEM, "v": pltpu.VMEM}
     return pl.pallas_call(
         kernel,
@@ -294,7 +340,7 @@
         out_specs=[pl.BlockSpec(memory_space=pltpu.VMEM) for _ in outs],
         out_shape=[jax.ShapeDtypeStruct(s, d) for s, d in outs],
         scratch_shapes=[pltpu.VMEM(s, d) for s, d in scratch],
-        compiler_params=pltpu.CompilerParams(vmem_limit_bytes=VMEM_LIMIT),
+        compiler_params=pltpu.CompilerParams(vmem_limit_bytes=limit * 2**20),
         cost_estimate=pl.CostEstimate(flops=flops, bytes_accessed=2**20, transcendentals=0),
         name=kernel.__name__,
     )(*args)
@@ -306,17 +352,17 @@
     return got.astype(F32).sum(0)
 
 
-def sum_over_all(block, sizes):
-    near = ("x", "c", "grp")
+def near_sum(block, sizes):
     parts = sizes["x"] * sizes["c"] * sizes["grp"]
     rows = block.shape[0] // parts
-    got = lax.all_to_all(block.reshape(parts, rows, 128), near, 0, 0)
-    part = got.astype(F32).sum(0)
-    for axis in ("zl", "zh"):
-        if sizes[axis] > 1:
-            part = gather_sum(part.astype(BF), (axis,), sizes[axis])
-    copies = jnp.broadcast_to(part.astype(BF)[None], (parts, rows, 128))
-    return lax.all_to_all(copies, near, 0, 0).reshape(block.shape)
+    got = lax.all_to_all(block.reshape(parts, rows, 128), NEAR, 0, 0)
+    return got.astype(F32).sum(0).astype(BF)
+
+
+def near_gather(block, sizes):
+    parts = sizes["x"] * sizes["c"] * sizes["grp"]
+    copies = jnp.broadcast_to(block[None], (parts,) + block.shape)
+    return lax.all_to_all(copies, NEAR, 0, 0).reshape(parts * block.shape[0], 128)
 
 
 def from_behind(block, axes, devices, distance):
@@ -326,19 +372,16 @@
 
 def on_device(sizes, features, brick_count, send_list, halo_src, kernel, down_kernel, out_grad):
     face_hot, inner_hot, cap_hot, side_hot, down_hot = one_hot_tables()
-    tile = ("zh", "zl", "x", "c")
-    devices = sizes["zh"] * sizes["zl"] * sizes["x"] * sizes["c"]
-    conv5 = kernel.reshape(C, 3, 9, C)
-    conv = conv5.transpose(1, 0, 2, 3).reshape(192, 576)
-    conv_back = conv5.transpose(1, 3, 2, 0).reshape(192, 576)
-    down5 = down_kernel.reshape(C2, 2, 4, C)
-    down_cols = down5.transpose(0, 2, 1, 3).reshape(C2, 512)
-    down_rows = down5.transpose(1, 3, 2, 0).reshape(2 * C, 4 * C2)
-
-    table, outgoing = call(
+    tile = ("z", "x", "c")
+    devices = sizes["z"] * sizes["x"] * sizes["c"]
+    swap = [((CAP, C, 128), BF)] * NOFF
+    conv_back = kernel.reshape(C, 3, 9, C).transpose(1, 3, 2, 0).reshape(192, 576)
+
+    table, *outgoing = call(
         faces_kernel,
+        8,
         "ssvv",
-        [((LOCAL, C, 128), BF), ((NOFF, CAP, C, 128), BF)],
+        [((LOCAL, C, 128), BF)] + swap,
         [],
         2 * 256 * 512 * 768,
         brick_count,
@@ -346,25 +389,26 @@
         features,
         face_hot,
     )
-    received = jnp.stack(
-        [from_behind(outgoing[j], tile, devices, o) for j, o in enumerate(OFFSETS)]
-    )
+    received = [from_behind(b, tile, devices, o) for b, o in zip(outgoing, OFFSETS)]
     (grad_active,) = call(
         upper_kernel,
+        12,
         "vvv",
         [((SLOTS, 2 * C, 512), F32)],
         [],
         10**9,
         out_grad,
         down_hot,
-        down_rows,
+        down_kernel,
     )
     coarse, grad_preact, sums = call(
         main_kernel,
-        "ssvvvvvvvvvvv",
+        28,
+        "ss" + "v" * 14,
         [((1, SLOTS, 64, C2), BF), ((SLOTS, C, 1024), BF), ((1536, 128), BF)],
         [
             ((TABLE, C, 128), BF),
+            ((192, 576), BF),
             ((256, 26 * 128), BF),
             ((256, 1280), BF),
             ((576, 1280), BF),
@@ -377,9 +421,9 @@
         halo_src,
         features,
         table,
-        received,
-        conv,
-        down_cols,
+        *received,
+        kernel,
+        down_kernel,
         out_grad,
         grad_active,
         inner_hot,
@@ -387,16 +431,12 @@
         side_hot,
         down_hot,
     )
-    sums = sum_over_all(sums, sizes)
-    grad_kernel = sums[:960].reshape(5, 3, C, 128).transpose(2, 1, 0, 3).reshape(C, 3, 640)
-    grad_kernel = grad_kernel[:, :, :576].reshape(C, 1728).astype(F32)
-    grad_down = sums[960:1472].reshape(4, C2, 2, C).transpose(1, 2, 0, 3)
-    grad_down = grad_down.reshape(C2, 512).astype(F32)
-
-    interior, grad_local, grad_remote = call(
+    part = near_sum(sums, sizes)
+    interior, grad_local, *remote = call(
         fold_kernel,
+        24,
         "svvvvv",
-        [((256, 512), F32), ((LOCAL, C, 128), F32), ((NOFF, CAP, C, 128), BF)],
+        [((256, 512), F32), ((LOCAL, C, 128), F32)] + swap,
         [
             ((576, 1024), BF),
             ((256, 1280), BF),
@@ -412,12 +452,15 @@
         cap_hot,
         side_hot,
     )
-    returned = jnp.stack(
-        [from_behind(grad_remote[j], tile, devices, -o) for j, o in enumerate(OFFSETS)]
-    )
+    part, *remote = lax.optimization_barrier((part, *remote))
+    part = gather_sum(part, ("z",), sizes["z"])
+    returned = [from_behind(b, tile, devices, -o) for b, o in zip(remote, OFFSETS)]
+    part, *returned = lax.optimization_barrier((part, *returned))
+    sums = near_gather(part.astype(BF), sizes)
     (grad_features,) = call(
         finish_kernel,
-        "ssvvvv",
+        12,
+        "ss" + "v" * 7,
         [((1, SLOTS, C, 512), BF)],
         [((LOCAL, C, 128), F32), ((256, 768), BF)],
         2 * 256 * 512 * 768,
@@ -425,19 +468,20 @@
         send_list,
         interior,
         grad_local,
-        returned,
+        *returned,
         face_hot,
+    )
+    grad_kernel, grad_down = call(
+        unpack_kernel, 8, "v", [((C, 1728), F32), ((C2, 512), F32)], [], 10**6, sums
     )
     return coarse, grad_features, grad_kernel, grad_down
 
 
 def solution(mesh):
     tile, grp = mesh.shape["tile"], mesh.shape["grp"]
-    near = tile // 8
-    low = 4 if near % 4 == 0 else near
-    sizes = {"zh": near // low, "zl": low, "x": 4, "c": 2, "grp": grp}
+    sizes = {"z": tile // 8, "x": 4, "c": 2, "grp": grp}
     fine = Mesh(mesh.devices.reshape(tuple(sizes.values())), tuple(sizes))
-    line = ("zh", "zl", "x", "c")
+    line = ("z", "x", "c")
     in_specs = (
         P("grp", line, None, None),
         P("grp", line),

time: 128 us -> 103 us (0.80)
  the two profiles are of different devices: /device:TPU:32 before, /device:TPU:1 now
where the time goes in v2:
time: 103 us; the launch traced here: 102 us
  starting transfers between devices  59 us (57%)
  Pallas kernels  19.2 us (19%)
  waiting for transfers between devices  12.7 us (12%)
  local copies, waits for them, and re-layouts  9.62 us (9%)
  between operations  1.61 us (2%)
    ppermute x8, starting transfers between devices, from_behind(): return lax.ppermute(block, axes, route)  23.6 us
    pallas_call x6, Pallas kernels, call(): pl.pallas_call(kernel, in_specs=[pl.BlockSpec(memory_space=where[m]) for...  19.2 us
    all_to_all x1, starting transfers between devices, gather_sum(): got = lax.all_to_all(copies, axes, 0, 0)  16 us
    all_to_all x1, starting transfers between devices, near_sum(): got = lax.all_to_all(block.reshape(parts, rows, 128), NEAR, 0, 0)  10.9 us
    all_to_all x1, starting transfers between devices, near_gather(): lax.all_to_all(copies, NEAR, 0, 0).reshape(parts * block.shape[0], 128)  8.39 us
    all_to_all x1, waiting for transfers between devices, near_gather(): lax.all_to_all(copies, NEAR, 0, 0).reshape(parts * block.shape[0], 128)  8.31 us
    unnamed x37, local copies, waits for them, and re-layouts  7.36 us
    all_to_all x1, waiting for transfers between devices, near_sum(): got = lax.all_to_all(block.reshape(parts, rows, 128), NEAR, 0, 0)  2.47 us
  transfers between devices with their start and end apart: 11, of which 4 were waited for; matrix products, arithmetic and copies ran while one was open for 1% of the time, Pallas kernels for 8%

profile of v2, /device:TPU:1, one launch (start us, length us, event | category | flops | bytes accessed | tf_op | source)
XLA Modules:
  0.0 102.2 jit_solution(9394935463026311647)
XLA Ops:
  1.3 0.0 copy-start
  1.3 1.1 %copy-done = bf16[512,768]{1,0:T(8,128)(2,1)S(1)} copy-done((bf16[512,768]{1,0:T(8,128)(2,1)S(1)}, bf16[512,768]{1,0:T(8,128)(2,1)}, u32[]{:S(2)}) %copy-start) | copy-done | bytes 786456
  2.4 0.0 copy-start.2
  2.4 0.9 copy-done.2
  3.4 0.7 copy-done.5
  4.0 0.0 copy-start.8
  4.0 0.0 copy-start.10
  4.1 0.0 copy-start.16
  4.1 0.0 copy-start.17
  4.1 1.1 %faces_kernel.1 = (bf16[25,64,128]{2,1,0:T(8,128)(2,1)S(1)}, bf16[4,64,128]{2,1,0:T(8,128)(2,1)S(1)}, bf16[4,64,128]{2,1,0:T(8,128)(2,1)S(1)}, bf16[4,64,128]{2,1,0:T(8,128)(2,1)S(1)}, bf16[4,64,128]{2,1,0:T(8,128)(2,1)S(1)}) custom-call(s32[1,1]{1,0:T(1,128)S(6)} %copy.25.count, s32[1,1,4,4]{3,2,1,0:T(4,128)S(1)} %copy-done.5, ...), custom_call_target="tpu_custom_call" | custom-call | flops 201326592 | bytes 1048576 | tf_op jit(solution)/shard_map/faces_kernel/pallas_call | solution.py:337
  5.2 0.0 copy-start.3
  5.2 0.0 copy-start.4
  5.3 4.6 %collective-permute-start = (bf16[4,64,128]{2,1,0:T(8,128)(2,1)S(1)}, bf16[4,64,128]{2,1,0:T(8,128)(2,1)S(1)}, u32[]{:S(2)}, u32[]{:S(2)}) collective-permute-start(bf16[4,64,128]{2,1,0:T(8,128)(2,1)S(1)} %get-tuple-element.31), channel_id=1, source_target_pairs={{0,4},{4,8},{8,12},{12,16},{16,20},{20,24},{24,28},{28,32},{32,36}... | collective-permute-start | bytes 196616 | tf_op jit(solution)/shard_map/ppermute | solution.py:370
  9.9 5.6 %collective-permute-start.1 = (bf16[4,64,128]{2,1,0:T(8,128)(2,1)S(1)}, bf16[4,64,128]{2,1,0:T(8,128)(2,1)S(1)}, u32[]{:S(2)}, u32[]{:S(2)}) collective-permute-start(bf16[4,64,128]{2,1,0:T(8,128)(2,1)S(1)} %get-tuple-element.32), channel_id=1, source_target_pairs={{4,0},{8,4},{12,8},{16,12},{20,16},{24,20},{28,24},{32,28},{36,32}... | collective-permute-start | bytes 196616 | tf_op jit(solution)/shard_map/ppermute | solution.py:370
  15.5 1.3 %collective-permute-start.2 = (bf16[4,64,128]{2,1,0:T(8,128)(2,1)S(1)}, bf16[4,64,128]{2,1,0:T(8,128)(2,1)S(1)}, u32[]{:S(2)}, u32[]{:S(2)}) collective-permute-start(bf16[4,64,128]{2,1,0:T(8,128)(2,1)S(1)} %get-tuple-element.33), channel_id=1, source_target_pairs={{0,8},{4,12},{8,16},{12,20},{16,24},{20,28},{24,32},{28,36},{32,40... | collective-permute-start | bytes 196616 | tf_op jit(solution)/shard_map/ppermute | solution.py:370
  16.8 1.3 %collective-permute-start.3 = (bf16[4,64,128]{2,1,0:T(8,128)(2,1)S(1)}, bf16[4,64,128]{2,1,0:T(8,128)(2,1)S(1)}, u32[]{:S(2)}, u32[]{:S(2)}) collective-permute-start(bf16[4,64,128]{2,1,0:T(8,128)(2,1)S(1)} %get-tuple-element.34), channel_id=1, source_target_pairs={{8,0},{12,4},{16,8},{20,12},{24,16},{28,20},{32,24},{36,28},{40,32... | collective-permute-start | bytes 196616 | tf_op jit(solution)/shard_map/ppermute | solution.py:370
  18.1 0.0 copy-start.7
  18.1 0.9 copy-done.7
  19.0 0.8 copy-done.9
  19.8 0.9 copy-done.15
  20.8 1.5 %upper_kernel.1.grad_active = f32[4,128,512]{2,1,0:T(8,128)S(1)} custom-call(bf16[1,4,64,128]{3,2,1,0:T(8,128)(2,1)S(1)} %copy-done.9, bf16[256,512]{1,0:T(8,128)(2,1)S(1)} %copy-done.15, bf16[128,512]{1,0:T(8,128)(2,1)S(1)} %copy-done.7), custom_call_target="tpu_custom_call" | custom-call | flops 1000000000 | bytes 1048576 | tf_op jit(solution)/shard_map/upper_kernel/pallas_call | solution.py:337
  22.3 0.0 collective-permute-done.ahead
  22.3 0.0 collective-permute-done.1.behind
  22.3 0.0 collective-permute-done.2.ahead2
  22.3 0.2 collective-permute-done.3.behind2
  22.5 0.0 copy-done.8
  22.5 0.0 copy-done.10
  22.5 0.0 copy-done.11
  22.5 0.0 copy-done.14
  22.5 0.0 copy-done.16
  22.5 0.0 copy-done.17
  22.5 0.0 copy-done.3
  22.5 0.0 copy-done.4
  22.5 0.0 copy-done.12
  22.5 9.0 %main_kernel.1 = (bf16[1,4,64,128]{3,2,1,0:T(8,128)(2,1)}, bf16[4,64,1024]{2,1,0:T(8,128)(2,1)S(1)}, bf16[1536,128]{1,0:T(8,128)(2,1)}) custom-call(s32[1,1]{1,0:T(1,128)S(6)} %copy.25.count, s32[1,4,26]{2,1,0:T(4,128)S(1)} %copy-done.11, bf16[1,4,64,512]{3,2,1,0:T(8,128)(2,1)S(1)} %copy-done.3, bf16[25,64,128]{2,1,0:T(8,128)(2,1)S(1)} %get-tuple-element.30.table, ...), custom_call_target="tpu_custom_call" | custom-call | flops 5000000000 | bytes 1048576 | tf_op jit(solution)/shard_map/main_kernel/pallas_call | solution.py:337
  31.5 10.9 %all-to-all-start = ((bf16[32,48,128]{2,1,0:T(8,128)(2,1)}), bf16[32,48,128]{2,1,0:T(8,128)(2,1)S(1)}, u32[]{:S(2)}, u32[]{:S(2)}) async-start(bf16[32,48,128]{2,1,0:T(8,128)(2,1)} %bitcast.2), calls=%async_computation | async-start | bytes 786432 | tf_op jit(solution)/shard_map/all_to_all | solution.py:358
  42.5 0.3 copy.20
  42.7 0.3 copy.23
  43.1 0.4 reshape.26.conv_back
  43.5 0.0 copy-start.13
  43.5 1.6 %copy-done.13 = bf16[1024,1024]{1,0:T(8,128)(2,1)S(1)} copy-done((bf16[1024,1024]{1,0:T(8,128)(2,1)S(1)}, bf16[1024,1024]{1,0:T(8,128)(2,1)}, u32[]{:S(2)}) %copy-start.13) | copy-done | bytes 2097176
  45.1 4.9 %fold_kernel.1 = (f32[256,512]{1,0:T(8,128)S(1)}, f32[25,64,128]{2,1,0:T(8,128)S(1)}, bf16[4,64,128]{2,1,0:T(8,128)(2,1)S(1)}, bf16[4,64,128]{2,1,0:T(8,128)(2,1...) custom-call(s32[1,4,26]{2,1,0:T(4,128)S(1)} %copy-done.11, ...), custom_call_target="tpu_custom_call" | custom-call | flops 3000000000 | bytes 1048576 | tf_op jit(solution)/shard_map/fold_kernel/pallas_call | solution.py:337
  50.0 0.0 copy-start.1
  50.0 0.0 copy-start.6
  50.0 2.5 %all-to-all-done = bf16[32,48,128]{2,1,0:T(8,128)(2,1)S(1)} async-done(((bf16[32,48,128]{2,1,0:T(8,128)(2,1)}), bf16[32,48,128]{2,1,0:T(8,128)(2,1)S(1)}, u32[]{:S(2)}, u32[]{:S(2)}) %all-to-all-start) | async-done | bytes 393248 | tf_op jit(solution)/shard_map/all_to_all | solution.py:358
  52.5 0.1 reduce_sum.21
  52.6 0.7 broadcast_in_dim.4
  53.3 16.0 %all-to-all-start.1 = ((bf16[16,48,128]{2,1,0:T(8,128)(2,1)}), bf16[16,48,128]{2,1,0:T(8,128)(2,1)S(1)}, u32[]{:S(2)}, u32[]{:S(2)}) async-start(bf16[16,48,128]{2,1,0:T(8,128)(2,1)} %broadcast_in_dim.4), calls=%async_computation.1 | async-start | bytes 393216 | tf_op jit(solution)/shard_map/all_to_all | solution.py:351
  69.3 2.9 %collective-permute-start.4 = (bf16[4,64,128]{2,1,0:T(8,128)(2,1)S(1)}, bf16[4,64,128]{2,1,0:T(8,128)(2,1)S(1)}, u32[]{:S(2)}, u32[]{:S(2)}) collective-permute-start(bf16[4,64,128]{2,1,0:T(8,128)(2,1)S(1)} %get-tuple-element.45), channel_id=1, source_target_pairs={{4,0},{8,4},{12,8},{16,12},{20,16},{24,20},{28,24},{32,28},{36,32}... | collective-permute-start | bytes 196616 | tf_op jit(solution)/shard_map/ppermute | solution.py:370
  72.2 2.7 %collective-permute-start.5 = (bf16[4,64,128]{2,1,0:T(8,128)(2,1)S(1)}, bf16[4,64,128]{2,1,0:T(8,128)(2,1)S(1)}, u32[]{:S(2)}, u32[]{:S(2)}) collective-permute-start(bf16[4,64,128]{2,1,0:T(8,128)(2,1)S(1)} %get-tuple-element.46), channel_id=1, source_target_pairs={{0,4},{4,8},{8,12},{12,16},{16,20},{20,24},{24,28},{28,32},{32,36}... | collective-permute-start | bytes 196616 | tf_op jit(solution)/shard_map/ppermute | solution.py:370
  74.9 1.3 %collective-permute-start.6 = (bf16[4,64,128]{2,1,0:T(8,128)(2,1)S(1)}, bf16[4,64,128]{2,1,0:T(8,128)(2,1)S(1)}, u32[]{:S(2)}, u32[]{:S(2)}) collective-permute-start(bf16[4,64,128]{2,1,0:T(8,128)(2,1)S(1)} %get-tuple-element.47), channel_id=1, source_target_pairs={{8,0},{12,4},{16,8},{20,12},{24,16},{28,20},{32,24},{36,28},{40,32... | collective-permute-start | bytes 196616 | tf_op jit(solution)/shard_map/ppermute | solution.py:370
  76.2 4.0 %collective-permute-start.7 = (bf16[4,64,128]{2,1,0:T(8,128)(2,1)S(1)}, bf16[4,64,128]{2,1,0:T(8,128)(2,1)S(1)}, u32[]{:S(2)}, u32[]{:S(2)}) collective-permute-start(bf16[4,64,128]{2,1,0:T(8,128)(2,1)S(1)} %get-tuple-element.48), channel_id=1, source_target_pairs={{0,8},{4,12},{8,16},{12,20},{16,24},{20,28},{24,32},{28,36},{32,40... | collective-permute-start | bytes 196616 | tf_op jit(solution)/shard_map/ppermute | solution.py:370
  80.2 1.7 %all-to-all-done.1 = bf16[16,48,128]{2,1,0:T(8,128)(2,1)S(1)} async-done(((bf16[16,48,128]{2,1,0:T(8,128)(2,1)}), bf16[16,48,128]{2,1,0:T(8,128)(2,1)S(1)}, u32[]{:S(2)}, u32[]{:S(2)}) %all-to-all-start.1) | async-done | bytes 196640 | tf_op jit(solution)/shard_map/all_to_all | solution.py:351
  81.9 0.0 collective-permute-done.4.ahead
  81.9 0.0 collective-permute-done.5.behind
  81.9 0.0 collective-permute-done.6.ahead2
  81.9 0.0 collective-permute-done.7.behind2
  81.9 0.8 broadcast_in_dim.5
  82.7 8.4 %all-to-all-start.2 = ((bf16[32,48,128]{2,1,0:T(8,128)(2,1)}), bf16[32,48,128]{2,1,0:T(8,128)(2,1)S(1)}, u32[]{:S(2)}, u32[]{:S(2)}) async-start(bf16[32,48,128]{2,1,0:T(8,128)(2,1)} %broadcast_in_dim.5), calls=%async_computation.2 | async-start | bytes 786432 | tf_op jit(solution)/shard_map/all_to_all | solution.py:365
  91.1 0.0 copy-done.1
  91.1 0.0 copy-done.6
  91.1 1.8 %finish_kernel.1 = bf16[1,4,64,512]{3,2,1,0:T(8,128)(2,1)} custom-call(s32[1,1]{1,0:T(1,128)S(6)} %copy.25.count, s32[1,1,4,4]{3,2,1,0:T(4,128)S(1)} %copy-done.6, f32[256,512]{1,0:T(8,128)S(1)} %get-tuple-element.37.interior, f32[25,64,128]{2,1,0:T(8,128)S(1)} %get-tuple-element.38.grad_local, bf16[4,64,128]{2,1,0:T(8,128)(2,1)S(1)} %collective-permute-done.4.ahead, ...), custom_call_target="tpu_custom_call" | custom-call | flops 201326592 | bytes 1048576 | tf_op jit(solution)/shard_map/finish_kernel/pallas_call | solution.py:337
  92.9 8.3 %all-to-all-done.2 = bf16[32,48,128]{2,1,0:T(8,128)(2,1)S(1)} async-done(((bf16[32,48,128]{2,1,0:T(8,128)(2,1)}), bf16[32,48,128]{2,1,0:T(8,128)(2,1)S(1)}, u32[]{:S(2)}, u32[]{:S(2)}) %all-to-all-start.2) | async-done | bytes 393248 | tf_op jit(solution)/shard_map/all_to_all | solution.py:365
  101.2 0.9 unpack_kernel.1
  (7 shorter events, 0.0 us)
Async XLA Ops:
  1.3 1.1 %copy-start = (bf16[512,768]{1,0:T(8,128)(2,1)S(1)}, bf16[512,768]{1,0:T(8,128)(2,1)}, u32[]{:S(2)}) copy-start(bf16[512,768]{1,0:T(8,128)(2,1)} %constant.14.clone.face_hot) | copy-start | bytes 2359300
  2.4 0.9 copy-start.2
  3.4 0.7 copy-start.5
  4.0 18.4 %copy-start.8 = (bf16[128,512]{1,0:T(8,128)(2,1)S(1)}, bf16[128,512]{1,0:T(8,128)(2,1)}, u32[]{:S(2)}) copy-start(bf16[128,512]{1,0:T(8,128)(2,1)} %down_kernel.3) | copy-start | bytes 393220
  4.0 18.4 %copy-start.10 = (bf16[1,4,64,128]{3,2,1,0:T(8,128)(2,1)S(1)}, bf16[1,4,64,128]{3,2,1,0:T(8,128)(2,1)}, u32[]{:S(2)}) copy-start(bf16[1,4,64,128]{3,2,1,0:T(8,128)(2,1)} %out_grad.3) | copy-start | bytes 196612
  4.1 18.4 %copy-start.11 = (s32[1,4,26]{2,1,0:T(4,128)S(1)}, s32[1,4,26]{2,1,0:T(4,128)}, u32[]{:S(2)}) copy-start(s32[1,4,26]{2,1,0:T(4,128)} %sources.3) | copy-start | bytes 1252
  4.1 18.4 %copy-start.14 = (bf16[1152,128]{1,0:T(8,128)(2,1)S(1)}, bf16[1152,128]{1,0:T(8,128)(2,1)}, u32[]{:S(2)}) copy-start(bf16[1152,128]{1,0:T(8,128)(2,1)} %constant.17.clone.cap_hot) | copy-start | bytes 884740
  4.1 18.4 %copy-start.16 = (bf16[256,512]{1,0:T(8,128)(2,1)S(1)}, bf16[256,512]{1,0:T(8,128)(2,1)}, u32[]{:S(2)}) copy-start(bf16[256,512]{1,0:T(8,128)(2,1)} %constant.15.clone.down_hot) | copy-start | bytes 786436
  4.1 18.4 %copy-start.17 = (bf16[128,256]{1,0:T(8,128)(2,1)S(1)}, bf16[128,256]{1,0:T(8,128)(2,1)}, u32[]{:S(2)}) copy-start(bf16[128,256]{1,0:T(8,128)(2,1)} %constant.16.clone.inner_hot) | copy-start | bytes 196612
  5.2 17.3 %copy-start.3 = (bf16[1,4,64,512]{3,2,1,0:T(8,128)(2,1)S(1)}, bf16[1,4,64,512]{3,2,1,0:T(8,128)(2,1)}, u32[]{:S(2)}) copy-start(bf16[1,4,64,512]{3,2,1,0:T(8,128)(2,1)} %features.3) | copy-start | bytes 786436
  5.2 17.3 %copy-start.4 = (bf16[64,1728]{1,0:T(8,128)(2,1)S(1)}, bf16[64,1728]{1,0:T(8,128)(2,1)}, u32[]{:S(2)}) copy-start(bf16[64,1728]{1,0:T(8,128)(2,1)} %kernel.1) | copy-start | bytes 663556
  5.3 17.0 %collective-permute-start = (bf16[4,64,128]{2,1,0:T(8,128)(2,1)S(1)}, bf16[4,64,128]{2,1,0:T(8,128)(2,1)S(1)}, u32[]{:S(2)}, u32[]{:S(2)}) collective-permute-start(bf16[4,64,128]{2,1,0:T(8,128)(2,1)S(1)} %get-tuple-element.31), channel_id=1, source_target_pairs={{0,4},{4,8},{8,12},{12,16},{16,20},{20,24},{24,28},{28,32},{32,36}... | collective-permute-start | bytes 196616 | tf_op jit(solution)/shard_map/ppermute | solution.py:370
  9.9 12.4 %collective-permute-start.1 = (bf16[4,64,128]{2,1,0:T(8,128)(2,1)S(1)}, bf16[4,64,128]{2,1,0:T(8,128)(2,1)S(1)}, u32[]{:S(2)}, u32[]{:S(2)}) collective-permute-start(bf16[4,64,128]{2,1,0:T(8,128)(2,1)S(1)} %get-tuple-element.32), channel_id=1, source_target_pairs={{4,0},{8,4},{12,8},{16,12},{20,16},{24,20},{28,24},{32,28},{36,32}... | collective-permute-start | bytes 196616 | tf_op jit(solution)/shard_map/ppermute | solution.py:370
  15.5 6.8 %collective-permute-start.2 = (bf16[4,64,128]{2,1,0:T(8,128)(2,1)S(1)}, bf16[4,64,128]{2,1,0:T(8,128)(2,1)S(1)}, u32[]{:S(2)}, u32[]{:S(2)}) collective-permute-start(bf16[4,64,128]{2,1,0:T(8,128)(2,1)S(1)} %get-tuple-element.33), channel_id=1, source_target_pairs={{0,8},{4,12},{8,16},{12,20},{16,24},{20,28},{24,32},{28,36},{32,40... | collective-permute-start | bytes 196616 | tf_op jit(solution)/shard_map/ppermute | solution.py:370
  16.8 5.7 %collective-permute-start.3 = (bf16[4,64,128]{2,1,0:T(8,128)(2,1)S(1)}, bf16[4,64,128]{2,1,0:T(8,128)(2,1)S(1)}, u32[]{:S(2)}, u32[]{:S(2)}) collective-permute-start(bf16[4,64,128]{2,1,0:T(8,128)(2,1)S(1)} %get-tuple-element.34), channel_id=1, source_target_pairs={{8,0},{12,4},{16,8},{20,12},{24,16},{28,20},{32,24},{36,28},{40,32... | collective-permute-start | bytes 196616 | tf_op jit(solution)/shard_map/ppermute | solution.py:370
  18.1 0.9 copy-start.7
  19.0 0.8 copy-start.9
  19.8 0.9 copy-start.15
  20.8 1.8 %copy-start.12 = (bf16[1024,1024]{1,0:T(8,128)(2,1)S(1)}, bf16[1024,1024]{1,0:T(8,128)(2,1)}, u32[]{:S(2)}) copy-start(bf16[1024,1024]{1,0:T(8,128)(2,1)} %constant.18.clone.side_hot) | copy-start | bytes 6291460
  31.5 21.0 %all-to-all-start = ((bf16[32,48,128]{2,1,0:T(8,128)(2,1)}), bf16[32,48,128]{2,1,0:T(8,128)(2,1)S(1)}, u32[]{:S(2)}, u32[]{:S(2)}) async-start(bf16[32,48,128]{2,1,0:T(8,128)(2,1)} %bitcast.2), calls=%async_computation | async-start | bytes 786432 | tf_op jit(solution)/shard_map/all_to_all | solution.py:358
  43.5 1.6 %copy-start.13 = (bf16[1024,1024]{1,0:T(8,128)(2,1)S(1)}, bf16[1024,1024]{1,0:T(8,128)(2,1)}, u32[]{:S(2)}) copy-start(bf16[1024,1024]{1,0:T(8,128)(2,1)} %constant.18.clone.side_hot) | copy-start | bytes 6291460
  50.0 41.1 %copy-start.1 = (bf16[512,768]{1,0:T(8,128)(2,1)S(1)}, bf16[512,768]{1,0:T(8,128)(2,1)}, u32[]{:S(2)}) copy-start(bf16[512,768]{1,0:T(8,128)(2,1)} %constant.14.clone.face_hot) | copy-start | bytes 2359300
  50.0 41.1 %copy-start.6 = (s32[1,1,4,4]{3,2,1,0:T(4,128)S(1)}, s32[1,1,4,4]{3,2,1,0:T(4,128)}, u32[]{:S(2)}) copy-start(s32[1,1,4,4]{3,2,1,0:T(4,128)} %sends.3) | copy-start | bytes 196
  53.3 28.5 %all-to-all-start.1 = ((bf16[16,48,128]{2,1,0:T(8,128)(2,1)}), bf16[16,48,128]{2,1,0:T(8,128)(2,1)S(1)}, u32[]{:S(2)}, u32[]{:S(2)}) async-start(bf16[16,48,128]{2,1,0:T(8,128)(2,1)} %broadcast_in_dim.4), calls=%async_computation.1 | async-start | bytes 393216 | tf_op jit(solution)/shard_map/all_to_all | solution.py:351
  69.3 12.6 %collective-permute-start.4 = (bf16[4,64,128]{2,1,0:T(8,128)(2,1)S(1)}, bf16[4,64,128]{2,1,0:T(8,128)(2,1)S(1)}, u32[]{:S(2)}, u32[]{:S(2)}) collective-permute-start(bf16[4,64,128]{2,1,0:T(8,128)(2,1)S(1)} %get-tuple-element.45), channel_id=1, source_target_pairs={{4,0},{8,4},{12,8},{16,12},{20,16},{24,20},{28,24},{32,28},{36,32}... | collective-permute-start | bytes 196616 | tf_op jit(solution)/shard_map/ppermute | solution.py:370
  72.2 9.7 %collective-permute-start.5 = (bf16[4,64,128]{2,1,0:T(8,128)(2,1)S(1)}, bf16[4,64,128]{2,1,0:T(8,128)(2,1)S(1)}, u32[]{:S(2)}, u32[]{:S(2)}) collective-permute-start(bf16[4,64,128]{2,1,0:T(8,128)(2,1)S(1)} %get-tuple-element.46), channel_id=1, source_target_pairs={{0,4},{4,8},{8,12},{12,16},{16,20},{20,24},{24,28},{28,32},{32,36}... | collective-permute-start | bytes 196616 | tf_op jit(solution)/shard_map/ppermute | solution.py:370
  74.9 7.0 %collective-permute-start.6 = (bf16[4,64,128]{2,1,0:T(8,128)(2,1)S(1)}, bf16[4,64,128]{2,1,0:T(8,128)(2,1)S(1)}, u32[]{:S(2)}, u32[]{:S(2)}) collective-permute-start(bf16[4,64,128]{2,1,0:T(8,128)(2,1)S(1)} %get-tuple-element.47), channel_id=1, source_target_pairs={{8,0},{12,4},{16,8},{20,12},{24,16},{28,20},{32,24},{36,28},{40,32... | collective-permute-start | bytes 196616 | tf_op jit(solution)/shard_map/ppermute | solution.py:370
  76.2 5.7 %collective-permute-start.7 = (bf16[4,64,128]{2,1,0:T(8,128)(2,1)S(1)}, bf16[4,64,128]{2,1,0:T(8,128)(2,1)S(1)}, u32[]{:S(2)}, u32[]{:S(2)}) collective-permute-start(bf16[4,64,128]{2,1,0:T(8,128)(2,1)S(1)} %get-tuple-element.48), channel_id=1, source_target_pairs={{0,8},{4,12},{8,16},{12,20},{16,24},{20,28},{24,32},{28,36},{32,40... | collective-permute-start | bytes 196616 | tf_op jit(solution)/shard_map/ppermute | solution.py:370
  82.7 18.5 %all-to-all-start.2 = ((bf16[32,48,128]{2,1,0:T(8,128)(2,1)}), bf16[32,48,128]{2,1,0:T(8,128)(2,1)S(1)}, u32[]{:S(2)}, u32[]{:S(2)}) async-start(bf16[32,48,128]{2,1,0:T(8,128)(2,1)} %broadcast_in_dim.5), calls=%async_computation.2 | async-start | bytes 786432 | tf_op jit(solution)/shard_map/all_to_all | solution.py:365

commit v3 on v2

--- a/solution.py
+++ b/solution.py
@@ -18,7 +18,7 @@
 LOCAL = 6 * SLOTS + 1
 TABLE = LOCAL + NOFF * CAP
 OFFSETS = (1, -1, 2, -2)
-NEAR = ("x", "c", "grp")
+NEAR = ("zl", "x", "c", "grp")
 
 
 def rim_cells(d, full):
@@ -94,7 +94,22 @@
     )
 
 
-def faces_kernel(count, sends, features, face_hot, table, *outgoing):
+def fetch(sources, targets, done):
+    copies = [
+        pltpu.make_async_copy(a, b, done.at[i]) for i, (a, b) in enumerate(zip(sources, targets))
+    ]
+    for copy in copies:
+        copy.start()
+    return copies
+
+
+def faces_kernel(
+    count, sends_far, features_far, face_far, table, *rest
+):
+    outgoing, (sends, features, face_hot, done) = rest[:NOFF], rest[NOFF:]
+    copies = fetch((features_far, face_far, sends_far), (features, face_hot, sends), done)
+    for copy in copies:
+        copy.wait()
     masked = masked_rows(features, count[0, 0])
     for f in range(6):
         layer = nn(masked, face_hot[:, f * 128 : (f + 1) * 128]).astype(BF)
@@ -106,7 +121,29 @@
             outgoing[j][c] = table[sends[0, 0, j, c]]
 
 
-def upper_kernel(out_grad, down_hot, down_kernel, grad_active):
+def upper_kernel(
+    out_grad,
+    down_hot,
+    down_kernel,
+    kernel,
+    grad_active,
+    conv_back,
+    out_grad_kept,
+    down_hot_kept,
+    down_kernel_kept,
+    kernel_kept,
+    done,
+):
+    copies = fetch(
+        (out_grad, down_hot, down_kernel, kernel),
+        (out_grad_kept, down_hot_kept, down_kernel_kept, kernel_kept),
+        done,
+    )
+    tall = jnp.transpose(kernel[...].astype(F32)).astype(BF)
+    for o in range(3):
+        conv_back[o * C : (o + 1) * C] = jnp.concatenate(
+            [tall[(9 * o + k) * C : (9 * o + k + 1) * C] for k in range(9)], axis=1
+        )
     tall = jnp.transpose(down_kernel[...].astype(F32)).astype(BF)
     down_rows = jnp.concatenate(
         [
@@ -121,6 +158,8 @@
             [nn(turned, down_hot[t * 64 : (t + 1) * 64]).astype(BF) for t in range(4)], axis=0
         )
         grad_active[s] = nn(down_rows, spread)
+    for copy in copies:
+        copy.wait()
 
 
 def main_kernel(
@@ -333,13 +372,13 @@
 
 
 def call(kernel, limit, memories, outs, scratch, flops, *args):
-    where = {"s": pltpu.SMEM, "v": pltpu.VMEM}
+    where = {"s": pltpu.SMEM, "v": pltpu.VMEM, "h": pltpu.HBM}
     return pl.pallas_call(
         kernel,
         in_specs=[pl.BlockSpec(memory_space=where[m]) for m in memories],
         out_specs=[pl.BlockSpec(memory_space=pltpu.VMEM) for _ in outs],
         out_shape=[jax.ShapeDtypeStruct(s, d) for s, d in outs],
-        scratch_shapes=[pltpu.VMEM(s, d) for s, d in scratch],
+        scratch_shapes=[pltpu.VMEM(*s) if isinstance(s, tuple) else s for s in scratch],
         compiler_params=pltpu.CompilerParams(vmem_limit_bytes=limit * 2**20),
         cost_estimate=pl.CostEstimate(flops=flops, bytes_accessed=2**20, transcendentals=0),
         name=kernel.__name__,
@@ -353,14 +392,14 @@
 
 
 def near_sum(block, sizes):
-    parts = sizes["x"] * sizes["c"] * sizes["grp"]
+    parts = sizes["zl"] * sizes["x"] * sizes["c"] * sizes["grp"]
     rows = block.shape[0] // parts
     got = lax.all_to_all(block.reshape(parts, rows, 128), NEAR, 0, 0)
     return got.astype(F32).sum(0).astype(BF)
 
 
 def near_gather(block, sizes):
-    parts = sizes["x"] * sizes["c"] * sizes["grp"]
+    parts = sizes["zl"] * sizes["x"] * sizes["c"] * sizes["grp"]
     copies = jnp.broadcast_to(block[None], (parts,) + block.shape)
     return lax.all_to_all(copies, NEAR, 0, 0).reshape(parts * block.shape[0], 128)
 
@@ -372,17 +411,21 @@
 
 def on_device(sizes, features, brick_count, send_list, halo_src, kernel, down_kernel, out_grad):
     face_hot, inner_hot, cap_hot, side_hot, down_hot = one_hot_tables()
-    tile = ("z", "x", "c")
-    devices = sizes["z"] * sizes["x"] * sizes["c"]
+    tile = ("zh", "zl", "x", "c")
+    devices = sizes["zh"] * sizes["zl"] * sizes["x"] * sizes["c"]
     swap = [((CAP, C, 128), BF)] * NOFF
-    conv_back = kernel.reshape(C, 3, 9, C).transpose(1, 3, 2, 0).reshape(192, 576)
 
     table, *outgoing = call(
         faces_kernel,
-        8,
-        "ssvv",
+        56,
+        "shhh",
         [((LOCAL, C, 128), BF)] + swap,
-        [],
+        [
+            pltpu.SMEM((1, 1, NOFF, CAP), jnp.int32),
+            ((1, SLOTS, C, 512), BF),
+            ((512, 768), BF),
+            pltpu.SemaphoreType.DMA((3,)),
+        ],
         2 * 256 * 512 * 768,
         brick_count,
         send_list,
@@ -390,22 +433,34 @@
         face_hot,
     )
     received = [from_behind(b, tile, devices, o) for b, o in zip(outgoing, OFFSETS)]
-    (grad_active,) = call(
+    grad_active, conv_back, out_grad, down_hot, down_kernel, kernel = call(
         upper_kernel,
         12,
-        "vvv",
-        [((SLOTS, 2 * C, 512), F32)],
-        [],
+        "vvvv",
+        [
+            ((SLOTS, 2 * C, 512), F32),
+            ((192, 576), BF),
+            ((1, SLOTS, 64, C2), BF),
+            ((256, 512), BF),
+            ((C2, 512), BF),
+            ((C, 1728), BF),
+        ],
+        [pltpu.SemaphoreType.DMA((4,))],
         10**9,
         out_grad,
         down_hot,
         down_kernel,
+        kernel,
     )
     coarse, grad_preact, sums = call(
         main_kernel,
         28,
         "ss" + "v" * 14,
-        [((1, SLOTS, 64, C2), BF), ((SLOTS, C, 1024), BF), ((1536, 128), BF)],
+        [
+            ((1, SLOTS, 64, C2), BF),
+            ((SLOTS, C, 1024), BF),
+            ((1536, 128), BF),
+        ],
         [
             ((TABLE, C, 128), BF),
             ((192, 576), BF),
@@ -453,7 +508,7 @@
         side_hot,
     )
     part, *remote = lax.optimization_barrier((part, *remote))
-    part = gather_sum(part, ("z",), sizes["z"])
+    part = gather_sum(part, ("zh",), sizes["zh"])
     returned = [from_behind(b, tile, devices, -o) for b, o in zip(remote, OFFSETS)]
     part, *returned = lax.optimization_barrier((part, *returned))
     sums = near_gather(part.astype(BF), sizes)
@@ -479,9 +534,11 @@
 
 def solution(mesh):
     tile, grp = mesh.shape["tile"], mesh.shape["grp"]
-    sizes = {"z": tile // 8, "x": 4, "c": 2, "grp": grp}
+    planes = tile // 8
+    pair = 2 - planes % 2
+    sizes = {"zh": planes // pair, "zl": pair, "x": 4, "c": 2, "grp": grp}
     fine = Mesh(mesh.devices.reshape(tuple(sizes.values())), tuple(sizes))
-    line = ("z", "x", "c")
+    line = ("zh", "zl", "x", "c")
     in_specs = (
         P("grp", line, None, None),
         P("grp", line),

time: 103 us -> 107 us (1.039)
  local copies, waits for them, and re-layouts: 9.62 us -> 6.68 us
  waiting for transfers between devices: 12.7 us -> 15.5 us
  Pallas kernels: 19.2 us -> 21.4 us
    pallas_call x6, Pallas kernels: 19.2 us -> 21.4 us  [call(): pl.pallas_call(kernel, in_specs=[pl.BlockSpec(memory_space=where[m]) for...]
    all_to_all x1, waiting for transfers between devices: 2.47 us -> 4.57 us  [near_sum(): got = lax.all_to_all(block.reshape(parts, rows, 128), NEAR, 0, 0)]
    unnamed x37 -> x26, local copies, waits for them, and re-layouts: 7.36 us -> 5.26 us
  transfers between devices with their start and end apart: 11 -> 11, of which waited for: 4 -> 4; matrix products, arithmetic and copies ran while one was open for 1% -> 0% of each run, Pallas kernels for 8% -> 8%
where the time goes in v3:
time: 107 us; the launch traced here: 106 us
  starting transfers between devices  59.4 us (56%)
  Pallas kernels  21.4 us (20%)
  waiting for transfers between devices  15.5 us (14%)
  local copies, waits for them, and re-layouts  6.68 us (6%)
  between operations  1.57 us (1%)
  other arithmetic  1.09 us (1%)
    ppermute x8, starting transfers between devices, from_behind(): return lax.ppermute(block, axes, route)  23.6 us
    pallas_call x6, Pallas kernels, call(): pl.pallas_call(kernel, in_specs=[pl.BlockSpec(memory_space=where[m]) for...  21.4 us
    all_to_all x1, starting transfers between devices, gather_sum(): got = lax.all_to_all(copies, axes, 0, 0)  15.2 us
    all_to_all x1, starting transfers between devices, near_sum(): got = lax.all_to_all(block.reshape(parts, rows, 128), NEAR, 0, 0)  11.7 us
    all_to_all x1, waiting for transfers between devices, near_gather(): lax.all_to_all(copies, NEAR, 0, 0).reshape(parts * block.shape[0], 128)  9.36 us
    all_to_all x1, starting transfers between devices, near_gather(): lax.all_to_all(copies, NEAR, 0, 0).reshape(parts * block.shape[0], 128)  8.87 us
    unnamed x26, local copies, waits for them, and re-layouts  5.26 us
    all_to_all x1, waiting for transfers between devices, near_sum(): got = lax.all_to_all(block.reshape(parts, rows, 128), NEAR, 0, 0)  4.57 us
  transfers between devices with their start and end apart: 11, of which 4 were waited for; matrix products, arithmetic and copies ran while one was open for 0% of the time, Pallas kernels for 8%

profile of v3, /device:TPU:1, one launch (start us, length us, event | category | flops | bytes accessed | tf_op | source)
XLA Modules:
  0.0 105.6 jit_solution(7384968827165951709)
XLA Ops:
  1.3 0.0 copy-start.7
  1.3 0.0 copy-start.10
  1.3 0.0 copy-start.12
  1.3 2.7 %faces_kernel.1 = (bf16[25,64,128]{2,1,0:T(8,128)(2,1)}, bf16[4,64,128]{2,1,0:T(8,128)(2,1)}, bf16[4,64,128]{2,1,0:T(8,128)(2,1)}, bf16[4,64,128]{2,1,0:T(8,128)(2,1)}, bf16[4,64,128]{2,1,0:T(8,128)(2,1)}) custom-call(s32[1,1]{1,0:T(1,128)S(6)} %copy.16.count, s32[1,1,4,4]{3,2,1,0:T(4,128)} %sends.1, bf16[1,4,64,512]{3,2,1,0:T(8,128)(2,1)} %features.1, ...), custom_call_target="tpu_custom_call" | custom-call | flops 201326592 | bytes 1048576 | tf_op jit(solution)/shard_map/faces_kernel/pallas_call | solution.py:376
  4.0 0.0 copy-start.1
  4.0 0.0 copy-start.3
  4.0 4.6 %collective-permute-start = (bf16[4,64,128]{2,1,0:T(8,128)(2,1)}, bf16[4,64,128]{2,1,0:T(8,128)(2,1)S(1)}, u32[]{:S(2)}, u32[]{:S(2)}) collective-permute-start(bf16[4,64,128]{2,1,0:T(8,128)(2,1)} %get-tuple-element.37), channel_id=1, source_target_pairs={{0,4},{4,8},{8,12},{12,16},{16,20},{20,24},{24,28},{28,32},{32,36}... | collective-permute-start | bytes 196616 | tf_op jit(solution)/shard_map/ppermute | solution.py:409
  8.7 5.6 %collective-permute-start.1 = (bf16[4,64,128]{2,1,0:T(8,128)(2,1)}, bf16[4,64,128]{2,1,0:T(8,128)(2,1)S(1)}, u32[]{:S(2)}, u32[]{:S(2)}) collective-permute-start(bf16[4,64,128]{2,1,0:T(8,128)(2,1)} %get-tuple-element.38), channel_id=1, source_target_pairs={{4,0},{8,4},{12,8},{16,12},{20,16},{24,20},{28,24},{32,28},{36,32}... | collective-permute-start | bytes 196616 | tf_op jit(solution)/shard_map/ppermute | solution.py:409
  14.3 1.3 %collective-permute-start.2 = (bf16[4,64,128]{2,1,0:T(8,128)(2,1)}, bf16[4,64,128]{2,1,0:T(8,128)(2,1)S(1)}, u32[]{:S(2)}, u32[]{:S(2)}) collective-permute-start(bf16[4,64,128]{2,1,0:T(8,128)(2,1)} %get-tuple-element.39), channel_id=1, source_target_pairs={{0,8},{4,12},{8,16},{12,20},{16,24},{20,28},{24,32},{28,36},{32,40... | collective-permute-start | bytes 196616 | tf_op jit(solution)/shard_map/ppermute | solution.py:409
  15.6 1.3 %collective-permute-start.3 = (bf16[4,64,128]{2,1,0:T(8,128)(2,1)}, bf16[4,64,128]{2,1,0:T(8,128)(2,1)S(1)}, u32[]{:S(2)}, u32[]{:S(2)}) collective-permute-start(bf16[4,64,128]{2,1,0:T(8,128)(2,1)} %get-tuple-element.40), channel_id=1, source_target_pairs={{8,0},{12,4},{16,8},{20,12},{24,16},{28,20},{32,24},{36,28},{40,32... | collective-permute-start | bytes 196616 | tf_op jit(solution)/shard_map/ppermute | solution.py:409
  16.9 0.0 copy-start.4
  16.9 0.9 copy-done.4
  17.8 0.0 copy-start.5
  17.8 0.9 copy-done.5
  18.7 0.0 copy-start.6
  18.7 0.8 copy-done.6
  19.5 0.0 copy-start.11
  19.5 0.9 copy-done.11
  20.5 0.0 copy-start.8
  20.5 2.1 %upper_kernel.1 = (f32[4,128,512]{2,1,0:T(8,128)S(1)}, bf16[192,576]{1,0:T(8,128)(2,1)S(1)}, bf16[1,4,64,128]{3,2,1,0:T(8,128)(2,1)S(1)}, bf16[256,512]{1,0:T(8,...) custom-call(bf16[1,4,64,128]{3,2,1,0:T(8,128)(2,1)S(1)} %copy-done.6, ...), custom_call_target="tpu_custom_call" | custom-call | flops 1000000000 | bytes 1048576 | tf_op jit(solution)/shard_map/upper_kernel/pallas_call | solution.py:376
  22.6 0.0 collective-permute-done.ahead
  22.6 0.0 collective-permute-done.1.behind
  22.6 0.0 collective-permute-done.2.ahead2
  22.6 0.0 collective-permute-done.3.behind2
  22.6 0.0 copy-done.7
  22.6 0.0 copy-done.10
  22.6 0.0 copy-done.12
  22.6 0.0 copy-done.1
  22.7 0.0 copy-done.3
  22.7 0.0 copy-done.8
  22.7 9.0 %main_kernel.1 = (bf16[1,4,64,128]{3,2,1,0:T(8,128)(2,1)}, bf16[4,64,1024]{2,1,0:T(8,128)(2,1)S(1)}, bf16[1536,128]{1,0:T(8,128)(2,1)}) custom-call(s32[1,1]{1,0:T(1,128)S(6)} %copy.16.count, s32[1,4,26]{2,1,0:T(4,128)S(1)} %copy-done.7, bf16[1,4,64,512]{3,2,1,0:T(8,128)(2,1)S(1)} %copy-done.1, bf16[25,64,128]{2,1,0:T(8,128)(2,1)S(1)} %copy-done.3, ...), custom_call_target="tpu_custom_call" | custom-call | flops 5000000000 | bytes 1048576 | tf_op jit(solution)/shard_map/main_kernel/pallas_call | solution.py:376
  31.6 11.7 %all-to-all-start = ((bf16[64,24,128]{2,1,0:T(8,128)(2,1)}), bf16[64,24,128]{2,1,0:T(8,128)(2,1)}, u32[]{:S(2)}, u32[]{:S(2)}) async-start(bf16[64,24,128]{2,1,0:T(8,128)(2,1)} %bitcast), calls=%async_computation | async-start | bytes 786432 | tf_op jit(solution)/shard_map/all_to_all | solution.py:397
  43.3 0.0 copy-start.9
  43.4 1.6 %copy-done.9 = bf16[1024,1024]{1,0:T(8,128)(2,1)S(1)} copy-done((bf16[1024,1024]{1,0:T(8,128)(2,1)S(1)}, bf16[1024,1024]{1,0:T(8,128)(2,1)}, u32[]{:S(2)}) %copy-start.9) | copy-done | bytes 2097176
  44.9 0.0 copy-start.2
  44.9 4.9 %fold_kernel.1 = (f32[256,512]{1,0:T(8,128)S(1)}, f32[25,64,128]{2,1,0:T(8,128)S(1)}, bf16[4,64,128]{2,1,0:T(8,128)(2,1)S(1)}, bf16[4,64,128]{2,1,0:T(8,128)(2,1...) custom-call(s32[1,4,26]{2,1,0:T(4,128)S(1)} %copy-done.7, ...), custom_call_target="tpu_custom_call" | custom-call | flops 3000000000 | bytes 1048576 | tf_op jit(solution)/shard_map/fold_kernel/pallas_call | solution.py:376
  49.9 0.0 copy-start
  49.9 4.6 %all-to-all-done = bf16[64,24,128]{2,1,0:T(8,128)(2,1)} async-done(((bf16[64,24,128]{2,1,0:T(8,128)(2,1)}), bf16[64,24,128]{2,1,0:T(8,128)(2,1)}, u32[]{:S(2)}, u32[]{:S(2)}) %all-to-all-start) | async-done | bytes 393248 | tf_op jit(solution)/shard_map/all_to_all | solution.py:397
  54.4 1.1 %reduce_sum.21 = bf16[24,128]{1,0:T(8,128)(2,1)S(1)} reduce(bf16[64,24,128]{2,1,0:T(8,128)(2,1)} %all-to-all-done, bf16[]{:T(256)} %constant.12.clone.1), dimensions={0}, to_apply=%region_0.0 | reduce | flops 193536 | bytes 399362 | tf_op jit(solution)/shard_map/reduce_sum | solution.py:398
  55.5 0.6 broadcast_in_dim.4
  56.2 15.2 %all-to-all-start.1 = ((bf16[8,24,128]{2,1,0:T(8,128)(2,1)}), bf16[8,24,128]{2,1,0:T(8,128)(2,1)S(1)}, u32[]{:S(2)}, u32[]{:S(2)}) async-start(bf16[8,24,128]{2,1,0:T(8,128)(2,1)} %broadcast_in_dim.4), calls=%async_computation.1 | async-start | bytes 98304 | tf_op jit(solution)/shard_map/all_to_all | solution.py:390
  71.4 2.8 %collective-permute-start.4 = (bf16[4,64,128]{2,1,0:T(8,128)(2,1)S(1)}, bf16[4,64,128]{2,1,0:T(8,128)(2,1)S(1)}, u32[]{:S(2)}, u32[]{:S(2)}) collective-permute-start(bf16[4,64,128]{2,1,0:T(8,128)(2,1)S(1)} %get-tuple-element.57), channel_id=1, source_target_pairs={{4,0},{8,4},{12,8},{16,12},{20,16},{24,20},{28,24},{32,28},{36,32}... | collective-permute-start | bytes 196616 | tf_op jit(solution)/shard_map/ppermute | solution.py:409
  74.1 2.8 %collective-permute-start.5 = (bf16[4,64,128]{2,1,0:T(8,128)(2,1)S(1)}, bf16[4,64,128]{2,1,0:T(8,128)(2,1)S(1)}, u32[]{:S(2)}, u32[]{:S(2)}) collective-permute-start(bf16[4,64,128]{2,1,0:T(8,128)(2,1)S(1)} %get-tuple-element.58), channel_id=1, source_target_pairs={{0,4},{4,8},{8,12},{12,16},{16,20},{20,24},{24,28},{28,32},{32,36}... | collective-permute-start | bytes 196616 | tf_op jit(solution)/shard_map/ppermute | solution.py:409
  76.9 1.3 %collective-permute-start.6 = (bf16[4,64,128]{2,1,0:T(8,128)(2,1)S(1)}, bf16[4,64,128]{2,1,0:T(8,128)(2,1)S(1)}, u32[]{:S(2)}, u32[]{:S(2)}) collective-permute-start(bf16[4,64,128]{2,1,0:T(8,128)(2,1)S(1)} %get-tuple-element.59), channel_id=1, source_target_pairs={{8,0},{12,4},{16,8},{20,12},{24,16},{28,20},{32,24},{36,28},{40,32... | collective-permute-start | bytes 196616 | tf_op jit(solution)/shard_map/ppermute | solution.py:409
  78.2 4.0 %collective-permute-start.7 = (bf16[4,64,128]{2,1,0:T(8,128)(2,1)S(1)}, bf16[4,64,128]{2,1,0:T(8,128)(2,1)S(1)}, u32[]{:S(2)}, u32[]{:S(2)}) collective-permute-start(bf16[4,64,128]{2,1,0:T(8,128)(2,1)S(1)} %get-tuple-element.60), channel_id=1, source_target_pairs={{0,8},{4,12},{8,16},{12,20},{16,24},{20,28},{24,32},{28,36},{32,40... | collective-permute-start | bytes 196616 | tf_op jit(solution)/shard_map/ppermute | solution.py:409
  82.2 1.3 %all-to-all-done.1 = bf16[8,24,128]{2,1,0:T(8,128)(2,1)S(1)} async-done(((bf16[8,24,128]{2,1,0:T(8,128)(2,1)}), bf16[8,24,128]{2,1,0:T(8,128)(2,1)S(1)}, u32[]{:S(2)}, u32[]{:S(2)}) %all-to-all-start.1) | async-done | bytes 49184 | tf_op jit(solution)/shard_map/all_to_all | solution.py:390
  83.5 0.0 collective-permute-done.4.ahead
  83.6 0.0 collective-permute-done.5.behind
  83.6 0.0 collective-permute-done.6.ahead2
  83.6 0.3 collective-permute-done.7.behind2
  83.8 0.8 broadcast_in_dim.5
  84.6 8.9 %all-to-all-start.2 = ((bf16[64,24,128]{2,1,0:T(8,128)(2,1)}), bf16[64,24,128]{2,1,0:T(8,128)(2,1)S(1)}, u32[]{:S(2)}, u32[]{:S(2)}) async-start(bf16[64,24,128]{2,1,0:T(8,128)(2,1)} %broadcast_in_dim.5), calls=%async_computation.2 | async-start | bytes 786432 | tf_op jit(solution)/shard_map/all_to_all | solution.py:404
  93.5 0.0 copy-done.2
  93.5 0.0 copy-done
  93.5 1.8 %finish_kernel.1 = bf16[1,4,64,512]{3,2,1,0:T(8,128)(2,1)} custom-call(s32[1,1]{1,0:T(1,128)S(6)} %copy.16.count, s32[1,1,4,4]{3,2,1,0:T(4,128)S(1)} %copy-done.2, f32[256,512]{1,0:T(8,128)S(1)} %get-tuple-element.49.interior, f32[25,64,128]{2,1,0:T(8,128)S(1)} %get-tuple-element.50.grad_local, bf16[4,64,128]{2,1,0:T(8,128)(2,1)S(1)} %collective-permute-done.4.ahead, ...), custom_call_target="tpu_custom_call" | custom-call | flops 201326592 | bytes 1048576 | tf_op jit(solution)/shard_map/finish_kernel/pallas_call | solution.py:376
  95.3 9.4 %all-to-all-done.2 = bf16[64,24,128]{2,1,0:T(8,128)(2,1)S(1)} async-done(((bf16[64,24,128]{2,1,0:T(8,128)(2,1)}), bf16[64,24,128]{2,1,0:T(8,128)(2,1)S(1)}, u32[]{:S(2)}, u32[]{:S(2)}) %all-to-all-start.2) | async-done | bytes 393248 | tf_op jit(solution)/shard_map/all_to_all | solution.py:404
  104.7 0.9 unpack_kernel.1
  (1 shorter events, 0.0 us)
Async XLA Ops:
  1.3 21.3 %copy-start.7 = (s32[1,4,26]{2,1,0:T(4,128)S(1)}, s32[1,4,26]{2,1,0:T(4,128)}, u32[]{:S(2)}) copy-start(s32[1,4,26]{2,1,0:T(4,128)} %sources.3) | copy-start | bytes 1252
  1.3 21.3 %copy-start.10 = (bf16[1152,128]{1,0:T(8,128)(2,1)S(1)}, bf16[1152,128]{1,0:T(8,128)(2,1)}, u32[]{:S(2)}) copy-start(bf16[1152,128]{1,0:T(8,128)(2,1)} %constant.17.clone.cap_hot) | copy-start | bytes 884740
  1.3 21.3 %copy-start.12 = (bf16[128,256]{1,0:T(8,128)(2,1)S(1)}, bf16[128,256]{1,0:T(8,128)(2,1)}, u32[]{:S(2)}) copy-start(bf16[128,256]{1,0:T(8,128)(2,1)} %constant.16.clone.inner_hot) | copy-start | bytes 196612
  4.0 18.6 %copy-start.1 = (bf16[1,4,64,512]{3,2,1,0:T(8,128)(2,1)S(1)}, bf16[1,4,64,512]{3,2,1,0:T(8,128)(2,1)}, u32[]{:S(2)}) copy-start(bf16[1,4,64,512]{3,2,1,0:T(8,128)(2,1)} %features.1) | copy-start | bytes 786436
  4.0 18.6 %copy-start.3 = (bf16[25,64,128]{2,1,0:T(8,128)(2,1)S(1)}, bf16[25,64,128]{2,1,0:T(8,128)(2,1)}, u32[]{:S(2)}) copy-start(bf16[25,64,128]{2,1,0:T(8,128)(2,1)} %get-tuple-element.36.table) | copy-start | bytes 1228804
  4.0 18.6 %collective-permute-start = (bf16[4,64,128]{2,1,0:T(8,128)(2,1)}, bf16[4,64,128]{2,1,0:T(8,128)(2,1)S(1)}, u32[]{:S(2)}, u32[]{:S(2)}) collective-permute-start(bf16[4,64,128]{2,1,0:T(8,128)(2,1)} %get-tuple-element.37), channel_id=1, source_target_pairs={{0,4},{4,8},{8,12},{12,16},{16,20},{20,24},{24,28},{28,32},{32,36}... | collective-permute-start | bytes 196616 | tf_op jit(solution)/shard_map/ppermute | solution.py:409
  8.7 13.9 %collective-permute-start.1 = (bf16[4,64,128]{2,1,0:T(8,128)(2,1)}, bf16[4,64,128]{2,1,0:T(8,128)(2,1)S(1)}, u32[]{:S(2)}, u32[]{:S(2)}) collective-permute-start(bf16[4,64,128]{2,1,0:T(8,128)(2,1)} %get-tuple-element.38), channel_id=1, source_target_pairs={{4,0},{8,4},{12,8},{16,12},{20,16},{24,20},{28,24},{32,28},{36,32}... | collective-permute-start | bytes 196616 | tf_op jit(solution)/shard_map/ppermute | solution.py:409
  14.3 8.3 %collective-permute-start.2 = (bf16[4,64,128]{2,1,0:T(8,128)(2,1)}, bf16[4,64,128]{2,1,0:T(8,128)(2,1)S(1)}, u32[]{:S(2)}, u32[]{:S(2)}) collective-permute-start(bf16[4,64,128]{2,1,0:T(8,128)(2,1)} %get-tuple-element.39), channel_id=1, source_target_pairs={{0,8},{4,12},{8,16},{12,20},{16,24},{20,28},{24,32},{28,36},{32,40... | collective-permute-start | bytes 196616 | tf_op jit(solution)/shard_map/ppermute | solution.py:409
  15.6 7.1 %collective-permute-start.3 = (bf16[4,64,128]{2,1,0:T(8,128)(2,1)}, bf16[4,64,128]{2,1,0:T(8,128)(2,1)S(1)}, u32[]{:S(2)}, u32[]{:S(2)}) collective-permute-start(bf16[4,64,128]{2,1,0:T(8,128)(2,1)} %get-tuple-element.40), channel_id=1, source_target_pairs={{8,0},{12,4},{16,8},{20,12},{24,16},{28,20},{32,24},{36,28},{40,32... | collective-permute-start | bytes 196616 | tf_op jit(solution)/shard_map/ppermute | solution.py:409
  16.9 0.9 copy-start.4
  17.8 0.9 copy-start.5
  18.7 0.8 copy-start.6
  19.5 0.9 copy-start.11
  20.5 2.2 %copy-start.8 = (bf16[1024,1024]{1,0:T(8,128)(2,1)S(1)}, bf16[1024,1024]{1,0:T(8,128)(2,1)}, u32[]{:S(2)}) copy-start(bf16[1024,1024]{1,0:T(8,128)(2,1)} %constant.18.clone.side_hot) | copy-start | bytes 6291460
  31.6 22.8 %all-to-all-start = ((bf16[64,24,128]{2,1,0:T(8,128)(2,1)}), bf16[64,24,128]{2,1,0:T(8,128)(2,1)}, u32[]{:S(2)}, u32[]{:S(2)}) async-start(bf16[64,24,128]{2,1,0:T(8,128)(2,1)} %bitcast), calls=%async_computation | async-start | bytes 786432 | tf_op jit(solution)/shard_map/all_to_all | solution.py:397
  43.3 1.6 %copy-start.9 = (bf16[1024,1024]{1,0:T(8,128)(2,1)S(1)}, bf16[1024,1024]{1,0:T(8,128)(2,1)}, u32[]{:S(2)}) copy-start(bf16[1024,1024]{1,0:T(8,128)(2,1)} %constant.18.clone.side_hot) | copy-start | bytes 6291460
  44.9 48.6 %copy-start.2 = (s32[1,1,4,4]{3,2,1,0:T(4,128)S(1)}, s32[1,1,4,4]{3,2,1,0:T(4,128)}, u32[]{:S(2)}) copy-start(s32[1,1,4,4]{3,2,1,0:T(4,128)} %sends.1) | copy-start | bytes 196
  49.9 43.7 %copy-start = (bf16[512,768]{1,0:T(8,128)(2,1)S(1)}, bf16[512,768]{1,0:T(8,128)(2,1)}, u32[]{:S(2)}) copy-start(bf16[512,768]{1,0:T(8,128)(2,1)} %constant.14.clone.face_far.face_hot) | copy-start | bytes 2359300
  56.2 27.4 %all-to-all-start.1 = ((bf16[8,24,128]{2,1,0:T(8,128)(2,1)}), bf16[8,24,128]{2,1,0:T(8,128)(2,1)S(1)}, u32[]{:S(2)}, u32[]{:S(2)}) async-start(bf16[8,24,128]{2,1,0:T(8,128)(2,1)} %broadcast_in_dim.4), calls=%async_computation.1 | async-start | bytes 98304 | tf_op jit(solution)/shard_map/all_to_all | solution.py:390
  71.4 12.2 %collective-permute-start.4 = (bf16[4,64,128]{2,1,0:T(8,128)(2,1)S(1)}, bf16[4,64,128]{2,1,0:T(8,128)(2,1)S(1)}, u32[]{:S(2)}, u32[]{:S(2)}) collective-permute-start(bf16[4,64,128]{2,1,0:T(8,128)(2,1)S(1)} %get-tuple-element.57), channel_id=1, source_target_pairs={{4,0},{8,4},{12,8},{16,12},{20,16},{24,20},{28,24},{32,28},{36,32}... | collective-permute-start | bytes 196616 | tf_op jit(solution)/shard_map/ppermute | solution.py:409
  74.1 9.4 %collective-permute-start.5 = (bf16[4,64,128]{2,1,0:T(8,128)(2,1)S(1)}, bf16[4,64,128]{2,1,0:T(8,128)(2,1)S(1)}, u32[]{:S(2)}, u32[]{:S(2)}) collective-permute-start(bf16[4,64,128]{2,1,0:T(8,128)(2,1)S(1)} %get-tuple-element.58), channel_id=1, source_target_pairs={{0,4},{4,8},{8,12},{12,16},{16,20},{20,24},{24,28},{28,32},{32,36}... | collective-permute-start | bytes 196616 | tf_op jit(solution)/shard_map/ppermute | solution.py:409
  76.9 6.6 %collective-permute-start.6 = (bf16[4,64,128]{2,1,0:T(8,128)(2,1)S(1)}, bf16[4,64,128]{2,1,0:T(8,128)(2,1)S(1)}, u32[]{:S(2)}, u32[]{:S(2)}) collective-permute-start(bf16[4,64,128]{2,1,0:T(8,128)(2,1)S(1)} %get-tuple-element.59), channel_id=1, source_target_pairs={{8,0},{12,4},{16,8},{20,12},{24,16},{28,20},{32,24},{36,28},{40,32... | collective-permute-start | bytes 196616 | tf_op jit(solution)/shard_map/ppermute | solution.py:409
  78.2 5.6 %collective-permute-start.7 = (bf16[4,64,128]{2,1,0:T(8,128)(2,1)S(1)}, bf16[4,64,128]{2,1,0:T(8,128)(2,1)S(1)}, u32[]{:S(2)}, u32[]{:S(2)}) collective-permute-start(bf16[4,64,128]{2,1,0:T(8,128)(2,1)S(1)} %get-tuple-element.60), channel_id=1, source_target_pairs={{0,8},{4,12},{8,16},{12,20},{16,24},{20,28},{24,32},{28,36},{32,40... | collective-permute-start | bytes 196616 | tf_op jit(solution)/shard_map/ppermute | solution.py:409
  84.6 20.0 %all-to-all-start.2 = ((bf16[64,24,128]{2,1,0:T(8,128)(2,1)}), bf16[64,24,128]{2,1,0:T(8,128)(2,1)S(1)}, u32[]{:S(2)}, u32[]{:S(2)}) async-start(bf16[64,24,128]{2,1,0:T(8,128)(2,1)} %broadcast_in_dim.5), calls=%async_computation.2 | async-start | bytes 786432 | tf_op jit(solution)/shard_map/all_to_all | solution.py:404

commit v4 on v2

--- a/solution.py
+++ b/solution.py
@@ -17,6 +17,7 @@
 SLOTS, C, C2, NOFF, CAP = 4, 64, 128, 4, 4
 LOCAL = 6 * SLOTS + 1
 TABLE = LOCAL + NOFF * CAP
+PLACES = list(range(9)) + [None] + list(range(9, 26)) + [None]
 OFFSETS = (1, -1, 2, -2)
 NEAR = ("x", "c", "grp")
 
@@ -45,8 +46,8 @@
         for y in range(8):
             for z in range(8):
                 inner[s, y * 8 + z, s, (y + 1) * 10 + z + 1] = 1
-    cap = np.zeros((9, 128, 128), np.float32)
-    side = np.zeros((8, 128, 8, 128), np.float32)
+    cap = np.zeros((10, 64, 128), np.float32)
+    side = np.zeros((8, 64, 8, 128), np.float32)
     for m, d in enumerate([d for d in DIRECTIONS if d[0] == 0]):
         if d[1] != 0:
             yy = 0 if d[1] == -1 else 9
@@ -62,21 +63,32 @@
         for i, yy in rim_cells(dy, 8):
             for k, zz in rim_cells(dz, 8):
                 cap[m, i * 8 + k, yy * 10 + zz] = 1
-    down = np.zeros((2, 2, 4, 4, 4, 4, 128), np.float32)
+    window = np.zeros((2, 128, 9, 2, 64), np.float32)
+    for k, shift in enumerate(SHIFTS):
+        for y in range(8):
+            for z in range(8):
+                for p in range(2):
+                    window[p, (y + 1) * 10 + z + 1 + shift, k, p, y * 8 + z] = 1
+    spread = np.zeros((4, 4, 4, 2, 2, 4, 64), np.float32)
+    pick = np.zeros((2, 2, 2, 4, 4, 2, 64), np.float32)
     for ty in range(2):
         for tz in range(2):
-            for X in range(4):
-                for Y in range(4):
-                    for Z in range(4):
-                        lane = (2 * Y + ty + 1) * 10 + 2 * Z + tz + 1
-                        down[ty, tz, X, Y, Z, X, lane] = 1
+            for Y in range(4):
+                for Z in range(4):
+                    lane = (2 * Y + ty) * 8 + 2 * Z + tz
+                    for X in range(4):
+                        spread[X, Y, Z, ty, tz, X, lane] = 1
+                    for tx in range(2):
+                        pick[tx, ty, tz, Y, Z, tx, lane] = 1
     b = ml_dtypes.bfloat16
     return (
         faces.reshape(512, 768).astype(b),
         inner.reshape(128, 256).astype(b),
-        cap.reshape(1152, 128).astype(b),
-        side.reshape(1024, 1024).astype(b),
-        down.reshape(256, 512).astype(b),
+        cap.reshape(640, 128).astype(b),
+        side.reshape(512, 1024).astype(b),
+        window.reshape(256, 1152).astype(b),
+        spread.reshape(64, 1024).astype(b),
+        pick.reshape(128, 128).astype(b),
     )
 
 
@@ -94,7 +106,22 @@
     )
 
 
-def faces_kernel(count, sends, features, face_hot, table, *outgoing):
+def fetch(sources, targets, done):
+    copies = [
+        pltpu.make_async_copy(a, b, done.at[i]) for i, (a, b) in enumerate(zip(sources, targets))
+    ]
+    for copy in copies:
+        copy.start()
+    return copies
+
+
+def faces_kernel(
+    count, sends_far, features_far, face_far, table, *rest
+):
+    outgoing, (sends, features, face_hot, done) = rest[:NOFF], rest[NOFF:]
+    copies = fetch((features_far, face_far, sends_far), (features, face_hot, sends), done)
+    for copy in copies:
+        copy.wait()
     masked = masked_rows(features, count[0, 0])
     for f in range(6):
         layer = nn(masked, face_hot[:, f * 128 : (f + 1) * 128]).astype(BF)
@@ -104,23 +131,6 @@
     for j in range(NOFF):
         for c in range(CAP):
             outgoing[j][c] = table[sends[0, 0, j, c]]
-
-
-def upper_kernel(out_grad, down_hot, down_kernel, grad_active):
-    tall = jnp.transpose(down_kernel[...].astype(F32)).astype(BF)
-    down_rows = jnp.concatenate(
-        [
-            jnp.concatenate([tall[(4 * tx + t) * C : (4 * tx + t + 1) * C] for t in range(4)], axis=1)
-            for tx in range(2)
-        ],
-        axis=0,
-    )
-    for s in range(SLOTS):
-        turned = jnp.transpose(out_grad[0, s].astype(F32)).astype(BF)
-        spread = jnp.concatenate(
-            [nn(turned, down_hot[t * 64 : (t + 1) * 64]).astype(BF) for t in range(4)], axis=0
-        )
-        grad_active[s] = nn(down_rows, spread)
 
 
 def main_kernel(
@@ -135,15 +145,18 @@
     kernel,
     down_kernel,
     out_grad,
-    grad_active,
     inner_hot,
     cap_hot,
     side_hot,
-    down_hot,
+    window_hot,
+    spread_hot,
+    pick_hot,
     coarse,
     grad_preact,
     sums,
+    conv_back,
     halo,
+    halo_high,
     conv,
     entries,
     padded,
@@ -155,72 +168,100 @@
     halo[0:LOCAL] = table[...]
     for j in range(NOFF):
         halo[LOCAL + j * CAP : LOCAL + (j + 1) * CAP] = (ahead, behind, ahead2, behind2)[j][...]
+    halo_high[...] = pltpu.roll(halo[...].reshape(TABLE * C, 128), 64, 1).reshape(TABLE, C, 128)
     for s in range(SLOTS):
-        for k in range(26):
-            entries[s * C : (s + 1) * C, k * 128 : (k + 1) * 128] = halo[sources[0, s, k]]
+        for t in range(14):
+            even, odd = PLACES[2 * t], PLACES[2 * t + 1]
+            block = halo[sources[0, s, even]]
+            if odd is not None:
+                block = block + halo_high[sources[0, s, odd]]
+            entries[s * C : (s + 1) * C, t * 128 : (t + 1) * 128] = block
+    masked = masked_rows(features, count[0, 0])
+    padded[:, 0:128] = nn(entries[:, 0:640], cap_hot[...]).astype(BF)
+    padded[:, 1152:1280] = nn(entries[:, 1152:1792], cap_hot[...]).astype(BF)
+    for i in range(4):
+        block = nn(entries[:, 640:1152], side_hot[:, i * 256 : (i + 1) * 256])
+        block = block + nn(masked[:, i * 128 : (i + 1) * 128], inner_hot[...])
+        padded[:, 128 + i * 256 : 384 + i * 256] = block.astype(BF)
+    for i in range(5):
+        planes = nn(padded[:, i * 256 : (i + 1) * 256], window_hot[...]).astype(BF)
+        for s in range(SLOTS):
+            lanes = slice((s % 2) * 640 + i * 128, (s % 2) * 640 + (i + 1) * 128)
+            for k in range(9):
+                block = planes[s * C : (s + 1) * C, k * 128 : (k + 1) * 128]
+                stack[s // 2, k * C : (k + 1) * C, lanes] = block
+
     for o in range(3):
         conv[o * C : (o + 1) * C] = kernel[:, o * 576 : (o + 1) * 576]
-    masked = masked_rows(features, count[0, 0])
-    padded[:, 0:128] = nn(entries[:, 0:1152], cap_hot[...]).astype(BF)
-    padded[:, 1152:1280] = nn(entries[:, 2176:3328], cap_hot[...]).astype(BF)
-    for i in range(4):
-        block = nn(entries[:, 1152:2176], side_hot[:, i * 256 : (i + 1) * 256])
-        block = block + nn(masked[:, i * 128 : (i + 1) * 128], inner_hot[...])
-        padded[:, 128 + i * 256 : 384 + i * 256] = block.astype(BF)
-
-    lane = lax.broadcasted_iota(jnp.int32, (C, 1024), 1) & 127
-    row, column = lane // 10, lane % 10
-    valid = (row >= 1) & (row <= 8) & (column >= 1) & (column <= 8)
-    shifted[...] = jnp.zeros_like(shifted)
+    tall = jnp.transpose(kernel[...].astype(F32)).astype(BF)
+    for o in range(3):
+        conv_back[o * C : (o + 1) * C] = jnp.concatenate(
+            [tall[(9 * o + k) * C : (9 * o + k + 1) * C] for k in range(9)], axis=1
+        )
+    tall = jnp.transpose(down_kernel[...].astype(F32)).astype(BF)
+    down_rows = jnp.concatenate(
+        [
+            jnp.concatenate([tall[(4 * tx + t) * C : (4 * tx + t + 1) * C] for t in range(4)], axis=1)
+            for tx in range(2)
+        ],
+        axis=0,
+    )
+    left = lax.broadcasted_iota(jnp.int32, (16, 128), 1) < 64
+    edge = jnp.zeros((C, 64), BF)
+    wide = jnp.zeros((C, 128), BF)
     total[...] = jnp.zeros_like(total)
 
-    def brick(s, carry):
-        filled = jnp.where(s < count[0, 0], 1.0, 0.0).astype(F32)
-        here = pl.ds(pl.multiple_of(s * C, C), C)
-        for x in range(10):
-            plane = padded[here, x * 128 : (x + 1) * 128]
-            for k, shift in enumerate(SHIFTS):
-                moved = plane if shift == 0 else pltpu.roll(plane, (-shift) % 128, 1)
-                stack[k * C : (k + 1) * C, x * 128 : (x + 1) * 128] = moved
-        triple = nn(conv[...], stack[...])
-        preact = triple[0:C, 0:1024] + triple[C : 2 * C, 128:1152] + triple[2 * C :, 256:1280]
-        sigmoid = jax.nn.sigmoid(preact)
-        active = jnp.where(valid, preact * sigmoid * filled, 0.0).astype(BF)
-        halves = jnp.concatenate(
-            [
-                jnp.concatenate(
-                    [active[:, (2 * X + tx) * 128 : (2 * X + tx + 1) * 128] for X in range(4)],
-                    axis=1,
-                )
-                for tx in range(2)
-            ],
-            axis=0,
-        )
-        picked = nt(down_hot[...], halves).astype(BF)
-        for t in range(4):
-            lowered[here, t * 128 : (t + 1) * 128] = picked[t * 64 : (t + 1) * 64]
-        upper = jnp.concatenate(
-            [
-                grad_active[s, (x % 2) * C : (x % 2 + 1) * C, (x // 2) * 128 : (x // 2 + 1) * 128]
-                for x in range(8)
-            ],
-            axis=1,
-        )
-        grads = upper * sigmoid * (1.0 + preact * (1.0 - sigmoid)) * filled
-        grads = jnp.where(valid, grads, 0.0).astype(BF)
-        grad_preact[s] = grads
-        for o in range(3):
-            shifted[o * C : (o + 1) * C, o * 128 : o * 128 + 1024] = grads
-        total[...] += nt(shifted[...], stack[...])
+    def pair(p, carry):
+        triple = nn(conv[...], stack[p])
+        for j in range(2):
+            s = 2 * p + j
+            filled = jnp.where(s < count[0, 0], 1.0, 0.0).astype(F32)
+            base = j * 640
+            preact = (
+                triple[0:C, base : base + 512]
+                + triple[C : 2 * C, base + 64 : base + 576]
+                + triple[2 * C :, base + 128 : base + 640]
+            )
+            sigmoid = jax.nn.sigmoid(preact)
+            active = (preact * sigmoid * filled).astype(BF)
+            for h in range(2):
+                halves = [active[:, (2 * h + i) * 128 : (2 * h + i + 1) * 128] for i in range(2)]
+                rows = jnp.concatenate([halves[0], halves[0], halves[1], halves[1]], axis=0)
+                picked = nt(pick_hot[...], rows)
+                for i in range(2):
+                    X = 2 * h + i
+                    for q in range(4):
+                        lanes = slice(i * 128, (i + 1) * 128)
+                        block = jnp.where(
+                            left,
+                            picked[32 * q : 32 * q + 16, lanes],
+                            picked[32 * q + 16 : 32 * q + 32, lanes],
+                        )
+                        lowered[s, X * 16 : (X + 1) * 16, q * 128 : (q + 1) * 128] = block.astype(BF)
+            turned = jnp.transpose(out_grad[0, s].astype(F32)).astype(BF)
+            spread = nn(turned, spread_hot[...]).astype(BF)
+            spread = jnp.concatenate([spread[:, t * 256 : (t + 1) * 256] for t in range(4)], axis=0)
+            grown = nn(down_rows, spread)
+            upper = jnp.concatenate(
+                [
+                    grown[tx * C : (tx + 1) * C, X * 64 : (X + 1) * 64]
+                    for X in range(4)
+                    for tx in range(2)
+                ],
+                axis=1,
+            )
+            grads = upper * sigmoid * (1.0 + preact * (1.0 - sigmoid)) * filled
+            grads = grads.astype(BF)
+            grad_preact[s] = grads
+            shifted[0:C, base : base + 640] = jnp.concatenate([grads, wide], axis=1)
+            shifted[C : 2 * C, base : base + 640] = jnp.concatenate([edge, grads, edge], axis=1)
+            shifted[2 * C :, base : base + 640] = jnp.concatenate([wide, grads], axis=1)
+        total[...] += nt(shifted[...], stack[p])
         return carry
 
-    lax.fori_loop(0, SLOTS, brick, 0)
-    rows = lowered[...]
-    down_cols = jnp.concatenate(
-        [down_kernel[:, (4 * tx + t) * C : (4 * tx + t + 1) * C] for t in range(4) for tx in range(2)],
-        axis=1,
-    )
-    coarse[...] = nt(rows, down_cols).astype(BF).reshape(coarse.shape)
+    lax.fori_loop(0, SLOTS // 2, pair, 0)
+    rows = lowered[...].reshape(SLOTS * 64, 512)
+    coarse[...] = nt(rows, down_kernel[...]).astype(BF).reshape(coarse.shape)
     turned = jnp.transpose(out_grad[...].reshape(SLOTS * 64, C2).astype(F32)).astype(BF)
     grad_down = nn(turned, rows)
     for j in range(5):
@@ -245,18 +286,24 @@
     to_behind,
     to_ahead2,
     to_behind2,
+    planes,
     stack,
     high,
     low,
     rims,
     grad_table,
+    grad_table_high,
 ):
+    rows = grad_preact[...].reshape(SLOTS * C, 512)
+    for i in range(4):
+        block = nn(rows[:, i * 128 : (i + 1) * 128], inner_hot[...])
+        planes[:, i * 256 : (i + 1) * 256] = block.astype(BF)
     high[...] = jnp.zeros_like(high)
 
     def brick(s, carry):
         here = pl.ds(pl.multiple_of(s * C, C), C)
         for x in range(8):
-            plane = grad_preact[s, :, x * 128 : (x + 1) * 128]
+            plane = planes[here, x * 128 : (x + 1) * 128]
             for k, shift in enumerate(SHIFTS):
                 moved = plane if shift == 0 else pltpu.roll(plane, shift % 128, 1)
                 stack[k * C : (k + 1) * C, x * 128 : (x + 1) * 128] = moved
@@ -273,14 +320,19 @@
         return carry
 
     lax.fori_loop(0, SLOTS, brick, 0)
-    rims[:, 0:1152] = nt(high[:, 0:128], cap_hot[...])
-    rims[:, 1152:2176] = nt(high[:, 128:1152], side_hot[...])
-    rims[:, 2176:3328] = nt(high[:, 1152:1280], cap_hot[...])
+    rims[:, 0:640] = nt(high[:, 0:128], cap_hot[...])
+    rims[:, 640:1152] = nt(high[:, 128:1152], side_hot[...])
+    rims[:, 1152:1792] = nt(high[:, 1152:1280], cap_hot[...])
     grad_table[...] = jnp.zeros_like(grad_table)
+    grad_table_high[...] = jnp.zeros_like(grad_table_high)
     for s in range(SLOTS):
-        for k in range(26):
-            place = sources[0, s, k]
-            grad_table[place] += rims[s * C : (s + 1) * C, k * 128 : (k + 1) * 128]
+        for t in range(14):
+            block = rims[s * C : (s + 1) * C, t * 128 : (t + 1) * 128]
+            grad_table[sources[0, s, PLACES[2 * t]]] += block
+            if PLACES[2 * t + 1] is not None:
+                grad_table_high[sources[0, s, PLACES[2 * t + 1]]] += block
+    turned = pltpu.roll(grad_table_high[...].reshape(TABLE * C, 128), 64, 1)
+    grad_table[...] += turned.reshape(TABLE, C, 128)
     for i in range(4):
         lanes = slice(128 + i * 256, 384 + i * 256)
         interior[:, i * 128 : (i + 1) * 128] = nt(high[:, lanes], inner_hot[...]) + nt(
@@ -299,9 +351,7 @@
         parts.append(jnp.concatenate(tiles, axis=1)[:, :576])
     grad_kernel[...] = jnp.concatenate(parts, axis=1)
     tiles = [sums[960 + t * C2 : 960 + (t + 1) * C2].astype(F32) for t in range(4)]
-    grad_down[...] = jnp.concatenate(
-        [tiles[t][:, tx * C : (tx + 1) * C] for tx in range(2) for t in range(4)], axis=1
-    )
+    grad_down[...] = jnp.concatenate(tiles, axis=1)
 
 
 def finish_kernel(
@@ -333,13 +383,13 @@
 
 
 def call(kernel, limit, memories, outs, scratch, flops, *args):
-    where = {"s": pltpu.SMEM, "v": pltpu.VMEM}
+    where = {"s": pltpu.SMEM, "v": pltpu.VMEM, "h": pltpu.HBM}
     return pl.pallas_call(
         kernel,
         in_specs=[pl.BlockSpec(memory_space=where[m]) for m in memories],
         out_specs=[pl.BlockSpec(memory_space=pltpu.VMEM) for _ in outs],
         out_shape=[jax.ShapeDtypeStruct(s, d) for s, d in outs],
-        scratch_shapes=[pltpu.VMEM(s, d) for s, d in scratch],
+        scratch_shapes=[pltpu.VMEM(*s) if isinstance(s, tuple) else s for s in scratch],
         compiler_params=pltpu.CompilerParams(vmem_limit_bytes=limit * 2**20),
         cost_estimate=pl.CostEstimate(flops=flops, bytes_accessed=2**20, transcendentals=0),
         name=kernel.__name__,
@@ -371,18 +421,22 @@
 
 
 def on_device(sizes, features, brick_count, send_list, halo_src, kernel, down_kernel, out_grad):
-    face_hot, inner_hot, cap_hot, side_hot, down_hot = one_hot_tables()
+    face_hot, inner_hot, cap_hot, side_hot, window_hot, spread_hot, pick_hot = one_hot_tables()
     tile = ("z", "x", "c")
     devices = sizes["z"] * sizes["x"] * sizes["c"]
     swap = [((CAP, C, 128), BF)] * NOFF
-    conv_back = kernel.reshape(C, 3, 9, C).transpose(1, 3, 2, 0).reshape(192, 576)
 
     table, *outgoing = call(
         faces_kernel,
-        8,
-        "ssvv",
+        56,
+        "shhh",
         [((LOCAL, C, 128), BF)] + swap,
-        [],
+        [
+            pltpu.SMEM((1, 1, NOFF, CAP), jnp.int32),
+            ((1, SLOTS, C, 512), BF),
+            ((512, 768), BF),
+            pltpu.SemaphoreType.DMA((3,)),
+        ],
         2 * 256 * 512 * 768,
         brick_count,
         send_list,
@@ -390,30 +444,25 @@
         face_hot,
     )
     received = [from_behind(b, tile, devices, o) for b, o in zip(outgoing, OFFSETS)]
-    (grad_active,) = call(
-        upper_kernel,
-        12,
-        "vvv",
-        [((SLOTS, 2 * C, 512), F32)],
-        [],
-        10**9,
-        out_grad,
-        down_hot,
-        down_kernel,
-    )
-    coarse, grad_preact, sums = call(
+    coarse, grad_preact, sums, conv_back = call(
         main_kernel,
         28,
-        "ss" + "v" * 14,
-        [((1, SLOTS, 64, C2), BF), ((SLOTS, C, 1024), BF), ((1536, 128), BF)],
+        "ss" + "v" * 15,
+        [
+            ((1, SLOTS, 64, C2), BF),
+            ((SLOTS, C, 512), BF),
+            ((1536, 128), BF),
+            ((192, 576), BF),
+        ],
         [
             ((TABLE, C, 128), BF),
+            ((TABLE, C, 128), BF),
             ((192, 576), BF),
-            ((256, 26 * 128), BF),
+            ((256, 14 * 128), BF),
             ((256, 1280), BF),
-            ((576, 1280), BF),
+            ((2, 576, 1280), BF),
             ((192, 1280), BF),
-            ((256, 512), BF),
+            ((SLOTS, 64, 512), BF),
             ((192, 576), F32),
         ],
         5 * 10**9,
@@ -425,11 +474,12 @@
         kernel,
         down_kernel,
         out_grad,
-        grad_active,
         inner_hot,
         cap_hot,
         side_hot,
-        down_hot,
+        window_hot,
+        spread_hot,
+        pick_hot,
     )
     part = near_sum(sums, sizes)
     interior, grad_local, *remote = call(
@@ -438,10 +488,12 @@
         "svvvvv",
         [((256, 512), F32), ((LOCAL, C, 128), F32)] + swap,
         [
+            ((256, 1024), BF),
             ((576, 1024), BF),
             ((256, 1280), BF),
             ((256, 1280), BF),
-            ((256, 26 * 128), F32),
+            ((256, 14 * 128), F32),
+            ((TABLE, C, 128), F32),
             ((TABLE, C, 128), F32),
         ],
         3 * 10**9,

time: 103 us -> 104 us (level)
  waiting for transfers between devices: 12.7 us -> 17.6 us
  local copies, waits for them, and re-layouts: 9.62 us -> 7.48 us
  Pallas kernels: 19.2 us -> 17.7 us
    ppermute x8, waiting for transfers between devices: 0.2 us -> 4.6 us  [from_behind(): return lax.ppermute(block, axes, route)]
    pallas_call x6 -> x5, Pallas kernels: 19.2 us -> 17.7 us  [call(): pl.pallas_call(kernel, in_specs=[pl.BlockSpec(memory_space=where[m]) for...]
    all_to_all x1, waiting for transfers between devices: 2.47 us -> 3.86 us  [near_sum(): got = lax.all_to_all(block.reshape(parts, rows, 128), NEAR, 0, 0)]
    unnamed x37 -> x30, local copies, waits for them, and re-layouts: 7.36 us -> 5.98 us
  transfers between devices with their start and end apart: 11 -> 11, of which waited for: 4 -> 5; matrix products, arithmetic and copies ran while one was open for 1% -> 0% of each run, Pallas kernels for 8% -> 7%
where the time goes in v4:
time: 104 us; the launch traced here: 103 us
  starting transfers between devices  59 us (57%)
  Pallas kernels  17.7 us (17%)
  waiting for transfers between devices  17.6 us (17%)
  local copies, waits for them, and re-layouts  7.48 us (7%)
  between operations  1.58 us (2%)
    ppermute x8, starting transfers between devices, from_behind(): return lax.ppermute(block, axes, route)  23.6 us
    pallas_call x5, Pallas kernels, call(): pl.pallas_call(kernel, in_specs=[pl.BlockSpec(memory_space=where[m]) for...  17.7 us
    all_to_all x1, starting transfers between devices, gather_sum(): got = lax.all_to_all(copies, axes, 0, 0)  16 us
    all_to_all x1, starting transfers between devices, near_sum(): got = lax.all_to_all(block.reshape(parts, rows, 128), NEAR, 0, 0)  10.9 us
    all_to_all x1, starting transfers between devices, near_gather(): lax.all_to_all(copies, NEAR, 0, 0).reshape(parts * block.shape[0], 128)  8.39 us
    all_to_all x1, waiting for transfers between devices, near_gather(): lax.all_to_all(copies, NEAR, 0, 0).reshape(parts * block.shape[0], 128)  7.65 us
    unnamed x30, local copies, waits for them, and re-layouts  5.98 us
    ppermute x8, waiting for transfers between devices, from_behind(): return lax.ppermute(block, axes, route)  4.6 us
  transfers between devices with their start and end apart: 11, of which 5 were waited for; matrix products, arithmetic and copies ran while one was open for 0% of the time, Pallas kernels for 7%

profile of v4, /device:TPU:1, one launch (start us, length us, event | category | flops | bytes accessed | tf_op | source)
XLA Modules:
  0.0 103.4 jit_solution(4960661073890287849)
XLA Ops:
  1.3 0.0 copy-start.1
  1.3 0.0 copy-start.4
  1.3 0.0 copy-start.5
  1.3 0.0 copy-start.6
  1.3 0.0 copy-start.11
  1.3 0.0 copy-start.12
  1.3 0.0 copy-start.13
  1.4 2.7 %faces_kernel.1 = (bf16[25,64,128]{2,1,0:T(8,128)(2,1)}, bf16[4,64,128]{2,1,0:T(8,128)(2,1)}, bf16[4,64,128]{2,1,0:T(8,128)(2,1)}, bf16[4,64,128]{2,1,0:T(8,128)(2,1)}, bf16[4,64,128]{2,1,0:T(8,128)(2,1)}) custom-call(s32[1,1]{1,0:T(1,128)S(6)} %copy.18.count, s32[1,1,4,4]{3,2,1,0:T(4,128)} %sends.1, bf16[1,4,64,512]{3,2,1,0:T(8,128)(2,1)} %features.1, ...), custom_call_target="tpu_custom_call" | custom-call | flops 201326592 | bytes 1048576 | tf_op jit(solution)/shard_map/faces_kernel/pallas_call | solution.py:387
  4.1 4.5 %collective-permute-start = (bf16[4,64,128]{2,1,0:T(8,128)(2,1)}, bf16[4,64,128]{2,1,0:T(8,128)(2,1)S(1)}, u32[]{:S(2)}, u32[]{:S(2)}) collective-permute-start(bf16[4,64,128]{2,1,0:T(8,128)(2,1)} %get-tuple-element.32), channel_id=1, source_target_pairs={{0,4},{4,8},{8,12},{12,16},{16,20},{20,24},{24,28},{28,32},{32,36}... | collective-permute-start | bytes 196616 | tf_op jit(solution)/shard_map/ppermute | solution.py:420
  8.6 5.6 %collective-permute-start.1 = (bf16[4,64,128]{2,1,0:T(8,128)(2,1)}, bf16[4,64,128]{2,1,0:T(8,128)(2,1)S(1)}, u32[]{:S(2)}, u32[]{:S(2)}) collective-permute-start(bf16[4,64,128]{2,1,0:T(8,128)(2,1)} %get-tuple-element.33), channel_id=1, source_target_pairs={{4,0},{8,4},{12,8},{16,12},{20,16},{24,20},{28,24},{32,28},{36,32}... | collective-permute-start | bytes 196616 | tf_op jit(solution)/shard_map/ppermute | solution.py:420
  14.2 0.0 copy-start.7
  14.2 1.3 %collective-permute-start.2 = (bf16[4,64,128]{2,1,0:T(8,128)(2,1)}, bf16[4,64,128]{2,1,0:T(8,128)(2,1)S(1)}, u32[]{:S(2)}, u32[]{:S(2)}) collective-permute-start(bf16[4,64,128]{2,1,0:T(8,128)(2,1)} %get-tuple-element.34), channel_id=1, source_target_pairs={{0,8},{4,12},{8,16},{12,20},{16,24},{20,28},{24,32},{28,36},{32,40... | collective-permute-start | bytes 196616 | tf_op jit(solution)/shard_map/ppermute | solution.py:420
  15.5 1.3 %collective-permute-start.3 = (bf16[4,64,128]{2,1,0:T(8,128)(2,1)}, bf16[4,64,128]{2,1,0:T(8,128)(2,1)S(1)}, u32[]{:S(2)}, u32[]{:S(2)}) collective-permute-start(bf16[4,64,128]{2,1,0:T(8,128)(2,1)} %get-tuple-element.35), channel_id=1, source_target_pairs={{8,0},{12,4},{16,8},{20,12},{24,16},{28,20},{32,24},{36,28},{40,32... | collective-permute-start | bytes 196616 | tf_op jit(solution)/shard_map/ppermute | solution.py:420
  16.8 0.0 collective-permute-done.ahead
  16.8 0.0 collective-permute-done.1.behind
  16.8 0.5 collective-permute-done.2.ahead2
  17.2 4.1 %collective-permute-done.3.behind2 = bf16[4,64,128]{2,1,0:T(8,128)(2,1)S(1)} collective-permute-done((bf16[4,64,128]{2,1,0:T(8,128)(2,1)}, bf16[4,64,128]{2,1,0:T(8,128)(2,1)S(1)}, u32[]{:S(2)}, u32[]{:S(2)}) %collective-permute-start.3) | collective-permute-done | bytes 65568 | tf_op jit(solution)/shard_map/ppermute | solution.py:420
  21.4 0.0 copy-done.1
  21.4 0.0 copy-done.4
  21.4 0.0 copy-done.5
  21.4 0.0 copy-done.6
  21.4 0.0 copy-done.11
  21.4 0.0 copy-done.12
  21.4 0.0 copy-done.13
  21.4 0.0 copy-done.7
  21.4 0.0 copy-start.3
  21.4 1.0 copy-done.3
  22.4 0.0 copy-start.8
  22.4 1.2 %copy-done.8 = bf16[512,1024]{1,0:T(8,128)(2,1)S(1)} copy-done((bf16[512,1024]{1,0:T(8,128)(2,1)S(1)}, bf16[512,1024]{1,0:T(8,128)(2,1)}, u32[]{:S(2)}) %copy-start.8) | copy-done | bytes 1048600
  23.7 0.0 copy-start.10
  23.7 1.1 %copy-done.10 = bf16[256,1152]{1,0:T(8,128)(2,1)S(1)} copy-done((bf16[256,1152]{1,0:T(8,128)(2,1)S(1)}, bf16[256,1152]{1,0:T(8,128)(2,1)}, u32[]{:S(2)}) %copy-start.10) | copy-done | bytes 589848
  24.7 0.0 copy-start.14
  24.7 0.8 copy-done.14
  25.5 7.3 %main_kernel.1 = (bf16[1,4,64,128]{3,2,1,0:T(8,128)(2,1)}, bf16[4,64,512]{2,1,0:T(8,128)(2,1)S(1)}, bf16[1536,128]{1,0:T(8,128)(2,1)}, bf16[192,576]{1,0:T(8,128)(2,1)S(1)}) custom-call(s32[1,1]{1,0:T(1,128)S(6)} %copy.18.count, s32[1,4,26]{2,1,0:T(4,128)S(1)} %copy-done.7, bf16[1,4,64,512]{3,2,1,0:T(8,128)(2,1)S(1)} %copy-done.1, ...), custom_call_target="tpu_custom_call" | custom-call | flops 5000000000 | bytes 1048576 | tf_op jit(solution)/shard_map/main_kernel/pallas_call | solution.py:387
  32.8 10.9 %all-to-all-start = ((bf16[32,48,128]{2,1,0:T(8,128)(2,1)}), bf16[32,48,128]{2,1,0:T(8,128)(2,1)S(1)}, u32[]{:S(2)}, u32[]{:S(2)}) async-start(bf16[32,48,128]{2,1,0:T(8,128)(2,1)} %bitcast), calls=%async_computation | async-start | bytes 786432 | tf_op jit(solution)/shard_map/all_to_all | solution.py:408
  43.8 0.0 copy-start.9
  43.8 1.2 %copy-done.9 = bf16[512,1024]{1,0:T(8,128)(2,1)S(1)} copy-done((bf16[512,1024]{1,0:T(8,128)(2,1)S(1)}, bf16[512,1024]{1,0:T(8,128)(2,1)}, u32[]{:S(2)}) %copy-start.9) | copy-done | bytes 1048600
  45.0 4.9 %fold_kernel.1 = (f32[256,512]{1,0:T(8,128)S(1)}, f32[25,64,128]{2,1,0:T(8,128)S(1)}, bf16[4,64,128]{2,1,0:T(8,128)(2,1)S(1)}, bf16[4,64,128]{2,1,0:T(8,128)(2,1...) custom-call(s32[1,4,26]{2,1,0:T(4,128)S(1)} %copy-done.7, ...), custom_call_target="tpu_custom_call" | custom-call | flops 3000000000 | bytes 1048576 | tf_op jit(solution)/shard_map/fold_kernel/pallas_call | solution.py:387
  49.9 3.9 %all-to-all-done = bf16[32,48,128]{2,1,0:T(8,128)(2,1)S(1)} async-done(((bf16[32,48,128]{2,1,0:T(8,128)(2,1)}), bf16[32,48,128]{2,1,0:T(8,128)(2,1)S(1)}, u32[]{:S(2)}, u32[]{:S(2)}) %all-to-all-start) | async-done | bytes 393248 | tf_op jit(solution)/shard_map/all_to_all | solution.py:408
  53.8 0.1 reduce_sum.21
  53.9 0.7 broadcast_in_dim.4
  54.6 16.0 %all-to-all-start.1 = ((bf16[16,48,128]{2,1,0:T(8,128)(2,1)}), bf16[16,48,128]{2,1,0:T(8,128)(2,1)S(1)}, u32[]{:S(2)}, u32[]{:S(2)}) async-start(bf16[16,48,128]{2,1,0:T(8,128)(2,1)} %broadcast_in_dim.4), calls=%async_computation.1 | async-start | bytes 393216 | tf_op jit(solution)/shard_map/all_to_all | solution.py:401
  70.6 0.0 copy-start
  70.6 3.0 %collective-permute-start.4 = (bf16[4,64,128]{2,1,0:T(8,128)(2,1)S(1)}, bf16[4,64,128]{2,1,0:T(8,128)(2,1)S(1)}, u32[]{:S(2)}, u32[]{:S(2)}) collective-permute-start(bf16[4,64,128]{2,1,0:T(8,128)(2,1)S(1)} %get-tuple-element.47), channel_id=1, source_target_pairs={{4,0},{8,4},{12,8},{16,12},{20,16},{24,20},{28,24},{32,28},{36,32}... | collective-permute-start | bytes 196616 | tf_op jit(solution)/shard_map/ppermute | solution.py:420
  73.6 2.7 %collective-permute-start.5 = (bf16[4,64,128]{2,1,0:T(8,128)(2,1)S(1)}, bf16[4,64,128]{2,1,0:T(8,128)(2,1)S(1)}, u32[]{:S(2)}, u32[]{:S(2)}) collective-permute-start(bf16[4,64,128]{2,1,0:T(8,128)(2,1)S(1)} %get-tuple-element.48), channel_id=1, source_target_pairs={{0,4},{4,8},{8,12},{12,16},{16,20},{20,24},{24,28},{28,32},{32,36}... | collective-permute-start | bytes 196616 | tf_op jit(solution)/shard_map/ppermute | solution.py:420
  76.3 1.3 %collective-permute-start.6 = (bf16[4,64,128]{2,1,0:T(8,128)(2,1)S(1)}, bf16[4,64,128]{2,1,0:T(8,128)(2,1)S(1)}, u32[]{:S(2)}, u32[]{:S(2)}) collective-permute-start(bf16[4,64,128]{2,1,0:T(8,128)(2,1)S(1)} %get-tuple-element.49), channel_id=1, source_target_pairs={{8,0},{12,4},{16,8},{20,12},{24,16},{28,20},{32,24},{36,28},{40,32... | collective-permute-start | bytes 196616 | tf_op jit(solution)/shard_map/ppermute | solution.py:420
  77.6 4.0 %collective-permute-start.7 = (bf16[4,64,128]{2,1,0:T(8,128)(2,1)S(1)}, bf16[4,64,128]{2,1,0:T(8,128)(2,1)S(1)}, u32[]{:S(2)}, u32[]{:S(2)}) collective-permute-start(bf16[4,64,128]{2,1,0:T(8,128)(2,1)S(1)} %get-tuple-element.50), channel_id=1, source_target_pairs={{0,8},{4,12},{8,16},{12,20},{16,24},{20,28},{24,32},{28,36},{32,40... | collective-permute-start | bytes 196616 | tf_op jit(solution)/shard_map/ppermute | solution.py:420
  81.6 1.5 %all-to-all-done.1 = bf16[16,48,128]{2,1,0:T(8,128)(2,1)S(1)} async-done(((bf16[16,48,128]{2,1,0:T(8,128)(2,1)}), bf16[16,48,128]{2,1,0:T(8,128)(2,1)S(1)}, u32[]{:S(2)}, u32[]{:S(2)}) %all-to-all-start.1) | async-done | bytes 196640 | tf_op jit(solution)/shard_map/all_to_all | solution.py:401
  83.1 0.0 collective-permute-done.4.ahead
  83.2 0.0 collective-permute-done.5.behind
  83.2 0.0 collective-permute-done.6.ahead2
  83.2 0.0 collective-permute-done.7.behind2
  83.2 0.8 broadcast_in_dim.5
  84.0 8.4 %all-to-all-start.2 = ((bf16[32,48,128]{2,1,0:T(8,128)(2,1)}), bf16[32,48,128]{2,1,0:T(8,128)(2,1)S(1)}, u32[]{:S(2)}, u32[]{:S(2)}) async-start(bf16[32,48,128]{2,1,0:T(8,128)(2,1)} %broadcast_in_dim.5), calls=%async_computation.2 | async-start | bytes 786432 | tf_op jit(solution)/shard_map/all_to_all | solution.py:415
  92.4 0.0 copy-start.2
  92.4 0.0 copy-done
  92.4 0.7 copy-done.2
  93.1 1.8 %finish_kernel.1 = bf16[1,4,64,512]{3,2,1,0:T(8,128)(2,1)} custom-call(s32[1,1]{1,0:T(1,128)S(6)} %copy.18.count, s32[1,1,4,4]{3,2,1,0:T(4,128)S(1)} %copy-done.2, f32[256,512]{1,0:T(8,128)S(1)} %get-tuple-element.39.interior, f32[25,64,128]{2,1,0:T(8,128)S(1)} %get-tuple-element.40.grad_local, bf16[4,64,128]{2,1,0:T(8,128)(2,1)S(1)} %collective-permute-done.4.ahead, ...), custom_call_target="tpu_custom_call" | custom-call | flops 201326592 | bytes 1048576 | tf_op jit(solution)/shard_map/finish_kernel/pallas_call | solution.py:387
  94.9 7.7 %all-to-all-done.2 = bf16[32,48,128]{2,1,0:T(8,128)(2,1)S(1)} async-done(((bf16[32,48,128]{2,1,0:T(8,128)(2,1)}), bf16[32,48,128]{2,1,0:T(8,128)(2,1)S(1)}, u32[]{:S(2)}, u32[]{:S(2)}) %all-to-all-start.2) | async-done | bytes 393248 | tf_op jit(solution)/shard_map/all_to_all | solution.py:415
  102.5 0.9 unpack_kernel.1
  (1 shorter events, 0.0 us)
Async XLA Ops:
  1.3 20.1 %copy-start.1 = (bf16[1,4,64,512]{3,2,1,0:T(8,128)(2,1)S(1)}, bf16[1,4,64,512]{3,2,1,0:T(8,128)(2,1)}, u32[]{:S(2)}) copy-start(bf16[1,4,64,512]{3,2,1,0:T(8,128)(2,1)} %features.1) | copy-start | bytes 786436
  1.3 20.1 %copy-start.4 = (bf16[64,1728]{1,0:T(8,128)(2,1)S(1)}, bf16[64,1728]{1,0:T(8,128)(2,1)}, u32[]{:S(2)}) copy-start(bf16[64,1728]{1,0:T(8,128)(2,1)} %kernel.1) | copy-start | bytes 663556
  1.3 20.1 %copy-start.5 = (bf16[128,512]{1,0:T(8,128)(2,1)S(1)}, bf16[128,512]{1,0:T(8,128)(2,1)}, u32[]{:S(2)}) copy-start(bf16[128,512]{1,0:T(8,128)(2,1)} %down_kernel.1) | copy-start | bytes 393220
  1.3 20.1 %copy-start.6 = (bf16[1,4,64,128]{3,2,1,0:T(8,128)(2,1)S(1)}, bf16[1,4,64,128]{3,2,1,0:T(8,128)(2,1)}, u32[]{:S(2)}) copy-start(bf16[1,4,64,128]{3,2,1,0:T(8,128)(2,1)} %out_grad.1) | copy-start | bytes 196612
  1.3 20.1 %copy-start.11 = (bf16[640,128]{1,0:T(8,128)(2,1)S(1)}, bf16[640,128]{1,0:T(8,128)(2,1)}, u32[]{:S(2)}) copy-start(bf16[640,128]{1,0:T(8,128)(2,1)} %constant.20.clone.cap_hot) | copy-start | bytes 491524
  1.3 20.1 %copy-start.12 = (bf16[64,1024]{1,0:T(8,128)(2,1)S(1)}, bf16[64,1024]{1,0:T(8,128)(2,1)}, u32[]{:S(2)}) copy-start(bf16[64,1024]{1,0:T(8,128)(2,1)} %constant.23.clone.spread_hot) | copy-start | bytes 393220
  1.3 20.1 %copy-start.13 = (bf16[128,256]{1,0:T(8,128)(2,1)S(1)}, bf16[128,256]{1,0:T(8,128)(2,1)}, u32[]{:S(2)}) copy-start(bf16[128,256]{1,0:T(8,128)(2,1)} %constant.19.clone.inner_hot) | copy-start | bytes 196612
  4.1 12.7 %collective-permute-start = (bf16[4,64,128]{2,1,0:T(8,128)(2,1)}, bf16[4,64,128]{2,1,0:T(8,128)(2,1)S(1)}, u32[]{:S(2)}, u32[]{:S(2)}) collective-permute-start(bf16[4,64,128]{2,1,0:T(8,128)(2,1)} %get-tuple-element.32), channel_id=1, source_target_pairs={{0,4},{4,8},{8,12},{12,16},{16,20},{20,24},{24,28},{28,32},{32,36}... | collective-permute-start | bytes 196616 | tf_op jit(solution)/shard_map/ppermute | solution.py:420
  8.6 8.2 %collective-permute-start.1 = (bf16[4,64,128]{2,1,0:T(8,128)(2,1)}, bf16[4,64,128]{2,1,0:T(8,128)(2,1)S(1)}, u32[]{:S(2)}, u32[]{:S(2)}) collective-permute-start(bf16[4,64,128]{2,1,0:T(8,128)(2,1)} %get-tuple-element.33), channel_id=1, source_target_pairs={{4,0},{8,4},{12,8},{16,12},{20,16},{24,20},{28,24},{32,28},{36,32}... | collective-permute-start | bytes 196616 | tf_op jit(solution)/shard_map/ppermute | solution.py:420
  14.2 7.3 %copy-start.7 = (s32[1,4,26]{2,1,0:T(4,128)S(1)}, s32[1,4,26]{2,1,0:T(4,128)}, u32[]{:S(2)}) copy-start(s32[1,4,26]{2,1,0:T(4,128)} %sources.3) | copy-start | bytes 1252
  14.2 3.1 %collective-permute-start.2 = (bf16[4,64,128]{2,1,0:T(8,128)(2,1)}, bf16[4,64,128]{2,1,0:T(8,128)(2,1)S(1)}, u32[]{:S(2)}, u32[]{:S(2)}) collective-permute-start(bf16[4,64,128]{2,1,0:T(8,128)(2,1)} %get-tuple-element.34), channel_id=1, source_target_pairs={{0,8},{4,12},{8,16},{12,20},{16,24},{20,28},{24,32},{28,36},{32,40... | collective-permute-start | bytes 196616 | tf_op jit(solution)/shard_map/ppermute | solution.py:420
  15.5 5.9 %collective-permute-start.3 = (bf16[4,64,128]{2,1,0:T(8,128)(2,1)}, bf16[4,64,128]{2,1,0:T(8,128)(2,1)S(1)}, u32[]{:S(2)}, u32[]{:S(2)}) collective-permute-start(bf16[4,64,128]{2,1,0:T(8,128)(2,1)} %get-tuple-element.35), channel_id=1, source_target_pairs={{8,0},{12,4},{16,8},{20,12},{24,16},{28,20},{32,24},{36,28},{40,32... | collective-permute-start | bytes 196616 | tf_op jit(solution)/shard_map/ppermute | solution.py:420
  21.4 1.0 copy-start.3
  22.4 1.2 %copy-start.8 = (bf16[512,1024]{1,0:T(8,128)(2,1)S(1)}, bf16[512,1024]{1,0:T(8,128)(2,1)}, u32[]{:S(2)}) copy-start(bf16[512,1024]{1,0:T(8,128)(2,1)} %constant.21.clone.side_hot) | copy-start | bytes 3145732
  23.7 1.1 %copy-start.10 = (bf16[256,1152]{1,0:T(8,128)(2,1)S(1)}, bf16[256,1152]{1,0:T(8,128)(2,1)}, u32[]{:S(2)}) copy-start(bf16[256,1152]{1,0:T(8,128)(2,1)} %constant.22.clone.window_hot) | copy-start | bytes 1769476
  24.7 0.8 copy-start.14
  32.8 21.0 %all-to-all-start = ((bf16[32,48,128]{2,1,0:T(8,128)(2,1)}), bf16[32,48,128]{2,1,0:T(8,128)(2,1)S(1)}, u32[]{:S(2)}, u32[]{:S(2)}) async-start(bf16[32,48,128]{2,1,0:T(8,128)(2,1)} %bitcast), calls=%async_computation | async-start | bytes 786432 | tf_op jit(solution)/shard_map/all_to_all | solution.py:408
  43.8 1.2 %copy-start.9 = (bf16[512,1024]{1,0:T(8,128)(2,1)S(1)}, bf16[512,1024]{1,0:T(8,128)(2,1)}, u32[]{:S(2)}) copy-start(bf16[512,1024]{1,0:T(8,128)(2,1)} %constant.21.clone.side_hot) | copy-start | bytes 3145732
  54.6 28.5 %all-to-all-start.1 = ((bf16[16,48,128]{2,1,0:T(8,128)(2,1)}), bf16[16,48,128]{2,1,0:T(8,128)(2,1)S(1)}, u32[]{:S(2)}, u32[]{:S(2)}) async-start(bf16[16,48,128]{2,1,0:T(8,128)(2,1)} %broadcast_in_dim.4), calls=%async_computation.1 | async-start | bytes 393216 | tf_op jit(solution)/shard_map/all_to_all | solution.py:401
  70.6 21.8 %copy-start = (bf16[512,768]{1,0:T(8,128)(2,1)S(1)}, bf16[512,768]{1,0:T(8,128)(2,1)}, u32[]{:S(2)}) copy-start(bf16[512,768]{1,0:T(8,128)(2,1)} %constant.18.clone.face_far.face_hot) | copy-start | bytes 2359300
  70.6 12.6 %collective-permute-start.4 = (bf16[4,64,128]{2,1,0:T(8,128)(2,1)S(1)}, bf16[4,64,128]{2,1,0:T(8,128)(2,1)S(1)}, u32[]{:S(2)}, u32[]{:S(2)}) collective-permute-start(bf16[4,64,128]{2,1,0:T(8,128)(2,1)S(1)} %get-tuple-element.47), channel_id=1, source_target_pairs={{4,0},{8,4},{12,8},{16,12},{20,16},{24,20},{28,24},{32,28},{36,32}... | collective-permute-start | bytes 196616 | tf_op jit(solution)/shard_map/ppermute | solution.py:420
  73.6 9.5 %collective-permute-start.5 = (bf16[4,64,128]{2,1,0:T(8,128)(2,1)S(1)}, bf16[4,64,128]{2,1,0:T(8,128)(2,1)S(1)}, u32[]{:S(2)}, u32[]{:S(2)}) collective-permute-start(bf16[4,64,128]{2,1,0:T(8,128)(2,1)S(1)} %get-tuple-element.48), channel_id=1, source_target_pairs={{0,4},{4,8},{8,12},{12,16},{16,20},{20,24},{24,28},{28,32},{32,36}... | collective-permute-start | bytes 196616 | tf_op jit(solution)/shard_map/ppermute | solution.py:420
  76.3 6.9 %collective-permute-start.6 = (bf16[4,64,128]{2,1,0:T(8,128)(2,1)S(1)}, bf16[4,64,128]{2,1,0:T(8,128)(2,1)S(1)}, u32[]{:S(2)}, u32[]{:S(2)}) collective-permute-start(bf16[4,64,128]{2,1,0:T(8,128)(2,1)S(1)} %get-tuple-element.49), channel_id=1, source_target_pairs={{8,0},{12,4},{16,8},{20,12},{24,16},{28,20},{32,24},{36,28},{40,32... | collective-permute-start | bytes 196616 | tf_op jit(solution)/shard_map/ppermute | solution.py:420
  77.6 5.6 %collective-permute-start.7 = (bf16[4,64,128]{2,1,0:T(8,128)(2,1)S(1)}, bf16[4,64,128]{2,1,0:T(8,128)(2,1)S(1)}, u32[]{:S(2)}, u32[]{:S(2)}) collective-permute-start(bf16[4,64,128]{2,1,0:T(8,128)(2,1)S(1)} %get-tuple-element.50), channel_id=1, source_target_pairs={{0,8},{4,12},{8,16},{12,20},{16,24},{20,28},{24,32},{28,36},{32,40... | collective-permute-start | bytes 196616 | tf_op jit(solution)/shard_map/ppermute | solution.py:420
  84.0 18.5 %all-to-all-start.2 = ((bf16[32,48,128]{2,1,0:T(8,128)(2,1)}), bf16[32,48,128]{2,1,0:T(8,128)(2,1)S(1)}, u32[]{:S(2)}, u32[]{:S(2)}) async-start(bf16[32,48,128]{2,1,0:T(8,128)(2,1)} %broadcast_in_dim.5), calls=%async_computation.2 | async-start | bytes 786432 | tf_op jit(solution)/shard_map/all_to_all | solution.py:415
  92.4 0.7 copy-start.2

commit v5 on v4

--- a/solution.py
+++ b/solution.py
@@ -47,18 +47,18 @@
             for z in range(8):
                 inner[s, y * 8 + z, s, (y + 1) * 10 + z + 1] = 1
     cap = np.zeros((10, 64, 128), np.float32)
-    side = np.zeros((8, 64, 8, 128), np.float32)
+    side = np.zeros((8, 64, 128), np.float32)
     for m, d in enumerate([d for d in DIRECTIONS if d[0] == 0]):
         if d[1] != 0:
             yy = 0 if d[1] == -1 else 9
             for x in range(8):
                 for i, zz in rim_cells(d[2], 8):
-                    side[m, x * 8 + i, x, yy * 10 + zz] = 1
+                    side[m, x * 8 + i, yy * 10 + zz] = 1
         else:
             zz = 0 if d[2] == -1 else 9
             for x in range(8):
                 for y in range(8):
-                    side[m, x * 8 + y, x, (y + 1) * 10 + zz] = 1
+                    side[m, x * 8 + y, (y + 1) * 10 + zz] = 1
     for m, (dy, dz) in enumerate([(b, c) for b in (-1, 0, 1) for c in (-1, 0, 1)]):
         for i, yy in rim_cells(dy, 8):
             for k, zz in rim_cells(dz, 8):
@@ -80,16 +80,43 @@
                         spread[X, Y, Z, ty, tz, X, lane] = 1
                     for tx in range(2):
                         pick[tx, ty, tz, Y, Z, tx, lane] = 1
+    def stacked(table):
+        rows, lanes = table.shape
+        return table.reshape(rows, lanes // 128, 128).transpose(1, 0, 2).reshape(-1, 128)
+
+    placing = np.concatenate(
+        [
+            cap.reshape(640, 128),
+            side.reshape(512, 128),
+            stacked(inner.reshape(128, 256)),
+            pick.reshape(128, 128),
+            stacked(spread.reshape(64, 1024)),
+            stacked(window.reshape(256, 1152)),
+        ]
+    )
     b = ml_dtypes.bfloat16
-    return (
-        faces.reshape(512, 768).astype(b),
-        inner.reshape(128, 256).astype(b),
-        cap.reshape(640, 128).astype(b),
-        side.reshape(512, 1024).astype(b),
-        window.reshape(256, 1152).astype(b),
-        spread.reshape(64, 1024).astype(b),
-        pick.reshape(128, 128).astype(b),
-    )
+    return faces.reshape(512, 768).astype(b), placing.astype(b)
+
+
+CAP_ROWS, SIDE_ROWS, INNER_ROWS, PICK_ROWS, SPREAD_ROWS = 0, 640, 1152, 1408, 1536
+WINDOW_ROWS, FOLD_ROWS, ALL_ROWS = 2048, 1408, 4352
+
+
+def tiles_of(table, start, rows, first, count):
+    blocks = [table[start + (first + i) * rows : start + (first + i + 1) * rows] for i in range(count)]
+    return jnp.concatenate(blocks, axis=1)
+
+
+def side_tiles(table, first, count):
+    side = table[SIDE_ROWS : SIDE_ROWS + 512]
+    plane = (lax.broadcasted_iota(jnp.int32, (512, 128), 0) // 8) % 8
+    return jnp.concatenate(
+        [jnp.where(plane == first + i, side, jnp.zeros_like(side)) for i in range(count)], axis=1
+    )
+
+
+def low_lanes(shape):
+    return lax.broadcasted_iota(jnp.int32, shape, 1) < 64
 
 
 def nn(a, b):
@@ -115,13 +142,16 @@
     return copies
 
 
+def wait(copies):
+    for copy in copies:
+        copy.wait()
+
+
 def faces_kernel(
     count, sends_far, features_far, face_far, table, *rest
 ):
     outgoing, (sends, features, face_hot, done) = rest[:NOFF], rest[NOFF:]
-    copies = fetch((features_far, face_far, sends_far), (features, face_hot, sends), done)
-    for copy in copies:
-        copy.wait()
+    wait(fetch((features_far, face_far, sends_far), (features, face_hot, sends), done))
     masked = masked_rows(features, count[0, 0])
     for f in range(6):
         layer = nn(masked, face_hot[:, f * 128 : (f + 1) * 128]).astype(BF)
@@ -129,32 +159,35 @@
             table[6 * s + f] = layer[s * C : (s + 1) * C]
     table[6 * SLOTS] = jnp.zeros((C, 128), BF)
     for j in range(NOFF):
-        for c in range(CAP):
-            outgoing[j][c] = table[sends[0, 0, j, c]]
+        for q in range(CAP // 2):
+            high = table[sends[0, 0, j, 2 * q + 1]]
+            outgoing[j][q] = table[sends[0, 0, j, 2 * q]] + pltpu.roll(high, 64, 1)
 
 
 def main_kernel(
     count,
-    sources,
-    features,
+    sources_far,
     table,
     ahead,
     behind,
     ahead2,
     behind2,
-    kernel,
-    down_kernel,
-    out_grad,
-    inner_hot,
-    cap_hot,
-    side_hot,
-    window_hot,
-    spread_hot,
-    pick_hot,
+    features_far,
+    placing_far,
+    kernel_far,
+    down_far,
+    out_far,
     coarse,
     grad_preact,
     sums,
     conv_back,
+    sources,
+    arrived,
+    features,
+    placing,
+    kernel,
+    down_kernel,
+    out_grad,
     halo,
     halo_high,
     conv,
@@ -164,11 +197,29 @@
     shifted,
     lowered,
     total,
+    done,
 ):
-    halo[0:LOCAL] = table[...]
+    copies = fetch(
+        (ahead, behind, ahead2, behind2, table, sources_far)
+        + (features_far, placing_far, kernel_far, down_far, out_far),
+        [arrived.at[j] for j in range(NOFF)]
+        + [halo.at[0:LOCAL], sources, features, placing, kernel, down_kernel, out_grad],
+        done,
+    )
+    wait(copies[: NOFF + 2])
+    low = low_lanes((C, 128))
+    none = jnp.zeros((C, 128), BF)
+    halo_high[0:LOCAL] = pltpu.roll(
+        halo[0:LOCAL].reshape(LOCAL * C, 128), 64, 1
+    ).reshape(LOCAL, C, 128)
     for j in range(NOFF):
-        halo[LOCAL + j * CAP : LOCAL + (j + 1) * CAP] = (ahead, behind, ahead2, behind2)[j][...]
-    halo_high[...] = pltpu.roll(halo[...].reshape(TABLE * C, 128), 64, 1).reshape(TABLE, C, 128)
+        for q in range(CAP // 2):
+            block, place = arrived[j, q], LOCAL + j * CAP + 2 * q
+            turned = pltpu.roll(block, 64, 1)
+            halo[place] = jnp.where(low, block, none)
+            halo[place + 1] = jnp.where(low, turned, none)
+            halo_high[place] = jnp.where(low, none, turned)
+            halo_high[place + 1] = jnp.where(low, none, block)
     for s in range(SLOTS):
         for t in range(14):
             even, odd = PLACES[2 * t], PLACES[2 * t + 1]
@@ -176,15 +227,20 @@
             if odd is not None:
                 block = block + halo_high[sources[0, s, odd]]
             entries[s * C : (s + 1) * C, t * 128 : (t + 1) * 128] = block
+    wait(copies[NOFF + 2 :])
+    cap_hot = placing[CAP_ROWS : CAP_ROWS + 640]
+    inner_hot = tiles_of(placing, INNER_ROWS, 128, 0, 2)
+    pick_hot = placing[PICK_ROWS : PICK_ROWS + 128]
     masked = masked_rows(features, count[0, 0])
-    padded[:, 0:128] = nn(entries[:, 0:640], cap_hot[...]).astype(BF)
-    padded[:, 1152:1280] = nn(entries[:, 1152:1792], cap_hot[...]).astype(BF)
+    padded[:, 0:128] = nn(entries[:, 0:640], cap_hot).astype(BF)
+    padded[:, 1152:1280] = nn(entries[:, 1152:1792], cap_hot).astype(BF)
     for i in range(4):
-        block = nn(entries[:, 640:1152], side_hot[:, i * 256 : (i + 1) * 256])
-        block = block + nn(masked[:, i * 128 : (i + 1) * 128], inner_hot[...])
+        block = nn(entries[:, 640:1152], side_tiles(placing, 2 * i, 2))
+        block = block + nn(masked[:, i * 128 : (i + 1) * 128], inner_hot)
         padded[:, 128 + i * 256 : 384 + i * 256] = block.astype(BF)
+    window_hot = tiles_of(placing, WINDOW_ROWS, 256, 0, 9)
     for i in range(5):
-        planes = nn(padded[:, i * 256 : (i + 1) * 256], window_hot[...]).astype(BF)
+        planes = nn(padded[:, i * 256 : (i + 1) * 256], window_hot).astype(BF)
         for s in range(SLOTS):
             lanes = slice((s % 2) * 640 + i * 128, (s % 2) * 640 + (i + 1) * 128)
             for k in range(9):
@@ -206,7 +262,7 @@
         ],
         axis=0,
     )
-    left = lax.broadcasted_iota(jnp.int32, (16, 128), 1) < 64
+    left = low_lanes((16, 128))
     edge = jnp.zeros((C, 64), BF)
     wide = jnp.zeros((C, 128), BF)
     total[...] = jnp.zeros_like(total)
@@ -227,7 +283,7 @@
             for h in range(2):
                 halves = [active[:, (2 * h + i) * 128 : (2 * h + i + 1) * 128] for i in range(2)]
                 rows = jnp.concatenate([halves[0], halves[0], halves[1], halves[1]], axis=0)
-                picked = nt(pick_hot[...], rows)
+                picked = nt(pick_hot, rows)
                 for i in range(2):
                     X = 2 * h + i
                     for q in range(4):
@@ -239,7 +295,7 @@
                         )
                         lowered[s, X * 16 : (X + 1) * 16, q * 128 : (q + 1) * 128] = block.astype(BF)
             turned = jnp.transpose(out_grad[0, s].astype(F32)).astype(BF)
-            spread = nn(turned, spread_hot[...]).astype(BF)
+            spread = nn(turned, tiles_of(placing, SPREAD_ROWS, 64, 0, 8)).astype(BF)
             spread = jnp.concatenate([spread[:, t * 256 : (t + 1) * 256] for t in range(4)], axis=0)
             grown = nn(down_rows, spread)
             upper = jnp.concatenate(
@@ -275,17 +331,18 @@
 
 def fold_kernel(
     sources,
-    grad_preact,
-    conv_back,
-    inner_hot,
-    cap_hot,
-    side_hot,
+    grads_far,
+    conv_far,
+    placing_far,
     interior,
     grad_local,
     to_ahead,
     to_behind,
     to_ahead2,
     to_behind2,
+    grad_preact,
+    conv_back,
+    placing,
     planes,
     stack,
     high,
@@ -293,10 +350,19 @@
     rims,
     grad_table,
     grad_table_high,
+    done,
 ):
+    copies = fetch(
+        (grads_far, conv_far, placing_far.at[0:FOLD_ROWS]), (grad_preact, conv_back, placing), done
+    )
+    grad_table[...] = jnp.zeros_like(grad_table)
+    grad_table_high[...] = jnp.zeros_like(grad_table_high)
+    wait(copies)
+    cap_hot = placing[CAP_ROWS : CAP_ROWS + 640]
+    inner_hot = tiles_of(placing, INNER_ROWS, 128, 0, 2)
     rows = grad_preact[...].reshape(SLOTS * C, 512)
     for i in range(4):
-        block = nn(rows[:, i * 128 : (i + 1) * 128], inner_hot[...])
+        block = nn(rows[:, i * 128 : (i + 1) * 128], inner_hot)
         planes[:, i * 256 : (i + 1) * 256] = block.astype(BF)
     high[...] = jnp.zeros_like(high)
 
@@ -320,11 +386,9 @@
         return carry
 
     lax.fori_loop(0, SLOTS, brick, 0)
-    rims[:, 0:640] = nt(high[:, 0:128], cap_hot[...])
-    rims[:, 640:1152] = nt(high[:, 128:1152], side_hot[...])
-    rims[:, 1152:1792] = nt(high[:, 1152:1280], cap_hot[...])
-    grad_table[...] = jnp.zeros_like(grad_table)
-    grad_table_high[...] = jnp.zeros_like(grad_table_high)
+    rims[:, 0:640] = nt(high[:, 0:128], cap_hot)
+    rims[:, 640:1152] = nt(high[:, 128:1152], side_tiles(placing, 0, 8))
+    rims[:, 1152:1792] = nt(high[:, 1152:1280], cap_hot)
     for s in range(SLOTS):
         for t in range(14):
             block = rims[s * C : (s + 1) * C, t * 128 : (t + 1) * 128]
@@ -335,13 +399,16 @@
     grad_table[...] += turned.reshape(TABLE, C, 128)
     for i in range(4):
         lanes = slice(128 + i * 256, 384 + i * 256)
-        interior[:, i * 128 : (i + 1) * 128] = nt(high[:, lanes], inner_hot[...]) + nt(
-            low[:, lanes], inner_hot[...]
+        interior[:, i * 128 : (i + 1) * 128] = nt(high[:, lanes], inner_hot) + nt(
+            low[:, lanes], inner_hot
         )
     grad_local[...] = grad_table[0:LOCAL]
+    left = low_lanes((C, 128))
     for j in range(NOFF):
-        block = grad_table[LOCAL + j * CAP : LOCAL + (j + 1) * CAP].astype(BF)
-        (to_ahead, to_behind, to_ahead2, to_behind2)[j][...] = block
+        for q in range(CAP // 2):
+            place = LOCAL + j * CAP + 2 * q
+            block = jnp.where(left, grad_table[place], pltpu.roll(grad_table[place + 1], 64, 1))
+            (to_ahead, to_behind, to_ahead2, to_behind2)[j][q] = block.astype(BF)
 
 
 def unpack_kernel(sums, grad_kernel, grad_down):
@@ -370,9 +437,10 @@
 ):
     table[...] = grad_local[...]
     for j in range(NOFF):
-        for c in range(CAP):
-            block = (ahead, behind, ahead2, behind2)[j][c]
-            table[sends[0, 0, j, c]] += block.astype(F32)
+        for q in range(CAP // 2):
+            block = (ahead, behind, ahead2, behind2)[j][q].astype(F32)
+            table[sends[0, 0, j, 2 * q]] += block
+            table[sends[0, 0, j, 2 * q + 1]] += pltpu.roll(block, 64, 1)
     for s in range(SLOTS):
         for f in range(6):
             layers[s * C : (s + 1) * C, f * 128 : (f + 1) * 128] = table[6 * s + f].astype(BF)
@@ -390,7 +458,7 @@
         out_specs=[pl.BlockSpec(memory_space=pltpu.VMEM) for _ in outs],
         out_shape=[jax.ShapeDtypeStruct(s, d) for s, d in outs],
         scratch_shapes=[pltpu.VMEM(*s) if isinstance(s, tuple) else s for s in scratch],
-        compiler_params=pltpu.CompilerParams(vmem_limit_bytes=limit * 2**20),
+        compiler_params=pltpu.CompilerParams(vmem_limit_bytes=int(limit * 2**20)),
         cost_estimate=pl.CostEstimate(flops=flops, bytes_accessed=2**20, transcendentals=0),
         name=kernel.__name__,
     )(*args)
@@ -421,10 +489,10 @@
 
 
 def on_device(sizes, features, brick_count, send_list, halo_src, kernel, down_kernel, out_grad):
-    face_hot, inner_hot, cap_hot, side_hot, window_hot, spread_hot, pick_hot = one_hot_tables()
+    face_hot, placing = one_hot_tables()
     tile = ("z", "x", "c")
     devices = sizes["z"] * sizes["x"] * sizes["c"]
-    swap = [((CAP, C, 128), BF)] * NOFF
+    swap = [((CAP // 2, C, 128), BF)] * NOFF
 
     table, *outgoing = call(
         faces_kernel,
@@ -446,8 +514,8 @@
     received = [from_behind(b, tile, devices, o) for b, o in zip(outgoing, OFFSETS)]
     coarse, grad_preact, sums, conv_back = call(
         main_kernel,
-        28,
-        "ss" + "v" * 15,
+        53.8,
+        "s" + "h" * 11,
         [
             ((1, SLOTS, 64, C2), BF),
             ((SLOTS, C, 512), BF),
@@ -455,6 +523,13 @@
             ((192, 576), BF),
         ],
         [
+            pltpu.SMEM((1, SLOTS, 26), jnp.int32),
+            ((NOFF, CAP // 2, C, 128), BF),
+            ((1, SLOTS, C, 512), BF),
+            ((ALL_ROWS, 128), BF),
+            ((C, 1728), BF),
+            ((C2, 512), BF),
+            ((1, SLOTS, 64, C2), BF),
             ((TABLE, C, 128), BF),
             ((TABLE, C, 128), BF),
             ((192, 576), BF),
@@ -464,30 +539,29 @@
             ((192, 1280), BF),
             ((SLOTS, 64, 512), BF),
             ((192, 576), F32),
+            pltpu.SemaphoreType.DMA((11,)),
         ],
         5 * 10**9,
         brick_count,
         halo_src,
-        features,
         table,
         *received,
+        features,
+        placing,
         kernel,
         down_kernel,
         out_grad,
-        inner_hot,
-        cap_hot,
-        side_hot,
-        window_hot,
-        spread_hot,
-        pick_hot,
     )
     part = near_sum(sums, sizes)
     interior, grad_local, *remote = call(
         fold_kernel,
-        24,
-        "svvvvv",
+        56,
+        "shhh",
         [((256, 512), F32), ((LOCAL, C, 128), F32)] + swap,
         [
+            ((SLOTS, C, 512), BF),
+            ((192, 576), BF),
+            ((FOLD_ROWS, 128), BF),
             ((256, 1024), BF),
             ((576, 1024), BF),
             ((256, 1280), BF),
@@ -495,14 +569,13 @@
             ((256, 14 * 128), F32),
             ((TABLE, C, 128), F32),
             ((TABLE, C, 128), F32),
+            pltpu.SemaphoreType.DMA((3,)),
         ],
         3 * 10**9,
         halo_src,
         grad_preact,
         conv_back,
-        inner_hot,
-        cap_hot,
-        side_hot,
+        placing,
     )
     part, *remote = lax.optimization_barrier((part, *remote))
     part = gather_sum(part, ("z",), sizes["z"])

time: 104 us -> 101 us (0.971)
  local copies, waits for them, and re-layouts: 7.48 us -> 2.21 us
  Pallas kernels: 17.7 us -> 20.7 us
    unnamed x30 -> x10, local copies, waits for them, and re-layouts: 5.98 us -> 0.7 us
    pallas_call x5, Pallas kernels: 17.7 us -> 20.7 us  [call(): pl.pallas_call(kernel, in_specs=[pl.BlockSpec(memory_space=where[m]) for...]
    all_to_all x1, waiting for transfers between devices: 3.86 us -> 2.82 us  [near_sum(): got = lax.all_to_all(block.reshape(parts, rows, 128), NEAR, 0, 0)]
  transfers between devices with their start and end apart: 11 -> 11, of which waited for: 5 -> 4; matrix products, arithmetic and copies ran while one was open for 0% -> 0% of each run, Pallas kernels for 7% -> 9%
where the time goes in v5:
time: 101 us; the launch traced here: 100 us
  starting transfers between devices  59.2 us (59%)
  Pallas kernels  20.7 us (20%)
  waiting for transfers between devices  16.6 us (16%)
  local copies, waits for them, and re-layouts  2.21 us (2%)
  between operations  1.51 us (1%)
    ppermute x8, starting transfers between devices, from_behind(): return lax.ppermute(block, axes, route)  23.5 us
    pallas_call x5, Pallas kernels, call(): pl.pallas_call(kernel, in_specs=[pl.BlockSpec(memory_space=where[m]) for...  20.7 us
    all_to_all x1, starting transfers between devices, gather_sum(): got = lax.all_to_all(copies, axes, 0, 0)  16 us
    all_to_all x1, starting transfers between devices, near_sum(): got = lax.all_to_all(block.reshape(parts, rows, 128), NEAR, 0, 0)  11.3 us
    all_to_all x1, starting transfers between devices, near_gather(): lax.all_to_all(copies, NEAR, 0, 0).reshape(parts * block.shape[0], 128)  8.39 us
    all_to_all x1, waiting for transfers between devices, near_gather(): lax.all_to_all(copies, NEAR, 0, 0).reshape(parts * block.shape[0], 128)  8.24 us
    ppermute x8, waiting for transfers between devices, from_behind(): return lax.ppermute(block, axes, route)  3.89 us
    all_to_all x1, waiting for transfers between devices, near_sum(): got = lax.all_to_all(block.reshape(parts, rows, 128), NEAR, 0, 0)  2.82 us
  transfers between devices with their start and end apart: 11, of which 4 were waited for; matrix products, arithmetic and copies ran while one was open for 0% of the time, Pallas kernels for 9%

profile of v5, /device:TPU:1, one launch (start us, length us, event | category | flops | bytes accessed | tf_op | source)
XLA Modules:
  0.0 100.3 jit_solution(9922521268182526384)
XLA Ops:
  1.3 2.6 %faces_kernel.1 = (bf16[25,64,128]{2,1,0:T(8,128)(2,1)}, bf16[2,64,128]{2,1,0:T(8,128)(2,1)}, bf16[2,64,128]{2,1,0:T(8,128)(2,1)}, bf16[2,64,128]{2,1,0:T(8,128)(2,1)}, bf16[2,64,128]{2,1,0:T(8,128)(2,1)}) custom-call(s32[1,1]{1,0:T(1,128)S(6)} %copy.13.count, s32[1,1,4,4]{3,2,1,0:T(4,128)} %sends.1, bf16[1,4,64,512]{3,2,1,0:T(8,128)(2,1)} %features_far.3, ...), custom_call_target="tpu_custom_call" | custom-call | flops 201326592 | bytes 1048576 | tf_op jit(solution)/shard_map/faces_kernel/pallas_call | solution.py:455
  3.9 4.5 %collective-permute-start = (bf16[2,64,128]{2,1,0:T(8,128)(2,1)}, bf16[2,64,128]{2,1,0:T(8,128)(2,1)S(1)}, u32[]{:S(2)}, u32[]{:S(2)}) collective-permute-start(bf16[2,64,128]{2,1,0:T(8,128)(2,1)} %get-tuple-element.32), channel_id=1, source_target_pairs={{0,4},{4,8},{8,12},{12,16},{16,20},{20,24},{24,28},{28,32},{32,36}... | collective-permute-start | bytes 98312 | tf_op jit(solution)/shard_map/ppermute | solution.py:488
  8.4 5.6 %collective-permute-start.1 = (bf16[2,64,128]{2,1,0:T(8,128)(2,1)}, bf16[2,64,128]{2,1,0:T(8,128)(2,1)S(1)}, u32[]{:S(2)}, u32[]{:S(2)}) collective-permute-start(bf16[2,64,128]{2,1,0:T(8,128)(2,1)} %get-tuple-element.33), channel_id=1, source_target_pairs={{4,0},{8,4},{12,8},{16,12},{20,16},{24,20},{28,24},{32,28},{36,32}... | collective-permute-start | bytes 98312 | tf_op jit(solution)/shard_map/ppermute | solution.py:488
  14.0 1.3 %collective-permute-start.2 = (bf16[2,64,128]{2,1,0:T(8,128)(2,1)}, bf16[2,64,128]{2,1,0:T(8,128)(2,1)S(1)}, u32[]{:S(2)}, u32[]{:S(2)}) collective-permute-start(bf16[2,64,128]{2,1,0:T(8,128)(2,1)} %get-tuple-element.34), channel_id=1, source_target_pairs={{0,8},{4,12},{8,16},{12,20},{16,24},{20,28},{24,32},{28,36},{32,40... | collective-permute-start | bytes 98312 | tf_op jit(solution)/shard_map/ppermute | solution.py:488
  15.3 1.3 %collective-permute-start.3 = (bf16[2,64,128]{2,1,0:T(8,128)(2,1)}, bf16[2,64,128]{2,1,0:T(8,128)(2,1)S(1)}, u32[]{:S(2)}, u32[]{:S(2)}) collective-permute-start(bf16[2,64,128]{2,1,0:T(8,128)(2,1)} %get-tuple-element.35), channel_id=1, source_target_pairs={{8,0},{12,4},{16,8},{20,12},{24,16},{28,20},{32,24},{36,28},{40,32... | collective-permute-start | bytes 98312 | tf_op jit(solution)/shard_map/ppermute | solution.py:488
  16.6 0.0 collective-permute-done.ahead
  16.6 0.0 collective-permute-done.1.behind
  16.6 0.0 collective-permute-done.2.ahead2
  16.6 3.9 %collective-permute-done.3.behind2 = bf16[2,64,128]{2,1,0:T(8,128)(2,1)S(1)} collective-permute-done((bf16[2,64,128]{2,1,0:T(8,128)(2,1)}, bf16[2,64,128]{2,1,0:T(8,128)(2,1)S(1)}, u32[]{:S(2)}, u32[]{:S(2)}) %collective-permute-start.3) | collective-permute-done | bytes 32800 | tf_op jit(solution)/shard_map/ppermute | solution.py:488
  20.5 0.0 copy-start.4
  20.5 0.7 copy-done.4
  21.2 8.2 %main_kernel.1 = (bf16[1,4,64,128]{3,2,1,0:T(8,128)(2,1)}, bf16[4,64,512]{2,1,0:T(8,128)(2,1)}, bf16[1536,128]{1,0:T(8,128)(2,1)}, bf16[192,576]{1,0:T(8,128)(2,1)}) custom-call(s32[1,1]{1,0:T(1,128)S(6)} %copy.13.count, s32[1,4,26]{2,1,0:T(4,128)S(1)} %copy-done.4, bf16[25,64,128]{2,1,0:T(8,128)(2,1)} %get-tuple-element.31.table, ...), custom_call_target="tpu_custom_call" | custom-call | flops 5000000000 | bytes 1048576 | tf_op jit(solution)/shard_map/main_kernel/pallas_call | solution.py:455
  29.4 11.3 %all-to-all-start = ((bf16[32,48,128]{2,1,0:T(8,128)(2,1)}), bf16[32,48,128]{2,1,0:T(8,128)(2,1)S(1)}, u32[]{:S(2)}, u32[]{:S(2)}) async-start(bf16[32,48,128]{2,1,0:T(8,128)(2,1)} %bitcast.3), calls=%async_computation | async-start | bytes 786432 | tf_op jit(solution)/shard_map/all_to_all | solution.py:476
  40.7 7.2 %fold_kernel.1 = (f32[256,512]{1,0:T(8,128)}, f32[25,64,128]{2,1,0:T(8,128)}, bf16[2,64,128]{2,1,0:T(8,128)(2,1)}, bf16[2,64,128]{2,1,0:T(8,128)(2,1)}, bf16[2,6...) custom-call(s32[1,4,26]{2,1,0:T(4,128)} %sources.1, bf16[4,64,512]{2,1,0:T(8,128)(2,1)} %get-tuple-element.37.grads_far, ...), custom_call_target="tpu_custom_call" | custom-call | flops 3000000000 | bytes 1048576 | tf_op jit(solution)/shard_map/fold_kernel/pallas_call | solution.py:455
  47.9 0.0 copy-start
  47.9 0.0 copy-start.1
  47.9 0.0 copy-start.2
  47.9 0.0 copy-start.3
  47.9 2.8 %all-to-all-done = bf16[32,48,128]{2,1,0:T(8,128)(2,1)S(1)} async-done(((bf16[32,48,128]{2,1,0:T(8,128)(2,1)}), bf16[32,48,128]{2,1,0:T(8,128)(2,1)S(1)}, u32[]{:S(2)}, u32[]{:S(2)}) %all-to-all-start) | async-done | bytes 393248 | tf_op jit(solution)/shard_map/all_to_all | solution.py:476
  50.7 0.1 reduce_sum.21
  50.8 0.7 broadcast_in_dim.4
  51.5 16.0 %all-to-all-start.1 = ((bf16[16,48,128]{2,1,0:T(8,128)(2,1)}), bf16[16,48,128]{2,1,0:T(8,128)(2,1)S(1)}, u32[]{:S(2)}, u32[]{:S(2)}) async-start(bf16[16,48,128]{2,1,0:T(8,128)(2,1)} %broadcast_in_dim.4), calls=%async_computation.1 | async-start | bytes 393216 | tf_op jit(solution)/shard_map/all_to_all | solution.py:469
  67.5 2.9 %collective-permute-start.4 = (bf16[2,64,128]{2,1,0:T(8,128)(2,1)}, bf16[2,64,128]{2,1,0:T(8,128)(2,1)S(1)}, u32[]{:S(2)}, u32[]{:S(2)}) collective-permute-start(bf16[2,64,128]{2,1,0:T(8,128)(2,1)} %get-tuple-element.47), channel_id=1, source_target_pairs={{4,0},{8,4},{12,8},{16,12},{20,16},{24,20},{28,24},{32,28},{36,32}... | collective-permute-start | bytes 98312 | tf_op jit(solution)/shard_map/ppermute | solution.py:488
  70.4 2.7 %collective-permute-start.5 = (bf16[2,64,128]{2,1,0:T(8,128)(2,1)}, bf16[2,64,128]{2,1,0:T(8,128)(2,1)S(1)}, u32[]{:S(2)}, u32[]{:S(2)}) collective-permute-start(bf16[2,64,128]{2,1,0:T(8,128)(2,1)} %get-tuple-element.48), channel_id=1, source_target_pairs={{0,4},{4,8},{8,12},{12,16},{16,20},{20,24},{24,28},{28,32},{32,36}... | collective-permute-start | bytes 98312 | tf_op jit(solution)/shard_map/ppermute | solution.py:488
  73.1 1.3 %collective-permute-start.6 = (bf16[2,64,128]{2,1,0:T(8,128)(2,1)}, bf16[2,64,128]{2,1,0:T(8,128)(2,1)S(1)}, u32[]{:S(2)}, u32[]{:S(2)}) collective-permute-start(bf16[2,64,128]{2,1,0:T(8,128)(2,1)} %get-tuple-element.49), channel_id=1, source_target_pairs={{8,0},{12,4},{16,8},{20,12},{24,16},{28,20},{32,24},{36,28},{40,32... | collective-permute-start | bytes 98312 | tf_op jit(solution)/shard_map/ppermute | solution.py:488
  74.4 4.0 %collective-permute-start.7 = (bf16[2,64,128]{2,1,0:T(8,128)(2,1)}, bf16[2,64,128]{2,1,0:T(8,128)(2,1)S(1)}, u32[]{:S(2)}, u32[]{:S(2)}) collective-permute-start(bf16[2,64,128]{2,1,0:T(8,128)(2,1)} %get-tuple-element.50), channel_id=1, source_target_pairs={{0,8},{4,12},{8,16},{12,20},{16,24},{20,28},{24,32},{28,36},{32,40... | collective-permute-start | bytes 98312 | tf_op jit(solution)/shard_map/ppermute | solution.py:488
  78.4 1.7 %all-to-all-done.1 = bf16[16,48,128]{2,1,0:T(8,128)(2,1)S(1)} async-done(((bf16[16,48,128]{2,1,0:T(8,128)(2,1)}), bf16[16,48,128]{2,1,0:T(8,128)(2,1)S(1)}, u32[]{:S(2)}, u32[]{:S(2)}) %all-to-all-start.1) | async-done | bytes 196640 | tf_op jit(solution)/shard_map/all_to_all | solution.py:469
  80.1 0.0 collective-permute-done.4.ahead
  80.1 0.0 collective-permute-done.5.behind
  80.1 0.0 collective-permute-done.6.ahead2
  80.1 0.0 collective-permute-done.7.behind2
  80.1 0.8 broadcast_in_dim.5
  80.9 8.4 %all-to-all-start.2 = ((bf16[32,48,128]{2,1,0:T(8,128)(2,1)}), bf16[32,48,128]{2,1,0:T(8,128)(2,1)S(1)}, u32[]{:S(2)}, u32[]{:S(2)}) async-start(bf16[32,48,128]{2,1,0:T(8,128)(2,1)} %broadcast_in_dim.5), calls=%async_computation.2 | async-start | bytes 786432 | tf_op jit(solution)/shard_map/all_to_all | solution.py:483
  89.3 0.0 copy-done
  89.3 0.0 copy-done.1
  89.3 0.0 copy-done.2
  89.3 0.0 copy-done.3
  89.4 1.8 %finish_kernel.1 = bf16[1,4,64,512]{3,2,1,0:T(8,128)(2,1)} custom-call(s32[1,1]{1,0:T(1,128)S(6)} %copy.13.count, s32[1,1,4,4]{3,2,1,0:T(4,128)S(1)} %copy-done.3, f32[256,512]{1,0:T(8,128)S(1)} %copy-done.2, f32[25,64,128]{2,1,0:T(8,128)S(1)} %copy-done.1, bf16[2,64,128]{2,1,0:T(8,128)(2,1)S(1)} %collective-permute-done.4.ahead, ...), custom_call_target="tpu_custom_call" | custom-call | flops 201326592 | bytes 1048576 | tf_op jit(solution)/shard_map/finish_kernel/pallas_call | solution.py:455
  91.2 8.2 %all-to-all-done.2 = bf16[32,48,128]{2,1,0:T(8,128)(2,1)S(1)} async-done(((bf16[32,48,128]{2,1,0:T(8,128)(2,1)}), bf16[32,48,128]{2,1,0:T(8,128)(2,1)S(1)}, u32[]{:S(2)}, u32[]{:S(2)}) %all-to-all-start.2) | async-done | bytes 393248 | tf_op jit(solution)/shard_map/all_to_all | solution.py:483
  99.4 0.9 unpack_kernel.1
  (1 shorter events, 0.0 us)
Async XLA Ops:
  3.9 12.7 %collective-permute-start = (bf16[2,64,128]{2,1,0:T(8,128)(2,1)}, bf16[2,64,128]{2,1,0:T(8,128)(2,1)S(1)}, u32[]{:S(2)}, u32[]{:S(2)}) collective-permute-start(bf16[2,64,128]{2,1,0:T(8,128)(2,1)} %get-tuple-element.32), channel_id=1, source_target_pairs={{0,4},{4,8},{8,12},{12,16},{16,20},{20,24},{24,28},{28,32},{32,36}... | collective-permute-start | bytes 98312 | tf_op jit(solution)/shard_map/ppermute | solution.py:488
  8.4 8.2 %collective-permute-start.1 = (bf16[2,64,128]{2,1,0:T(8,128)(2,1)}, bf16[2,64,128]{2,1,0:T(8,128)(2,1)S(1)}, u32[]{:S(2)}, u32[]{:S(2)}) collective-permute-start(bf16[2,64,128]{2,1,0:T(8,128)(2,1)} %get-tuple-element.33), channel_id=1, source_target_pairs={{4,0},{8,4},{12,8},{16,12},{20,16},{24,20},{28,24},{32,28},{36,32}... | collective-permute-start | bytes 98312 | tf_op jit(solution)/shard_map/ppermute | solution.py:488
  14.0 2.6 %collective-permute-start.2 = (bf16[2,64,128]{2,1,0:T(8,128)(2,1)}, bf16[2,64,128]{2,1,0:T(8,128)(2,1)S(1)}, u32[]{:S(2)}, u32[]{:S(2)}) collective-permute-start(bf16[2,64,128]{2,1,0:T(8,128)(2,1)} %get-tuple-element.34), channel_id=1, source_target_pairs={{0,8},{4,12},{8,16},{12,20},{16,24},{20,28},{24,32},{28,36},{32,40... | collective-permute-start | bytes 98312 | tf_op jit(solution)/shard_map/ppermute | solution.py:488
  15.3 5.2 %collective-permute-start.3 = (bf16[2,64,128]{2,1,0:T(8,128)(2,1)}, bf16[2,64,128]{2,1,0:T(8,128)(2,1)S(1)}, u32[]{:S(2)}, u32[]{:S(2)}) collective-permute-start(bf16[2,64,128]{2,1,0:T(8,128)(2,1)} %get-tuple-element.35), channel_id=1, source_target_pairs={{8,0},{12,4},{16,8},{20,12},{24,16},{28,20},{32,24},{36,28},{40,32... | collective-permute-start | bytes 98312 | tf_op jit(solution)/shard_map/ppermute | solution.py:488
  20.5 0.7 copy-start.4
  29.4 21.4 %all-to-all-start = ((bf16[32,48,128]{2,1,0:T(8,128)(2,1)}), bf16[32,48,128]{2,1,0:T(8,128)(2,1)S(1)}, u32[]{:S(2)}, u32[]{:S(2)}) async-start(bf16[32,48,128]{2,1,0:T(8,128)(2,1)} %bitcast.3), calls=%async_computation | async-start | bytes 786432 | tf_op jit(solution)/shard_map/all_to_all | solution.py:476
  47.9 41.5 %copy-start = (bf16[512,768]{1,0:T(8,128)(2,1)S(1)}, bf16[512,768]{1,0:T(8,128)(2,1)}, u32[]{:S(2)}) copy-start(bf16[512,768]{1,0:T(8,128)(2,1)} %constant.8.clone.face_far.face_hot) | copy-start | bytes 2359300
  47.9 41.5 %copy-start.1 = (f32[25,64,128]{2,1,0:T(8,128)S(1)}, f32[25,64,128]{2,1,0:T(8,128)}, u32[]{:S(2)}) copy-start(f32[25,64,128]{2,1,0:T(8,128)} %get-tuple-element.40.grad_local) | copy-start | bytes 2457604
  47.9 41.5 %copy-start.2 = (f32[256,512]{1,0:T(8,128)S(1)}, f32[256,512]{1,0:T(8,128)}, u32[]{:S(2)}) copy-start(f32[256,512]{1,0:T(8,128)} %get-tuple-element.39.interior) | copy-start | bytes 1572868
  47.9 41.5 %copy-start.3 = (s32[1,1,4,4]{3,2,1,0:T(4,128)S(1)}, s32[1,1,4,4]{3,2,1,0:T(4,128)}, u32[]{:S(2)}) copy-start(s32[1,1,4,4]{3,2,1,0:T(4,128)} %sends.1) | copy-start | bytes 196
  51.5 28.5 %all-to-all-start.1 = ((bf16[16,48,128]{2,1,0:T(8,128)(2,1)}), bf16[16,48,128]{2,1,0:T(8,128)(2,1)S(1)}, u32[]{:S(2)}, u32[]{:S(2)}) async-start(bf16[16,48,128]{2,1,0:T(8,128)(2,1)} %broadcast_in_dim.4), calls=%async_computation.1 | async-start | bytes 393216 | tf_op jit(solution)/shard_map/all_to_all | solution.py:469
  67.5 12.6 %collective-permute-start.4 = (bf16[2,64,128]{2,1,0:T(8,128)(2,1)}, bf16[2,64,128]{2,1,0:T(8,128)(2,1)S(1)}, u32[]{:S(2)}, u32[]{:S(2)}) collective-permute-start(bf16[2,64,128]{2,1,0:T(8,128)(2,1)} %get-tuple-element.47), channel_id=1, source_target_pairs={{4,0},{8,4},{12,8},{16,12},{20,16},{24,20},{28,24},{32,28},{36,32}... | collective-permute-start | bytes 98312 | tf_op jit(solution)/shard_map/ppermute | solution.py:488
  70.4 9.7 %collective-permute-start.5 = (bf16[2,64,128]{2,1,0:T(8,128)(2,1)}, bf16[2,64,128]{2,1,0:T(8,128)(2,1)S(1)}, u32[]{:S(2)}, u32[]{:S(2)}) collective-permute-start(bf16[2,64,128]{2,1,0:T(8,128)(2,1)} %get-tuple-element.48), channel_id=1, source_target_pairs={{0,4},{4,8},{8,12},{12,16},{16,20},{20,24},{24,28},{28,32},{32,36}... | collective-permute-start | bytes 98312 | tf_op jit(solution)/shard_map/ppermute | solution.py:488
  73.1 7.0 %collective-permute-start.6 = (bf16[2,64,128]{2,1,0:T(8,128)(2,1)}, bf16[2,64,128]{2,1,0:T(8,128)(2,1)S(1)}, u32[]{:S(2)}, u32[]{:S(2)}) collective-permute-start(bf16[2,64,128]{2,1,0:T(8,128)(2,1)} %get-tuple-element.49), channel_id=1, source_target_pairs={{8,0},{12,4},{16,8},{20,12},{24,16},{28,20},{32,24},{36,28},{40,32... | collective-permute-start | bytes 98312 | tf_op jit(solution)/shard_map/ppermute | solution.py:488
  74.4 5.7 %collective-permute-start.7 = (bf16[2,64,128]{2,1,0:T(8,128)(2,1)}, bf16[2,64,128]{2,1,0:T(8,128)(2,1)S(1)}, u32[]{:S(2)}, u32[]{:S(2)}) collective-permute-start(bf16[2,64,128]{2,1,0:T(8,128)(2,1)} %get-tuple-element.50), channel_id=1, source_target_pairs={{0,8},{4,12},{8,16},{12,20},{16,24},{20,28},{24,32},{28,36},{32,40... | collective-permute-start | bytes 98312 | tf_op jit(solution)/shard_map/ppermute | solution.py:488
  80.9 18.5 %all-to-all-start.2 = ((bf16[32,48,128]{2,1,0:T(8,128)(2,1)}), bf16[32,48,128]{2,1,0:T(8,128)(2,1)S(1)}, u32[]{:S(2)}, u32[]{:S(2)}) async-start(bf16[32,48,128]{2,1,0:T(8,128)(2,1)} %broadcast_in_dim.5), calls=%async_computation.2 | async-start | bytes 786432 | tf_op jit(solution)/shard_map/all_to_all | solution.py:483

commit v6 on v5

--- a/solution.py
+++ b/solution.py
@@ -95,7 +95,9 @@
         ]
     )
     b = ml_dtypes.bfloat16
-    return faces.reshape(512, 768).astype(b), placing.astype(b)
+    packed = faces[:, 2:, :64].reshape(512, 256)
+    inner = inner.reshape(128, 256)
+    return packed.astype(b), faces.reshape(512, 768).astype(b), inner.astype(b), placing.astype(b)
 
 
 CAP_ROWS, SIDE_ROWS, INNER_ROWS, PICK_ROWS, SPREAD_ROWS = 0, 640, 1152, 1408, 1536
@@ -153,8 +155,15 @@
     outgoing, (sends, features, face_hot, done) = rest[:NOFF], rest[NOFF:]
     wait(fetch((features_far, face_far, sends_far), (features, face_hot, sends), done))
     masked = masked_rows(features, count[0, 0])
+    low = low_lanes((SLOTS * C, 128))
+    none = jnp.zeros((SLOTS * C, 128), BF)
+    found = nn(masked, face_hot[...]).astype(BF)
+    pairs = (found[:, 0:128], found[:, 128:256])
+    layers = [masked[:, 0:128], pltpu.roll(masked[:, 384:512], 64, 1)]
+    for block in pairs:
+        layers += [block, pltpu.roll(block, 64, 1)]
     for f in range(6):
-        layer = nn(masked, face_hot[:, f * 128 : (f + 1) * 128]).astype(BF)
+        layer = jnp.where(low, layers[f], none)
         for s in range(SLOTS):
             table[6 * s + f] = layer[s * C : (s + 1) * C]
     table[6 * SLOTS] = jnp.zeros((C, 128), BF)
@@ -334,7 +343,7 @@
     grads_far,
     conv_far,
     placing_far,
-    interior,
+    folded,
     grad_local,
     to_ahead,
     to_behind,
@@ -346,25 +355,24 @@
     planes,
     stack,
     high,
-    low,
     rims,
     grad_table,
     grad_table_high,
     done,
 ):
     copies = fetch(
-        (grads_far, conv_far, placing_far.at[0:FOLD_ROWS]), (grad_preact, conv_back, placing), done
+        (grads_far, placing_far.at[0:FOLD_ROWS], conv_far), (grad_preact, placing, conv_back), done
     )
     grad_table[...] = jnp.zeros_like(grad_table)
     grad_table_high[...] = jnp.zeros_like(grad_table_high)
-    wait(copies)
+    wait(copies[:2])
     cap_hot = placing[CAP_ROWS : CAP_ROWS + 640]
     inner_hot = tiles_of(placing, INNER_ROWS, 128, 0, 2)
     rows = grad_preact[...].reshape(SLOTS * C, 512)
     for i in range(4):
         block = nn(rows[:, i * 128 : (i + 1) * 128], inner_hot)
         planes[:, i * 256 : (i + 1) * 256] = block.astype(BF)
-    high[...] = jnp.zeros_like(high)
+    wait(copies[2:])
 
     def brick(s, carry):
         here = pl.ds(pl.multiple_of(s * C, C), C)
@@ -380,9 +388,9 @@
                 if 0 <= x - o < 8:
                     part = triple[o * C : (o + 1) * C, (x - o) * 128 : (x - o + 1) * 128]
                     value = part if value is None else value + part
-            top = value.astype(BF)
-            high[here, x * 128 : (x + 1) * 128] = top
-            low[here, x * 128 : (x + 1) * 128] = (value - top.astype(F32)).astype(BF)
+            high[here, x * 128 : (x + 1) * 128] = value.astype(BF)
+            if 1 <= x <= 8:
+                folded[here, (x - 1) * 128 : x * 128] = value
         return carry
 
     lax.fori_loop(0, SLOTS, brick, 0)
@@ -397,11 +405,6 @@
                 grad_table_high[sources[0, s, PLACES[2 * t + 1]]] += block
     turned = pltpu.roll(grad_table_high[...].reshape(TABLE * C, 128), 64, 1)
     grad_table[...] += turned.reshape(TABLE, C, 128)
-    for i in range(4):
-        lanes = slice(128 + i * 256, 384 + i * 256)
-        interior[:, i * 128 : (i + 1) * 128] = nt(high[:, lanes], inner_hot) + nt(
-            low[:, lanes], inner_hot
-        )
     grad_local[...] = grad_table[0:LOCAL]
     left = low_lanes((C, 128))
     for j in range(NOFF):
@@ -424,13 +427,14 @@
 def finish_kernel(
     count,
     sends,
-    interior,
+    folded,
     grad_local,
     ahead,
     behind,
     ahead2,
     behind2,
     face_hot,
+    inner_hot,
     grad_features,
     table,
     layers,
@@ -444,7 +448,13 @@
     for s in range(SLOTS):
         for f in range(6):
             layers[s * C : (s + 1) * C, f * 128 : (f + 1) * 128] = table[6 * s + f].astype(BF)
-    whole = interior[...] + nt(layers[...], face_hot[...])
+    tiles = []
+    for i in range(4):
+        value = folded[:, i * 256 : (i + 1) * 256]
+        top = value.astype(BF)
+        rest = (value - top.astype(F32)).astype(BF)
+        tiles.append(nt(top, inner_hot[...]) + nt(rest, inner_hot[...]))
+    whole = jnp.concatenate(tiles, axis=1) + nt(layers[...], face_hot[...])
     for s in range(SLOTS):
         filled = jnp.where(s < count[0, 0], 1.0, 0.0).astype(F32)
         grad_features[0, s] = (whole[s * C : (s + 1) * C] * filled).astype(BF)
@@ -489,7 +499,7 @@
 
 
 def on_device(sizes, features, brick_count, send_list, halo_src, kernel, down_kernel, out_grad):
-    face_hot, placing = one_hot_tables()
+    face_packed, face_hot, inner_hot, placing = one_hot_tables()
     tile = ("z", "x", "c")
     devices = sizes["z"] * sizes["x"] * sizes["c"]
     swap = [((CAP // 2, C, 128), BF)] * NOFF
@@ -502,14 +512,14 @@
         [
             pltpu.SMEM((1, 1, NOFF, CAP), jnp.int32),
             ((1, SLOTS, C, 512), BF),
-            ((512, 768), BF),
+            ((512, 256), BF),
             pltpu.SemaphoreType.DMA((3,)),
         ],
         2 * 256 * 512 * 768,
         brick_count,
         send_list,
         features,
-        face_hot,
+        face_packed,
     )
     received = [from_behind(b, tile, devices, o) for b, o in zip(outgoing, OFFSETS)]
     coarse, grad_preact, sums, conv_back = call(
@@ -553,18 +563,17 @@
         out_grad,
     )
     part = near_sum(sums, sizes)
-    interior, grad_local, *remote = call(
+    folded, grad_local, *remote = call(
         fold_kernel,
         56,
         "shhh",
-        [((256, 512), F32), ((LOCAL, C, 128), F32)] + swap,
+        [((256, 1024), F32), ((LOCAL, C, 128), F32)] + swap,
         [
             ((SLOTS, C, 512), BF),
             ((192, 576), BF),
             ((FOLD_ROWS, 128), BF),
             ((256, 1024), BF),
             ((576, 1024), BF),
-            ((256, 1280), BF),
             ((256, 1280), BF),
             ((256, 14 * 128), F32),
             ((TABLE, C, 128), F32),
@@ -585,16 +594,17 @@
     (grad_features,) = call(
         finish_kernel,
         12,
-        "ss" + "v" * 7,
+        "ss" + "v" * 8,
         [((1, SLOTS, C, 512), BF)],
         [((LOCAL, C, 128), F32), ((256, 768), BF)],
         2 * 256 * 512 * 768,
         brick_count,
         send_list,
-        interior,
+        folded,
         grad_local,
         *returned,
         face_hot,
+        inner_hot,
     )
     grad_kernel, grad_down = call(
         unpack_kernel, 8, "v", [((C, 1728), F32), ((C2, 512), F32)], [], 10**6, sums

time: 101 us -> 101 us (level)
  no operation moved by 1% of the time
where the time goes in v6:
time: 101 us; the launch traced here: 99.9 us
  starting transfers between devices  59.2 us (59%)
  Pallas kernels  20.4 us (20%)
  waiting for transfers between devices  16.4 us (16%)
  local copies, waits for them, and re-layouts  2.21 us (2%)
  between operations  1.53 us (2%)
    ppermute x8, starting transfers between devices, from_behind(): return lax.ppermute(block, axes, route)  23.5 us
    pallas_call x5, Pallas kernels, call(): pl.pallas_call(kernel, in_specs=[pl.BlockSpec(memory_space=where[m]) for...  20.4 us
    all_to_all x1, starting transfers between devices, gather_sum(): got = lax.all_to_all(copies, axes, 0, 0)  16 us
    all_to_all x1, starting transfers between devices, near_sum(): got = lax.all_to_all(block.reshape(parts, rows, 128), NEAR, 0, 0)  11.3 us
    all_to_all x1, starting transfers between devices, near_gather(): lax.all_to_all(copies, NEAR, 0, 0).reshape(parts * block.shape[0], 128)  8.39 us
    all_to_all x1, waiting for transfers between devices, near_gather(): lax.all_to_all(copies, NEAR, 0, 0).reshape(parts * block.shape[0], 128)  8.11 us
    ppermute x8, waiting for transfers between devices, from_behind(): return lax.ppermute(block, axes, route)  3.89 us
    all_to_all x1, waiting for transfers between devices, near_sum(): got = lax.all_to_all(block.reshape(parts, rows, 128), NEAR, 0, 0)  2.73 us
  transfers between devices with their start and end apart: 11, of which 4 were waited for; matrix products, arithmetic and copies ran while one was open for 0% of the time, Pallas kernels for 9%

profile of v6, /device:TPU:1, one launch (start us, length us, event | category | flops | bytes accessed | tf_op | source)
XLA Modules:
  0.0 99.9 jit_solution(13979287247706366238)
XLA Ops:
  1.3 2.2 %faces_kernel.1 = (bf16[25,64,128]{2,1,0:T(8,128)(2,1)}, bf16[2,64,128]{2,1,0:T(8,128)(2,1)}, bf16[2,64,128]{2,1,0:T(8,128)(2,1)}, bf16[2,64,128]{2,1,0:T(8,128)(2,1)}, bf16[2,64,128]{2,1,0:T(8,128)(2,1)}) custom-call(s32[1,1]{1,0:T(1,128)S(6)} %copy.15.count, s32[1,1,4,4]{3,2,1,0:T(4,128)} %sends.1, bf16[1,4,64,512]{3,2,1,0:T(8,128)(2,1)} %features_far.3, ...), custom_call_target="tpu_custom_call" | custom-call | flops 201326592 | bytes 1048576 | tf_op jit(solution)/shard_map/faces_kernel/pallas_call | solution.py:465
  3.4 4.5 %collective-permute-start = (bf16[2,64,128]{2,1,0:T(8,128)(2,1)}, bf16[2,64,128]{2,1,0:T(8,128)(2,1)S(1)}, u32[]{:S(2)}, u32[]{:S(2)}) collective-permute-start(bf16[2,64,128]{2,1,0:T(8,128)(2,1)} %get-tuple-element.32), channel_id=1, source_target_pairs={{0,4},{4,8},{8,12},{12,16},{16,20},{20,24},{24,28},{28,32},{32,36}... | collective-permute-start | bytes 98312 | tf_op jit(solution)/shard_map/ppermute | solution.py:498
  8.0 5.6 %collective-permute-start.1 = (bf16[2,64,128]{2,1,0:T(8,128)(2,1)}, bf16[2,64,128]{2,1,0:T(8,128)(2,1)S(1)}, u32[]{:S(2)}, u32[]{:S(2)}) collective-permute-start(bf16[2,64,128]{2,1,0:T(8,128)(2,1)} %get-tuple-element.33), channel_id=1, source_target_pairs={{4,0},{8,4},{12,8},{16,12},{20,16},{24,20},{28,24},{32,28},{36,32}... | collective-permute-start | bytes 98312 | tf_op jit(solution)/shard_map/ppermute | solution.py:498
  13.5 1.3 %collective-permute-start.2 = (bf16[2,64,128]{2,1,0:T(8,128)(2,1)}, bf16[2,64,128]{2,1,0:T(8,128)(2,1)S(1)}, u32[]{:S(2)}, u32[]{:S(2)}) collective-permute-start(bf16[2,64,128]{2,1,0:T(8,128)(2,1)} %get-tuple-element.34), channel_id=1, source_target_pairs={{0,8},{4,12},{8,16},{12,20},{16,24},{20,28},{24,32},{28,36},{32,40... | collective-permute-start | bytes 98312 | tf_op jit(solution)/shard_map/ppermute | solution.py:498
  14.8 1.3 %collective-permute-start.3 = (bf16[2,64,128]{2,1,0:T(8,128)(2,1)}, bf16[2,64,128]{2,1,0:T(8,128)(2,1)S(1)}, u32[]{:S(2)}, u32[]{:S(2)}) collective-permute-start(bf16[2,64,128]{2,1,0:T(8,128)(2,1)} %get-tuple-element.35), channel_id=1, source_target_pairs={{8,0},{12,4},{16,8},{20,12},{24,16},{28,20},{32,24},{36,28},{40,32... | collective-permute-start | bytes 98312 | tf_op jit(solution)/shard_map/ppermute | solution.py:498
  16.1 0.0 collective-permute-done.ahead
  16.1 0.0 collective-permute-done.1.behind
  16.2 0.0 collective-permute-done.2.ahead2
  16.2 3.9 %collective-permute-done.3.behind2 = bf16[2,64,128]{2,1,0:T(8,128)(2,1)S(1)} collective-permute-done((bf16[2,64,128]{2,1,0:T(8,128)(2,1)}, bf16[2,64,128]{2,1,0:T(8,128)(2,1)S(1)}, u32[]{:S(2)}, u32[]{:S(2)}) %collective-permute-start.3) | collective-permute-done | bytes 32800 | tf_op jit(solution)/shard_map/ppermute | solution.py:498
  20.0 0.0 copy-start.5
  20.0 0.7 copy-done.5
  20.7 8.2 %main_kernel.1 = (bf16[1,4,64,128]{3,2,1,0:T(8,128)(2,1)}, bf16[4,64,512]{2,1,0:T(8,128)(2,1)}, bf16[1536,128]{1,0:T(8,128)(2,1)}, bf16[192,576]{1,0:T(8,128)(2,1)}) custom-call(s32[1,1]{1,0:T(1,128)S(6)} %copy.15.count, s32[1,4,26]{2,1,0:T(4,128)S(1)} %copy-done.5, bf16[25,64,128]{2,1,0:T(8,128)(2,1)} %get-tuple-element.31.table, ...), custom_call_target="tpu_custom_call" | custom-call | flops 5000000000 | bytes 1048576 | tf_op jit(solution)/shard_map/main_kernel/pallas_call | solution.py:465
  28.9 11.3 %all-to-all-start = ((bf16[32,48,128]{2,1,0:T(8,128)(2,1)}), bf16[32,48,128]{2,1,0:T(8,128)(2,1)S(1)}, u32[]{:S(2)}, u32[]{:S(2)}) async-start(bf16[32,48,128]{2,1,0:T(8,128)(2,1)} %bitcast.3), calls=%async_computation | async-start | bytes 786432 | tf_op jit(solution)/shard_map/all_to_all | solution.py:486
  40.2 0.0 copy-start.2
  40.2 7.2 %fold_kernel.1 = (f32[256,1024]{1,0:T(8,128)}, f32[25,64,128]{2,1,0:T(8,128)}, bf16[2,64,128]{2,1,0:T(8,128)(2,1)}, bf16[2,64,128]{2,1,0:T(8,128)(2,1)}, bf16[2,...) custom-call(s32[1,4,26]{2,1,0:T(4,128)} %sources.1, bf16[4,64,512]{2,1,0:T(8,128)(2,1)} %get-tuple-element.37.grads_far, ...), custom_call_target="tpu_custom_call" | custom-call | flops 3000000000 | bytes 1048576 | tf_op jit(solution)/shard_map/fold_kernel/pallas_call | solution.py:465
  47.5 0.0 copy-start
  47.5 0.0 copy-start.1
  47.5 0.0 copy-start.3
  47.5 0.0 copy-start.4
  47.5 2.7 %all-to-all-done = bf16[32,48,128]{2,1,0:T(8,128)(2,1)S(1)} async-done(((bf16[32,48,128]{2,1,0:T(8,128)(2,1)}), bf16[32,48,128]{2,1,0:T(8,128)(2,1)S(1)}, u32[]{:S(2)}, u32[]{:S(2)}) %all-to-all-start) | async-done | bytes 393248 | tf_op jit(solution)/shard_map/all_to_all | solution.py:486
  50.3 0.1 reduce_sum.21
  50.3 0.7 broadcast_in_dim.4
  51.0 16.0 %all-to-all-start.1 = ((bf16[16,48,128]{2,1,0:T(8,128)(2,1)}), bf16[16,48,128]{2,1,0:T(8,128)(2,1)S(1)}, u32[]{:S(2)}, u32[]{:S(2)}) async-start(bf16[16,48,128]{2,1,0:T(8,128)(2,1)} %broadcast_in_dim.4), calls=%async_computation.1 | async-start | bytes 393216 | tf_op jit(solution)/shard_map/all_to_all | solution.py:479
  67.0 2.9 %collective-permute-start.4 = (bf16[2,64,128]{2,1,0:T(8,128)(2,1)}, bf16[2,64,128]{2,1,0:T(8,128)(2,1)S(1)}, u32[]{:S(2)}, u32[]{:S(2)}) collective-permute-start(bf16[2,64,128]{2,1,0:T(8,128)(2,1)} %get-tuple-element.47), channel_id=1, source_target_pairs={{4,0},{8,4},{12,8},{16,12},{20,16},{24,20},{28,24},{32,28},{36,32}... | collective-permute-start | bytes 98312 | tf_op jit(solution)/shard_map/ppermute | solution.py:498
  69.9 2.7 %collective-permute-start.5 = (bf16[2,64,128]{2,1,0:T(8,128)(2,1)}, bf16[2,64,128]{2,1,0:T(8,128)(2,1)S(1)}, u32[]{:S(2)}, u32[]{:S(2)}) collective-permute-start(bf16[2,64,128]{2,1,0:T(8,128)(2,1)} %get-tuple-element.48), channel_id=1, source_target_pairs={{0,4},{4,8},{8,12},{12,16},{16,20},{20,24},{24,28},{28,32},{32,36}... | collective-permute-start | bytes 98312 | tf_op jit(solution)/shard_map/ppermute | solution.py:498
  72.6 1.3 %collective-permute-start.6 = (bf16[2,64,128]{2,1,0:T(8,128)(2,1)}, bf16[2,64,128]{2,1,0:T(8,128)(2,1)S(1)}, u32[]{:S(2)}, u32[]{:S(2)}) collective-permute-start(bf16[2,64,128]{2,1,0:T(8,128)(2,1)} %get-tuple-element.49), channel_id=1, source_target_pairs={{8,0},{12,4},{16,8},{20,12},{24,16},{28,20},{32,24},{36,28},{40,32... | collective-permute-start | bytes 98312 | tf_op jit(solution)/shard_map/ppermute | solution.py:498
  73.9 4.0 %collective-permute-start.7 = (bf16[2,64,128]{2,1,0:T(8,128)(2,1)}, bf16[2,64,128]{2,1,0:T(8,128)(2,1)S(1)}, u32[]{:S(2)}, u32[]{:S(2)}) collective-permute-start(bf16[2,64,128]{2,1,0:T(8,128)(2,1)} %get-tuple-element.50), channel_id=1, source_target_pairs={{0,8},{4,12},{8,16},{12,20},{16,24},{20,28},{24,32},{28,36},{32,40... | collective-permute-start | bytes 98312 | tf_op jit(solution)/shard_map/ppermute | solution.py:498
  77.9 1.7 %all-to-all-done.1 = bf16[16,48,128]{2,1,0:T(8,128)(2,1)S(1)} async-done(((bf16[16,48,128]{2,1,0:T(8,128)(2,1)}), bf16[16,48,128]{2,1,0:T(8,128)(2,1)S(1)}, u32[]{:S(2)}, u32[]{:S(2)}) %all-to-all-start.1) | async-done | bytes 196640 | tf_op jit(solution)/shard_map/all_to_all | solution.py:479
  79.6 0.0 collective-permute-done.4.ahead
  79.6 0.0 collective-permute-done.5.behind
  79.6 0.0 collective-permute-done.6.ahead2
  79.6 0.0 collective-permute-done.7.behind2
  79.7 0.8 broadcast_in_dim.5
  80.5 8.4 %all-to-all-start.2 = ((bf16[32,48,128]{2,1,0:T(8,128)(2,1)}), bf16[32,48,128]{2,1,0:T(8,128)(2,1)S(1)}, u32[]{:S(2)}, u32[]{:S(2)}) async-start(bf16[32,48,128]{2,1,0:T(8,128)(2,1)} %broadcast_in_dim.5), calls=%async_computation.2 | async-start | bytes 786432 | tf_op jit(solution)/shard_map/all_to_all | solution.py:493
  88.9 0.0 copy-done.2
  88.9 0.0 copy-done
  88.9 0.0 copy-done.1
  88.9 0.0 copy-done.3
  88.9 0.0 copy-done.4
  88.9 2.0 %finish_kernel.1 = bf16[1,4,64,512]{3,2,1,0:T(8,128)(2,1)} custom-call(s32[1,1]{1,0:T(1,128)S(6)} %copy.15.count, s32[1,1,4,4]{3,2,1,0:T(4,128)S(1)} %copy-done.4, f32[256,1024]{1,0:T(8,128)S(1)} %copy-done, f32[25,64,128]{2,1,0:T(8,128)S(1)} %copy-done.1, bf16[2,64,128]{2,1,0:T(8,128)(2,1)S(1)} %collective-permute-done.4.ahead, ...), custom_call_target="tpu_custom_call" | custom-call | flops 201326592 | bytes 1048576 | tf_op jit(solution)/shard_map/finish_kernel/pallas_call | solution.py:465
  90.9 8.1 %all-to-all-done.2 = bf16[32,48,128]{2,1,0:T(8,128)(2,1)S(1)} async-done(((bf16[32,48,128]{2,1,0:T(8,128)(2,1)}), bf16[32,48,128]{2,1,0:T(8,128)(2,1)S(1)}, u32[]{:S(2)}, u32[]{:S(2)}) %all-to-all-start.2) | async-done | bytes 393248 | tf_op jit(solution)/shard_map/all_to_all | solution.py:493
  99.0 0.9 unpack_kernel.1
  (1 shorter events, 0.0 us)
Async XLA Ops:
  3.4 12.7 %collective-permute-start = (bf16[2,64,128]{2,1,0:T(8,128)(2,1)}, bf16[2,64,128]{2,1,0:T(8,128)(2,1)S(1)}, u32[]{:S(2)}, u32[]{:S(2)}) collective-permute-start(bf16[2,64,128]{2,1,0:T(8,128)(2,1)} %get-tuple-element.32), channel_id=1, source_target_pairs={{0,4},{4,8},{8,12},{12,16},{16,20},{20,24},{24,28},{28,32},{32,36}... | collective-permute-start | bytes 98312 | tf_op jit(solution)/shard_map/ppermute | solution.py:498
  8.0 8.2 %collective-permute-start.1 = (bf16[2,64,128]{2,1,0:T(8,128)(2,1)}, bf16[2,64,128]{2,1,0:T(8,128)(2,1)S(1)}, u32[]{:S(2)}, u32[]{:S(2)}) collective-permute-start(bf16[2,64,128]{2,1,0:T(8,128)(2,1)} %get-tuple-element.33), channel_id=1, source_target_pairs={{4,0},{8,4},{12,8},{16,12},{20,16},{24,20},{28,24},{32,28},{36,32}... | collective-permute-start | bytes 98312 | tf_op jit(solution)/shard_map/ppermute | solution.py:498
  13.5 2.6 %collective-permute-start.2 = (bf16[2,64,128]{2,1,0:T(8,128)(2,1)}, bf16[2,64,128]{2,1,0:T(8,128)(2,1)S(1)}, u32[]{:S(2)}, u32[]{:S(2)}) collective-permute-start(bf16[2,64,128]{2,1,0:T(8,128)(2,1)} %get-tuple-element.34), channel_id=1, source_target_pairs={{0,8},{4,12},{8,16},{12,20},{16,24},{20,28},{24,32},{28,36},{32,40... | collective-permute-start | bytes 98312 | tf_op jit(solution)/shard_map/ppermute | solution.py:498
  14.8 5.2 %collective-permute-start.3 = (bf16[2,64,128]{2,1,0:T(8,128)(2,1)}, bf16[2,64,128]{2,1,0:T(8,128)(2,1)S(1)}, u32[]{:S(2)}, u32[]{:S(2)}) collective-permute-start(bf16[2,64,128]{2,1,0:T(8,128)(2,1)} %get-tuple-element.35), channel_id=1, source_target_pairs={{8,0},{12,4},{16,8},{20,12},{24,16},{28,20},{32,24},{36,28},{40,32... | collective-permute-start | bytes 98312 | tf_op jit(solution)/shard_map/ppermute | solution.py:498
  20.0 0.7 copy-start.5
  28.9 21.4 %all-to-all-start = ((bf16[32,48,128]{2,1,0:T(8,128)(2,1)}), bf16[32,48,128]{2,1,0:T(8,128)(2,1)S(1)}, u32[]{:S(2)}, u32[]{:S(2)}) async-start(bf16[32,48,128]{2,1,0:T(8,128)(2,1)} %bitcast.3), calls=%async_computation | async-start | bytes 786432 | tf_op jit(solution)/shard_map/all_to_all | solution.py:486
  40.2 48.6 %copy-start.2 = (bf16[512,768]{1,0:T(8,128)(2,1)S(1)}, bf16[512,768]{1,0:T(8,128)(2,1)}, u32[]{:S(2)}) copy-start(bf16[512,768]{1,0:T(8,128)(2,1)} %constant.14.clone.face_hot) | copy-start | bytes 2359300
  47.5 41.4 %copy-start = (f32[256,1024]{1,0:T(8,128)S(1)}, f32[256,1024]{1,0:T(8,128)}, u32[]{:S(2)}) copy-start(f32[256,1024]{1,0:T(8,128)} %get-tuple-element.39.folded) | copy-start | bytes 3145732
  47.5 41.4 %copy-start.1 = (f32[25,64,128]{2,1,0:T(8,128)S(1)}, f32[25,64,128]{2,1,0:T(8,128)}, u32[]{:S(2)}) copy-start(f32[25,64,128]{2,1,0:T(8,128)} %get-tuple-element.40.grad_local) | copy-start | bytes 2457604
  47.5 41.4 %copy-start.3 = (bf16[128,256]{1,0:T(8,128)(2,1)S(1)}, bf16[128,256]{1,0:T(8,128)(2,1)}, u32[]{:S(2)}) copy-start(bf16[128,256]{1,0:T(8,128)(2,1)} %constant.15.clone.inner_hot) | copy-start | bytes 196612
  47.5 41.4 %copy-start.4 = (s32[1,1,4,4]{3,2,1,0:T(4,128)S(1)}, s32[1,1,4,4]{3,2,1,0:T(4,128)}, u32[]{:S(2)}) copy-start(s32[1,1,4,4]{3,2,1,0:T(4,128)} %sends.1) | copy-start | bytes 196
  51.0 28.5 %all-to-all-start.1 = ((bf16[16,48,128]{2,1,0:T(8,128)(2,1)}), bf16[16,48,128]{2,1,0:T(8,128)(2,1)S(1)}, u32[]{:S(2)}, u32[]{:S(2)}) async-start(bf16[16,48,128]{2,1,0:T(8,128)(2,1)} %broadcast_in_dim.4), calls=%async_computation.1 | async-start | bytes 393216 | tf_op jit(solution)/shard_map/all_to_all | solution.py:479
  67.0 12.6 %collective-permute-start.4 = (bf16[2,64,128]{2,1,0:T(8,128)(2,1)}, bf16[2,64,128]{2,1,0:T(8,128)(2,1)S(1)}, u32[]{:S(2)}, u32[]{:S(2)}) collective-permute-start(bf16[2,64,128]{2,1,0:T(8,128)(2,1)} %get-tuple-element.47), channel_id=1, source_target_pairs={{4,0},{8,4},{12,8},{16,12},{20,16},{24,20},{28,24},{32,28},{36,32}... | collective-permute-start | bytes 98312 | tf_op jit(solution)/shard_map/ppermute | solution.py:498
  69.9 9.7 %collective-permute-start.5 = (bf16[2,64,128]{2,1,0:T(8,128)(2,1)}, bf16[2,64,128]{2,1,0:T(8,128)(2,1)S(1)}, u32[]{:S(2)}, u32[]{:S(2)}) collective-permute-start(bf16[2,64,128]{2,1,0:T(8,128)(2,1)} %get-tuple-element.48), channel_id=1, source_target_pairs={{0,4},{4,8},{8,12},{12,16},{16,20},{20,24},{24,28},{28,32},{32,36}... | collective-permute-start | bytes 98312 | tf_op jit(solution)/shard_map/ppermute | solution.py:498
  72.6 7.0 %collective-permute-start.6 = (bf16[2,64,128]{2,1,0:T(8,128)(2,1)}, bf16[2,64,128]{2,1,0:T(8,128)(2,1)S(1)}, u32[]{:S(2)}, u32[]{:S(2)}) collective-permute-start(bf16[2,64,128]{2,1,0:T(8,128)(2,1)} %get-tuple-element.49), channel_id=1, source_target_pairs={{8,0},{12,4},{16,8},{20,12},{24,16},{28,20},{32,24},{36,28},{40,32... | collective-permute-start | bytes 98312 | tf_op jit(solution)/shard_map/ppermute | solution.py:498
  73.9 5.7 %collective-permute-start.7 = (bf16[2,64,128]{2,1,0:T(8,128)(2,1)}, bf16[2,64,128]{2,1,0:T(8,128)(2,1)S(1)}, u32[]{:S(2)}, u32[]{:S(2)}) collective-permute-start(bf16[2,64,128]{2,1,0:T(8,128)(2,1)} %get-tuple-element.50), channel_id=1, source_target_pairs={{0,8},{4,12},{8,16},{12,20},{16,24},{20,28},{24,32},{28,36},{32,40... | collective-permute-start | bytes 98312 | tf_op jit(solution)/shard_map/ppermute | solution.py:498
  80.5 18.5 %all-to-all-start.2 = ((bf16[32,48,128]{2,1,0:T(8,128)(2,1)}), bf16[32,48,128]{2,1,0:T(8,128)(2,1)S(1)}, u32[]{:S(2)}, u32[]{:S(2)}) async-start(bf16[32,48,128]{2,1,0:T(8,128)(2,1)} %broadcast_in_dim.5), calls=%async_computation.2 | async-start | bytes 786432 | tf_op jit(solution)/shard_map/all_to_all | solution.py:493

commit v7 on v6

--- a/solution.py
+++ b/solution.py
@@ -19,7 +19,7 @@
 TABLE = LOCAL + NOFF * CAP
 PLACES = list(range(9)) + [None] + list(range(9, 26)) + [None]
 OFFSETS = (1, -1, 2, -2)
-NEAR = ("x", "c", "grp")
+NEAR = ("zl", "x", "c", "grp")
 
 
 def rim_cells(d, full):
@@ -481,14 +481,14 @@
 
 
 def near_sum(block, sizes):
-    parts = sizes["x"] * sizes["c"] * sizes["grp"]
+    parts = sizes["zl"] * sizes["x"] * sizes["c"] * sizes["grp"]
     rows = block.shape[0] // parts
     got = lax.all_to_all(block.reshape(parts, rows, 128), NEAR, 0, 0)
     return got.astype(F32).sum(0).astype(BF)
 
 
 def near_gather(block, sizes):
-    parts = sizes["x"] * sizes["c"] * sizes["grp"]
+    parts = sizes["zl"] * sizes["x"] * sizes["c"] * sizes["grp"]
     copies = jnp.broadcast_to(block[None], (parts,) + block.shape)
     return lax.all_to_all(copies, NEAR, 0, 0).reshape(parts * block.shape[0], 128)
 
@@ -500,8 +500,8 @@
 
 def on_device(sizes, features, brick_count, send_list, halo_src, kernel, down_kernel, out_grad):
     face_packed, face_hot, inner_hot, placing = one_hot_tables()
-    tile = ("z", "x", "c")
-    devices = sizes["z"] * sizes["x"] * sizes["c"]
+    tile = ("zh", "zl", "x", "c")
+    devices = sizes["zh"] * sizes["zl"] * sizes["x"] * sizes["c"]
     swap = [((CAP // 2, C, 128), BF)] * NOFF
 
     table, *outgoing = call(
@@ -587,7 +587,7 @@
         placing,
     )
     part, *remote = lax.optimization_barrier((part, *remote))
-    part = gather_sum(part, ("z",), sizes["z"])
+    part = gather_sum(part, ("zh",), sizes["zh"])
     returned = [from_behind(b, tile, devices, -o) for b, o in zip(remote, OFFSETS)]
     part, *returned = lax.optimization_barrier((part, *returned))
     sums = near_gather(part.astype(BF), sizes)
@@ -614,9 +614,11 @@
 
 def solution(mesh):
     tile, grp = mesh.shape["tile"], mesh.shape["grp"]
-    sizes = {"z": tile // 8, "x": 4, "c": 2, "grp": grp}
+    planes = tile // 8
+    pair = 2 - planes % 2
+    sizes = {"zh": planes // pair, "zl": pair, "x": 4, "c": 2, "grp": grp}
     fine = Mesh(mesh.devices.reshape(tuple(sizes.values())), tuple(sizes))
-    line = ("z", "x", "c")
+    line = ("zh", "zl", "x", "c")
     in_specs = (
         P("grp", line, None, None),
         P("grp", line),

time: 101 us -> 104 us (1.030)
  local copies, waits for them, and re-layouts: 2.21 us -> 3.27 us
    all_to_all x1, starting transfers between devices: 11.3 us -> 13.1 us  [near_sum(): got = lax.all_to_all(block.reshape(parts, rows, 128), NEAR, 0, 0)]
    all_to_all x1, starting transfers between devices: 16 us -> 14.5 us  [gather_sum(): got = lax.all_to_all(copies, axes, 0, 0)]
    unnamed x12, local copies, waits for them, and re-layouts: 0.71 us -> 1.84 us
    all_to_all x1, waiting for transfers between devices: 2.73 us -> 3.85 us  [near_sum(): got = lax.all_to_all(block.reshape(parts, rows, 128), NEAR, 0, 0)]
where the time goes in v7:
time: 104 us; the launch traced here: 103 us
  starting transfers between devices  60.1 us (58%)
  Pallas kernels  20.5 us (20%)
  waiting for transfers between devices  17.1 us (16%)
  local copies, waits for them, and re-layouts  3.27 us (3%)
  between operations  1.51 us (1%)
    ppermute x8, starting transfers between devices, from_behind(): return lax.ppermute(block, axes, route)  23.5 us
    pallas_call x5, Pallas kernels, call(): pl.pallas_call(kernel, in_specs=[pl.BlockSpec(memory_space=where[m]) for...  20.5 us
    all_to_all x1, starting transfers between devices, gather_sum(): got = lax.all_to_all(copies, axes, 0, 0)  14.5 us
    all_to_all x1, starting transfers between devices, near_sum(): got = lax.all_to_all(block.reshape(parts, rows, 128), NEAR, 0, 0)  13.1 us
    all_to_all x1, starting transfers between devices, near_gather(): lax.all_to_all(copies, NEAR, 0, 0).reshape(parts * block.shape[0], 128)  9.05 us
    all_to_all x1, waiting for transfers between devices, near_gather(): lax.all_to_all(copies, NEAR, 0, 0).reshape(parts * block.shape[0], 128)  8.02 us
    ppermute x8, waiting for transfers between devices, from_behind(): return lax.ppermute(block, axes, route)  3.89 us
    all_to_all x1, waiting for transfers between devices, near_sum(): got = lax.all_to_all(block.reshape(parts, rows, 128), NEAR, 0, 0)  3.85 us
  transfers between devices with their start and end apart: 11, of which 4 were waited for; matrix products, arithmetic and copies ran while one was open for 0% of the time, Pallas kernels for 9%

profile of v7, /device:TPU:1, one launch (start us, length us, event | category | flops | bytes accessed | tf_op | source)
XLA Modules:
  0.0 102.6 jit_solution(4914281449756235432)
XLA Ops:
  1.3 2.2 %faces_kernel.1 = (bf16[25,64,128]{2,1,0:T(8,128)(2,1)}, bf16[2,64,128]{2,1,0:T(8,128)(2,1)}, bf16[2,64,128]{2,1,0:T(8,128)(2,1)}, bf16[2,64,128]{2,1,0:T(8,128)(2,1)}, bf16[2,64,128]{2,1,0:T(8,128)(2,1)}) custom-call(s32[1,1]{1,0:T(1,128)S(6)} %copy.15.count, s32[1,1,4,4]{3,2,1,0:T(4,128)} %sends.1, bf16[1,4,64,512]{3,2,1,0:T(8,128)(2,1)} %features_far.3, ...), custom_call_target="tpu_custom_call" | custom-call | flops 201326592 | bytes 1048576 | tf_op jit(solution)/shard_map/faces_kernel/pallas_call | solution.py:465
  3.4 4.5 %collective-permute-start = (bf16[2,64,128]{2,1,0:T(8,128)(2,1)}, bf16[2,64,128]{2,1,0:T(8,128)(2,1)S(1)}, u32[]{:S(2)}, u32[]{:S(2)}) collective-permute-start(bf16[2,64,128]{2,1,0:T(8,128)(2,1)} %get-tuple-element.32), channel_id=1, source_target_pairs={{0,4},{4,8},{8,12},{12,16},{16,20},{20,24},{24,28},{28,32},{32,36}... | collective-permute-start | bytes 98312 | tf_op jit(solution)/shard_map/ppermute | solution.py:498
  8.0 5.6 %collective-permute-start.1 = (bf16[2,64,128]{2,1,0:T(8,128)(2,1)}, bf16[2,64,128]{2,1,0:T(8,128)(2,1)S(1)}, u32[]{:S(2)}, u32[]{:S(2)}) collective-permute-start(bf16[2,64,128]{2,1,0:T(8,128)(2,1)} %get-tuple-element.33), channel_id=1, source_target_pairs={{4,0},{8,4},{12,8},{16,12},{20,16},{24,20},{28,24},{32,28},{36,32}... | collective-permute-start | bytes 98312 | tf_op jit(solution)/shard_map/ppermute | solution.py:498
  13.5 1.3 %collective-permute-start.2 = (bf16[2,64,128]{2,1,0:T(8,128)(2,1)}, bf16[2,64,128]{2,1,0:T(8,128)(2,1)S(1)}, u32[]{:S(2)}, u32[]{:S(2)}) collective-permute-start(bf16[2,64,128]{2,1,0:T(8,128)(2,1)} %get-tuple-element.34), channel_id=1, source_target_pairs={{0,8},{4,12},{8,16},{12,20},{16,24},{20,28},{24,32},{28,36},{32,40... | collective-permute-start | bytes 98312 | tf_op jit(solution)/shard_map/ppermute | solution.py:498
  14.8 1.3 %collective-permute-start.3 = (bf16[2,64,128]{2,1,0:T(8,128)(2,1)}, bf16[2,64,128]{2,1,0:T(8,128)(2,1)S(1)}, u32[]{:S(2)}, u32[]{:S(2)}) collective-permute-start(bf16[2,64,128]{2,1,0:T(8,128)(2,1)} %get-tuple-element.35), channel_id=1, source_target_pairs={{8,0},{12,4},{16,8},{20,12},{24,16},{28,20},{32,24},{36,28},{40,32... | collective-permute-start | bytes 98312 | tf_op jit(solution)/shard_map/ppermute | solution.py:498
  16.1 0.0 collective-permute-done.ahead
  16.1 0.0 collective-permute-done.1.behind
  16.2 0.0 collective-permute-done.2.ahead2
  16.2 3.9 %collective-permute-done.3.behind2 = bf16[2,64,128]{2,1,0:T(8,128)(2,1)S(1)} collective-permute-done((bf16[2,64,128]{2,1,0:T(8,128)(2,1)}, bf16[2,64,128]{2,1,0:T(8,128)(2,1)S(1)}, u32[]{:S(2)}, u32[]{:S(2)}) %collective-permute-start.3) | collective-permute-done | bytes 32800 | tf_op jit(solution)/shard_map/ppermute | solution.py:498
  20.0 0.0 copy-start.5
  20.0 0.7 copy-done.5
  20.7 8.2 %main_kernel.1 = (bf16[1,4,64,128]{3,2,1,0:T(8,128)(2,1)}, bf16[4,64,512]{2,1,0:T(8,128)(2,1)}, bf16[1536,128]{1,0:T(8,128)(2,1)}, bf16[192,576]{1,0:T(8,128)(2,1)}) custom-call(s32[1,1]{1,0:T(1,128)S(6)} %copy.15.count, s32[1,4,26]{2,1,0:T(4,128)S(1)} %copy-done.5, bf16[25,64,128]{2,1,0:T(8,128)(2,1)} %get-tuple-element.31.table, ...), custom_call_target="tpu_custom_call" | custom-call | flops 5000000000 | bytes 1048576 | tf_op jit(solution)/shard_map/main_kernel/pallas_call | solution.py:465
  28.9 13.1 %all-to-all-start = ((bf16[64,24,128]{2,1,0:T(8,128)(2,1)}), bf16[64,24,128]{2,1,0:T(8,128)(2,1)S(1)}, u32[]{:S(2)}, u32[]{:S(2)}) async-start(bf16[64,24,128]{2,1,0:T(8,128)(2,1)} %bitcast.3), calls=%async_computation | async-start | bytes 786432 | tf_op jit(solution)/shard_map/all_to_all | solution.py:486
  42.0 0.0 copy-start.2
  42.0 7.3 %fold_kernel.1 = (f32[256,1024]{1,0:T(8,128)}, f32[25,64,128]{2,1,0:T(8,128)}, bf16[2,64,128]{2,1,0:T(8,128)(2,1)}, bf16[2,64,128]{2,1,0:T(8,128)(2,1)}, bf16[2,...) custom-call(s32[1,4,26]{2,1,0:T(4,128)} %sources.1, bf16[4,64,512]{2,1,0:T(8,128)(2,1)} %get-tuple-element.37.grads_far, ...), custom_call_target="tpu_custom_call" | custom-call | flops 3000000000 | bytes 1048576 | tf_op jit(solution)/shard_map/fold_kernel/pallas_call | solution.py:465
  49.3 0.0 copy-start
  49.3 0.0 copy-start.3
  49.3 0.0 copy-start.4
  49.3 3.9 %all-to-all-done = bf16[64,24,128]{2,1,0:T(8,128)(2,1)S(1)} async-done(((bf16[64,24,128]{2,1,0:T(8,128)(2,1)}), bf16[64,24,128]{2,1,0:T(8,128)(2,1)S(1)}, u32[]{:S(2)}, u32[]{:S(2)}) %all-to-all-start) | async-done | bytes 393248 | tf_op jit(solution)/shard_map/all_to_all | solution.py:486
  53.1 0.1 reduce_sum.21
  53.2 0.6 broadcast_in_dim.4
  53.9 14.5 %all-to-all-start.1 = ((bf16[8,24,128]{2,1,0:T(8,128)(2,1)}), bf16[8,24,128]{2,1,0:T(8,128)(2,1)S(1)}, u32[]{:S(2)}, u32[]{:S(2)}) async-start(bf16[8,24,128]{2,1,0:T(8,128)(2,1)} %broadcast_in_dim.4), calls=%async_computation.1 | async-start | bytes 98304 | tf_op jit(solution)/shard_map/all_to_all | solution.py:479
  68.4 2.8 %collective-permute-start.4 = (bf16[2,64,128]{2,1,0:T(8,128)(2,1)}, bf16[2,64,128]{2,1,0:T(8,128)(2,1)S(1)}, u32[]{:S(2)}, u32[]{:S(2)}) collective-permute-start(bf16[2,64,128]{2,1,0:T(8,128)(2,1)} %get-tuple-element.47), channel_id=1, source_target_pairs={{4,0},{8,4},{12,8},{16,12},{20,16},{24,20},{28,24},{32,28},{36,32}... | collective-permute-start | bytes 98312 | tf_op jit(solution)/shard_map/ppermute | solution.py:498
  71.2 2.8 %collective-permute-start.5 = (bf16[2,64,128]{2,1,0:T(8,128)(2,1)}, bf16[2,64,128]{2,1,0:T(8,128)(2,1)S(1)}, u32[]{:S(2)}, u32[]{:S(2)}) collective-permute-start(bf16[2,64,128]{2,1,0:T(8,128)(2,1)} %get-tuple-element.48), channel_id=1, source_target_pairs={{0,4},{4,8},{8,12},{12,16},{16,20},{20,24},{24,28},{28,32},{32,36}... | collective-permute-start | bytes 98312 | tf_op jit(solution)/shard_map/ppermute | solution.py:498
  74.0 1.3 %collective-permute-start.6 = (bf16[2,64,128]{2,1,0:T(8,128)(2,1)}, bf16[2,64,128]{2,1,0:T(8,128)(2,1)S(1)}, u32[]{:S(2)}, u32[]{:S(2)}) collective-permute-start(bf16[2,64,128]{2,1,0:T(8,128)(2,1)} %get-tuple-element.49), channel_id=1, source_target_pairs={{8,0},{12,4},{16,8},{20,12},{24,16},{28,20},{32,24},{36,28},{40,32... | collective-permute-start | bytes 98312 | tf_op jit(solution)/shard_map/ppermute | solution.py:498
  75.3 4.0 %collective-permute-start.7 = (bf16[2,64,128]{2,1,0:T(8,128)(2,1)}, bf16[2,64,128]{2,1,0:T(8,128)(2,1)S(1)}, u32[]{:S(2)}, u32[]{:S(2)}) collective-permute-start(bf16[2,64,128]{2,1,0:T(8,128)(2,1)} %get-tuple-element.50), channel_id=1, source_target_pairs={{0,8},{4,12},{8,16},{12,20},{16,24},{20,28},{24,32},{28,36},{32,40... | collective-permute-start | bytes 98312 | tf_op jit(solution)/shard_map/ppermute | solution.py:498
  79.3 1.3 %all-to-all-done.1 = bf16[8,24,128]{2,1,0:T(8,128)(2,1)S(1)} async-done(((bf16[8,24,128]{2,1,0:T(8,128)(2,1)}), bf16[8,24,128]{2,1,0:T(8,128)(2,1)S(1)}, u32[]{:S(2)}, u32[]{:S(2)}) %all-to-all-start.1) | async-done | bytes 49184 | tf_op jit(solution)/shard_map/all_to_all | solution.py:479
  80.6 0.0 collective-permute-done.4.ahead
  80.6 0.0 collective-permute-done.5.behind
  80.6 0.0 collective-permute-done.6.ahead2
  80.6 0.0 collective-permute-done.7.behind2
  80.6 0.8 broadcast_in_dim.5
  81.4 9.0 %all-to-all-start.2 = ((bf16[64,24,128]{2,1,0:T(8,128)(2,1)}), bf16[64,24,128]{2,1,0:T(8,128)(2,1)S(1)}, u32[]{:S(2)}, u32[]{:S(2)}) async-start(bf16[64,24,128]{2,1,0:T(8,128)(2,1)} %broadcast_in_dim.5), calls=%async_computation.2 | async-start | bytes 786432 | tf_op jit(solution)/shard_map/all_to_all | solution.py:493
  90.5 0.0 copy-done.2
  90.5 0.0 copy-done
  90.5 0.0 copy-done.3
  90.5 0.0 copy-done.4
  90.5 0.0 copy-start.1
  90.5 1.1 %copy-done.1 = f32[25,64,128]{2,1,0:T(8,128)S(1)} copy-done((f32[25,64,128]{2,1,0:T(8,128)S(1)}, f32[25,64,128]{2,1,0:T(8,128)}, u32[]{:S(2)}) %copy-start.1) | copy-done | bytes 819224
  91.7 2.0 %finish_kernel.1 = bf16[1,4,64,512]{3,2,1,0:T(8,128)(2,1)} custom-call(s32[1,1]{1,0:T(1,128)S(6)} %copy.15.count, s32[1,1,4,4]{3,2,1,0:T(4,128)S(1)} %copy-done.4, f32[256,1024]{1,0:T(8,128)S(1)} %copy-done, f32[25,64,128]{2,1,0:T(8,128)S(1)} %copy-done.1, bf16[2,64,128]{2,1,0:T(8,128)(2,1)S(1)} %collective-permute-done.4.ahead, ...), custom_call_target="tpu_custom_call" | custom-call | flops 201326592 | bytes 1048576 | tf_op jit(solution)/shard_map/finish_kernel/pallas_call | solution.py:465
  93.6 8.0 %all-to-all-done.2 = bf16[64,24,128]{2,1,0:T(8,128)(2,1)S(1)} async-done(((bf16[64,24,128]{2,1,0:T(8,128)(2,1)}), bf16[64,24,128]{2,1,0:T(8,128)(2,1)S(1)}, u32[]{:S(2)}, u32[]{:S(2)}) %all-to-all-start.2) | async-done | bytes 393248 | tf_op jit(solution)/shard_map/all_to_all | solution.py:493
  101.6 0.9 unpack_kernel.1
  (1 shorter events, 0.0 us)
Async XLA Ops:
  3.4 12.7 %collective-permute-start = (bf16[2,64,128]{2,1,0:T(8,128)(2,1)}, bf16[2,64,128]{2,1,0:T(8,128)(2,1)S(1)}, u32[]{:S(2)}, u32[]{:S(2)}) collective-permute-start(bf16[2,64,128]{2,1,0:T(8,128)(2,1)} %get-tuple-element.32), channel_id=1, source_target_pairs={{0,4},{4,8},{8,12},{12,16},{16,20},{20,24},{24,28},{28,32},{32,36}... | collective-permute-start | bytes 98312 | tf_op jit(solution)/shard_map/ppermute | solution.py:498
  8.0 8.2 %collective-permute-start.1 = (bf16[2,64,128]{2,1,0:T(8,128)(2,1)}, bf16[2,64,128]{2,1,0:T(8,128)(2,1)S(1)}, u32[]{:S(2)}, u32[]{:S(2)}) collective-permute-start(bf16[2,64,128]{2,1,0:T(8,128)(2,1)} %get-tuple-element.33), channel_id=1, source_target_pairs={{4,0},{8,4},{12,8},{16,12},{20,16},{24,20},{28,24},{32,28},{36,32}... | collective-permute-start | bytes 98312 | tf_op jit(solution)/shard_map/ppermute | solution.py:498
  13.5 2.6 %collective-permute-start.2 = (bf16[2,64,128]{2,1,0:T(8,128)(2,1)}, bf16[2,64,128]{2,1,0:T(8,128)(2,1)S(1)}, u32[]{:S(2)}, u32[]{:S(2)}) collective-permute-start(bf16[2,64,128]{2,1,0:T(8,128)(2,1)} %get-tuple-element.34), channel_id=1, source_target_pairs={{0,8},{4,12},{8,16},{12,20},{16,24},{20,28},{24,32},{28,36},{32,40... | collective-permute-start | bytes 98312 | tf_op jit(solution)/shard_map/ppermute | solution.py:498
  14.8 5.2 %collective-permute-start.3 = (bf16[2,64,128]{2,1,0:T(8,128)(2,1)}, bf16[2,64,128]{2,1,0:T(8,128)(2,1)S(1)}, u32[]{:S(2)}, u32[]{:S(2)}) collective-permute-start(bf16[2,64,128]{2,1,0:T(8,128)(2,1)} %get-tuple-element.35), channel_id=1, source_target_pairs={{8,0},{12,4},{16,8},{20,12},{24,16},{28,20},{32,24},{36,28},{40,32... | collective-permute-start | bytes 98312 | tf_op jit(solution)/shard_map/ppermute | solution.py:498
  20.0 0.7 copy-start.5
  28.9 24.2 %all-to-all-start = ((bf16[64,24,128]{2,1,0:T(8,128)(2,1)}), bf16[64,24,128]{2,1,0:T(8,128)(2,1)S(1)}, u32[]{:S(2)}, u32[]{:S(2)}) async-start(bf16[64,24,128]{2,1,0:T(8,128)(2,1)} %bitcast.3), calls=%async_computation | async-start | bytes 786432 | tf_op jit(solution)/shard_map/all_to_all | solution.py:486
  42.0 48.5 %copy-start.2 = (bf16[512,768]{1,0:T(8,128)(2,1)S(1)}, bf16[512,768]{1,0:T(8,128)(2,1)}, u32[]{:S(2)}) copy-start(bf16[512,768]{1,0:T(8,128)(2,1)} %constant.14.clone.face_hot) | copy-start | bytes 2359300
  49.3 41.2 %copy-start = (f32[256,1024]{1,0:T(8,128)S(1)}, f32[256,1024]{1,0:T(8,128)}, u32[]{:S(2)}) copy-start(f32[256,1024]{1,0:T(8,128)} %get-tuple-element.39.folded) | copy-start | bytes 3145732
  49.3 41.2 %copy-start.3 = (bf16[128,256]{1,0:T(8,128)(2,1)S(1)}, bf16[128,256]{1,0:T(8,128)(2,1)}, u32[]{:S(2)}) copy-start(bf16[128,256]{1,0:T(8,128)(2,1)} %constant.15.clone.inner_hot) | copy-start | bytes 196612
  49.3 41.2 %copy-start.4 = (s32[1,1,4,4]{3,2,1,0:T(4,128)S(1)}, s32[1,1,4,4]{3,2,1,0:T(4,128)}, u32[]{:S(2)}) copy-start(s32[1,1,4,4]{3,2,1,0:T(4,128)} %sends.1) | copy-start | bytes 196
  53.9 26.7 %all-to-all-start.1 = ((bf16[8,24,128]{2,1,0:T(8,128)(2,1)}), bf16[8,24,128]{2,1,0:T(8,128)(2,1)S(1)}, u32[]{:S(2)}, u32[]{:S(2)}) async-start(bf16[8,24,128]{2,1,0:T(8,128)(2,1)} %broadcast_in_dim.4), calls=%async_computation.1 | async-start | bytes 98304 | tf_op jit(solution)/shard_map/all_to_all | solution.py:479
  68.4 12.2 %collective-permute-start.4 = (bf16[2,64,128]{2,1,0:T(8,128)(2,1)}, bf16[2,64,128]{2,1,0:T(8,128)(2,1)S(1)}, u32[]{:S(2)}, u32[]{:S(2)}) collective-permute-start(bf16[2,64,128]{2,1,0:T(8,128)(2,1)} %get-tuple-element.47), channel_id=1, source_target_pairs={{4,0},{8,4},{12,8},{16,12},{20,16},{24,20},{28,24},{32,28},{36,32}... | collective-permute-start | bytes 98312 | tf_op jit(solution)/shard_map/ppermute | solution.py:498
  71.2 9.4 %collective-permute-start.5 = (bf16[2,64,128]{2,1,0:T(8,128)(2,1)}, bf16[2,64,128]{2,1,0:T(8,128)(2,1)S(1)}, u32[]{:S(2)}, u32[]{:S(2)}) collective-permute-start(bf16[2,64,128]{2,1,0:T(8,128)(2,1)} %get-tuple-element.48), channel_id=1, source_target_pairs={{0,4},{4,8},{8,12},{12,16},{16,20},{20,24},{24,28},{28,32},{32,36}... | collective-permute-start | bytes 98312 | tf_op jit(solution)/shard_map/ppermute | solution.py:498
  74.0 6.6 %collective-permute-start.6 = (bf16[2,64,128]{2,1,0:T(8,128)(2,1)}, bf16[2,64,128]{2,1,0:T(8,128)(2,1)S(1)}, u32[]{:S(2)}, u32[]{:S(2)}) collective-permute-start(bf16[2,64,128]{2,1,0:T(8,128)(2,1)} %get-tuple-element.49), channel_id=1, source_target_pairs={{8,0},{12,4},{16,8},{20,12},{24,16},{28,20},{32,24},{36,28},{40,32... | collective-permute-start | bytes 98312 | tf_op jit(solution)/shard_map/ppermute | solution.py:498
  75.3 5.4 %collective-permute-start.7 = (bf16[2,64,128]{2,1,0:T(8,128)(2,1)}, bf16[2,64,128]{2,1,0:T(8,128)(2,1)S(1)}, u32[]{:S(2)}, u32[]{:S(2)}) collective-permute-start(bf16[2,64,128]{2,1,0:T(8,128)(2,1)} %get-tuple-element.50), channel_id=1, source_target_pairs={{0,8},{4,12},{8,16},{12,20},{16,24},{20,28},{24,32},{28,36},{32,40... | collective-permute-start | bytes 98312 | tf_op jit(solution)/shard_map/ppermute | solution.py:498
  81.4 20.2 %all-to-all-start.2 = ((bf16[64,24,128]{2,1,0:T(8,128)(2,1)}), bf16[64,24,128]{2,1,0:T(8,128)(2,1)S(1)}, u32[]{:S(2)}, u32[]{:S(2)}) async-start(bf16[64,24,128]{2,1,0:T(8,128)(2,1)} %broadcast_in_dim.5), calls=%async_computation.2 | async-start | bytes 786432 | tf_op jit(solution)/shard_map/all_to_all | solution.py:493
  90.5 1.1 %copy-start.1 = (f32[25,64,128]{2,1,0:T(8,128)S(1)}, f32[25,64,128]{2,1,0:T(8,128)}, u32[]{:S(2)}) copy-start(f32[25,64,128]{2,1,0:T(8,128)} %get-tuple-element.40.grad_local) | copy-start | bytes 2457604

commit v8 on v6

--- a/solution.py
+++ b/solution.py
@@ -173,6 +173,58 @@
             outgoing[j][q] = table[sends[0, 0, j, 2 * q]] + pltpu.roll(high, 64, 1)
 
 
+def upper_kernel(
+    out_far,
+    down_far,
+    kernel_far,
+    placing_far,
+    grad_active,
+    conv_back,
+    out_grad,
+    down_kernel,
+    kernel,
+    spread_rows,
+    done,
+):
+    spread_far = placing_far.at[SPREAD_ROWS : SPREAD_ROWS + 512]
+    copies = fetch(
+        (out_far, down_far, spread_far, kernel_far),
+        (out_grad, down_kernel, spread_rows, kernel),
+        done,
+    )
+    wait(copies[:3])
+    turned = jnp.concatenate(
+        [jnp.transpose(out_grad[0, s].astype(F32)).astype(BF) for s in range(SLOTS)], axis=0
+    )
+    spread = nn(turned, tiles_of(spread_rows, 0, 64, 0, 8)).astype(BF)
+    tall = jnp.transpose(down_kernel[...].astype(F32)).astype(BF)
+    down_rows = jnp.concatenate(
+        [
+            jnp.concatenate([tall[(4 * tx + t) * C : (4 * tx + t + 1) * C] for t in range(4)], axis=1)
+            for tx in range(2)
+        ],
+        axis=0,
+    )
+    for s in range(SLOTS):
+        rows = slice(s * C2, (s + 1) * C2)
+        block = jnp.concatenate([spread[rows, t * 256 : (t + 1) * 256] for t in range(4)], axis=0)
+        grown = nn(down_rows, block)
+        grad_active[s] = jnp.concatenate(
+            [
+                grown[tx * C : (tx + 1) * C, X * 64 : (X + 1) * 64]
+                for X in range(4)
+                for tx in range(2)
+            ],
+            axis=1,
+        )
+    wait(copies[3:])
+    tall = jnp.transpose(kernel[...].astype(F32)).astype(BF)
+    for o in range(3):
+        conv_back[o * C : (o + 1) * C] = jnp.concatenate(
+            [tall[(9 * o + k) * C : (9 * o + k + 1) * C] for k in range(9)], axis=1
+        )
+
+
 def main_kernel(
     count,
     sources_far,
@@ -186,10 +238,10 @@
     kernel_far,
     down_far,
     out_far,
+    active_far,
     coarse,
     grad_preact,
     sums,
-    conv_back,
     sources,
     arrived,
     features,
@@ -197,6 +249,7 @@
     kernel,
     down_kernel,
     out_grad,
+    grad_active,
     halo,
     halo_high,
     conv,
@@ -210,9 +263,10 @@
 ):
     copies = fetch(
         (ahead, behind, ahead2, behind2, table, sources_far)
-        + (features_far, placing_far, kernel_far, down_far, out_far),
+        + (features_far, placing_far, kernel_far, down_far, out_far, active_far),
         [arrived.at[j] for j in range(NOFF)]
-        + [halo.at[0:LOCAL], sources, features, placing, kernel, down_kernel, out_grad],
+        + [halo.at[0:LOCAL], sources, features, placing, kernel, down_kernel, out_grad]
+        + [grad_active],
         done,
     )
     wait(copies[: NOFF + 2])
@@ -258,19 +312,6 @@
 
     for o in range(3):
         conv[o * C : (o + 1) * C] = kernel[:, o * 576 : (o + 1) * 576]
-    tall = jnp.transpose(kernel[...].astype(F32)).astype(BF)
-    for o in range(3):
-        conv_back[o * C : (o + 1) * C] = jnp.concatenate(
-            [tall[(9 * o + k) * C : (9 * o + k + 1) * C] for k in range(9)], axis=1
-        )
-    tall = jnp.transpose(down_kernel[...].astype(F32)).astype(BF)
-    down_rows = jnp.concatenate(
-        [
-            jnp.concatenate([tall[(4 * tx + t) * C : (4 * tx + t + 1) * C] for t in range(4)], axis=1)
-            for tx in range(2)
-        ],
-        axis=0,
-    )
     left = low_lanes((16, 128))
     edge = jnp.zeros((C, 64), BF)
     wide = jnp.zeros((C, 128), BF)
@@ -303,19 +344,7 @@
                             picked[32 * q + 16 : 32 * q + 32, lanes],
                         )
                         lowered[s, X * 16 : (X + 1) * 16, q * 128 : (q + 1) * 128] = block.astype(BF)
-            turned = jnp.transpose(out_grad[0, s].astype(F32)).astype(BF)
-            spread = nn(turned, tiles_of(placing, SPREAD_ROWS, 64, 0, 8)).astype(BF)
-            spread = jnp.concatenate([spread[:, t * 256 : (t + 1) * 256] for t in range(4)], axis=0)
-            grown = nn(down_rows, spread)
-            upper = jnp.concatenate(
-                [
-                    grown[tx * C : (tx + 1) * C, X * 64 : (X + 1) * 64]
-                    for X in range(4)
-                    for tx in range(2)
-                ],
-                axis=1,
-            )
-            grads = upper * sigmoid * (1.0 + preact * (1.0 - sigmoid)) * filled
+            grads = grad_active[s] * sigmoid * (1.0 + preact * (1.0 - sigmoid)) * filled
             grads = grads.astype(BF)
             grad_preact[s] = grads
             shifted[0:C, base : base + 640] = jnp.concatenate([grads, wide], axis=1)
@@ -522,15 +551,32 @@
         face_packed,
     )
     received = [from_behind(b, tile, devices, o) for b, o in zip(outgoing, OFFSETS)]
-    coarse, grad_preact, sums, conv_back = call(
+    grad_active, conv_back = call(
+        upper_kernel,
+        56,
+        "hhhh",
+        [((SLOTS, C, 512), F32), ((192, 576), BF)],
+        [
+            ((1, SLOTS, 64, C2), BF),
+            ((C2, 512), BF),
+            ((C, 1728), BF),
+            ((512, 128), BF),
+            pltpu.SemaphoreType.DMA((4,)),
+        ],
+        10**9,
+        out_grad,
+        down_kernel,
+        kernel,
+        placing,
+    )
+    coarse, grad_preact, sums = call(
         main_kernel,
         53.8,
-        "s" + "h" * 11,
+        "s" + "h" * 12,
         [
             ((1, SLOTS, 64, C2), BF),
             ((SLOTS, C, 512), BF),
             ((1536, 128), BF),
-            ((192, 576), BF),
         ],
         [
             pltpu.SMEM((1, SLOTS, 26), jnp.int32),
@@ -540,6 +586,7 @@
             ((C, 1728), BF),
             ((C2, 512), BF),
             ((1, SLOTS, 64, C2), BF),
+            ((SLOTS, C, 512), F32),
             ((TABLE, C, 128), BF),
             ((TABLE, C, 128), BF),
             ((192, 576), BF),
@@ -549,7 +596,7 @@
             ((192, 1280), BF),
             ((SLOTS, 64, 512), BF),
             ((192, 576), F32),
-            pltpu.SemaphoreType.DMA((11,)),
+            pltpu.SemaphoreType.DMA((12,)),
         ],
         5 * 10**9,
         brick_count,
@@ -561,6 +608,7 @@
         kernel,
         down_kernel,
         out_grad,
+        grad_active,
     )
     part = near_sum(sums, sizes)
     folded, grad_local, *remote = call(

time: 101 us -> 99 us (0.980)
  waiting for transfers between devices: 16.4 us -> 13.7 us
  Pallas kernels: 20.4 us -> 22.3 us
    ppermute x8, waiting for transfers between devices: 3.89 us -> 1.13 us  [from_behind(): return lax.ppermute(block, axes, route)]
    pallas_call x5 -> x6, Pallas kernels: 20.4 us -> 22.3 us  [call(): pl.pallas_call(kernel, in_specs=[pl.BlockSpec(memory_space=where[m]) for...]
  transfers between devices with their start and end apart: 11 -> 11, of which waited for: 4 -> 4; matrix products, arithmetic and copies ran while one was open for 0% -> 0% of each run, Pallas kernels for 9% -> 12%
where the time goes in v8:
time: 99 us; the launch traced here: 98.3 us
  starting transfers between devices  59.2 us (60%)
  Pallas kernels  22.3 us (23%)
  waiting for transfers between devices  13.7 us (14%)
  local copies, waits for them, and re-layouts  1.54 us (2%)
  between operations  1.54 us (2%)
    ppermute x8, starting transfers between devices, from_behind(): return lax.ppermute(block, axes, route)  23.5 us
    pallas_call x6, Pallas kernels, call(): pl.pallas_call(kernel, in_specs=[pl.BlockSpec(memory_space=where[m]) for...  22.3 us
    all_to_all x1, starting transfers between devices, gather_sum(): got = lax.all_to_all(copies, axes, 0, 0)  16 us
    all_to_all x1, starting transfers between devices, near_sum(): got = lax.all_to_all(block.reshape(parts, rows, 128), NEAR, 0, 0)  11.3 us
    all_to_all x1, starting transfers between devices, near_gather(): lax.all_to_all(copies, NEAR, 0, 0).reshape(parts * block.shape[0], 128)  8.39 us
    all_to_all x1, waiting for transfers between devices, near_gather(): lax.all_to_all(copies, NEAR, 0, 0).reshape(parts * block.shape[0], 128)  8.11 us
    all_to_all x1, waiting for transfers between devices, near_sum(): got = lax.all_to_all(block.reshape(parts, rows, 128), NEAR, 0, 0)  2.73 us
  transfers between devices with their start and end apart: 11, of which 4 were waited for; matrix products, arithmetic and copies ran while one was open for 0% of the time, Pallas kernels for 12%

profile of v8, /device:TPU:1, one launch (start us, length us, event | category | flops | bytes accessed | tf_op | source)
XLA Modules:
  0.0 98.3 jit_solution(4542253677477306607)
XLA Ops:
  1.3 2.1 %faces_kernel.1 = (bf16[25,64,128]{2,1,0:T(8,128)(2,1)}, bf16[2,64,128]{2,1,0:T(8,128)(2,1)}, bf16[2,64,128]{2,1,0:T(8,128)(2,1)}, bf16[2,64,128]{2,1,0:T(8,128)(2,1)}, bf16[2,64,128]{2,1,0:T(8,128)(2,1)}) custom-call(s32[1,1]{1,0:T(1,128)S(6)} %copy.15.count, s32[1,1,4,4]{3,2,1,0:T(4,128)} %sends.1, bf16[1,4,64,512]{3,2,1,0:T(8,128)(2,1)} %features_far.3, ...), custom_call_target="tpu_custom_call" | custom-call | flops 201326592 | bytes 1048576 | tf_op jit(solution)/shard_map/faces_kernel/pallas_call | solution.py:494
  3.4 4.5 %collective-permute-start = (bf16[2,64,128]{2,1,0:T(8,128)(2,1)}, bf16[2,64,128]{2,1,0:T(8,128)(2,1)S(1)}, u32[]{:S(2)}, u32[]{:S(2)}) collective-permute-start(bf16[2,64,128]{2,1,0:T(8,128)(2,1)} %get-tuple-element.33), channel_id=1, source_target_pairs={{0,4},{4,8},{8,12},{12,16},{16,20},{20,24},{24,28},{28,32},{32,36}... | collective-permute-start | bytes 98312 | tf_op jit(solution)/shard_map/ppermute | solution.py:527
  7.9 5.6 %collective-permute-start.1 = (bf16[2,64,128]{2,1,0:T(8,128)(2,1)}, bf16[2,64,128]{2,1,0:T(8,128)(2,1)S(1)}, u32[]{:S(2)}, u32[]{:S(2)}) collective-permute-start(bf16[2,64,128]{2,1,0:T(8,128)(2,1)} %get-tuple-element.34), channel_id=1, source_target_pairs={{4,0},{8,4},{12,8},{16,12},{20,16},{24,20},{28,24},{32,28},{36,32}... | collective-permute-start | bytes 98312 | tf_op jit(solution)/shard_map/ppermute | solution.py:527
  13.5 1.3 %collective-permute-start.2 = (bf16[2,64,128]{2,1,0:T(8,128)(2,1)}, bf16[2,64,128]{2,1,0:T(8,128)(2,1)S(1)}, u32[]{:S(2)}, u32[]{:S(2)}) collective-permute-start(bf16[2,64,128]{2,1,0:T(8,128)(2,1)} %get-tuple-element.35), channel_id=1, source_target_pairs={{0,8},{4,12},{8,16},{12,20},{16,24},{20,28},{24,32},{28,36},{32,40... | collective-permute-start | bytes 98312 | tf_op jit(solution)/shard_map/ppermute | solution.py:527
  14.8 0.0 copy-start.5
  14.8 1.3 %collective-permute-start.3 = (bf16[2,64,128]{2,1,0:T(8,128)(2,1)}, bf16[2,64,128]{2,1,0:T(8,128)(2,1)S(1)}, u32[]{:S(2)}, u32[]{:S(2)}) collective-permute-start(bf16[2,64,128]{2,1,0:T(8,128)(2,1)} %get-tuple-element.36), channel_id=1, source_target_pairs={{8,0},{12,4},{16,8},{20,12},{24,16},{28,20},{32,24},{36,28},{40,32... | collective-permute-start | bytes 98312 | tf_op jit(solution)/shard_map/ppermute | solution.py:527
  16.1 2.7 %upper_kernel.1 = (f32[4,64,512]{2,1,0:T(8,128)}, bf16[192,576]{1,0:T(8,128)(2,1)}) custom-call(bf16[1,4,64,128]{3,2,1,0:T(8,128)(2,1)} %out_far.3, bf16[128,512]{1,0:T(8,128)(2,1)} %down_far.3, bf16[64,1728]{1,0:T(8,128)(2,1)} %kernel_far.3, bf16[4352,128]{1,0:T(8,128)(2,1)} %constant.13.clone.placing_far), custom_call_target="tpu_custom_call" | custom-call | flops 1000000000 | bytes 1048576 | tf_op jit(solution)/shard_map/upper_kernel/pallas_call | solution.py:494
  18.9 0.0 collective-permute-done.ahead
  18.9 0.0 collective-permute-done.1.behind
  18.9 0.0 collective-permute-done.2.ahead2
  18.9 1.1 %collective-permute-done.3.behind2 = bf16[2,64,128]{2,1,0:T(8,128)(2,1)S(1)} collective-permute-done((bf16[2,64,128]{2,1,0:T(8,128)(2,1)}, bf16[2,64,128]{2,1,0:T(8,128)(2,1)S(1)}, u32[]{:S(2)}, u32[]{:S(2)}) %collective-permute-start.3) | collective-permute-done | bytes 32800 | tf_op jit(solution)/shard_map/ppermute | solution.py:527
  20.0 0.0 copy-done.5
  20.0 7.3 %main_kernel.1 = (bf16[1,4,64,128]{3,2,1,0:T(8,128)(2,1)}, bf16[4,64,512]{2,1,0:T(8,128)(2,1)}, bf16[1536,128]{1,0:T(8,128)(2,1)}) custom-call(s32[1,1]{1,0:T(1,128)S(6)} %copy.15.count, s32[1,4,26]{2,1,0:T(4,128)S(1)} %copy-done.5, bf16[25,64,128]{2,1,0:T(8,128)(2,1)} %get-tuple-element.32.table, bf16[2,64,128]{2,1,0:T(8,128)(2,1)S(1)} %collective-permute-done.ahead, ...), custom_call_target="tpu_custom_call" | custom-call | flops 5000000000 | bytes 1048576 | tf_op jit(solution)/shard_map/main_kernel/pallas_call | solution.py:494
  27.3 11.3 %all-to-all-start = ((bf16[32,48,128]{2,1,0:T(8,128)(2,1)}), bf16[32,48,128]{2,1,0:T(8,128)(2,1)S(1)}, u32[]{:S(2)}, u32[]{:S(2)}) async-start(bf16[32,48,128]{2,1,0:T(8,128)(2,1)} %bitcast.3), calls=%async_computation | async-start | bytes 786432 | tf_op jit(solution)/shard_map/all_to_all | solution.py:515
  38.6 0.0 copy-start.2
  38.7 7.3 %fold_kernel.1 = (f32[256,1024]{1,0:T(8,128)}, f32[25,64,128]{2,1,0:T(8,128)}, bf16[2,64,128]{2,1,0:T(8,128)(2,1)}, bf16[2,64,128]{2,1,0:T(8,128)(2,1)}, bf16[2,...) custom-call(s32[1,4,26]{2,1,0:T(4,128)} %sources.1, bf16[4,64,512]{2,1,0:T(8,128)(2,1)} %get-tuple-element.39.grads_far, ...), custom_call_target="tpu_custom_call" | custom-call | flops 3000000000 | bytes 1048576 | tf_op jit(solution)/shard_map/fold_kernel/pallas_call | solution.py:494
  45.9 0.0 copy-start
  45.9 0.0 copy-start.1
  45.9 0.0 copy-start.3
  45.9 0.0 copy-start.4
  46.0 2.7 %all-to-all-done = bf16[32,48,128]{2,1,0:T(8,128)(2,1)S(1)} async-done(((bf16[32,48,128]{2,1,0:T(8,128)(2,1)}), bf16[32,48,128]{2,1,0:T(8,128)(2,1)S(1)}, u32[]{:S(2)}, u32[]{:S(2)}) %all-to-all-start) | async-done | bytes 393248 | tf_op jit(solution)/shard_map/all_to_all | solution.py:515
  48.7 0.1 reduce_sum.21
  48.8 0.7 broadcast_in_dim.4
  49.5 16.0 %all-to-all-start.1 = ((bf16[16,48,128]{2,1,0:T(8,128)(2,1)}), bf16[16,48,128]{2,1,0:T(8,128)(2,1)S(1)}, u32[]{:S(2)}, u32[]{:S(2)}) async-start(bf16[16,48,128]{2,1,0:T(8,128)(2,1)} %broadcast_in_dim.4), calls=%async_computation.1 | async-start | bytes 393216 | tf_op jit(solution)/shard_map/all_to_all | solution.py:508
  65.5 2.9 %collective-permute-start.4 = (bf16[2,64,128]{2,1,0:T(8,128)(2,1)}, bf16[2,64,128]{2,1,0:T(8,128)(2,1)S(1)}, u32[]{:S(2)}, u32[]{:S(2)}) collective-permute-start(bf16[2,64,128]{2,1,0:T(8,128)(2,1)} %get-tuple-element.49), channel_id=1, source_target_pairs={{4,0},{8,4},{12,8},{16,12},{20,16},{24,20},{28,24},{32,28},{36,32}... | collective-permute-start | bytes 98312 | tf_op jit(solution)/shard_map/ppermute | solution.py:527
  68.4 2.7 %collective-permute-start.5 = (bf16[2,64,128]{2,1,0:T(8,128)(2,1)}, bf16[2,64,128]{2,1,0:T(8,128)(2,1)S(1)}, u32[]{:S(2)}, u32[]{:S(2)}) collective-permute-start(bf16[2,64,128]{2,1,0:T(8,128)(2,1)} %get-tuple-element.50), channel_id=1, source_target_pairs={{0,4},{4,8},{8,12},{12,16},{16,20},{20,24},{24,28},{28,32},{32,36}... | collective-permute-start | bytes 98312 | tf_op jit(solution)/shard_map/ppermute | solution.py:527
  71.0 1.3 %collective-permute-start.6 = (bf16[2,64,128]{2,1,0:T(8,128)(2,1)}, bf16[2,64,128]{2,1,0:T(8,128)(2,1)S(1)}, u32[]{:S(2)}, u32[]{:S(2)}) collective-permute-start(bf16[2,64,128]{2,1,0:T(8,128)(2,1)} %get-tuple-element.51), channel_id=1, source_target_pairs={{8,0},{12,4},{16,8},{20,12},{24,16},{28,20},{32,24},{36,28},{40,32... | collective-permute-start | bytes 98312 | tf_op jit(solution)/shard_map/ppermute | solution.py:527
  72.3 4.0 %collective-permute-start.7 = (bf16[2,64,128]{2,1,0:T(8,128)(2,1)}, bf16[2,64,128]{2,1,0:T(8,128)(2,1)S(1)}, u32[]{:S(2)}, u32[]{:S(2)}) collective-permute-start(bf16[2,64,128]{2,1,0:T(8,128)(2,1)} %get-tuple-element.52), channel_id=1, source_target_pairs={{0,8},{4,12},{8,16},{12,20},{16,24},{20,28},{24,32},{28,36},{32,40... | collective-permute-start | bytes 98312 | tf_op jit(solution)/shard_map/ppermute | solution.py:527
  76.3 1.7 %all-to-all-done.1 = bf16[16,48,128]{2,1,0:T(8,128)(2,1)S(1)} async-done(((bf16[16,48,128]{2,1,0:T(8,128)(2,1)}), bf16[16,48,128]{2,1,0:T(8,128)(2,1)S(1)}, u32[]{:S(2)}, u32[]{:S(2)}) %all-to-all-start.1) | async-done | bytes 196640 | tf_op jit(solution)/shard_map/all_to_all | solution.py:508
  78.0 0.0 collective-permute-done.4.ahead
  78.0 0.0 collective-permute-done.5.behind
  78.1 0.0 collective-permute-done.6.ahead2
  78.1 0.0 collective-permute-done.7.behind2
  78.1 0.8 broadcast_in_dim.5
  78.9 8.4 %all-to-all-start.2 = ((bf16[32,48,128]{2,1,0:T(8,128)(2,1)}), bf16[32,48,128]{2,1,0:T(8,128)(2,1)S(1)}, u32[]{:S(2)}, u32[]{:S(2)}) async-start(bf16[32,48,128]{2,1,0:T(8,128)(2,1)} %broadcast_in_dim.5), calls=%async_computation.2 | async-start | bytes 786432 | tf_op jit(solution)/shard_map/all_to_all | solution.py:522
  87.3 0.0 copy-done.2
  87.3 0.0 copy-done
  87.3 0.0 copy-done.1
  87.3 0.0 copy-done.3
  87.3 0.0 copy-done.4
  87.3 2.0 %finish_kernel.1 = bf16[1,4,64,512]{3,2,1,0:T(8,128)(2,1)} custom-call(s32[1,1]{1,0:T(1,128)S(6)} %copy.15.count, s32[1,1,4,4]{3,2,1,0:T(4,128)S(1)} %copy-done.4, f32[256,1024]{1,0:T(8,128)S(1)} %copy-done, f32[25,64,128]{2,1,0:T(8,128)S(1)} %copy-done.1, bf16[2,64,128]{2,1,0:T(8,128)(2,1)S(1)} %collective-permute-done.4.ahead, ...), custom_call_target="tpu_custom_call" | custom-call | flops 201326592 | bytes 1048576 | tf_op jit(solution)/shard_map/finish_kernel/pallas_call | solution.py:494
  89.3 8.1 %all-to-all-done.2 = bf16[32,48,128]{2,1,0:T(8,128)(2,1)S(1)} async-done(((bf16[32,48,128]{2,1,0:T(8,128)(2,1)}), bf16[32,48,128]{2,1,0:T(8,128)(2,1)S(1)}, u32[]{:S(2)}, u32[]{:S(2)}) %all-to-all-start.2) | async-done | bytes 393248 | tf_op jit(solution)/shard_map/all_to_all | solution.py:522
  97.4 0.9 unpack_kernel.1
  (1 shorter events, 0.0 us)
Async XLA Ops:
  3.4 15.5 %collective-permute-start = (bf16[2,64,128]{2,1,0:T(8,128)(2,1)}, bf16[2,64,128]{2,1,0:T(8,128)(2,1)S(1)}, u32[]{:S(2)}, u32[]{:S(2)}) collective-permute-start(bf16[2,64,128]{2,1,0:T(8,128)(2,1)} %get-tuple-element.33), channel_id=1, source_target_pairs={{0,4},{4,8},{8,12},{12,16},{16,20},{20,24},{24,28},{28,32},{32,36}... | collective-permute-start | bytes 98312 | tf_op jit(solution)/shard_map/ppermute | solution.py:527
  7.9 11.0 %collective-permute-start.1 = (bf16[2,64,128]{2,1,0:T(8,128)(2,1)}, bf16[2,64,128]{2,1,0:T(8,128)(2,1)S(1)}, u32[]{:S(2)}, u32[]{:S(2)}) collective-permute-start(bf16[2,64,128]{2,1,0:T(8,128)(2,1)} %get-tuple-element.34), channel_id=1, source_target_pairs={{4,0},{8,4},{12,8},{16,12},{20,16},{24,20},{28,24},{32,28},{36,32}... | collective-permute-start | bytes 98312 | tf_op jit(solution)/shard_map/ppermute | solution.py:527
  13.5 5.4 %collective-permute-start.2 = (bf16[2,64,128]{2,1,0:T(8,128)(2,1)}, bf16[2,64,128]{2,1,0:T(8,128)(2,1)S(1)}, u32[]{:S(2)}, u32[]{:S(2)}) collective-permute-start(bf16[2,64,128]{2,1,0:T(8,128)(2,1)} %get-tuple-element.35), channel_id=1, source_target_pairs={{0,8},{4,12},{8,16},{12,20},{16,24},{20,28},{24,32},{28,36},{32,40... | collective-permute-start | bytes 98312 | tf_op jit(solution)/shard_map/ppermute | solution.py:527
  14.8 5.2 %copy-start.5 = (s32[1,4,26]{2,1,0:T(4,128)S(1)}, s32[1,4,26]{2,1,0:T(4,128)}, u32[]{:S(2)}) copy-start(s32[1,4,26]{2,1,0:T(4,128)} %sources.1) | copy-start | bytes 1252
  14.8 5.2 %collective-permute-start.3 = (bf16[2,64,128]{2,1,0:T(8,128)(2,1)}, bf16[2,64,128]{2,1,0:T(8,128)(2,1)S(1)}, u32[]{:S(2)}, u32[]{:S(2)}) collective-permute-start(bf16[2,64,128]{2,1,0:T(8,128)(2,1)} %get-tuple-element.36), channel_id=1, source_target_pairs={{8,0},{12,4},{16,8},{20,12},{24,16},{28,20},{32,24},{36,28},{40,32... | collective-permute-start | bytes 98312 | tf_op jit(solution)/shard_map/ppermute | solution.py:527
  27.3 21.4 %all-to-all-start = ((bf16[32,48,128]{2,1,0:T(8,128)(2,1)}), bf16[32,48,128]{2,1,0:T(8,128)(2,1)S(1)}, u32[]{:S(2)}, u32[]{:S(2)}) async-start(bf16[32,48,128]{2,1,0:T(8,128)(2,1)} %bitcast.3), calls=%async_computation | async-start | bytes 786432 | tf_op jit(solution)/shard_map/all_to_all | solution.py:515
  38.6 48.6 %copy-start.2 = (bf16[512,768]{1,0:T(8,128)(2,1)S(1)}, bf16[512,768]{1,0:T(8,128)(2,1)}, u32[]{:S(2)}) copy-start(bf16[512,768]{1,0:T(8,128)(2,1)} %constant.14.clone.face_hot) | copy-start | bytes 2359300
  45.9 41.4 %copy-start = (f32[256,1024]{1,0:T(8,128)S(1)}, f32[256,1024]{1,0:T(8,128)}, u32[]{:S(2)}) copy-start(f32[256,1024]{1,0:T(8,128)} %get-tuple-element.41.folded) | copy-start | bytes 3145732
  45.9 41.4 %copy-start.1 = (f32[25,64,128]{2,1,0:T(8,128)S(1)}, f32[25,64,128]{2,1,0:T(8,128)}, u32[]{:S(2)}) copy-start(f32[25,64,128]{2,1,0:T(8,128)} %get-tuple-element.42.grad_local) | copy-start | bytes 2457604
  45.9 41.4 %copy-start.3 = (bf16[128,256]{1,0:T(8,128)(2,1)S(1)}, bf16[128,256]{1,0:T(8,128)(2,1)}, u32[]{:S(2)}) copy-start(bf16[128,256]{1,0:T(8,128)(2,1)} %constant.15.clone.inner_hot) | copy-start | bytes 196612
  45.9 41.4 %copy-start.4 = (s32[1,1,4,4]{3,2,1,0:T(4,128)S(1)}, s32[1,1,4,4]{3,2,1,0:T(4,128)}, u32[]{:S(2)}) copy-start(s32[1,1,4,4]{3,2,1,0:T(4,128)} %sends.1) | copy-start | bytes 196
  49.5 28.5 %all-to-all-start.1 = ((bf16[16,48,128]{2,1,0:T(8,128)(2,1)}), bf16[16,48,128]{2,1,0:T(8,128)(2,1)S(1)}, u32[]{:S(2)}, u32[]{:S(2)}) async-start(bf16[16,48,128]{2,1,0:T(8,128)(2,1)} %broadcast_in_dim.4), calls=%async_computation.1 | async-start | bytes 393216 | tf_op jit(solution)/shard_map/all_to_all | solution.py:508
  65.5 12.6 %collective-permute-start.4 = (bf16[2,64,128]{2,1,0:T(8,128)(2,1)}, bf16[2,64,128]{2,1,0:T(8,128)(2,1)S(1)}, u32[]{:S(2)}, u32[]{:S(2)}) collective-permute-start(bf16[2,64,128]{2,1,0:T(8,128)(2,1)} %get-tuple-element.49), channel_id=1, source_target_pairs={{4,0},{8,4},{12,8},{16,12},{20,16},{24,20},{28,24},{32,28},{36,32}... | collective-permute-start | bytes 98312 | tf_op jit(solution)/shard_map/ppermute | solution.py:527
  68.4 9.7 %collective-permute-start.5 = (bf16[2,64,128]{2,1,0:T(8,128)(2,1)}, bf16[2,64,128]{2,1,0:T(8,128)(2,1)S(1)}, u32[]{:S(2)}, u32[]{:S(2)}) collective-permute-start(bf16[2,64,128]{2,1,0:T(8,128)(2,1)} %get-tuple-element.50), channel_id=1, source_target_pairs={{0,4},{4,8},{8,12},{12,16},{16,20},{20,24},{24,28},{28,32},{32,36}... | collective-permute-start | bytes 98312 | tf_op jit(solution)/shard_map/ppermute | solution.py:527
  71.0 7.0 %collective-permute-start.6 = (bf16[2,64,128]{2,1,0:T(8,128)(2,1)}, bf16[2,64,128]{2,1,0:T(8,128)(2,1)S(1)}, u32[]{:S(2)}, u32[]{:S(2)}) collective-permute-start(bf16[2,64,128]{2,1,0:T(8,128)(2,1)} %get-tuple-element.51), channel_id=1, source_target_pairs={{8,0},{12,4},{16,8},{20,12},{24,16},{28,20},{32,24},{36,28},{40,32... | collective-permute-start | bytes 98312 | tf_op jit(solution)/shard_map/ppermute | solution.py:527
  72.3 5.7 %collective-permute-start.7 = (bf16[2,64,128]{2,1,0:T(8,128)(2,1)}, bf16[2,64,128]{2,1,0:T(8,128)(2,1)S(1)}, u32[]{:S(2)}, u32[]{:S(2)}) collective-permute-start(bf16[2,64,128]{2,1,0:T(8,128)(2,1)} %get-tuple-element.52), channel_id=1, source_target_pairs={{0,8},{4,12},{8,16},{12,20},{16,24},{20,28},{24,32},{28,36},{32,40... | collective-permute-start | bytes 98312 | tf_op jit(solution)/shard_map/ppermute | solution.py:527
  78.9 18.5 %all-to-all-start.2 = ((bf16[32,48,128]{2,1,0:T(8,128)(2,1)}), bf16[32,48,128]{2,1,0:T(8,128)(2,1)S(1)}, u32[]{:S(2)}, u32[]{:S(2)}) async-start(bf16[32,48,128]{2,1,0:T(8,128)(2,1)} %broadcast_in_dim.5), calls=%async_computation.2 | async-start | bytes 786432 | tf_op jit(solution)/shard_map/all_to_all | solution.py:522

commit v9 on v8

--- a/solution.py
+++ b/solution.py
@@ -18,7 +18,6 @@
 LOCAL = 6 * SLOTS + 1
 TABLE = LOCAL + NOFF * CAP
 PLACES = list(range(9)) + [None] + list(range(9, 26)) + [None]
-OFFSETS = (1, -1, 2, -2)
 NEAR = ("x", "c", "grp")
 
 
@@ -149,6 +148,17 @@
         copy.wait()
 
 
+def partners(mine):
+    first = lax.axis_index("c") == (0 if mine else 1)
+    second = lax.axis_index("x") % 2 == (0 if mine else 1)
+    return (
+        jnp.where(second, 3, 2),
+        jnp.where(second, 2, 3),
+        jnp.where(first, 1, 0),
+        jnp.where(first, 0, 1),
+    )
+
+
 def faces_kernel(
     count, sends_far, features_far, face_far, table, *rest
 ):
@@ -167,10 +177,10 @@
         for s in range(SLOTS):
             table[6 * s + f] = layer[s * C : (s + 1) * C]
     table[6 * SLOTS] = jnp.zeros((C, 128), BF)
-    for j in range(NOFF):
+    for p, j in enumerate(partners(True)):
         for q in range(CAP // 2):
             high = table[sends[0, 0, j, 2 * q + 1]]
-            outgoing[j][q] = table[sends[0, 0, j, 2 * q]] + pltpu.roll(high, 64, 1)
+            outgoing[p][q] = table[sends[0, 0, j, 2 * q]] + pltpu.roll(high, 64, 1)
 
 
 def upper_kernel(
@@ -229,10 +239,10 @@
     count,
     sources_far,
     table,
-    ahead,
-    behind,
-    ahead2,
-    behind2,
+    from_a,
+    from_b,
+    from_c,
+    from_d,
     features_far,
     placing_far,
     kernel_far,
@@ -262,7 +272,7 @@
     done,
 ):
     copies = fetch(
-        (ahead, behind, ahead2, behind2, table, sources_far)
+        (from_a, from_b, from_c, from_d, table, sources_far)
         + (features_far, placing_far, kernel_far, down_far, out_far, active_far),
         [arrived.at[j] for j in range(NOFF)]
         + [halo.at[0:LOCAL], sources, features, placing, kernel, down_kernel, out_grad]
@@ -275,9 +285,9 @@
     halo_high[0:LOCAL] = pltpu.roll(
         halo[0:LOCAL].reshape(LOCAL * C, 128), 64, 1
     ).reshape(LOCAL, C, 128)
-    for j in range(NOFF):
+    for p, j in enumerate(partners(False)):
         for q in range(CAP // 2):
-            block, place = arrived[j, q], LOCAL + j * CAP + 2 * q
+            block, place = arrived[p, q], LOCAL + j * CAP + 2 * q
             turned = pltpu.roll(block, 64, 1)
             halo[place] = jnp.where(low, block, none)
             halo[place + 1] = jnp.where(low, turned, none)
@@ -374,10 +384,10 @@
     placing_far,
     folded,
     grad_local,
-    to_ahead,
-    to_behind,
-    to_ahead2,
-    to_behind2,
+    to_four_a,
+    to_four_b,
+    to_four_c,
+    to_four_d,
     grad_preact,
     conv_back,
     placing,
@@ -436,11 +446,11 @@
     grad_table[...] += turned.reshape(TABLE, C, 128)
     grad_local[...] = grad_table[0:LOCAL]
     left = low_lanes((C, 128))
-    for j in range(NOFF):
+    for p, j in enumerate(partners(False)):
         for q in range(CAP // 2):
             place = LOCAL + j * CAP + 2 * q
             block = jnp.where(left, grad_table[place], pltpu.roll(grad_table[place + 1], 64, 1))
-            (to_ahead, to_behind, to_ahead2, to_behind2)[j][q] = block.astype(BF)
+            (to_four_a, to_four_b, to_four_c, to_four_d)[p][q] = block.astype(BF)
 
 
 def unpack_kernel(sums, grad_kernel, grad_down):
@@ -458,10 +468,10 @@
     sends,
     folded,
     grad_local,
-    ahead,
-    behind,
-    ahead2,
-    behind2,
+    from_a,
+    from_b,
+    from_c,
+    from_d,
     face_hot,
     inner_hot,
     grad_features,
@@ -469,9 +479,9 @@
     layers,
 ):
     table[...] = grad_local[...]
-    for j in range(NOFF):
+    for p, j in enumerate(partners(True)):
         for q in range(CAP // 2):
-            block = (ahead, behind, ahead2, behind2)[j][q].astype(F32)
+            block = (from_a, from_b, from_c, from_d)[p][q].astype(F32)
             table[sends[0, 0, j, 2 * q]] += block
             table[sends[0, 0, j, 2 * q + 1]] += pltpu.roll(block, 64, 1)
     for s in range(SLOTS):
@@ -522,22 +532,28 @@
     return lax.all_to_all(copies, NEAR, 0, 0).reshape(parts * block.shape[0], 128)
 
 
-def from_behind(block, axes, devices, distance):
-    route = [(i - distance, i) for i in range(devices) if 0 <= i - distance < devices]
-    return lax.ppermute(block, axes, route)
+def swap(blocks, axes, devices):
+    pairs = [
+        [(t, t + 2) for t in range(devices - 2) if t % 4 >= 2],
+        [(t, t + 2) for t in range(devices - 2) if t % 4 < 2],
+        [(t, t + 1) for t in range(devices - 1) if t % 2 == 1],
+        [(t, t + 1) for t in range(devices - 1) if t % 2 == 0],
+    ]
+    routes = [two + [(b, a) for a, b in two] for two in pairs]
+    return [lax.ppermute(block, axes, route) for block, route in zip(blocks, routes)]
 
 
 def on_device(sizes, features, brick_count, send_list, halo_src, kernel, down_kernel, out_grad):
     face_packed, face_hot, inner_hot, placing = one_hot_tables()
     tile = ("z", "x", "c")
     devices = sizes["z"] * sizes["x"] * sizes["c"]
-    swap = [((CAP // 2, C, 128), BF)] * NOFF
+    blocks = [((CAP // 2, C, 128), BF)] * NOFF
 
     table, *outgoing = call(
         faces_kernel,
         56,
         "shhh",
-        [((LOCAL, C, 128), BF)] + swap,
+        [((LOCAL, C, 128), BF)] + blocks,
         [
             pltpu.SMEM((1, 1, NOFF, CAP), jnp.int32),
             ((1, SLOTS, C, 512), BF),
@@ -550,7 +566,7 @@
         features,
         face_packed,
     )
-    received = [from_behind(b, tile, devices, o) for b, o in zip(outgoing, OFFSETS)]
+    received = swap(outgoing, tile, devices)
     grad_active, conv_back = call(
         upper_kernel,
         56,
@@ -615,7 +631,7 @@
         fold_kernel,
         56,
         "shhh",
-        [((256, 1024), F32), ((LOCAL, C, 128), F32)] + swap,
+        [((256, 1024), F32), ((LOCAL, C, 128), F32)] + blocks,
         [
             ((SLOTS, C, 512), BF),
             ((192, 576), BF),
@@ -636,7 +652,7 @@
     )
     part, *remote = lax.optimization_barrier((part, *remote))
     part = gather_sum(part, ("z",), sizes["z"])
-    returned = [from_behind(b, tile, devices, -o) for b, o in zip(remote, OFFSETS)]
+    returned = swap(remote, tile, devices)
     part, *returned = lax.optimization_barrier((part, *returned))
     sums = near_gather(part.astype(BF), sizes)
     (grad_features,) = call(

time: 99 us -> 94.3 us (0.953)
  starting transfers between devices: 59.2 us -> 54.3 us
    all_to_all x1, starting transfers between devices: 11.3 us -> 6 us  [near_sum(): got = lax.all_to_all(block.reshape(parts, rows, 128), NEAR, 0, 0)]
    all_to_all x1, starting transfers between devices: 16 us -> 14.2 us  [gather_sum(): got = lax.all_to_all(copies, axes, 0, 0)]
    all_to_all x1, waiting for transfers between devices: 1.68 us -> 3 us  [gather_sum(): got = lax.all_to_all(copies, axes, 0, 0)]
    all_to_all x1, starting transfers between devices: 8.39 us -> 9.67 us  [near_gather(): lax.all_to_all(copies, NEAR, 0, 0).reshape(parts * block.shape[0], 128)]
    ppermute x8, waiting for transfers between devices: 1.13 us -> 0.02 us  [swap(): lax.ppermute(block, axes, route)]
  transfers between devices with their start and end apart: 11 -> 11, of which waited for: 4 -> 3; matrix products, arithmetic and copies ran while one was open for 0% -> 0% of each run, Pallas kernels for 12% -> 13%
where the time goes in v9:
time: 94.3 us; the launch traced here: 93.6 us
  starting transfers between devices  54.3 us (58%)
  Pallas kernels  22.1 us (23%)
  waiting for transfers between devices  14 us (15%)
  between operations  1.56 us (2%)
  local copies, waits for them, and re-layouts  1.54 us (2%)
    ppermute x8, starting transfers between devices, swap(): lax.ppermute(block, axes, route)  24.4 us
    pallas_call x6, Pallas kernels, call(): pl.pallas_call(kernel, in_specs=[pl.BlockSpec(memory_space=where[m]) for...  22.1 us
    all_to_all x1, starting transfers between devices, gather_sum(): got = lax.all_to_all(copies, axes, 0, 0)  14.2 us
    all_to_all x1, starting transfers between devices, near_gather(): lax.all_to_all(copies, NEAR, 0, 0).reshape(parts * block.shape[0], 128)  9.67 us
    all_to_all x1, waiting for transfers between devices, near_gather(): lax.all_to_all(copies, NEAR, 0, 0).reshape(parts * block.shape[0], 128)  8.04 us
    all_to_all x1, starting transfers between devices, near_sum(): got = lax.all_to_all(block.reshape(parts, rows, 128), NEAR, 0, 0)  6 us
    all_to_all x1, waiting for transfers between devices, gather_sum(): got = lax.all_to_all(copies, axes, 0, 0)  3 us
    all_to_all x1, waiting for transfers between devices, near_sum(): got = lax.all_to_all(block.reshape(parts, rows, 128), NEAR, 0, 0)  2.97 us
  transfers between devices with their start and end apart: 11, of which 3 were waited for; matrix products, arithmetic and copies ran while one was open for 0% of the time, Pallas kernels for 13%

profile of v9, /device:TPU:1, one launch (start us, length us, event | category | flops | bytes accessed | tf_op | source)
XLA Modules:
  0.0 93.6 jit_solution(11602266453532524948)
XLA Ops:
  1.3 2.2 %faces_kernel.1 = (bf16[25,64,128]{2,1,0:T(8,128)(2,1)}, bf16[2,64,128]{2,1,0:T(8,128)(2,1)}, bf16[2,64,128]{2,1,0:T(8,128)(2,1)}, bf16[2,64,128]{2,1,0:T(8,128)(2,1)}, bf16[2,64,128]{2,1,0:T(8,128)(2,1)}) custom-call(s32[1,1]{1,0:T(1,128)S(6)} %copy.15.count, s32[1,1,4,4]{3,2,1,0:T(4,128)} %sends.1, bf16[1,4,64,512]{3,2,1,0:T(8,128)(2,1)} %features_far.3, ...), custom_call_target="tpu_custom_call" | custom-call | flops 201326592 | bytes 1048576 | tf_op jit(solution)/shard_map/faces_kernel/pallas_call | solution.py:504
  3.4 0.7 collective-permute-start
  4.1 6.4 %collective-permute-start.1 = (bf16[2,64,128]{2,1,0:T(8,128)(2,1)}, bf16[2,64,128]{2,1,0:T(8,128)(2,1)S(1)}, u32[]{:S(2)}, u32[]{:S(2)}) collective-permute-start(bf16[2,64,128]{2,1,0:T(8,128)(2,1)} %get-tuple-element.34), channel_id=1, source_target_pairs={{0,8},{4,12},{16,24},{20,28},{32,40},{36,44},{48,56},{52,60},{64,7... | collective-permute-start | bytes 98312 | tf_op jit(solution)/shard_map/ppermute | solution.py:543
  10.5 5.9 %collective-permute-start.2 = (bf16[2,64,128]{2,1,0:T(8,128)(2,1)}, bf16[2,64,128]{2,1,0:T(8,128)(2,1)S(1)}, u32[]{:S(2)}, u32[]{:S(2)}) collective-permute-start(bf16[2,64,128]{2,1,0:T(8,128)(2,1)} %get-tuple-element.35), channel_id=1, source_target_pairs={{4,8},{12,16},{20,24},{28,32},{36,40},{44,48},{52,56},{60,64},{68,... | collective-permute-start | bytes 98312 | tf_op jit(solution)/shard_map/ppermute | solution.py:543
  16.4 0.0 copy-start.5
  16.5 1.9 %collective-permute-start.3 = (bf16[2,64,128]{2,1,0:T(8,128)(2,1)}, bf16[2,64,128]{2,1,0:T(8,128)(2,1)S(1)}, u32[]{:S(2)}, u32[]{:S(2)}) collective-permute-start(bf16[2,64,128]{2,1,0:T(8,128)(2,1)} %get-tuple-element.36), channel_id=1, source_target_pairs={{0,4},{8,12},{16,20},{24,28},{32,36},{40,44},{48,52},{56,60},{64,6... | collective-permute-start | bytes 98312 | tf_op jit(solution)/shard_map/ppermute | solution.py:543
  18.4 2.7 %upper_kernel.1 = (f32[4,64,512]{2,1,0:T(8,128)}, bf16[192,576]{1,0:T(8,128)(2,1)}) custom-call(bf16[1,4,64,128]{3,2,1,0:T(8,128)(2,1)} %out_far.3, bf16[128,512]{1,0:T(8,128)(2,1)} %down_far.3, bf16[64,1728]{1,0:T(8,128)(2,1)} %kernel_far.3, bf16[4352,128]{1,0:T(8,128)(2,1)} %constant.13.clone.placing_far), custom_call_target="tpu_custom_call" | custom-call | flops 1000000000 | bytes 1048576 | tf_op jit(solution)/shard_map/upper_kernel/pallas_call | solution.py:504
  21.1 0.0 collective-permute-done.from_a
  21.2 0.0 collective-permute-done.1.from_b
  21.2 0.0 collective-permute-done.2.from_c
  21.2 0.0 collective-permute-done.3.from_d
  21.2 0.0 copy-done.5
  21.2 7.3 %main_kernel.1 = (bf16[1,4,64,128]{3,2,1,0:T(8,128)(2,1)}, bf16[4,64,512]{2,1,0:T(8,128)(2,1)}, bf16[1536,128]{1,0:T(8,128)(2,1)}) custom-call(s32[1,1]{1,0:T(1,128)S(6)} %copy.15.count, s32[1,4,26]{2,1,0:T(4,128)S(1)} %copy-done.5, bf16[25,64,128]{2,1,0:T(8,128)(2,1)} %get-tuple-element.32.table, bf16[2,64,128]{2,1,0:T(8,128)(2,1)S(1)} %collective-permute-done.from_a, ...), custom_call_target="tpu_custom_call" | custom-call | flops 5000000000 | bytes 1048576 | tf_op jit(solution)/shard_map/main_kernel/pallas_call | solution.py:504
  28.5 6.0 %all-to-all-start = ((bf16[32,48,128]{2,1,0:T(8,128)(2,1)}), bf16[32,48,128]{2,1,0:T(8,128)(2,1)S(1)}, u32[]{:S(2)}, u32[]{:S(2)}) async-start(bf16[32,48,128]{2,1,0:T(8,128)(2,1)} %bitcast.3), calls=%async_computation | async-start | bytes 786432 | tf_op jit(solution)/shard_map/all_to_all | solution.py:525
  34.5 0.0 copy-start.2
  34.5 7.0 %fold_kernel.1 = (f32[256,1024]{1,0:T(8,128)}, f32[25,64,128]{2,1,0:T(8,128)}, bf16[2,64,128]{2,1,0:T(8,128)(2,1)}, bf16[2,64,128]{2,1,0:T(8,128)(2,1)}, bf16[2,...) custom-call(s32[1,4,26]{2,1,0:T(4,128)} %sources.1, bf16[4,64,512]{2,1,0:T(8,128)(2,1)} %get-tuple-element.39.grads_far, ...), custom_call_target="tpu_custom_call" | custom-call | flops 3000000000 | bytes 1048576 | tf_op jit(solution)/shard_map/fold_kernel/pallas_call | solution.py:504
  41.5 0.0 copy-start
  41.6 0.0 copy-start.1
  41.6 0.0 copy-start.3
  41.6 0.0 copy-start.4
  41.6 3.0 %all-to-all-done = bf16[32,48,128]{2,1,0:T(8,128)(2,1)S(1)} async-done(((bf16[32,48,128]{2,1,0:T(8,128)(2,1)}), bf16[32,48,128]{2,1,0:T(8,128)(2,1)S(1)}, u32[]{:S(2)}, u32[]{:S(2)}) %all-to-all-start) | async-done | bytes 393248 | tf_op jit(solution)/shard_map/all_to_all | solution.py:525
  44.6 0.1 reduce_sum.21
  44.6 0.7 broadcast_in_dim.4
  45.3 14.2 %all-to-all-start.1 = ((bf16[16,48,128]{2,1,0:T(8,128)(2,1)}), bf16[16,48,128]{2,1,0:T(8,128)(2,1)S(1)}, u32[]{:S(2)}, u32[]{:S(2)}) async-start(bf16[16,48,128]{2,1,0:T(8,128)(2,1)} %broadcast_in_dim.4), calls=%async_computation.1 | async-start | bytes 393216 | tf_op jit(solution)/shard_map/all_to_all | solution.py:518
  59.6 0.7 collective-permute-start.4
  60.3 4.0 %collective-permute-start.5 = (bf16[2,64,128]{2,1,0:T(8,128)(2,1)}, bf16[2,64,128]{2,1,0:T(8,128)(2,1)S(1)}, u32[]{:S(2)}, u32[]{:S(2)}) collective-permute-start(bf16[2,64,128]{2,1,0:T(8,128)(2,1)} %get-tuple-element.50), channel_id=1, source_target_pairs={{0,8},{4,12},{16,24},{20,28},{32,40},{36,44},{48,56},{52,60},{64,7... | collective-permute-start | bytes 98312 | tf_op jit(solution)/shard_map/ppermute | solution.py:543
  64.3 2.9 %collective-permute-start.6 = (bf16[2,64,128]{2,1,0:T(8,128)(2,1)}, bf16[2,64,128]{2,1,0:T(8,128)(2,1)S(1)}, u32[]{:S(2)}, u32[]{:S(2)}) collective-permute-start(bf16[2,64,128]{2,1,0:T(8,128)(2,1)} %get-tuple-element.51), channel_id=1, source_target_pairs={{4,8},{12,16},{20,24},{28,32},{36,40},{44,48},{52,56},{60,64},{68,... | collective-permute-start | bytes 98312 | tf_op jit(solution)/shard_map/ppermute | solution.py:543
  67.2 1.9 %collective-permute-start.7 = (bf16[2,64,128]{2,1,0:T(8,128)(2,1)}, bf16[2,64,128]{2,1,0:T(8,128)(2,1)S(1)}, u32[]{:S(2)}, u32[]{:S(2)}) collective-permute-start(bf16[2,64,128]{2,1,0:T(8,128)(2,1)} %get-tuple-element.52), channel_id=1, source_target_pairs={{0,4},{8,12},{16,20},{24,28},{32,36},{40,44},{48,52},{56,60},{64,6... | collective-permute-start | bytes 98312 | tf_op jit(solution)/shard_map/ppermute | solution.py:543
  69.1 3.0 %all-to-all-done.1 = bf16[16,48,128]{2,1,0:T(8,128)(2,1)S(1)} async-done(((bf16[16,48,128]{2,1,0:T(8,128)(2,1)}), bf16[16,48,128]{2,1,0:T(8,128)(2,1)S(1)}, u32[]{:S(2)}, u32[]{:S(2)}) %all-to-all-start.1) | async-done | bytes 196640 | tf_op jit(solution)/shard_map/all_to_all | solution.py:518
  72.2 0.0 collective-permute-done.4.from_a
  72.2 0.0 collective-permute-done.5.from_b
  72.2 0.0 collective-permute-done.6.from_c
  72.2 0.0 collective-permute-done.7.from_d
  72.2 0.8 broadcast_in_dim.5
  73.0 9.7 %all-to-all-start.2 = ((bf16[32,48,128]{2,1,0:T(8,128)(2,1)}), bf16[32,48,128]{2,1,0:T(8,128)(2,1)S(1)}, u32[]{:S(2)}, u32[]{:S(2)}) async-start(bf16[32,48,128]{2,1,0:T(8,128)(2,1)} %broadcast_in_dim.5), calls=%async_computation.2 | async-start | bytes 786432 | tf_op jit(solution)/shard_map/all_to_all | solution.py:532
  82.7 0.0 copy-done.2
  82.7 0.0 copy-done
  82.7 0.0 copy-done.1
  82.7 0.0 copy-done.3
  82.7 0.0 copy-done.4
  82.7 2.0 %finish_kernel.1 = bf16[1,4,64,512]{3,2,1,0:T(8,128)(2,1)} custom-call(s32[1,1]{1,0:T(1,128)S(6)} %copy.15.count, s32[1,1,4,4]{3,2,1,0:T(4,128)S(1)} %copy-done.4, f32[256,1024]{1,0:T(8,128)S(1)} %copy-done, f32[25,64,128]{2,1,0:T(8,128)S(1)} %copy-done.1, bf16[2,64,128]{2,1,0:T(8,128)(2,1)S(1)} %collective-permute-done.4.from_a, ...), custom_call_target="tpu_custom_call" | custom-call | flops 201326592 | bytes 1048576 | tf_op jit(solution)/shard_map/finish_kernel/pallas_call | solution.py:504
  84.7 8.0 %all-to-all-done.2 = bf16[32,48,128]{2,1,0:T(8,128)(2,1)S(1)} async-done(((bf16[32,48,128]{2,1,0:T(8,128)(2,1)}), bf16[32,48,128]{2,1,0:T(8,128)(2,1)S(1)}, u32[]{:S(2)}, u32[]{:S(2)}) %all-to-all-start.2) | async-done | bytes 393248 | tf_op jit(solution)/shard_map/all_to_all | solution.py:532
  92.7 0.9 unpack_kernel.1
  (1 shorter events, 0.0 us)
Async XLA Ops:
  3.4 17.7 %collective-permute-start = (bf16[2,64,128]{2,1,0:T(8,128)(2,1)}, bf16[2,64,128]{2,1,0:T(8,128)(2,1)S(1)}, u32[]{:S(2)}, u32[]{:S(2)}) collective-permute-start(bf16[2,64,128]{2,1,0:T(8,128)(2,1)} %get-tuple-element.33), channel_id=1, source_target_pairs={{8,16},{12,20},{24,32},{28,36},{40,48},{44,52},{56,64},{60,68},{72... | collective-permute-start | bytes 98312 | tf_op jit(solution)/shard_map/ppermute | solution.py:543
  4.1 17.0 %collective-permute-start.1 = (bf16[2,64,128]{2,1,0:T(8,128)(2,1)}, bf16[2,64,128]{2,1,0:T(8,128)(2,1)S(1)}, u32[]{:S(2)}, u32[]{:S(2)}) collective-permute-start(bf16[2,64,128]{2,1,0:T(8,128)(2,1)} %get-tuple-element.34), channel_id=1, source_target_pairs={{0,8},{4,12},{16,24},{20,28},{32,40},{36,44},{48,56},{52,60},{64,7... | collective-permute-start | bytes 98312 | tf_op jit(solution)/shard_map/ppermute | solution.py:543
  10.5 10.6 %collective-permute-start.2 = (bf16[2,64,128]{2,1,0:T(8,128)(2,1)}, bf16[2,64,128]{2,1,0:T(8,128)(2,1)S(1)}, u32[]{:S(2)}, u32[]{:S(2)}) collective-permute-start(bf16[2,64,128]{2,1,0:T(8,128)(2,1)} %get-tuple-element.35), channel_id=1, source_target_pairs={{4,8},{12,16},{20,24},{28,32},{36,40},{44,48},{52,56},{60,64},{68,... | collective-permute-start | bytes 98312 | tf_op jit(solution)/shard_map/ppermute | solution.py:543
  16.4 4.7 %copy-start.5 = (s32[1,4,26]{2,1,0:T(4,128)S(1)}, s32[1,4,26]{2,1,0:T(4,128)}, u32[]{:S(2)}) copy-start(s32[1,4,26]{2,1,0:T(4,128)} %sources.1) | copy-start | bytes 1252
  16.5 4.7 %collective-permute-start.3 = (bf16[2,64,128]{2,1,0:T(8,128)(2,1)}, bf16[2,64,128]{2,1,0:T(8,128)(2,1)S(1)}, u32[]{:S(2)}, u32[]{:S(2)}) collective-permute-start(bf16[2,64,128]{2,1,0:T(8,128)(2,1)} %get-tuple-element.36), channel_id=1, source_target_pairs={{0,4},{8,12},{16,20},{24,28},{32,36},{40,44},{48,52},{56,60},{64,6... | collective-permute-start | bytes 98312 | tf_op jit(solution)/shard_map/ppermute | solution.py:543
  28.5 16.1 %all-to-all-start = ((bf16[32,48,128]{2,1,0:T(8,128)(2,1)}), bf16[32,48,128]{2,1,0:T(8,128)(2,1)S(1)}, u32[]{:S(2)}, u32[]{:S(2)}) async-start(bf16[32,48,128]{2,1,0:T(8,128)(2,1)} %bitcast.3), calls=%async_computation | async-start | bytes 786432 | tf_op jit(solution)/shard_map/all_to_all | solution.py:525
  34.5 48.2 %copy-start.2 = (bf16[512,768]{1,0:T(8,128)(2,1)S(1)}, bf16[512,768]{1,0:T(8,128)(2,1)}, u32[]{:S(2)}) copy-start(bf16[512,768]{1,0:T(8,128)(2,1)} %constant.14.clone.face_hot) | copy-start | bytes 2359300
  41.5 41.2 %copy-start = (f32[256,1024]{1,0:T(8,128)S(1)}, f32[256,1024]{1,0:T(8,128)}, u32[]{:S(2)}) copy-start(f32[256,1024]{1,0:T(8,128)} %get-tuple-element.41.folded) | copy-start | bytes 3145732
  41.6 41.2 %copy-start.1 = (f32[25,64,128]{2,1,0:T(8,128)S(1)}, f32[25,64,128]{2,1,0:T(8,128)}, u32[]{:S(2)}) copy-start(f32[25,64,128]{2,1,0:T(8,128)} %get-tuple-element.42.grad_local) | copy-start | bytes 2457604
  41.6 41.2 %copy-start.3 = (bf16[128,256]{1,0:T(8,128)(2,1)S(1)}, bf16[128,256]{1,0:T(8,128)(2,1)}, u32[]{:S(2)}) copy-start(bf16[128,256]{1,0:T(8,128)(2,1)} %constant.15.clone.inner_hot) | copy-start | bytes 196612
  41.6 41.2 %copy-start.4 = (s32[1,1,4,4]{3,2,1,0:T(4,128)S(1)}, s32[1,1,4,4]{3,2,1,0:T(4,128)}, u32[]{:S(2)}) copy-start(s32[1,1,4,4]{3,2,1,0:T(4,128)} %sends.1) | copy-start | bytes 196
  45.3 26.8 %all-to-all-start.1 = ((bf16[16,48,128]{2,1,0:T(8,128)(2,1)}), bf16[16,48,128]{2,1,0:T(8,128)(2,1)S(1)}, u32[]{:S(2)}, u32[]{:S(2)}) async-start(bf16[16,48,128]{2,1,0:T(8,128)(2,1)} %broadcast_in_dim.4), calls=%async_computation.1 | async-start | bytes 393216 | tf_op jit(solution)/shard_map/all_to_all | solution.py:518
  59.6 12.6 %collective-permute-start.4 = (bf16[2,64,128]{2,1,0:T(8,128)(2,1)}, bf16[2,64,128]{2,1,0:T(8,128)(2,1)S(1)}, u32[]{:S(2)}, u32[]{:S(2)}) collective-permute-start(bf16[2,64,128]{2,1,0:T(8,128)(2,1)} %get-tuple-element.49), channel_id=1, source_target_pairs={{8,16},{12,20},{24,32},{28,36},{40,48},{44,52},{56,64},{60,68},{72... | collective-permute-start | bytes 98312 | tf_op jit(solution)/shard_map/ppermute | solution.py:543
  60.3 11.9 %collective-permute-start.5 = (bf16[2,64,128]{2,1,0:T(8,128)(2,1)}, bf16[2,64,128]{2,1,0:T(8,128)(2,1)S(1)}, u32[]{:S(2)}, u32[]{:S(2)}) collective-permute-start(bf16[2,64,128]{2,1,0:T(8,128)(2,1)} %get-tuple-element.50), channel_id=1, source_target_pairs={{0,8},{4,12},{16,24},{20,28},{32,40},{36,44},{48,56},{52,60},{64,7... | collective-permute-start | bytes 98312 | tf_op jit(solution)/shard_map/ppermute | solution.py:543
  64.3 7.9 %collective-permute-start.6 = (bf16[2,64,128]{2,1,0:T(8,128)(2,1)}, bf16[2,64,128]{2,1,0:T(8,128)(2,1)S(1)}, u32[]{:S(2)}, u32[]{:S(2)}) collective-permute-start(bf16[2,64,128]{2,1,0:T(8,128)(2,1)} %get-tuple-element.51), channel_id=1, source_target_pairs={{4,8},{12,16},{20,24},{28,32},{36,40},{44,48},{52,56},{60,64},{68,... | collective-permute-start | bytes 98312 | tf_op jit(solution)/shard_map/ppermute | solution.py:543
  67.2 5.0 %collective-permute-start.7 = (bf16[2,64,128]{2,1,0:T(8,128)(2,1)}, bf16[2,64,128]{2,1,0:T(8,128)(2,1)S(1)}, u32[]{:S(2)}, u32[]{:S(2)}) collective-permute-start(bf16[2,64,128]{2,1,0:T(8,128)(2,1)} %get-tuple-element.52), channel_id=1, source_target_pairs={{0,4},{8,12},{16,20},{24,28},{32,36},{40,44},{48,52},{56,60},{64,6... | collective-permute-start | bytes 98312 | tf_op jit(solution)/shard_map/ppermute | solution.py:543
  73.0 19.7 %all-to-all-start.2 = ((bf16[32,48,128]{2,1,0:T(8,128)(2,1)}), bf16[32,48,128]{2,1,0:T(8,128)(2,1)S(1)}, u32[]{:S(2)}, u32[]{:S(2)}) async-start(bf16[32,48,128]{2,1,0:T(8,128)(2,1)} %broadcast_in_dim.5), calls=%async_computation.2 | async-start | bytes 786432 | tf_op jit(solution)/shard_map/all_to_all | solution.py:532

commit v10 on v9

--- a/solution.py
+++ b/solution.py
@@ -363,7 +363,7 @@
         total[...] += nt(shifted[...], stack[p])
         return carry
 
-    lax.fori_loop(0, SLOTS // 2, pair, 0)
+    lax.fori_loop(0, SLOTS // 2, pair, 0, unroll=True)
     rows = lowered[...].reshape(SLOTS * 64, 512)
     coarse[...] = nt(rows, down_kernel[...]).astype(BF).reshape(coarse.shape)
     turned = jnp.transpose(out_grad[...].reshape(SLOTS * 64, C2).astype(F32)).astype(BF)
@@ -382,7 +382,7 @@
     grads_far,
     conv_far,
     placing_far,
-    folded,
+    folded_far,
     grad_local,
     to_four_a,
     to_four_b,
@@ -397,7 +397,9 @@
     rims,
     grad_table,
     grad_table_high,
+    folded,
     done,
+    sent,
 ):
     copies = fetch(
         (grads_far, placing_far.at[0:FOLD_ROWS], conv_far), (grad_preact, placing, conv_back), done
@@ -430,9 +432,10 @@
             high[here, x * 128 : (x + 1) * 128] = value.astype(BF)
             if 1 <= x <= 8:
                 folded[here, (x - 1) * 128 : x * 128] = value
+        pltpu.make_async_copy(folded.at[here], folded_far.at[here], sent.at[s]).start()
         return carry
 
-    lax.fori_loop(0, SLOTS, brick, 0)
+    lax.fori_loop(0, SLOTS, brick, 0, unroll=2)
     rims[:, 0:640] = nt(high[:, 0:128], cap_hot)
     rims[:, 640:1152] = nt(high[:, 128:1152], side_tiles(placing, 0, 8))
     rims[:, 1152:1792] = nt(high[:, 1152:1280], cap_hot)
@@ -445,6 +448,9 @@
     turned = pltpu.roll(grad_table_high[...].reshape(TABLE * C, 128), 64, 1)
     grad_table[...] += turned.reshape(TABLE, C, 128)
     grad_local[...] = grad_table[0:LOCAL]
+    for s in range(SLOTS):
+        rows = pl.ds(s * C, C)
+        pltpu.make_async_copy(folded.at[rows], folded_far.at[rows], sent.at[s]).wait()
     left = low_lanes((C, 128))
     for p, j in enumerate(partners(False)):
         for q in range(CAP // 2):
@@ -499,12 +505,12 @@
         grad_features[0, s] = (whole[s * C : (s + 1) * C] * filled).astype(BF)
 
 
-def call(kernel, limit, memories, outs, scratch, flops, *args):
+def call(kernel, limit, memories, outs, scratch, flops, *args, out_memories=None):
     where = {"s": pltpu.SMEM, "v": pltpu.VMEM, "h": pltpu.HBM}
     return pl.pallas_call(
         kernel,
         in_specs=[pl.BlockSpec(memory_space=where[m]) for m in memories],
-        out_specs=[pl.BlockSpec(memory_space=pltpu.VMEM) for _ in outs],
+        out_specs=[pl.BlockSpec(memory_space=where[m]) for m in out_memories or "v" * len(outs)],
         out_shape=[jax.ShapeDtypeStruct(s, d) for s, d in outs],
         scratch_shapes=[pltpu.VMEM(*s) if isinstance(s, tuple) else s for s in scratch],
         compiler_params=pltpu.CompilerParams(vmem_limit_bytes=int(limit * 2**20)),
@@ -642,13 +648,16 @@
             ((256, 14 * 128), F32),
             ((TABLE, C, 128), F32),
             ((TABLE, C, 128), F32),
+            ((256, 1024), F32),
             pltpu.SemaphoreType.DMA((3,)),
+            pltpu.SemaphoreType.DMA((SLOTS,)),
         ],
         3 * 10**9,
         halo_src,
         grad_preact,
         conv_back,
         placing,
+        out_memories="hv" + "v" * NOFF,
     )
     part, *remote = lax.optimization_barrier((part, *remote))
     part = gather_sum(part, ("z",), sizes["z"])

time: 94.3 us -> 93.3 us (0.989)
  Pallas kernels: 22.1 us -> 21.1 us
    pallas_call x6, Pallas kernels: 22.1 us -> 21.1 us  [call(): pl.pallas_call(kernel, in_specs=[pl.BlockSpec(memory_space=where[m]) for...]
  transfers between devices with their start and end apart: 11 -> 11, of which waited for: 3 -> 3; matrix products, arithmetic and copies ran while one was open for 0% -> 0% of each run, Pallas kernels for 13% -> 12%
where the time goes in v10:
time: 93.3 us; the launch traced here: 92.6 us
  starting transfers between devices  53.8 us (58%)
  Pallas kernels  21.1 us (23%)
  waiting for transfers between devices  14.6 us (16%)
  between operations  1.56 us (2%)
  local copies, waits for them, and re-layouts  1.54 us (2%)
    ppermute x8, starting transfers between devices, swap(): lax.ppermute(block, axes, route)  24.4 us
    pallas_call x6, Pallas kernels, call(): pl.pallas_call(kernel, in_specs=[pl.BlockSpec(memory_space=where[m]) for...  21.1 us
    all_to_all x1, starting transfers between devices, gather_sum(): got = lax.all_to_all(copies, axes, 0, 0)  14.2 us
    all_to_all x1, starting transfers between devices, near_gather(): lax.all_to_all(copies, NEAR, 0, 0).reshape(parts * block.shape[0], 128)  9.09 us
    all_to_all x1, waiting for transfers between devices, near_gather(): lax.all_to_all(copies, NEAR, 0, 0).reshape(parts * block.shape[0], 128)  8.03 us
    all_to_all x1, starting transfers between devices, near_sum(): got = lax.all_to_all(block.reshape(parts, rows, 128), NEAR, 0, 0)  5.99 us
    all_to_all x1, waiting for transfers between devices, near_sum(): got = lax.all_to_all(block.reshape(parts, rows, 128), NEAR, 0, 0)  3.51 us
    all_to_all x1, waiting for transfers between devices, gather_sum(): got = lax.all_to_all(copies, axes, 0, 0)  3 us
  transfers between devices with their start and end apart: 11, of which 3 were waited for; matrix products, arithmetic and copies ran while one was open for 0% of the time, Pallas kernels for 12%

profile of v10, /device:TPU:1, one launch (start us, length us, event | category | flops | bytes accessed | tf_op | source)
XLA Modules:
  0.0 92.6 jit_solution(13655957740341433260)
XLA Ops:
  1.3 2.2 %faces_kernel.1 = (bf16[25,64,128]{2,1,0:T(8,128)(2,1)}, bf16[2,64,128]{2,1,0:T(8,128)(2,1)}, bf16[2,64,128]{2,1,0:T(8,128)(2,1)}, bf16[2,64,128]{2,1,0:T(8,128)(2,1)}, bf16[2,64,128]{2,1,0:T(8,128)(2,1)}) custom-call(s32[1,1]{1,0:T(1,128)S(6)} %copy.15.count, s32[1,1,4,4]{3,2,1,0:T(4,128)} %sends.1, bf16[1,4,64,512]{3,2,1,0:T(8,128)(2,1)} %features_far.3, ...), custom_call_target="tpu_custom_call" | custom-call | flops 201326592 | bytes 1048576 | tf_op jit(solution)/shard_map/faces_kernel/pallas_call | solution.py:510
  3.4 0.7 collective-permute-start
  4.1 6.4 %collective-permute-start.1 = (bf16[2,64,128]{2,1,0:T(8,128)(2,1)}, bf16[2,64,128]{2,1,0:T(8,128)(2,1)S(1)}, u32[]{:S(2)}, u32[]{:S(2)}) collective-permute-start(bf16[2,64,128]{2,1,0:T(8,128)(2,1)} %get-tuple-element.34), channel_id=1, source_target_pairs={{0,8},{4,12},{16,24},{20,28},{32,40},{36,44},{48,56},{52,60},{64,7... | collective-permute-start | bytes 98312 | tf_op jit(solution)/shard_map/ppermute | solution.py:549
  10.5 5.9 %collective-permute-start.2 = (bf16[2,64,128]{2,1,0:T(8,128)(2,1)}, bf16[2,64,128]{2,1,0:T(8,128)(2,1)S(1)}, u32[]{:S(2)}, u32[]{:S(2)}) collective-permute-start(bf16[2,64,128]{2,1,0:T(8,128)(2,1)} %get-tuple-element.35), channel_id=1, source_target_pairs={{4,8},{12,16},{20,24},{28,32},{36,40},{44,48},{52,56},{60,64},{68,... | collective-permute-start | bytes 98312 | tf_op jit(solution)/shard_map/ppermute | solution.py:549
  16.4 0.0 copy-start.5
  16.5 1.9 %collective-permute-start.3 = (bf16[2,64,128]{2,1,0:T(8,128)(2,1)}, bf16[2,64,128]{2,1,0:T(8,128)(2,1)S(1)}, u32[]{:S(2)}, u32[]{:S(2)}) collective-permute-start(bf16[2,64,128]{2,1,0:T(8,128)(2,1)} %get-tuple-element.36), channel_id=1, source_target_pairs={{0,4},{8,12},{16,20},{24,28},{32,36},{40,44},{48,52},{56,60},{64,6... | collective-permute-start | bytes 98312 | tf_op jit(solution)/shard_map/ppermute | solution.py:549
  18.4 2.7 %upper_kernel.1 = (f32[4,64,512]{2,1,0:T(8,128)}, bf16[192,576]{1,0:T(8,128)(2,1)}) custom-call(bf16[1,4,64,128]{3,2,1,0:T(8,128)(2,1)} %out_far.3, bf16[128,512]{1,0:T(8,128)(2,1)} %down_far.3, bf16[64,1728]{1,0:T(8,128)(2,1)} %kernel_far.3, bf16[4352,128]{1,0:T(8,128)(2,1)} %constant.13.clone.placing_far), custom_call_target="tpu_custom_call" | custom-call | flops 1000000000 | bytes 1048576 | tf_op jit(solution)/shard_map/upper_kernel/pallas_call | solution.py:510
  21.1 0.0 collective-permute-done.from_a
  21.2 0.0 collective-permute-done.1.from_b
  21.2 0.0 collective-permute-done.2.from_c
  21.2 0.0 collective-permute-done.3.from_d
  21.2 0.0 copy-done.5
  21.2 6.9 %main_kernel.1 = (bf16[1,4,64,128]{3,2,1,0:T(8,128)(2,1)}, bf16[4,64,512]{2,1,0:T(8,128)(2,1)}, bf16[1536,128]{1,0:T(8,128)(2,1)}) custom-call(s32[1,1]{1,0:T(1,128)S(6)} %copy.15.count, s32[1,4,26]{2,1,0:T(4,128)S(1)} %copy-done.5, bf16[25,64,128]{2,1,0:T(8,128)(2,1)} %get-tuple-element.32.table, bf16[2,64,128]{2,1,0:T(8,128)(2,1)S(1)} %collective-permute-done.from_a, ...), custom_call_target="tpu_custom_call" | custom-call | flops 5000000000 | bytes 1048576 | tf_op jit(solution)/shard_map/main_kernel/pallas_call | solution.py:510
  28.1 6.0 %all-to-all-start = ((bf16[32,48,128]{2,1,0:T(8,128)(2,1)}), bf16[32,48,128]{2,1,0:T(8,128)(2,1)S(1)}, u32[]{:S(2)}, u32[]{:S(2)}) async-start(bf16[32,48,128]{2,1,0:T(8,128)(2,1)} %bitcast.3), calls=%async_computation | async-start | bytes 786432 | tf_op jit(solution)/shard_map/all_to_all | solution.py:531
  34.1 0.0 copy-start.2
  34.1 6.5 %fold_kernel.1 = (f32[256,1024]{1,0:T(8,128)}, f32[25,64,128]{2,1,0:T(8,128)}, bf16[2,64,128]{2,1,0:T(8,128)(2,1)}, bf16[2,64,128]{2,1,0:T(8,128)(2,1)}, bf16[2,...) custom-call(s32[1,4,26]{2,1,0:T(4,128)} %sources.1, bf16[4,64,512]{2,1,0:T(8,128)(2,1)} %get-tuple-element.39.grads_far, ...), custom_call_target="tpu_custom_call" | custom-call | flops 3000000000 | bytes 1048576 | tf_op jit(solution)/shard_map/fold_kernel/pallas_call | solution.py:510
  40.6 0.0 copy-start
  40.6 0.0 copy-start.1
  40.6 0.0 copy-start.3
  40.6 0.0 copy-start.4
  40.6 3.5 %all-to-all-done = bf16[32,48,128]{2,1,0:T(8,128)(2,1)S(1)} async-done(((bf16[32,48,128]{2,1,0:T(8,128)(2,1)}), bf16[32,48,128]{2,1,0:T(8,128)(2,1)S(1)}, u32[]{:S(2)}, u32[]{:S(2)}) %all-to-all-start) | async-done | bytes 393248 | tf_op jit(solution)/shard_map/all_to_all | solution.py:531
  44.1 0.1 reduce_sum.21
  44.2 0.7 broadcast_in_dim.4
  44.9 14.2 %all-to-all-start.1 = ((bf16[16,48,128]{2,1,0:T(8,128)(2,1)}), bf16[16,48,128]{2,1,0:T(8,128)(2,1)S(1)}, u32[]{:S(2)}, u32[]{:S(2)}) async-start(bf16[16,48,128]{2,1,0:T(8,128)(2,1)} %broadcast_in_dim.4), calls=%async_computation.1 | async-start | bytes 393216 | tf_op jit(solution)/shard_map/all_to_all | solution.py:524
  59.2 0.7 collective-permute-start.4
  59.8 4.0 %collective-permute-start.5 = (bf16[2,64,128]{2,1,0:T(8,128)(2,1)}, bf16[2,64,128]{2,1,0:T(8,128)(2,1)S(1)}, u32[]{:S(2)}, u32[]{:S(2)}) collective-permute-start(bf16[2,64,128]{2,1,0:T(8,128)(2,1)} %get-tuple-element.50), channel_id=1, source_target_pairs={{0,8},{4,12},{16,24},{20,28},{32,40},{36,44},{48,56},{52,60},{64,7... | collective-permute-start | bytes 98312 | tf_op jit(solution)/shard_map/ppermute | solution.py:549
  63.9 2.9 %collective-permute-start.6 = (bf16[2,64,128]{2,1,0:T(8,128)(2,1)}, bf16[2,64,128]{2,1,0:T(8,128)(2,1)S(1)}, u32[]{:S(2)}, u32[]{:S(2)}) collective-permute-start(bf16[2,64,128]{2,1,0:T(8,128)(2,1)} %get-tuple-element.51), channel_id=1, source_target_pairs={{4,8},{12,16},{20,24},{28,32},{36,40},{44,48},{52,56},{60,64},{68,... | collective-permute-start | bytes 98312 | tf_op jit(solution)/shard_map/ppermute | solution.py:549
  66.8 1.9 %collective-permute-start.7 = (bf16[2,64,128]{2,1,0:T(8,128)(2,1)}, bf16[2,64,128]{2,1,0:T(8,128)(2,1)S(1)}, u32[]{:S(2)}, u32[]{:S(2)}) collective-permute-start(bf16[2,64,128]{2,1,0:T(8,128)(2,1)} %get-tuple-element.52), channel_id=1, source_target_pairs={{0,4},{8,12},{16,20},{24,28},{32,36},{40,44},{48,52},{56,60},{64,6... | collective-permute-start | bytes 98312 | tf_op jit(solution)/shard_map/ppermute | solution.py:549
  68.7 3.0 %all-to-all-done.1 = bf16[16,48,128]{2,1,0:T(8,128)(2,1)S(1)} async-done(((bf16[16,48,128]{2,1,0:T(8,128)(2,1)}), bf16[16,48,128]{2,1,0:T(8,128)(2,1)S(1)}, u32[]{:S(2)}, u32[]{:S(2)}) %all-to-all-start.1) | async-done | bytes 196640 | tf_op jit(solution)/shard_map/all_to_all | solution.py:524
  71.7 0.0 collective-permute-done.4.from_a
  71.8 0.0 collective-permute-done.5.from_b
  71.8 0.0 collective-permute-done.6.from_c
  71.8 0.0 collective-permute-done.7.from_d
  71.8 0.8 broadcast_in_dim.5
  72.6 9.1 %all-to-all-start.2 = ((bf16[32,48,128]{2,1,0:T(8,128)(2,1)}), bf16[32,48,128]{2,1,0:T(8,128)(2,1)S(1)}, u32[]{:S(2)}, u32[]{:S(2)}) async-start(bf16[32,48,128]{2,1,0:T(8,128)(2,1)} %broadcast_in_dim.5), calls=%async_computation.2 | async-start | bytes 786432 | tf_op jit(solution)/shard_map/all_to_all | solution.py:538
  81.7 0.0 copy-done.2
  81.7 0.0 copy-done
  81.7 0.0 copy-done.1
  81.7 0.0 copy-done.3
  81.7 0.0 copy-done.4
  81.7 2.0 %finish_kernel.1 = bf16[1,4,64,512]{3,2,1,0:T(8,128)(2,1)} custom-call(s32[1,1]{1,0:T(1,128)S(6)} %copy.15.count, s32[1,1,4,4]{3,2,1,0:T(4,128)S(1)} %copy-done.4, f32[256,1024]{1,0:T(8,128)S(1)} %copy-done, f32[25,64,128]{2,1,0:T(8,128)S(1)} %copy-done.1, bf16[2,64,128]{2,1,0:T(8,128)(2,1)S(1)} %collective-permute-done.4.from_a, ...), custom_call_target="tpu_custom_call" | custom-call | flops 201326592 | bytes 1048576 | tf_op jit(solution)/shard_map/finish_kernel/pallas_call | solution.py:510
  83.7 8.0 %all-to-all-done.2 = bf16[32,48,128]{2,1,0:T(8,128)(2,1)S(1)} async-done(((bf16[32,48,128]{2,1,0:T(8,128)(2,1)}), bf16[32,48,128]{2,1,0:T(8,128)(2,1)S(1)}, u32[]{:S(2)}, u32[]{:S(2)}) %all-to-all-start.2) | async-done | bytes 393248 | tf_op jit(solution)/shard_map/all_to_all | solution.py:538
  91.7 0.9 unpack_kernel.1
  (1 shorter events, 0.0 us)
Async XLA Ops:
  3.4 17.7 %collective-permute-start = (bf16[2,64,128]{2,1,0:T(8,128)(2,1)}, bf16[2,64,128]{2,1,0:T(8,128)(2,1)S(1)}, u32[]{:S(2)}, u32[]{:S(2)}) collective-permute-start(bf16[2,64,128]{2,1,0:T(8,128)(2,1)} %get-tuple-element.33), channel_id=1, source_target_pairs={{8,16},{12,20},{24,32},{28,36},{40,48},{44,52},{56,64},{60,68},{72... | collective-permute-start | bytes 98312 | tf_op jit(solution)/shard_map/ppermute | solution.py:549
  4.1 17.0 %collective-permute-start.1 = (bf16[2,64,128]{2,1,0:T(8,128)(2,1)}, bf16[2,64,128]{2,1,0:T(8,128)(2,1)S(1)}, u32[]{:S(2)}, u32[]{:S(2)}) collective-permute-start(bf16[2,64,128]{2,1,0:T(8,128)(2,1)} %get-tuple-element.34), channel_id=1, source_target_pairs={{0,8},{4,12},{16,24},{20,28},{32,40},{36,44},{48,56},{52,60},{64,7... | collective-permute-start | bytes 98312 | tf_op jit(solution)/shard_map/ppermute | solution.py:549
  10.5 10.6 %collective-permute-start.2 = (bf16[2,64,128]{2,1,0:T(8,128)(2,1)}, bf16[2,64,128]{2,1,0:T(8,128)(2,1)S(1)}, u32[]{:S(2)}, u32[]{:S(2)}) collective-permute-start(bf16[2,64,128]{2,1,0:T(8,128)(2,1)} %get-tuple-element.35), channel_id=1, source_target_pairs={{4,8},{12,16},{20,24},{28,32},{36,40},{44,48},{52,56},{60,64},{68,... | collective-permute-start | bytes 98312 | tf_op jit(solution)/shard_map/ppermute | solution.py:549
  16.4 4.7 %copy-start.5 = (s32[1,4,26]{2,1,0:T(4,128)S(1)}, s32[1,4,26]{2,1,0:T(4,128)}, u32[]{:S(2)}) copy-start(s32[1,4,26]{2,1,0:T(4,128)} %sources.1) | copy-start | bytes 1252
  16.5 4.7 %collective-permute-start.3 = (bf16[2,64,128]{2,1,0:T(8,128)(2,1)}, bf16[2,64,128]{2,1,0:T(8,128)(2,1)S(1)}, u32[]{:S(2)}, u32[]{:S(2)}) collective-permute-start(bf16[2,64,128]{2,1,0:T(8,128)(2,1)} %get-tuple-element.36), channel_id=1, source_target_pairs={{0,4},{8,12},{16,20},{24,28},{32,36},{40,44},{48,52},{56,60},{64,6... | collective-permute-start | bytes 98312 | tf_op jit(solution)/shard_map/ppermute | solution.py:549
  28.1 16.0 %all-to-all-start = ((bf16[32,48,128]{2,1,0:T(8,128)(2,1)}), bf16[32,48,128]{2,1,0:T(8,128)(2,1)S(1)}, u32[]{:S(2)}, u32[]{:S(2)}) async-start(bf16[32,48,128]{2,1,0:T(8,128)(2,1)} %bitcast.3), calls=%async_computation | async-start | bytes 786432 | tf_op jit(solution)/shard_map/all_to_all | solution.py:531
  34.1 47.6 %copy-start.2 = (bf16[512,768]{1,0:T(8,128)(2,1)S(1)}, bf16[512,768]{1,0:T(8,128)(2,1)}, u32[]{:S(2)}) copy-start(bf16[512,768]{1,0:T(8,128)(2,1)} %constant.14.clone.face_hot) | copy-start | bytes 2359300
  40.6 41.1 %copy-start = (f32[256,1024]{1,0:T(8,128)S(1)}, f32[256,1024]{1,0:T(8,128)}, u32[]{:S(2)}) copy-start(f32[256,1024]{1,0:T(8,128)} %get-tuple-element.41.folded) | copy-start | bytes 3145732
  40.6 41.1 %copy-start.1 = (f32[25,64,128]{2,1,0:T(8,128)S(1)}, f32[25,64,128]{2,1,0:T(8,128)}, u32[]{:S(2)}) copy-start(f32[25,64,128]{2,1,0:T(8,128)} %get-tuple-element.42.grad_local) | copy-start | bytes 2457604
  40.6 41.1 %copy-start.3 = (bf16[128,256]{1,0:T(8,128)(2,1)S(1)}, bf16[128,256]{1,0:T(8,128)(2,1)}, u32[]{:S(2)}) copy-start(bf16[128,256]{1,0:T(8,128)(2,1)} %constant.15.clone.inner_hot) | copy-start | bytes 196612
  40.6 41.1 %copy-start.4 = (s32[1,1,4,4]{3,2,1,0:T(4,128)S(1)}, s32[1,1,4,4]{3,2,1,0:T(4,128)}, u32[]{:S(2)}) copy-start(s32[1,1,4,4]{3,2,1,0:T(4,128)} %sends.1) | copy-start | bytes 196
  44.9 26.8 %all-to-all-start.1 = ((bf16[16,48,128]{2,1,0:T(8,128)(2,1)}), bf16[16,48,128]{2,1,0:T(8,128)(2,1)S(1)}, u32[]{:S(2)}, u32[]{:S(2)}) async-start(bf16[16,48,128]{2,1,0:T(8,128)(2,1)} %broadcast_in_dim.4), calls=%async_computation.1 | async-start | bytes 393216 | tf_op jit(solution)/shard_map/all_to_all | solution.py:524
  59.2 12.6 %collective-permute-start.4 = (bf16[2,64,128]{2,1,0:T(8,128)(2,1)}, bf16[2,64,128]{2,1,0:T(8,128)(2,1)S(1)}, u32[]{:S(2)}, u32[]{:S(2)}) collective-permute-start(bf16[2,64,128]{2,1,0:T(8,128)(2,1)} %get-tuple-element.49), channel_id=1, source_target_pairs={{8,16},{12,20},{24,32},{28,36},{40,48},{44,52},{56,64},{60,68},{72... | collective-permute-start | bytes 98312 | tf_op jit(solution)/shard_map/ppermute | solution.py:549
  59.8 11.9 %collective-permute-start.5 = (bf16[2,64,128]{2,1,0:T(8,128)(2,1)}, bf16[2,64,128]{2,1,0:T(8,128)(2,1)S(1)}, u32[]{:S(2)}, u32[]{:S(2)}) collective-permute-start(bf16[2,64,128]{2,1,0:T(8,128)(2,1)} %get-tuple-element.50), channel_id=1, source_target_pairs={{0,8},{4,12},{16,24},{20,28},{32,40},{36,44},{48,56},{52,60},{64,7... | collective-permute-start | bytes 98312 | tf_op jit(solution)/shard_map/ppermute | solution.py:549
  63.9 7.9 %collective-permute-start.6 = (bf16[2,64,128]{2,1,0:T(8,128)(2,1)}, bf16[2,64,128]{2,1,0:T(8,128)(2,1)S(1)}, u32[]{:S(2)}, u32[]{:S(2)}) collective-permute-start(bf16[2,64,128]{2,1,0:T(8,128)(2,1)} %get-tuple-element.51), channel_id=1, source_target_pairs={{4,8},{12,16},{20,24},{28,32},{36,40},{44,48},{52,56},{60,64},{68,... | collective-permute-start | bytes 98312 | tf_op jit(solution)/shard_map/ppermute | solution.py:549
  66.8 5.0 %collective-permute-start.7 = (bf16[2,64,128]{2,1,0:T(8,128)(2,1)}, bf16[2,64,128]{2,1,0:T(8,128)(2,1)S(1)}, u32[]{:S(2)}, u32[]{:S(2)}) collective-permute-start(bf16[2,64,128]{2,1,0:T(8,128)(2,1)} %get-tuple-element.52), channel_id=1, source_target_pairs={{0,4},{8,12},{16,20},{24,28},{32,36},{40,44},{48,52},{56,60},{64,6... | collective-permute-start | bytes 98312 | tf_op jit(solution)/shard_map/ppermute | solution.py:549
  72.6 19.1 %all-to-all-start.2 = ((bf16[32,48,128]{2,1,0:T(8,128)(2,1)}), bf16[32,48,128]{2,1,0:T(8,128)(2,1)S(1)}, u32[]{:S(2)}, u32[]{:S(2)}) async-start(bf16[32,48,128]{2,1,0:T(8,128)(2,1)} %broadcast_in_dim.5), calls=%async_computation.2 | async-start | bytes 786432 | tf_op jit(solution)/shard_map/all_to_all | solution.py:538

commit v11 on v10

--- a/solution.py
+++ b/solution.py
@@ -186,23 +186,20 @@
 def upper_kernel(
     out_far,
     down_far,
-    kernel_far,
     placing_far,
     grad_active,
-    conv_back,
     out_grad,
     down_kernel,
-    kernel,
     spread_rows,
     done,
 ):
     spread_far = placing_far.at[SPREAD_ROWS : SPREAD_ROWS + 512]
     copies = fetch(
-        (out_far, down_far, spread_far, kernel_far),
-        (out_grad, down_kernel, spread_rows, kernel),
+        (out_far, down_far, spread_far),
+        (out_grad, down_kernel, spread_rows),
         done,
     )
-    wait(copies[:3])
+    wait(copies)
     turned = jnp.concatenate(
         [jnp.transpose(out_grad[0, s].astype(F32)).astype(BF) for s in range(SLOTS)], axis=0
     )
@@ -226,12 +223,6 @@
                 for tx in range(2)
             ],
             axis=1,
-        )
-    wait(copies[3:])
-    tall = jnp.transpose(kernel[...].astype(F32)).astype(BF)
-    for o in range(3):
-        conv_back[o * C : (o + 1) * C] = jnp.concatenate(
-            [tall[(9 * o + k) * C : (9 * o + k + 1) * C] for k in range(9)], axis=1
         )
 
 
@@ -380,7 +371,7 @@
 def fold_kernel(
     sources,
     grads_far,
-    conv_far,
+    kernel_far,
     placing_far,
     folded_far,
     grad_local,
@@ -389,8 +380,9 @@
     to_four_c,
     to_four_d,
     grad_preact,
+    kernel,
+    placing,
     conv_back,
-    placing,
     planes,
     stack,
     high,
@@ -402,18 +394,23 @@
     sent,
 ):
     copies = fetch(
-        (grads_far, placing_far.at[0:FOLD_ROWS], conv_far), (grad_preact, placing, conv_back), done
+        (kernel_far, grads_far, placing_far.at[0:FOLD_ROWS]), (kernel, grad_preact, placing), done
     )
     grad_table[...] = jnp.zeros_like(grad_table)
     grad_table_high[...] = jnp.zeros_like(grad_table_high)
-    wait(copies[:2])
+    wait(copies[:1])
+    tall = jnp.transpose(kernel[...].astype(F32)).astype(BF)
+    for o in range(3):
+        conv_back[o * C : (o + 1) * C] = jnp.concatenate(
+            [tall[(9 * o + k) * C : (9 * o + k + 1) * C] for k in range(9)], axis=1
+        )
+    wait(copies[1:])
     cap_hot = placing[CAP_ROWS : CAP_ROWS + 640]
     inner_hot = tiles_of(placing, INNER_ROWS, 128, 0, 2)
     rows = grad_preact[...].reshape(SLOTS * C, 512)
     for i in range(4):
         block = nn(rows[:, i * 128 : (i + 1) * 128], inner_hot)
         planes[:, i * 256 : (i + 1) * 256] = block.astype(BF)
-    wait(copies[2:])
 
     def brick(s, carry):
         here = pl.ds(pl.multiple_of(s * C, C), C)
@@ -573,22 +570,20 @@
         face_packed,
     )
     received = swap(outgoing, tile, devices)
-    grad_active, conv_back = call(
+    (grad_active,) = call(
         upper_kernel,
         56,
-        "hhhh",
-        [((SLOTS, C, 512), F32), ((192, 576), BF)],
+        "hhh",
+        [((SLOTS, C, 512), F32)],
         [
             ((1, SLOTS, 64, C2), BF),
             ((C2, 512), BF),
-            ((C, 1728), BF),
             ((512, 128), BF),
-            pltpu.SemaphoreType.DMA((4,)),
+            pltpu.SemaphoreType.DMA((3,)),
         ],
         10**9,
         out_grad,
         down_kernel,
-        kernel,
         placing,
     )
     coarse, grad_preact, sums = call(
@@ -640,8 +635,9 @@
         [((256, 1024), F32), ((LOCAL, C, 128), F32)] + blocks,
         [
             ((SLOTS, C, 512), BF),
+            ((C, 1728), BF),
+            ((FOLD_ROWS, 128), BF),
             ((192, 576), BF),
-            ((FOLD_ROWS, 128), BF),
             ((256, 1024), BF),
             ((576, 1024), BF),
             ((256, 1280), BF),
@@ -655,7 +651,7 @@
         3 * 10**9,
         halo_src,
         grad_preact,
-        conv_back,
+        kernel,
         placing,
         out_memories="hv" + "v" * NOFF,
     )

time: 93.3 us -> 93.2 us (level)
  no operation moved by 1% of the time
where the time goes in v11:
time: 93.2 us; the launch traced here: 92.5 us
  starting transfers between devices  53.8 us (58%)
  Pallas kernels  21.1 us (23%)
  waiting for transfers between devices  14.4 us (15%)
  between operations  1.56 us (2%)
  local copies, waits for them, and re-layouts  1.54 us (2%)
    ppermute x8, starting transfers between devices, swap(): lax.ppermute(block, axes, route)  24.4 us
    pallas_call x6, Pallas kernels, call(): pl.pallas_call(kernel, in_specs=[pl.BlockSpec(memory_space=where[m]) for...  21.1 us
    all_to_all x1, starting transfers between devices, gather_sum(): got = lax.all_to_all(copies, axes, 0, 0)  14.2 us
    all_to_all x1, starting transfers between devices, near_gather(): lax.all_to_all(copies, NEAR, 0, 0).reshape(parts * block.shape[0], 128)  9.1 us
    all_to_all x1, waiting for transfers between devices, near_gather(): lax.all_to_all(copies, NEAR, 0, 0).reshape(parts * block.shape[0], 128)  8.04 us
    all_to_all x1, starting transfers between devices, near_sum(): got = lax.all_to_all(block.reshape(parts, rows, 128), NEAR, 0, 0)  5.99 us
    all_to_all x1, waiting for transfers between devices, near_sum(): got = lax.all_to_all(block.reshape(parts, rows, 128), NEAR, 0, 0)  3.37 us
    all_to_all x1, waiting for transfers between devices, gather_sum(): got = lax.all_to_all(copies, axes, 0, 0)  3 us
  transfers between devices with their start and end apart: 11, of which 3 were waited for; matrix products, arithmetic and copies ran while one was open for 0% of the time, Pallas kernels for 12%

profile of v11, /device:TPU:1, one launch (start us, length us, event | category | flops | bytes accessed | tf_op | source)
XLA Modules:
  0.0 92.5 jit_solution(641472815432351308)
XLA Ops:
  1.3 2.2 %faces_kernel.1 = (bf16[25,64,128]{2,1,0:T(8,128)(2,1)}, bf16[2,64,128]{2,1,0:T(8,128)(2,1)}, bf16[2,64,128]{2,1,0:T(8,128)(2,1)}, bf16[2,64,128]{2,1,0:T(8,128)(2,1)}, bf16[2,64,128]{2,1,0:T(8,128)(2,1)}) custom-call(s32[1,1]{1,0:T(1,128)S(6)} %copy.15.count, s32[1,1,4,4]{3,2,1,0:T(4,128)} %sends.1, bf16[1,4,64,512]{3,2,1,0:T(8,128)(2,1)} %features_far.3, ...), custom_call_target="tpu_custom_call" | custom-call | flops 201326592 | bytes 1048576 | tf_op jit(solution)/shard_map/faces_kernel/pallas_call | solution.py:507
  3.4 0.7 collective-permute-start
  4.1 6.4 %collective-permute-start.1 = (bf16[2,64,128]{2,1,0:T(8,128)(2,1)}, bf16[2,64,128]{2,1,0:T(8,128)(2,1)S(1)}, u32[]{:S(2)}, u32[]{:S(2)}) collective-permute-start(bf16[2,64,128]{2,1,0:T(8,128)(2,1)} %get-tuple-element.32), channel_id=1, source_target_pairs={{0,8},{4,12},{16,24},{20,28},{32,40},{36,44},{48,56},{52,60},{64,7... | collective-permute-start | bytes 98312 | tf_op jit(solution)/shard_map/ppermute | solution.py:546
  10.5 5.9 %collective-permute-start.2 = (bf16[2,64,128]{2,1,0:T(8,128)(2,1)}, bf16[2,64,128]{2,1,0:T(8,128)(2,1)S(1)}, u32[]{:S(2)}, u32[]{:S(2)}) collective-permute-start(bf16[2,64,128]{2,1,0:T(8,128)(2,1)} %get-tuple-element.33), channel_id=1, source_target_pairs={{4,8},{12,16},{20,24},{28,32},{36,40},{44,48},{52,56},{60,64},{68,... | collective-permute-start | bytes 98312 | tf_op jit(solution)/shard_map/ppermute | solution.py:546
  16.5 0.0 copy-start.5
  16.5 1.9 %collective-permute-start.3 = (bf16[2,64,128]{2,1,0:T(8,128)(2,1)}, bf16[2,64,128]{2,1,0:T(8,128)(2,1)S(1)}, u32[]{:S(2)}, u32[]{:S(2)}) collective-permute-start(bf16[2,64,128]{2,1,0:T(8,128)(2,1)} %get-tuple-element.34), channel_id=1, source_target_pairs={{0,4},{8,12},{16,20},{24,28},{32,36},{40,44},{48,52},{56,60},{64,6... | collective-permute-start | bytes 98312 | tf_op jit(solution)/shard_map/ppermute | solution.py:546
  18.4 2.6 %upper_kernel.1.active_far = f32[4,64,512]{2,1,0:T(8,128)} custom-call(bf16[1,4,64,128]{3,2,1,0:T(8,128)(2,1)} %out_far.3, bf16[128,512]{1,0:T(8,128)(2,1)} %down_far.3, bf16[4352,128]{1,0:T(8,128)(2,1)} %constant.13.clone.placing_far), custom_call_target="tpu_custom_call" | custom-call | flops 1000000000 | bytes 1048576 | tf_op jit(solution)/shard_map/upper_kernel/pallas_call | solution.py:507
  21.0 0.0 collective-permute-done.from_a
  21.0 0.0 collective-permute-done.1.from_b
  21.0 0.0 collective-permute-done.2.from_c
  21.0 0.0 collective-permute-done.3.from_d
  21.0 0.0 copy-done.5
  21.0 6.9 %main_kernel.1 = (bf16[1,4,64,128]{3,2,1,0:T(8,128)(2,1)}, bf16[4,64,512]{2,1,0:T(8,128)(2,1)}, bf16[1536,128]{1,0:T(8,128)(2,1)}) custom-call(s32[1,1]{1,0:T(1,128)S(6)} %copy.15.count, s32[1,4,26]{2,1,0:T(4,128)S(1)} %copy-done.5, bf16[25,64,128]{2,1,0:T(8,128)(2,1)} %get-tuple-element.30.table, bf16[2,64,128]{2,1,0:T(8,128)(2,1)S(1)} %collective-permute-done.from_a, ...), custom_call_target="tpu_custom_call" | custom-call | flops 5000000000 | bytes 1048576 | tf_op jit(solution)/shard_map/main_kernel/pallas_call | solution.py:507
  27.9 6.0 %all-to-all-start = ((bf16[32,48,128]{2,1,0:T(8,128)(2,1)}), bf16[32,48,128]{2,1,0:T(8,128)(2,1)S(1)}, u32[]{:S(2)}, u32[]{:S(2)}) async-start(bf16[32,48,128]{2,1,0:T(8,128)(2,1)} %bitcast.3), calls=%async_computation | async-start | bytes 786432 | tf_op jit(solution)/shard_map/all_to_all | solution.py:528
  33.9 0.0 copy-start.2
  33.9 6.6 %fold_kernel.1 = (f32[256,1024]{1,0:T(8,128)}, f32[25,64,128]{2,1,0:T(8,128)}, bf16[2,64,128]{2,1,0:T(8,128)(2,1)}, bf16[2,64,128]{2,1,0:T(8,128)(2,1)}, bf16[2,...) custom-call(s32[1,4,26]{2,1,0:T(4,128)} %sources.1, bf16[4,64,512]{2,1,0:T(8,128)(2,1)} %get-tuple-element.36.grads_far, ...), custom_call_target="tpu_custom_call" | custom-call | flops 3000000000 | bytes 1048576 | tf_op jit(solution)/shard_map/fold_kernel/pallas_call | solution.py:507
  40.6 0.0 copy-start
  40.6 0.0 copy-start.1
  40.6 0.0 copy-start.3
  40.6 0.0 copy-start.4
  40.6 3.4 %all-to-all-done = bf16[32,48,128]{2,1,0:T(8,128)(2,1)S(1)} async-done(((bf16[32,48,128]{2,1,0:T(8,128)(2,1)}), bf16[32,48,128]{2,1,0:T(8,128)(2,1)S(1)}, u32[]{:S(2)}, u32[]{:S(2)}) %all-to-all-start) | async-done | bytes 393248 | tf_op jit(solution)/shard_map/all_to_all | solution.py:528
  44.0 0.1 reduce_sum.21
  44.0 0.7 broadcast_in_dim.4
  44.7 14.2 %all-to-all-start.1 = ((bf16[16,48,128]{2,1,0:T(8,128)(2,1)}), bf16[16,48,128]{2,1,0:T(8,128)(2,1)S(1)}, u32[]{:S(2)}, u32[]{:S(2)}) async-start(bf16[16,48,128]{2,1,0:T(8,128)(2,1)} %broadcast_in_dim.4), calls=%async_computation.1 | async-start | bytes 393216 | tf_op jit(solution)/shard_map/all_to_all | solution.py:521
  59.0 0.7 collective-permute-start.4
  59.7 4.0 %collective-permute-start.5 = (bf16[2,64,128]{2,1,0:T(8,128)(2,1)}, bf16[2,64,128]{2,1,0:T(8,128)(2,1)S(1)}, u32[]{:S(2)}, u32[]{:S(2)}) collective-permute-start(bf16[2,64,128]{2,1,0:T(8,128)(2,1)} %get-tuple-element.46), channel_id=1, source_target_pairs={{0,8},{4,12},{16,24},{20,28},{32,40},{36,44},{48,56},{52,60},{64,7... | collective-permute-start | bytes 98312 | tf_op jit(solution)/shard_map/ppermute | solution.py:546
  63.7 2.9 %collective-permute-start.6 = (bf16[2,64,128]{2,1,0:T(8,128)(2,1)}, bf16[2,64,128]{2,1,0:T(8,128)(2,1)S(1)}, u32[]{:S(2)}, u32[]{:S(2)}) collective-permute-start(bf16[2,64,128]{2,1,0:T(8,128)(2,1)} %get-tuple-element.47), channel_id=1, source_target_pairs={{4,8},{12,16},{20,24},{28,32},{36,40},{44,48},{52,56},{60,64},{68,... | collective-permute-start | bytes 98312 | tf_op jit(solution)/shard_map/ppermute | solution.py:546
  66.6 1.9 %collective-permute-start.7 = (bf16[2,64,128]{2,1,0:T(8,128)(2,1)}, bf16[2,64,128]{2,1,0:T(8,128)(2,1)S(1)}, u32[]{:S(2)}, u32[]{:S(2)}) collective-permute-start(bf16[2,64,128]{2,1,0:T(8,128)(2,1)} %get-tuple-element.48), channel_id=1, source_target_pairs={{0,4},{8,12},{16,20},{24,28},{32,36},{40,44},{48,52},{56,60},{64,6... | collective-permute-start | bytes 98312 | tf_op jit(solution)/shard_map/ppermute | solution.py:546
  68.5 3.0 %all-to-all-done.1 = bf16[16,48,128]{2,1,0:T(8,128)(2,1)S(1)} async-done(((bf16[16,48,128]{2,1,0:T(8,128)(2,1)}), bf16[16,48,128]{2,1,0:T(8,128)(2,1)S(1)}, u32[]{:S(2)}, u32[]{:S(2)}) %all-to-all-start.1) | async-done | bytes 196640 | tf_op jit(solution)/shard_map/all_to_all | solution.py:521
  71.6 0.0 collective-permute-done.4.from_a
  71.6 0.0 collective-permute-done.5.from_b
  71.6 0.0 collective-permute-done.6.from_c
  71.6 0.0 collective-permute-done.7.from_d
  71.6 0.8 broadcast_in_dim.5
  72.4 9.1 %all-to-all-start.2 = ((bf16[32,48,128]{2,1,0:T(8,128)(2,1)}), bf16[32,48,128]{2,1,0:T(8,128)(2,1)S(1)}, u32[]{:S(2)}, u32[]{:S(2)}) async-start(bf16[32,48,128]{2,1,0:T(8,128)(2,1)} %broadcast_in_dim.5), calls=%async_computation.2 | async-start | bytes 786432 | tf_op jit(solution)/shard_map/all_to_all | solution.py:535
  81.5 0.0 copy-done.2
  81.5 0.0 copy-done
  81.6 0.0 copy-done.1
  81.6 0.0 copy-done.3
  81.6 0.0 copy-done.4
  81.6 2.0 %finish_kernel.1 = bf16[1,4,64,512]{3,2,1,0:T(8,128)(2,1)} custom-call(s32[1,1]{1,0:T(1,128)S(6)} %copy.15.count, s32[1,1,4,4]{3,2,1,0:T(4,128)S(1)} %copy-done.4, f32[256,1024]{1,0:T(8,128)S(1)} %copy-done, f32[25,64,128]{2,1,0:T(8,128)S(1)} %copy-done.1, bf16[2,64,128]{2,1,0:T(8,128)(2,1)S(1)} %collective-permute-done.4.from_a, ...), custom_call_target="tpu_custom_call" | custom-call | flops 201326592 | bytes 1048576 | tf_op jit(solution)/shard_map/finish_kernel/pallas_call | solution.py:507
  83.5 8.0 %all-to-all-done.2 = bf16[32,48,128]{2,1,0:T(8,128)(2,1)S(1)} async-done(((bf16[32,48,128]{2,1,0:T(8,128)(2,1)}), bf16[32,48,128]{2,1,0:T(8,128)(2,1)S(1)}, u32[]{:S(2)}, u32[]{:S(2)}) %all-to-all-start.2) | async-done | bytes 393248 | tf_op jit(solution)/shard_map/all_to_all | solution.py:535
  91.6 0.9 unpack_kernel.1
  (1 shorter events, 0.0 us)
Async XLA Ops:
  3.4 17.5 %collective-permute-start = (bf16[2,64,128]{2,1,0:T(8,128)(2,1)}, bf16[2,64,128]{2,1,0:T(8,128)(2,1)S(1)}, u32[]{:S(2)}, u32[]{:S(2)}) collective-permute-start(bf16[2,64,128]{2,1,0:T(8,128)(2,1)} %get-tuple-element.31), channel_id=1, source_target_pairs={{8,16},{12,20},{24,32},{28,36},{40,48},{44,52},{56,64},{60,68},{72... | collective-permute-start | bytes 98312 | tf_op jit(solution)/shard_map/ppermute | solution.py:546
  4.1 16.9 %collective-permute-start.1 = (bf16[2,64,128]{2,1,0:T(8,128)(2,1)}, bf16[2,64,128]{2,1,0:T(8,128)(2,1)S(1)}, u32[]{:S(2)}, u32[]{:S(2)}) collective-permute-start(bf16[2,64,128]{2,1,0:T(8,128)(2,1)} %get-tuple-element.32), channel_id=1, source_target_pairs={{0,8},{4,12},{16,24},{20,28},{32,40},{36,44},{48,56},{52,60},{64,7... | collective-permute-start | bytes 98312 | tf_op jit(solution)/shard_map/ppermute | solution.py:546
  10.5 10.5 %collective-permute-start.2 = (bf16[2,64,128]{2,1,0:T(8,128)(2,1)}, bf16[2,64,128]{2,1,0:T(8,128)(2,1)S(1)}, u32[]{:S(2)}, u32[]{:S(2)}) collective-permute-start(bf16[2,64,128]{2,1,0:T(8,128)(2,1)} %get-tuple-element.33), channel_id=1, source_target_pairs={{4,8},{12,16},{20,24},{28,32},{36,40},{44,48},{52,56},{60,64},{68,... | collective-permute-start | bytes 98312 | tf_op jit(solution)/shard_map/ppermute | solution.py:546
  16.5 4.6 %copy-start.5 = (s32[1,4,26]{2,1,0:T(4,128)S(1)}, s32[1,4,26]{2,1,0:T(4,128)}, u32[]{:S(2)}) copy-start(s32[1,4,26]{2,1,0:T(4,128)} %sources.1) | copy-start | bytes 1252
  16.5 4.5 %collective-permute-start.3 = (bf16[2,64,128]{2,1,0:T(8,128)(2,1)}, bf16[2,64,128]{2,1,0:T(8,128)(2,1)S(1)}, u32[]{:S(2)}, u32[]{:S(2)}) collective-permute-start(bf16[2,64,128]{2,1,0:T(8,128)(2,1)} %get-tuple-element.34), channel_id=1, source_target_pairs={{0,4},{8,12},{16,20},{24,28},{32,36},{40,44},{48,52},{56,60},{64,6... | collective-permute-start | bytes 98312 | tf_op jit(solution)/shard_map/ppermute | solution.py:546
  27.9 16.0 %all-to-all-start = ((bf16[32,48,128]{2,1,0:T(8,128)(2,1)}), bf16[32,48,128]{2,1,0:T(8,128)(2,1)S(1)}, u32[]{:S(2)}, u32[]{:S(2)}) async-start(bf16[32,48,128]{2,1,0:T(8,128)(2,1)} %bitcast.3), calls=%async_computation | async-start | bytes 786432 | tf_op jit(solution)/shard_map/all_to_all | solution.py:528
  33.9 47.6 %copy-start.2 = (bf16[512,768]{1,0:T(8,128)(2,1)S(1)}, bf16[512,768]{1,0:T(8,128)(2,1)}, u32[]{:S(2)}) copy-start(bf16[512,768]{1,0:T(8,128)(2,1)} %constant.14.clone.face_hot) | copy-start | bytes 2359300
  40.6 41.0 %copy-start = (f32[256,1024]{1,0:T(8,128)S(1)}, f32[256,1024]{1,0:T(8,128)}, u32[]{:S(2)}) copy-start(f32[256,1024]{1,0:T(8,128)} %get-tuple-element.37.folded) | copy-start | bytes 3145732
  40.6 41.0 %copy-start.1 = (f32[25,64,128]{2,1,0:T(8,128)S(1)}, f32[25,64,128]{2,1,0:T(8,128)}, u32[]{:S(2)}) copy-start(f32[25,64,128]{2,1,0:T(8,128)} %get-tuple-element.38.grad_local) | copy-start | bytes 2457604
  40.6 41.0 %copy-start.3 = (bf16[128,256]{1,0:T(8,128)(2,1)S(1)}, bf16[128,256]{1,0:T(8,128)(2,1)}, u32[]{:S(2)}) copy-start(bf16[128,256]{1,0:T(8,128)(2,1)} %constant.15.clone.inner_hot) | copy-start | bytes 196612
  40.6 41.0 %copy-start.4 = (s32[1,1,4,4]{3,2,1,0:T(4,128)S(1)}, s32[1,1,4,4]{3,2,1,0:T(4,128)}, u32[]{:S(2)}) copy-start(s32[1,1,4,4]{3,2,1,0:T(4,128)} %sends.1) | copy-start | bytes 196
  44.7 26.8 %all-to-all-start.1 = ((bf16[16,48,128]{2,1,0:T(8,128)(2,1)}), bf16[16,48,128]{2,1,0:T(8,128)(2,1)S(1)}, u32[]{:S(2)}, u32[]{:S(2)}) async-start(bf16[16,48,128]{2,1,0:T(8,128)(2,1)} %broadcast_in_dim.4), calls=%async_computation.1 | async-start | bytes 393216 | tf_op jit(solution)/shard_map/all_to_all | solution.py:521
  59.0 12.6 %collective-permute-start.4 = (bf16[2,64,128]{2,1,0:T(8,128)(2,1)}, bf16[2,64,128]{2,1,0:T(8,128)(2,1)S(1)}, u32[]{:S(2)}, u32[]{:S(2)}) collective-permute-start(bf16[2,64,128]{2,1,0:T(8,128)(2,1)} %get-tuple-element.45), channel_id=1, source_target_pairs={{8,16},{12,20},{24,32},{28,36},{40,48},{44,52},{56,64},{60,68},{72... | collective-permute-start | bytes 98312 | tf_op jit(solution)/shard_map/ppermute | solution.py:546
  59.7 11.9 %collective-permute-start.5 = (bf16[2,64,128]{2,1,0:T(8,128)(2,1)}, bf16[2,64,128]{2,1,0:T(8,128)(2,1)S(1)}, u32[]{:S(2)}, u32[]{:S(2)}) collective-permute-start(bf16[2,64,128]{2,1,0:T(8,128)(2,1)} %get-tuple-element.46), channel_id=1, source_target_pairs={{0,8},{4,12},{16,24},{20,28},{32,40},{36,44},{48,56},{52,60},{64,7... | collective-permute-start | bytes 98312 | tf_op jit(solution)/shard_map/ppermute | solution.py:546
  63.7 7.9 %collective-permute-start.6 = (bf16[2,64,128]{2,1,0:T(8,128)(2,1)}, bf16[2,64,128]{2,1,0:T(8,128)(2,1)S(1)}, u32[]{:S(2)}, u32[]{:S(2)}) collective-permute-start(bf16[2,64,128]{2,1,0:T(8,128)(2,1)} %get-tuple-element.47), channel_id=1, source_target_pairs={{4,8},{12,16},{20,24},{28,32},{36,40},{44,48},{52,56},{60,64},{68,... | collective-permute-start | bytes 98312 | tf_op jit(solution)/shard_map/ppermute | solution.py:546
  66.6 5.0 %collective-permute-start.7 = (bf16[2,64,128]{2,1,0:T(8,128)(2,1)}, bf16[2,64,128]{2,1,0:T(8,128)(2,1)S(1)}, u32[]{:S(2)}, u32[]{:S(2)}) collective-permute-start(bf16[2,64,128]{2,1,0:T(8,128)(2,1)} %get-tuple-element.48), channel_id=1, source_target_pairs={{0,4},{8,12},{16,20},{24,28},{32,36},{40,44},{48,52},{56,60},{64,6... | collective-permute-start | bytes 98312 | tf_op jit(solution)/shard_map/ppermute | solution.py:546
  72.4 19.2 %all-to-all-start.2 = ((bf16[32,48,128]{2,1,0:T(8,128)(2,1)}), bf16[32,48,128]{2,1,0:T(8,128)(2,1)S(1)}, u32[]{:S(2)}, u32[]{:S(2)}) async-start(bf16[32,48,128]{2,1,0:T(8,128)(2,1)} %broadcast_in_dim.5), calls=%async_computation.2 | async-start | bytes 786432 | tf_op jit(solution)/shard_map/all_to_all | solution.py:535

commit v12 on v11

--- a/solution.py
+++ b/solution.py
@@ -432,7 +432,7 @@
         pltpu.make_async_copy(folded.at[here], folded_far.at[here], sent.at[s]).start()
         return carry
 
-    lax.fori_loop(0, SLOTS, brick, 0, unroll=2)
+    lax.fori_loop(0, SLOTS, brick, 0, unroll=True)
     rims[:, 0:640] = nt(high[:, 0:128], cap_hot)
     rims[:, 640:1152] = nt(high[:, 128:1152], side_tiles(placing, 0, 8))
     rims[:, 1152:1792] = nt(high[:, 1152:1280], cap_hot)

time: 93.2 us -> 92.7 us (level)
  no operation moved by 1% of the time
where the time goes in v12:
time: 92.7 us; the launch traced here: 92 us
  starting transfers between devices  53.3 us (57%)
  Pallas kernels  20.7 us (22%)
  waiting for transfers between devices  14.8 us (16%)
  between operations  1.56 us (2%)
  local copies, waits for them, and re-layouts  1.54 us (2%)
    ppermute x8, starting transfers between devices, swap(): lax.ppermute(block, axes, route)  24.4 us
    pallas_call x6, Pallas kernels, call(): pl.pallas_call(kernel, in_specs=[pl.BlockSpec(memory_space=where[m]) for...  20.7 us
    all_to_all x1, starting transfers between devices, gather_sum(): got = lax.all_to_all(copies, axes, 0, 0)  14.3 us
    all_to_all x1, starting transfers between devices, near_gather(): lax.all_to_all(copies, NEAR, 0, 0).reshape(parts * block.shape[0], 128)  8.62 us
    all_to_all x1, waiting for transfers between devices, near_gather(): lax.all_to_all(copies, NEAR, 0, 0).reshape(parts * block.shape[0], 128)  8.04 us
    all_to_all x1, starting transfers between devices, near_sum(): got = lax.all_to_all(block.reshape(parts, rows, 128), NEAR, 0, 0)  5.97 us
    all_to_all x1, waiting for transfers between devices, near_sum(): got = lax.all_to_all(block.reshape(parts, rows, 128), NEAR, 0, 0)  3.75 us
    all_to_all x1, waiting for transfers between devices, gather_sum(): got = lax.all_to_all(copies, axes, 0, 0)  3 us
  transfers between devices with their start and end apart: 11, of which 3 were waited for; matrix products, arithmetic and copies ran while one was open for 0% of the time, Pallas kernels for 12%

profile of v12, /device:TPU:1, one launch (start us, length us, event | category | flops | bytes accessed | tf_op | source)
XLA Modules:
  0.0 92.0 jit_solution(4361504333424181569)
XLA Ops:
  1.3 2.2 %faces_kernel.1 = (bf16[25,64,128]{2,1,0:T(8,128)(2,1)}, bf16[2,64,128]{2,1,0:T(8,128)(2,1)}, bf16[2,64,128]{2,1,0:T(8,128)(2,1)}, bf16[2,64,128]{2,1,0:T(8,128)(2,1)}, bf16[2,64,128]{2,1,0:T(8,128)(2,1)}) custom-call(s32[1,1]{1,0:T(1,128)S(6)} %copy.15.count, s32[1,1,4,4]{3,2,1,0:T(4,128)} %sends.1, bf16[1,4,64,512]{3,2,1,0:T(8,128)(2,1)} %features_far.3, ...), custom_call_target="tpu_custom_call" | custom-call | flops 201326592 | bytes 1048576 | tf_op jit(solution)/shard_map/faces_kernel/pallas_call | solution.py:507
  3.4 0.7 collective-permute-start
  4.1 6.4 %collective-permute-start.1 = (bf16[2,64,128]{2,1,0:T(8,128)(2,1)}, bf16[2,64,128]{2,1,0:T(8,128)(2,1)S(1)}, u32[]{:S(2)}, u32[]{:S(2)}) collective-permute-start(bf16[2,64,128]{2,1,0:T(8,128)(2,1)} %get-tuple-element.32), channel_id=1, source_target_pairs={{0,8},{4,12},{16,24},{20,28},{32,40},{36,44},{48,56},{52,60},{64,7... | collective-permute-start | bytes 98312 | tf_op jit(solution)/shard_map/ppermute | solution.py:546
  10.5 5.9 %collective-permute-start.2 = (bf16[2,64,128]{2,1,0:T(8,128)(2,1)}, bf16[2,64,128]{2,1,0:T(8,128)(2,1)S(1)}, u32[]{:S(2)}, u32[]{:S(2)}) collective-permute-start(bf16[2,64,128]{2,1,0:T(8,128)(2,1)} %get-tuple-element.33), channel_id=1, source_target_pairs={{4,8},{12,16},{20,24},{28,32},{36,40},{44,48},{52,56},{60,64},{68,... | collective-permute-start | bytes 98312 | tf_op jit(solution)/shard_map/ppermute | solution.py:546
  16.5 0.0 copy-start.5
  16.5 1.9 %collective-permute-start.3 = (bf16[2,64,128]{2,1,0:T(8,128)(2,1)}, bf16[2,64,128]{2,1,0:T(8,128)(2,1)S(1)}, u32[]{:S(2)}, u32[]{:S(2)}) collective-permute-start(bf16[2,64,128]{2,1,0:T(8,128)(2,1)} %get-tuple-element.34), channel_id=1, source_target_pairs={{0,4},{8,12},{16,20},{24,28},{32,36},{40,44},{48,52},{56,60},{64,6... | collective-permute-start | bytes 98312 | tf_op jit(solution)/shard_map/ppermute | solution.py:546
  18.4 2.6 %upper_kernel.1.active_far = f32[4,64,512]{2,1,0:T(8,128)} custom-call(bf16[1,4,64,128]{3,2,1,0:T(8,128)(2,1)} %out_far.3, bf16[128,512]{1,0:T(8,128)(2,1)} %down_far.3, bf16[4352,128]{1,0:T(8,128)(2,1)} %constant.13.clone.placing_far), custom_call_target="tpu_custom_call" | custom-call | flops 1000000000 | bytes 1048576 | tf_op jit(solution)/shard_map/upper_kernel/pallas_call | solution.py:507
  21.0 0.0 collective-permute-done.from_a
  21.0 0.0 collective-permute-done.1.from_b
  21.0 0.0 collective-permute-done.2.from_c
  21.0 0.0 collective-permute-done.3.from_d
  21.0 0.0 copy-done.5
  21.0 6.9 %main_kernel.1 = (bf16[1,4,64,128]{3,2,1,0:T(8,128)(2,1)}, bf16[4,64,512]{2,1,0:T(8,128)(2,1)}, bf16[1536,128]{1,0:T(8,128)(2,1)}) custom-call(s32[1,1]{1,0:T(1,128)S(6)} %copy.15.count, s32[1,4,26]{2,1,0:T(4,128)S(1)} %copy-done.5, bf16[25,64,128]{2,1,0:T(8,128)(2,1)} %get-tuple-element.30.table, bf16[2,64,128]{2,1,0:T(8,128)(2,1)S(1)} %collective-permute-done.from_a, ...), custom_call_target="tpu_custom_call" | custom-call | flops 5000000000 | bytes 1048576 | tf_op jit(solution)/shard_map/main_kernel/pallas_call | solution.py:507
  27.9 6.0 %all-to-all-start = ((bf16[32,48,128]{2,1,0:T(8,128)(2,1)}), bf16[32,48,128]{2,1,0:T(8,128)(2,1)S(1)}, u32[]{:S(2)}, u32[]{:S(2)}) async-start(bf16[32,48,128]{2,1,0:T(8,128)(2,1)} %bitcast.3), calls=%async_computation | async-start | bytes 786432 | tf_op jit(solution)/shard_map/all_to_all | solution.py:528
  33.9 0.0 copy-start.2
  33.9 6.2 %fold_kernel.1 = (f32[256,1024]{1,0:T(8,128)}, f32[25,64,128]{2,1,0:T(8,128)}, bf16[2,64,128]{2,1,0:T(8,128)(2,1)}, bf16[2,64,128]{2,1,0:T(8,128)(2,1)}, bf16[2,...) custom-call(s32[1,4,26]{2,1,0:T(4,128)} %sources.1, bf16[4,64,512]{2,1,0:T(8,128)(2,1)} %get-tuple-element.36.grads_far, ...), custom_call_target="tpu_custom_call" | custom-call | flops 3000000000 | bytes 1048576 | tf_op jit(solution)/shard_map/fold_kernel/pallas_call | solution.py:507
  40.2 0.0 copy-start
  40.2 0.0 copy-start.1
  40.2 0.0 copy-start.3
  40.2 0.0 copy-start.4
  40.2 3.8 %all-to-all-done = bf16[32,48,128]{2,1,0:T(8,128)(2,1)S(1)} async-done(((bf16[32,48,128]{2,1,0:T(8,128)(2,1)}), bf16[32,48,128]{2,1,0:T(8,128)(2,1)S(1)}, u32[]{:S(2)}, u32[]{:S(2)}) %all-to-all-start) | async-done | bytes 393248 | tf_op jit(solution)/shard_map/all_to_all | solution.py:528
  44.0 0.1 reduce_sum.21
  44.0 0.7 broadcast_in_dim.4
  44.7 14.3 %all-to-all-start.1 = ((bf16[16,48,128]{2,1,0:T(8,128)(2,1)}), bf16[16,48,128]{2,1,0:T(8,128)(2,1)S(1)}, u32[]{:S(2)}, u32[]{:S(2)}) async-start(bf16[16,48,128]{2,1,0:T(8,128)(2,1)} %broadcast_in_dim.4), calls=%async_computation.1 | async-start | bytes 393216 | tf_op jit(solution)/shard_map/all_to_all | solution.py:521
  59.0 0.7 collective-permute-start.4
  59.7 4.0 %collective-permute-start.5 = (bf16[2,64,128]{2,1,0:T(8,128)(2,1)}, bf16[2,64,128]{2,1,0:T(8,128)(2,1)S(1)}, u32[]{:S(2)}, u32[]{:S(2)}) collective-permute-start(bf16[2,64,128]{2,1,0:T(8,128)(2,1)} %get-tuple-element.46), channel_id=1, source_target_pairs={{0,8},{4,12},{16,24},{20,28},{32,40},{36,44},{48,56},{52,60},{64,7... | collective-permute-start | bytes 98312 | tf_op jit(solution)/shard_map/ppermute | solution.py:546
  63.7 2.9 %collective-permute-start.6 = (bf16[2,64,128]{2,1,0:T(8,128)(2,1)}, bf16[2,64,128]{2,1,0:T(8,128)(2,1)S(1)}, u32[]{:S(2)}, u32[]{:S(2)}) collective-permute-start(bf16[2,64,128]{2,1,0:T(8,128)(2,1)} %get-tuple-element.47), channel_id=1, source_target_pairs={{4,8},{12,16},{20,24},{28,32},{36,40},{44,48},{52,56},{60,64},{68,... | collective-permute-start | bytes 98312 | tf_op jit(solution)/shard_map/ppermute | solution.py:546
  66.6 1.9 %collective-permute-start.7 = (bf16[2,64,128]{2,1,0:T(8,128)(2,1)}, bf16[2,64,128]{2,1,0:T(8,128)(2,1)S(1)}, u32[]{:S(2)}, u32[]{:S(2)}) collective-permute-start(bf16[2,64,128]{2,1,0:T(8,128)(2,1)} %get-tuple-element.48), channel_id=1, source_target_pairs={{0,4},{8,12},{16,20},{24,28},{32,36},{40,44},{48,52},{56,60},{64,6... | collective-permute-start | bytes 98312 | tf_op jit(solution)/shard_map/ppermute | solution.py:546
  68.5 3.0 %all-to-all-done.1 = bf16[16,48,128]{2,1,0:T(8,128)(2,1)S(1)} async-done(((bf16[16,48,128]{2,1,0:T(8,128)(2,1)}), bf16[16,48,128]{2,1,0:T(8,128)(2,1)S(1)}, u32[]{:S(2)}, u32[]{:S(2)}) %all-to-all-start.1) | async-done | bytes 196640 | tf_op jit(solution)/shard_map/all_to_all | solution.py:521
  71.6 0.0 collective-permute-done.4.from_a
  71.6 0.0 collective-permute-done.5.from_b
  71.6 0.0 collective-permute-done.6.from_c
  71.6 0.0 collective-permute-done.7.from_d
  71.6 0.8 broadcast_in_dim.5
  72.4 8.6 %all-to-all-start.2 = ((bf16[32,48,128]{2,1,0:T(8,128)(2,1)}), bf16[32,48,128]{2,1,0:T(8,128)(2,1)S(1)}, u32[]{:S(2)}, u32[]{:S(2)}) async-start(bf16[32,48,128]{2,1,0:T(8,128)(2,1)} %broadcast_in_dim.5), calls=%async_computation.2 | async-start | bytes 786432 | tf_op jit(solution)/shard_map/all_to_all | solution.py:535
  81.1 0.0 copy-done.2
  81.1 0.0 copy-done
  81.1 0.0 copy-done.1
  81.1 0.0 copy-done.3
  81.1 0.0 copy-done.4
  81.1 2.0 %finish_kernel.1 = bf16[1,4,64,512]{3,2,1,0:T(8,128)(2,1)} custom-call(s32[1,1]{1,0:T(1,128)S(6)} %copy.15.count, s32[1,1,4,4]{3,2,1,0:T(4,128)S(1)} %copy-done.4, f32[256,1024]{1,0:T(8,128)S(1)} %copy-done, f32[25,64,128]{2,1,0:T(8,128)S(1)} %copy-done.1, bf16[2,64,128]{2,1,0:T(8,128)(2,1)S(1)} %collective-permute-done.4.from_a, ...), custom_call_target="tpu_custom_call" | custom-call | flops 201326592 | bytes 1048576 | tf_op jit(solution)/shard_map/finish_kernel/pallas_call | solution.py:507
  83.1 8.0 %all-to-all-done.2 = bf16[32,48,128]{2,1,0:T(8,128)(2,1)S(1)} async-done(((bf16[32,48,128]{2,1,0:T(8,128)(2,1)}), bf16[32,48,128]{2,1,0:T(8,128)(2,1)S(1)}, u32[]{:S(2)}, u32[]{:S(2)}) %all-to-all-start.2) | async-done | bytes 393248 | tf_op jit(solution)/shard_map/all_to_all | solution.py:535
  91.1 0.9 unpack_kernel.1
  (1 shorter events, 0.0 us)
Async XLA Ops:
  3.4 17.5 %collective-permute-start = (bf16[2,64,128]{2,1,0:T(8,128)(2,1)}, bf16[2,64,128]{2,1,0:T(8,128)(2,1)S(1)}, u32[]{:S(2)}, u32[]{:S(2)}) collective-permute-start(bf16[2,64,128]{2,1,0:T(8,128)(2,1)} %get-tuple-element.31), channel_id=1, source_target_pairs={{8,16},{12,20},{24,32},{28,36},{40,48},{44,52},{56,64},{60,68},{72... | collective-permute-start | bytes 98312 | tf_op jit(solution)/shard_map/ppermute | solution.py:546
  4.1 16.9 %collective-permute-start.1 = (bf16[2,64,128]{2,1,0:T(8,128)(2,1)}, bf16[2,64,128]{2,1,0:T(8,128)(2,1)S(1)}, u32[]{:S(2)}, u32[]{:S(2)}) collective-permute-start(bf16[2,64,128]{2,1,0:T(8,128)(2,1)} %get-tuple-element.32), channel_id=1, source_target_pairs={{0,8},{4,12},{16,24},{20,28},{32,40},{36,44},{48,56},{52,60},{64,7... | collective-permute-start | bytes 98312 | tf_op jit(solution)/shard_map/ppermute | solution.py:546
  10.5 10.5 %collective-permute-start.2 = (bf16[2,64,128]{2,1,0:T(8,128)(2,1)}, bf16[2,64,128]{2,1,0:T(8,128)(2,1)S(1)}, u32[]{:S(2)}, u32[]{:S(2)}) collective-permute-start(bf16[2,64,128]{2,1,0:T(8,128)(2,1)} %get-tuple-element.33), channel_id=1, source_target_pairs={{4,8},{12,16},{20,24},{28,32},{36,40},{44,48},{52,56},{60,64},{68,... | collective-permute-start | bytes 98312 | tf_op jit(solution)/shard_map/ppermute | solution.py:546
  16.5 4.6 %copy-start.5 = (s32[1,4,26]{2,1,0:T(4,128)S(1)}, s32[1,4,26]{2,1,0:T(4,128)}, u32[]{:S(2)}) copy-start(s32[1,4,26]{2,1,0:T(4,128)} %sources.1) | copy-start | bytes 1252
  16.5 4.5 %collective-permute-start.3 = (bf16[2,64,128]{2,1,0:T(8,128)(2,1)}, bf16[2,64,128]{2,1,0:T(8,128)(2,1)S(1)}, u32[]{:S(2)}, u32[]{:S(2)}) collective-permute-start(bf16[2,64,128]{2,1,0:T(8,128)(2,1)} %get-tuple-element.34), channel_id=1, source_target_pairs={{0,4},{8,12},{16,20},{24,28},{32,36},{40,44},{48,52},{56,60},{64,6... | collective-permute-start | bytes 98312 | tf_op jit(solution)/shard_map/ppermute | solution.py:546
  27.9 16.0 %all-to-all-start = ((bf16[32,48,128]{2,1,0:T(8,128)(2,1)}), bf16[32,48,128]{2,1,0:T(8,128)(2,1)S(1)}, u32[]{:S(2)}, u32[]{:S(2)}) async-start(bf16[32,48,128]{2,1,0:T(8,128)(2,1)} %bitcast.3), calls=%async_computation | async-start | bytes 786432 | tf_op jit(solution)/shard_map/all_to_all | solution.py:528
  33.9 47.1 %copy-start.2 = (bf16[512,768]{1,0:T(8,128)(2,1)S(1)}, bf16[512,768]{1,0:T(8,128)(2,1)}, u32[]{:S(2)}) copy-start(bf16[512,768]{1,0:T(8,128)(2,1)} %constant.14.clone.face_hot) | copy-start | bytes 2359300
  40.2 40.9 %copy-start = (f32[256,1024]{1,0:T(8,128)S(1)}, f32[256,1024]{1,0:T(8,128)}, u32[]{:S(2)}) copy-start(f32[256,1024]{1,0:T(8,128)} %get-tuple-element.37.folded) | copy-start | bytes 3145732
  40.2 40.9 %copy-start.1 = (f32[25,64,128]{2,1,0:T(8,128)S(1)}, f32[25,64,128]{2,1,0:T(8,128)}, u32[]{:S(2)}) copy-start(f32[25,64,128]{2,1,0:T(8,128)} %get-tuple-element.38.grad_local) | copy-start | bytes 2457604
  40.2 40.9 %copy-start.3 = (bf16[128,256]{1,0:T(8,128)(2,1)S(1)}, bf16[128,256]{1,0:T(8,128)(2,1)}, u32[]{:S(2)}) copy-start(bf16[128,256]{1,0:T(8,128)(2,1)} %constant.15.clone.inner_hot) | copy-start | bytes 196612
  40.2 40.9 %copy-start.4 = (s32[1,1,4,4]{3,2,1,0:T(4,128)S(1)}, s32[1,1,4,4]{3,2,1,0:T(4,128)}, u32[]{:S(2)}) copy-start(s32[1,1,4,4]{3,2,1,0:T(4,128)} %sends.1) | copy-start | bytes 196
  44.7 26.8 %all-to-all-start.1 = ((bf16[16,48,128]{2,1,0:T(8,128)(2,1)}), bf16[16,48,128]{2,1,0:T(8,128)(2,1)S(1)}, u32[]{:S(2)}, u32[]{:S(2)}) async-start(bf16[16,48,128]{2,1,0:T(8,128)(2,1)} %broadcast_in_dim.4), calls=%async_computation.1 | async-start | bytes 393216 | tf_op jit(solution)/shard_map/all_to_all | solution.py:521
  59.0 12.6 %collective-permute-start.4 = (bf16[2,64,128]{2,1,0:T(8,128)(2,1)}, bf16[2,64,128]{2,1,0:T(8,128)(2,1)S(1)}, u32[]{:S(2)}, u32[]{:S(2)}) collective-permute-start(bf16[2,64,128]{2,1,0:T(8,128)(2,1)} %get-tuple-element.45), channel_id=1, source_target_pairs={{8,16},{12,20},{24,32},{28,36},{40,48},{44,52},{56,64},{60,68},{72... | collective-permute-start | bytes 98312 | tf_op jit(solution)/shard_map/ppermute | solution.py:546
  59.7 11.9 %collective-permute-start.5 = (bf16[2,64,128]{2,1,0:T(8,128)(2,1)}, bf16[2,64,128]{2,1,0:T(8,128)(2,1)S(1)}, u32[]{:S(2)}, u32[]{:S(2)}) collective-permute-start(bf16[2,64,128]{2,1,0:T(8,128)(2,1)} %get-tuple-element.46), channel_id=1, source_target_pairs={{0,8},{4,12},{16,24},{20,28},{32,40},{36,44},{48,56},{52,60},{64,7... | collective-permute-start | bytes 98312 | tf_op jit(solution)/shard_map/ppermute | solution.py:546
  63.7 7.9 %collective-permute-start.6 = (bf16[2,64,128]{2,1,0:T(8,128)(2,1)}, bf16[2,64,128]{2,1,0:T(8,128)(2,1)S(1)}, u32[]{:S(2)}, u32[]{:S(2)}) collective-permute-start(bf16[2,64,128]{2,1,0:T(8,128)(2,1)} %get-tuple-element.47), channel_id=1, source_target_pairs={{4,8},{12,16},{20,24},{28,32},{36,40},{44,48},{52,56},{60,64},{68,... | collective-permute-start | bytes 98312 | tf_op jit(solution)/shard_map/ppermute | solution.py:546
  66.6 5.0 %collective-permute-start.7 = (bf16[2,64,128]{2,1,0:T(8,128)(2,1)}, bf16[2,64,128]{2,1,0:T(8,128)(2,1)S(1)}, u32[]{:S(2)}, u32[]{:S(2)}) collective-permute-start(bf16[2,64,128]{2,1,0:T(8,128)(2,1)} %get-tuple-element.48), channel_id=1, source_target_pairs={{0,4},{8,12},{16,20},{24,28},{32,36},{40,44},{48,52},{56,60},{64,6... | collective-permute-start | bytes 98312 | tf_op jit(solution)/shard_map/ppermute | solution.py:546
  72.4 18.7 %all-to-all-start.2 = ((bf16[32,48,128]{2,1,0:T(8,128)(2,1)}), bf16[32,48,128]{2,1,0:T(8,128)(2,1)S(1)}, u32[]{:S(2)}, u32[]{:S(2)}) async-start(bf16[32,48,128]{2,1,0:T(8,128)(2,1)} %broadcast_in_dim.5), calls=%async_computation.2 | async-start | bytes 786432 | tf_op jit(solution)/shard_map/all_to_all | solution.py:535
